TPU v7x, 128 devices: a whole 4x4x4 slice. The times are simulated.
128 devices in a mesh: front: 8 (over z, core), grid: 16 (over x, y).
Axes of the slice: x: 4, y: 4, z: 4, core: 2. Of those that a mesh axis runs over, the one named last changes fastest.
Arguments:
- front_entries: float32 [8, 2, 16, 128, 4096], P('front', None, 'grid'), may hold values from -1 to 2.5, as said below
- child_tiles: float32 [8, 2048, 128, 128], P('front', 'grid'), may hold values from -6 to 6
- tile_owner: int32 [8, 2048, 1], P('front', 'grid'), may hold values from 0 to 127; in each aligned block of 128 rows (0 to 127, 128 to 255, ..., all dimensions but the last counted through in order) at most 2 rows name the same one
- tile_rows: int32 [8, 2048], P('front', 'grid'), may hold values from 0 to 1
- tile_picks: int32 [8, 2048], P('front', 'grid'), may hold values from 0 to 31
Outputs:
- factored: float32 [8, 2, 16, 128, 4096], P('front', None, 'grid')
Inputs may be any that keep to these rules, and one draw needn't show every extreme that they name: `tile_owner`: destination device is front index * 16 + grid index. Each device sends at most 2 of its tiles to any one device, and some device sends exactly 2 to one device. `front_entries`: entries above each front's diagonal are zero; the leading 2 * 512 rows and columns of each front form a positive definite block.
All inputs are finite; a program needn't handle non-finite values.
Results may differ from a plain program's by a relative error of at most 0.0001.
Values sent between devices are 32-bit elements; how exact they have to be, the bound alone decides.
No kernel may reach another device: no remote copies, remote signals or barrier semaphores. Data moves between devices by JAX's collectives and lax.ppermute only.
A program may use at most 192 MiB of HBM per device.

v0:
```python
import jax
import jax.numpy as jnp
from jax import lax
from jax.sharding import PartitionSpec as P

BLOCK = 128
PANEL = 512
PANELS = 2


highest = lax.Precision.HIGHEST


def factor_block(block):
    symmetric = jnp.tril(block) + jnp.tril(block, -1).T
    return jnp.linalg.cholesky(symmetric)


def panel_rows(source, row_index, factor, first_col, last_col):
    solved = jax.scipy.linalg.solve_triangular(factor, source.T, lower=True).T
    inside = factor[jnp.clip(row_index - first_col, 0, PANEL - 1)]
    return jnp.where(
        (row_index >= last_col)[:, None],
        solved,
        jnp.where((row_index >= first_col)[:, None], inside, 0.0),
    )


def extend_add(matrix, arrived, labels_in, position, groups, blocks_dev, lead_blocks):
    tile_data = arrived.reshape(-1, BLOCK, BLOCK)
    labels_in = labels_in.reshape(-1, 2)
    filled = labels_in[:, 0] >= 0
    local_rows = jnp.maximum(labels_in[:, 0], 0)
    shifted = local_rows + (local_rows * groups + position < lead_blocks).astype(jnp.int32)
    row_block = shifted * groups + position
    col_block = jnp.maximum(labels_in[:, 1], 0) % (row_block + 1)
    tile_data = jnp.where(filled[:, None, None], tile_data, 0.0)
    blocked = matrix.reshape(blocks_dev, BLOCK, -1, BLOCK)
    blocked = blocked.at[shifted, :, col_block, :].add(tile_data)
    return blocked.reshape(matrix.shape)


def local(front_entries, child_tiles, tile_owner, tile_rows, tile_picks):
    groups = lax.axis_size("grid")
    fronts = lax.axis_size("front")
    devices = groups * fronts
    position = lax.axis_index("grid")
    shard_rows = front_entries[0, :, 0]
    blocks_dev = shard_rows.shape[0]
    front_order = shard_rows.shape[2]
    lead_blocks = PANELS * PANEL // BLOCK
    tiles_held = child_tiles.shape[1]
    slots = max(2, (2 * tiles_held + devices - 1) // devices)
    row_index = (
        (jnp.arange(blocks_dev)[:, None] * groups + position) * BLOCK + jnp.arange(BLOCK)[None, :]
    ).reshape(-1)
    col_index = jnp.arange(front_order)
    matrix = shard_rows.reshape(-1, front_order)
    tile_data = child_tiles[0]
    owners = tile_owner[0, :, 0]
    onehot = (owners[:, None] == jnp.arange(devices)[None, :]).astype(jnp.int32)
    earlier = jnp.cumsum(onehot, axis=0) - onehot
    slot_index = jnp.sum(earlier * onehot, axis=1)
    outgoing = (
        jnp.zeros((devices, slots, BLOCK, BLOCK), jnp.float32).at[owners, slot_index].set(tile_data)
    )
    labels = jnp.stack([tile_rows[0], tile_picks[0]], axis=1)
    out_labels = jnp.full((devices, slots, 2), -1, jnp.int32).at[owners, slot_index].set(labels)
    arrived, labels_in = (
        lax.all_to_all(outgoing, ("front", "grid"), split_axis=0, concat_axis=0, tiled=True),
        lax.all_to_all(out_labels, ("front", "grid"), split_axis=0, concat_axis=0, tiled=True),
    )
    matrix = extend_add(matrix, arrived, labels_in, position, groups, blocks_dev, lead_blocks)
    for panel_step in range(PANELS):
        first_col = panel_step * PANEL
        last_col = first_col + PANEL
        panel_cols = matrix[:, first_col:last_col]
        column_slab = lax.all_gather(
            panel_cols.reshape(blocks_dev, 1, BLOCK, PANEL), "grid", axis=1, tiled=True
        )
        column_slab = column_slab.reshape(-1, PANEL)
        factor = factor_block(column_slab[first_col:last_col])
        all_rows = panel_rows(column_slab, jnp.arange(front_order), factor, first_col, last_col)
        own_rows = lax.dynamic_slice_in_dim(
            all_rows.reshape(blocks_dev, groups, BLOCK, PANEL), position, 1, 1
        )
        own_rows = own_rows.reshape(-1, PANEL)
        update = jnp.dot(own_rows, all_rows.T, precision=highest)
        trailing = (row_index[:, None] >= last_col) & (col_index[None, :] >= last_col)
        matrix = jnp.where(trailing, matrix - update, matrix)
        matrix = matrix.at[:, first_col:last_col].set(own_rows)
    matrix = jnp.where(col_index[None, :] <= row_index[:, None], matrix, 0.0)
    return matrix.reshape(1, blocks_dev, 1, BLOCK, front_order)


def solution(mesh):
    return jax.shard_map(
        local,
        mesh=mesh,
        in_specs=(
            P("front", None, "grid", None, None),
            P("front", "grid", None, None),
            P("front", "grid", None),
            P("front", "grid"),
            P("front", "grid"),
        ),
        out_specs=P("front", None, "grid", None, None),
        check_vma=False,
    )
```

profile of v0, /device:TPU:0, one launch (start us, length us, event | category | flops | bytes accessed | tf_op | source)
XLA Modules:
  0.0 1006.2 jit_solution(12154602690803013216)
XLA Ops:
  10.4 13.8 %scatter_fusion = s32[128,2,2]{2,1,0:T(2,128)} fusion(s32[128,2,2]{2,1,0:T(2,128)} %broadcast_in_dim.81, s32[128]{0:T(128)S(1)} %fusion.82, s32[128,2]{1,0:T(8,128)S(1)} %copy.54), kind=kCustom, calls=%fused_computation.2 | custom fusion | bytes 4096 | tf_op jit(solution)/shard_map/scatter | solution.py:68
  24.2 11.1 %all-to-all-start = ((s32[128,2,2]{2,1,0:T(2,128)}), s32[128,2,2]{2,1,0:T(2,128)S(1)}, u32[]{:S(2)}, u32[]{:S(2)}) async-start(s32[128,2,2]{2,1,0:T(2,128)} %scatter_fusion), calls=%async_computation | async-start | bytes 262144 | tf_op jit(solution)/shard_map/all_to_all | solution.py:71
  35.4 7.8 broadcast_in_dim.83
  43.2 24.7 %scatter_fusion.1 = f32[128,2,128,128]{3,2,1,0:T(8,128)} fusion(f32[128,2,128,128]{3,2,1,0:T(8,128)} %broadcast_in_dim.83, s32[128]{0:T(128)S(1)} %fusion.82, f32[128,128,128]{2,1,0:T(8,128)} %bitcast.205), kind=kCustom, calls=%fused_computation.3 | custom fusion | bytes 25166848 | tf_op jit(solution)/shard_map/scatter | solution.py:65
  68.0 10.2 %all-to-all-start.1 = ((f32[128,2,128,128]{3,2,1,0:T(8,128)}), f32[128,2,128,128]{3,2,1,0:T(8,128)}, u32[]{:S(2)}, u32[]{:S(2)}) async-start(f32[128,2,128,128]{3,2,1,0:T(8,128)} %scatter_fusion.1), calls=%async_computation.1 | async-start | bytes 33554432 | tf_op jit(solution)/shard_map/all_to_all | solution.py:70
  78.4 5.6 copy.53
  84.0 5.7 copy.57
  90.2 226.1 %all-to-all-done.1 = f32[128,2,128,128]{3,2,1,0:T(8,128)} async-done(((f32[128,2,128,128]{3,2,1,0:T(8,128)}), f32[128,2,128,128]{3,2,1,0:T(8,128)}, u32[]{:S(2)}, u32[]{:S(2)}) %all-to-all-start.1) | async-done | bytes 16777248 | tf_op jit(solution)/shard_map/all_to_all | solution.py:70
  316.3 11.6 %bitcast_select_fusion = f32[256,128,128]{2,1,0:T(8,128)} fusion(f32[128,2,128,128]{3,2,1,0:T(8,128)} %all-to-all-done.1, pred[256]{0:T(512)(128)(4,1)S(1)} %compare_reduce_fusion), kind=kLoop, calls=%fused_computation.9 | loop fusion | flops 4194304 | bytes 33554688 | tf_op jit(solution)/shard_map/jit(_where)/select_n | solution.py:37
  327.8 54.7 %scatter_fusion.2 = f32[2,128,32,128]{3,1,2,0:T(8,128)} fusion(f32[2,128,32,128]{3,1,2,0:T(8,128)} %copy.57, s32[256]{0:T(256)S(1)} %bitcast.193, f32[256,128,128]{2,1,0:T(8,128)} %bitcast_select_fusion), kind=kCustom, calls=%fused_computation.4 | custom fusion | flops 4194304 | bytes 50333696 | tf_op jit(solution)/shard_map/scatter-add | solution.py:39
  382.5 4.6 copy.58
  387.1 3.9 copy.110
  392.8 71.4 %all-gather.3.cloned.1.call-done = f32[2,16,128,512]{3,2,0,1:T(8,128)} async-done(((f32[2,1,128,512]{3,2,0,1:T(8,128)}), f32[2,16,128,512]{3,2,0,1:T(8,128)}) %all-gather.3.cloned.1.call-update) | async-done | bytes 8388624 | tf_op jit(solution)/shard_map/all_gather | solution.py:78
  464.2 10.6 %copy.59 = f32[2,16,128,512]{2,1,0,3:T(8,128)} copy(f32[2,16,128,512]{3,2,0,1:T(8,128)} %all-gather.3.cloned.1.call-done) | data formatting | bytes 16777216 | tf_op jit(solution)/shard_map/all_gather | solution.py:78
  474.8 11.5 %copy.111 = f32[64,8,32,128]{3,1,2,0:T(8,128)S(1)} copy(f32[64,8,32,128]{3,2,1,0:T(8,128)} %bitcast.192) | data formatting | bytes 16777216
  492.0 12.1 %cholesky.286 = f32[128,128]{1,0:T(8,128)S(1)} custom-call(f32[128,128]{1,0:T(8,128)S(1)} %copy.63), custom_call_target="Cholesky" | custom-call | tf_op jit(solution)/shard_map/jit(cholesky)/cholesky | solution.py:16
  504.2 9.8 custom-call.33
  515.1 11.7 %cholesky.305 = f32[128,128]{1,0:T(8,128)S(1)} custom-call(f32[128,128]{1,0:T(8,128)S(1)} %copy.65), custom_call_target="Cholesky" | custom-call | tf_op jit(solution)/shard_map/jit(cholesky)/cholesky | solution.py:16
  526.9 9.8 custom-call.34
  537.6 11.9 %cholesky.326 = f32[128,128]{1,0:T(8,128)S(1)} custom-call(f32[128,128]{1,0:T(8,128)S(1)} %copy.67), custom_call_target="Cholesky" | custom-call | tf_op jit(solution)/shard_map/jit(cholesky)/cholesky | solution.py:16
  550.3 9.8 custom-call.35
  560.9 11.7 %cholesky.343 = f32[128,128]{1,0:T(8,128)S(1)} custom-call(f32[128,128]{1,0:T(8,128)S(1)} %copy.69), custom_call_target="Cholesky" | custom-call | tf_op jit(solution)/shard_map/jit(cholesky)/cholesky | solution.py:16
  576.8 8.3 while.6
  585.2 39.7 %custom-call.36 = f32[4,128,128]{1,2,0:T(8,128)S(1)} custom-call(f32[4,128,128]{2,1,0:T(8,128)S(1)} %get-tuple-element.45), custom_call_target="InvertDiagBlocksLowerTriangular" | custom-call | tf_op jit(solution)/shard_map/jit(_solve_triangular)/triangular_solve | solution.py:20
  628.4 3.6 convolution_subtract_fusion.3
  634.0 4.8 convolution_subtract_fusion.2
  640.8 6.6 fusion.17
  650.6 16.8 %gather_fusion = f32[4096,512]{1,0:T(8,128)} fusion(f32[512,512]{1,0:T(8,128)S(1)} %get-tuple-element.66, s32[4096]{0:T(1024)S(1)} %broadcast_clamp_fusion.1), kind=kCustom, calls=%fused_computation | custom fusion | bytes 16793600 | tf_op jit(solution)/shard_map/gather | solution.py:21
  667.4 8.9 copy.70
  676.3 6.0 fusion.43
  686.8 12.3 %subtract_select_fusion.1 = f32[256,4096]{1,0:T(8,128)S(1)} fusion(f32[256,512]{1,0:T(8,128)S(1)} %bitcast.211, pred[4096]{0:T(1024)(128)(4,1)S(1)} %iota_compare_fusion.6, pred[256]{0:T(512)(128)(4,1)S(1)} %get-tuple-element.96, f32[4096,512]{0,1:T(8,128)} %copy.70, f32[128,4096]{1,0:T(8,128)} %fusion.64, f32[128,4096]{1,0:T(8,128)} %copy-done.4, ...), kind=kOutput, calls=%fused_computation.28 | convolution fusion | flops 6453985280 | bytes 25694464 | tf_op jit(solution)/shard_map/dot_general | solution.py:88
  704.6 68.7 %all-gather.5.cloned.1.call-done = f32[2,16,128,512]{3,2,1,0:T(8,128)} async-done(((f32[2,1,128,512]{3,2,1,0:T(8,128)}), f32[2,16,128,512]{3,2,1,0:T(8,128)}) %all-gather.5.cloned.1.call-update) | async-done | bytes 8388624 | tf_op jit(solution)/shard_map/all_gather | solution.py:78
  777.1 11.7 %cholesky.358 = f32[128,128]{1,0:T(8,128)S(1)} custom-call(f32[128,128]{1,0:T(8,128)S(1)} %cholesky.439), custom_call_target="Cholesky" | custom-call | tf_op jit(solution)/shard_map/jit(cholesky)/cholesky | solution.py:16
  788.9 9.8 custom-call.37
  799.4 11.7 %cholesky.377 = f32[128,128]{1,0:T(8,128)S(1)} custom-call(f32[128,128]{1,0:T(8,128)S(1)} %cholesky.443), custom_call_target="Cholesky" | custom-call | tf_op jit(solution)/shard_map/jit(cholesky)/cholesky | solution.py:16
  812.5 9.9 custom-call.38
  823.1 11.7 %cholesky.398 = f32[128,128]{1,0:T(8,128)S(1)} custom-call(f32[128,128]{1,0:T(8,128)S(1)} %cholesky.448), custom_call_target="Cholesky" | custom-call | tf_op jit(solution)/shard_map/jit(cholesky)/cholesky | solution.py:16
  835.5 9.8 custom-call.39
  846.0 12.1 %cholesky.415 = f32[128,128]{1,0:T(8,128)S(1)} custom-call(f32[128,128]{1,0:T(8,128)S(1)} %convolution_subtract_fusion.8), custom_call_target="Cholesky" | custom-call | tf_op jit(solution)/shard_map/jit(cholesky)/cholesky | solution.py:16
  861.7 7.7 while.7
  869.4 39.3 %custom-call.40 = f32[4,128,128]{1,2,0:T(8,128)S(1)} custom-call(f32[4,128,128]{2,1,0:T(8,128)S(1)} %get-tuple-element.46), custom_call_target="InvertDiagBlocksLowerTriangular" | custom-call | tf_op jit(solution)/shard_map/jit(_solve_triangular)/triangular_solve | solution.py:20
  912.3 5.2 convolution_subtract_fusion.1
  919.5 9.7 convolution_subtract_fusion
  931.2 13.4 %fusion.14 = f32[128,4096]{0,1:T(8,128)S(1)} fusion(f32[128,4096]{1,0:T(8,128)S(1)} %fusion.59, f32[128,4096]{1,0:T(8,128)S(1)} %fusion.61, f32[128,4096]{1,0:T(8,128)S(1)} %fusion.27, f32[512,4096]{0,1:T(8,128)} %bitcast.202, f32[512,512]{1,0:T(8,128)} %copy-done.6), kind=kOutput, calls=%fused_computation.33 | convolution fusion | flops 2419589120 | bytes 10682368 | tf_op jit(solution)/shard_map/jit(_solve_triangular)/triangular_solve | solution.py:20
  947.9 16.8 %gather_fusion.1 = f32[4096,512]{1,0:T(8,128)} fusion(f32[512,512]{1,0:T(8,128)S(1)} %get-tuple-element.64, s32[4096]{0:T(1024)S(1)} %broadcast_clamp_fusion), kind=kCustom, calls=%fused_computation.1 | custom fusion | bytes 16793600 | tf_op jit(solution)/shard_map/gather | solution.py:21
  964.7 8.9 copy.79
  973.6 6.1 fusion.89
  984.1 11.5 %subtract_select_fusion = f32[256,4096]{1,0:T(8,128)S(1)} fusion(f32[256,4096]{1,0:T(8,128)} %copy-done.8, f32[256,512]{1,0:T(8,128)S(1)} %bitcast.209, pred[4096]{0:T(1024)(128)(4,1)S(1)} %iota_compare_fusion.7, pred[256]{0:T(512)(128)(4,1)S(1)} %get-tuple-element.95, f32[128,4096]{1,0:T(8,128)} %fusion.58, f32[128,4096]{1,0:T(8,128)} %copy-done.3, ...), kind=kOutput, calls=%fused_computation.27 | convolution fusion | flops 6456082432 | bytes 25698560 | tf_op jit(solution)/shard_map/dot_general | solution.py:88
  (147 shorter events, 81.1 us)
Async XLA Ops:
  24.2 43.7 %all-to-all-start = ((s32[128,2,2]{2,1,0:T(2,128)}), s32[128,2,2]{2,1,0:T(2,128)S(1)}, u32[]{:S(2)}, u32[]{:S(2)}) async-start(s32[128,2,2]{2,1,0:T(2,128)} %scatter_fusion), calls=%async_computation | async-start | bytes 262144 | tf_op jit(solution)/shard_map/all_to_all | solution.py:71
  68.0 248.3 %all-to-all-start.1 = ((f32[128,2,128,128]{3,2,1,0:T(8,128)}), f32[128,2,128,128]{3,2,1,0:T(8,128)}, u32[]{:S(2)}, u32[]{:S(2)}) async-start(f32[128,2,128,128]{3,2,1,0:T(8,128)} %scatter_fusion.1), calls=%async_computation.1 | async-start | bytes 33554432 | tf_op jit(solution)/shard_map/all_to_all | solution.py:70
  78.2 385.9 %all-gather.3.cloned.1.call-start = ((), (), s32[]{:S(2)}) async-start(), calls=%async_computation.2 | async-start | bytes 8912896 | tf_op jit(solution)/shard_map/all_gather | solution.py:78
  387.1 3.9 copy-start.5
  392.0 381.3 %all-gather.5.cloned.1.call-start = ((), (), s32[]{:S(2)}) async-start(), calls=%async_computation.3 | async-start | bytes 8912896 | tf_op jit(solution)/shard_map/all_gather | solution.py:78
  486.2 3.2 copy-start
  585.2 39.7 %copy-start.7 = (f32[512,512]{1,0:T(8,128)}, f32[512,512]{1,0:T(8,128)S(1)}, u32[]{:S(2)}) copy-start(f32[512,512]{1,0:T(8,128)S(1)} %get-tuple-element.198) | copy-start | bytes 3145732
  633.9 6.8 copy-start.2
  640.7 6.6 copy-start.4
  699.9 2.0 copy-start.8
  869.4 39.3 %copy-start.6 = (f32[512,512]{1,0:T(8,128)}, f32[512,512]{1,0:T(8,128)S(1)}, u32[]{:S(2)}) copy-start(f32[512,512]{1,0:T(8,128)S(1)} %get-tuple-element.197) | copy-start | bytes 3145732
  919.4 11.7 %copy-start.1 = (f32[128,4096]{1,0:T(8,128)}, f32[128,4096]{1,0:T(8,128)S(1)}, u32[]{:S(2)}) copy-start(f32[128,4096]{1,0:T(8,128)S(1)} %fusion.61) | copy-start | bytes 6291460
  931.2 13.4 %copy-start.3 = (f32[128,4096]{1,0:T(8,128)}, f32[128,4096]{1,0:T(8,128)S(1)}, u32[]{:S(2)}) copy-start(f32[128,4096]{1,0:T(8,128)S(1)} %fusion.59) | copy-start | bytes 6291460
Sparse Core Ops, SparseCore 0:
  392.1 72.0 all-gather.2
  702.9 70.2 all-gather.4
where the time goes:
time: 1010 us
  waiting for transfers between devices  366 us (36%)
  other arithmetic  331 us (33%)
  local copies, waits for them, and re-layouts  175 us (17%)
  matrix products  92.7 us (9%)
  starting transfers between devices  21.6 us (2%)
  between operations  19.6 us (2%)
    all_to_all x1, waiting for transfers between devices, local(): lax.all_to_all(outgoing, ('front', 'grid'), split_axis=0, concat_axis=0,...  226 us
    another operation x29, other arithmetic, factor_block(): return jnp.linalg.cholesky(symmetric)  159 us
    all_gather x2, waiting for transfers between devices, local(): lax.all_gather(panel_cols.reshape(blocks_dev, 1, BLOCK, PANEL), 'grid', a...  140 us
    another operation x5, other arithmetic, panel_rows(): solved = jax.scipy.linalg.solve_triangular(factor, source.T, lower=True).T  79.6 us
    another operation x14, matrix products, panel_rows(): solved = jax.scipy.linalg.solve_triangular(factor, source.T, lower=True).T  64.6 us
    scatter-add x1, other arithmetic, extend_add(): blocked = blocked.at[shifted, :, col_block, :].add(tile_data)  54.7 us
    gather x4, local copies, waits for them, and re-layouts, panel_rows(): inside = factor[jnp.clip(row_index - first_col, 0, PANEL - 1)]  51.5 us
    unnamed x25, local copies, waits for them, and re-layouts  30.1 us
  transfers between devices with their start and end apart: 4, of which 3 were waited for; matrix products, arithmetic and copies ran while one was open for 5% of the time, Pallas kernels for 0%

commit v1 on v0

v1 whole, which is shorter than its diff:
```python
import functools
import jax
import jax.numpy as jnp
from jax import lax
from jax.experimental import pallas as pl
from jax.experimental.pallas import tpu as pltpu
from jax.sharding import PartitionSpec as P

BLOCK = 128
LEAD = 1024
LB = LEAD // BLOCK
FRONTS = 8
GRID = 16
SIDE = 4
DEVICES = FRONTS * GRID
FB = 32
TB = FB - LB
TILES = 128
PBINS = FRONTS * TB * LB
TSLOTS = 32
TBINS = DEVICES * TSLOTS
BINS = PBINS + TBINS
SUB = 8
ACCS = 8
UNROLL = 32
VMEM_LIMIT = 60 << 20

highest = lax.Precision.HIGHEST
ANY = pl.BlockSpec(memory_space=pl.ANY)
VMEM = pl.BlockSpec(memory_space=pltpu.VMEM)
SMEM = pl.BlockSpec(memory_space=pltpu.SMEM)


def tdot(a, b):
    return lax.dot_general(
        a, b, (((0,), (0,)), ((), ())), precision=highest, preferred_element_type=jnp.float32
    )


def gather_small(values, axis, size):
    bit = 1
    while bit < size:
        other = lax.ppermute(values, axis, [(i, i ^ bit) for i in range(size)])
        upper = (lax.axis_index(axis) & bit) != 0
        values = jnp.where(
            upper, jnp.concatenate([other, values], 0), jnp.concatenate([values, other], 0)
        )
        bit *= 2
    return values


def ring_perm(along_x, step):
    def to(i):
        x, y = divmod(i, SIDE)
        return ((x + step) % SIDE) * SIDE + y if along_x else x * SIDE + (y + step) % SIDE

    return [(i, to(i)) for i in range(GRID)]


def ring(block, along_x):
    up, down = ring_perm(along_x, 1), ring_perm(along_x, -1)
    half = block.shape[0] // 2
    from_prev = lax.ppermute(block, "grid", up)
    from_next = lax.ppermute(block, "grid", down)
    far_a = lax.ppermute(from_prev[:half], "grid", up)
    far_b = lax.ppermute(from_next[half:], "grid", down)
    return block, from_next, far_a, far_b, from_prev


def gather_rings(rows):
    half = rows.shape[0] // 2
    out = []
    for part, first_x in ((rows[:half], True), (rows[half:], False)):
        own, nxt, far_a, far_b, prv = ring(part, first_x)
        line = jnp.stack([own, nxt, jnp.concatenate([far_a, far_b], 0), prv], 0)
        out.extend(ring(line, not first_x))
    return out


def copy_pieces(pieces, dst, sem, position, start_row, rows):
    x, y = position // SIDE, position % SIDE
    half = rows // 2
    copies = []
    for h in range(2):
        own, nxt, far_a, far_b, prv = pieces[5 * h : 5 * h + 5]
        for outer in range(SIDE):
            for inner in range(SIDE):
                if outer == 2:
                    src = (far_a if inner < 2 else far_b).at[inner % 2]
                else:
                    src = (own, nxt, None, prv)[outer].at[inner]
                dx, dy = (inner, outer) if h == 0 else (outer, inner)
                g = ((x + dx) % SIDE) * SIDE + (y + dy) % SIDE
                copies.append(
                    pltpu.make_async_copy(
                        src,
                        dst.at[
                            pl.ds(start_row + h * half, half),
                            pl.ds(pl.multiple_of(g * SUB, SUB), SUB),
                            :,
                        ],
                        sem.at[h * 16 + outer * 4 + inner],
                    )
                )
    return copies


def combine_kernel(bins, x, panel, trail, *accs):
    for acc in accs:
        acc[...] = jnp.zeros_like(acc)

    def body(b, carry):
        base = pl.multiple_of(b * UNROLL, UNROLL)
        for first in range(0, UNROLL, ACCS):
            at = [bins[base + first + m] for m in range(ACCS)]
            rows = [x[pl.ds(base + first + m, 1), :] for m in range(ACCS)]
            sums = [accs[m][pl.ds(at[m], 1), :] + rows[m] for m in range(ACCS)]
            for m in range(ACCS):
                accs[m][pl.ds(at[m], 1), :] = sums[m]
        return carry

    lax.fori_loop(0, x.shape[0] // UNROLL, body, 0)
    step = 256

    def finish(out, offset):
        def add(b, carry):
            start = pl.multiple_of(b * step, step)
            total = accs[0][pl.ds(offset + start, step), :]
            for acc in accs[1:]:
                total = total + acc[pl.ds(offset + start, step), :]
            out[pl.ds(start, step), :] = total
            return carry

        lax.fori_loop(0, out.shape[0] // step, add, 0)

    finish(panel, 0)
    finish(trail, PBINS)


def combine(bins, rows):
    return pl.pallas_call(
        combine_kernel,
        out_shape=[
            jax.ShapeDtypeStruct((PBINS, BLOCK), jnp.float32),
            jax.ShapeDtypeStruct((TBINS, BLOCK), jnp.float32),
        ],
        in_specs=[SMEM, VMEM],
        out_specs=[VMEM, VMEM],
        scratch_shapes=[pltpu.VMEM((BINS, BLOCK), jnp.float32)] * ACCS,
        compiler_params=pltpu.CompilerParams(vmem_limit_bytes=VMEM_LIMIT),
        name="combine",
    )(bins, rows)


def factor_rows(rows, first, sub):
    for j in range(SUB):
        scale = lax.rsqrt(rows[j : j + 1, first + j : first + j + 1])
        pivot = rows[j : j + 1, :] * scale
        weight = jnp.where(sub > j, rows[:, first + j : first + j + 1] * scale, 0.0)
        rows = jnp.where(sub == j, pivot, rows - weight * pivot)
    return rows


def factor_kernel(position, *refs):
    pieces, (own_rows, inverse, entries, work, diag, pair, sem) = refs[:10], refs[10:]
    copies = copy_pieces(pieces, entries, sem, position[0], 0, LB)
    for copy in copies:
        copy.start()
    for copy in copies:
        copy.wait()
    sub = lax.broadcasted_iota(jnp.int32, (SUB, 1), 0)
    row = lax.broadcasted_iota(jnp.int32, (BLOCK, BLOCK), 0)
    col = lax.broadcasted_iota(jnp.int32, (BLOCK, BLOCK), 1)
    eye = jnp.where(row == col, 1.0, 0.0)
    for r in range(LB):
        for c in range(r + 1):
            block = entries[r, :, c * BLOCK : (c + 1) * BLOCK]
            if r == c:
                block = jnp.where(col <= row, block, 0.0)
                block = block + jnp.where(col < row, block, 0.0).T
                work[r * BLOCK : (r + 1) * BLOCK, r * BLOCK : (r + 1) * BLOCK] = block
            else:
                work[c * BLOCK : (c + 1) * BLOCK, r * BLOCK : (r + 1) * BLOCK] = block.T

    def step(k, carry):
        at = pl.ds(pl.multiple_of(k * BLOCK, BLOCK), BLOCK)
        pair[:, :BLOCK] = work[at, at]
        pair[:, BLOCK:] = eye
        for q in range(BLOCK // SUB):
            first = SUB * q
            rows = pair[first : first + SUB, :]
            if q > 0:
                rows = rows - tdot(pair[0:first, first : first + SUB], pair[0:first, :])
            pair[first : first + SUB, :] = factor_rows(rows, first, sub)
        block_inverse = pair[:, BLOCK:]
        diag[k] = pair[:, :BLOCK]
        work[at, :] = jnp.dot(
            block_inverse, work[at, :], precision=highest, preferred_element_type=jnp.float32
        )
        work[at, at] = block_inverse

        def update(i, inner):
            below = pl.ds(pl.multiple_of(i * BLOCK, BLOCK), BLOCK)
            work[below, at] = jnp.zeros((BLOCK, BLOCK), jnp.float32)
            work[below, :] = work[below, :] - tdot(work[at, below], work[at, :])
            return inner

        lax.fori_loop(k + 1, LB, update, 0)
        return carry

    lax.fori_loop(0, LB, step, 0)
    for k in range(LB):
        at = slice(k * BLOCK, (k + 1) * BLOCK)
        inverse[at, : (k + 1) * BLOCK] = work[at, : (k + 1) * BLOCK]
        if k + 1 < LB:
            inverse[at, (k + 1) * BLOCK :] = jnp.zeros((BLOCK, LEAD - (k + 1) * BLOCK), jnp.float32)
    mine = jnp.minimum(position[0], LB - 1)
    mine_at = pl.ds(pl.multiple_of(mine * BLOCK, BLOCK), BLOCK)
    for k in range(LB):
        at = slice(k * BLOCK, (k + 1) * BLOCK)
        block = jnp.where(k == mine, jnp.where(row <= col, diag[k], 0.0), work[at, mine_at])
        own_rows[:, at] = jnp.where(k <= mine, block, 0.0).T


def factor(position, pieces):
    return pl.pallas_call(
        factor_kernel,
        out_shape=[
            jax.ShapeDtypeStruct((BLOCK, LEAD), jnp.float32),
            jax.ShapeDtypeStruct((LEAD, LEAD), jnp.float32),
        ],
        in_specs=[SMEM] + [ANY] * 10,
        out_specs=[VMEM, VMEM],
        scratch_shapes=[
            pltpu.VMEM((LB, BLOCK, LEAD), jnp.float32),
            pltpu.VMEM((LEAD, LEAD), jnp.float32),
            pltpu.VMEM((LB, BLOCK, BLOCK), jnp.float32),
            pltpu.VMEM((BLOCK, 2 * BLOCK), jnp.float32),
            pltpu.SemaphoreType.DMA((32,)),
        ],
        compiler_params=pltpu.CompilerParams(vmem_limit_bytes=VMEM_LIMIT),
        cost_estimate=pl.CostEstimate(flops=120 * 10**9, bytes_accessed=20 << 20, transcendentals=1024),
        name="factor",
    )(position, *pieces)


def split(values):
    high = values.astype(jnp.bfloat16)
    return high, (values - high.astype(jnp.float32)).astype(jnp.bfloat16)


def update_kernel(position, *refs):
    pieces, (entries, lead_rows, extra, out, solved, high, low, sem) = refs[:10], refs[10:]
    g = position[0]
    copies = copy_pieces(pieces, solved, sem, g, 0, TB)
    for copy in copies:
        copy.start()
    for copy in copies:
        copy.wait()

    def halves(b, carry):
        high[b], low[b] = split(solved[b])
        return carry

    lax.fori_loop(0, TB, halves, 0)
    top = jnp.maximum(g - LB, 0)
    bottom = FB // 2 + g - LB
    own_high = jnp.concatenate([high[top], high[bottom]], 0)
    own_low = jnp.concatenate([low[top], low[bottom]], 0)
    out[0, :, :LEAD] = jnp.where(g < LB, lead_rows[...], solved[top])
    out[1, :, :LEAD] = solved[bottom]
    row = lax.broadcasted_iota(jnp.int32, (BLOCK, BLOCK), 0)
    col = lax.broadcasted_iota(jnp.int32, (BLOCK, BLOCK), 1)

    def mul(a, b):
        return lax.dot_general(a, b, (((1,), (1,)), ((), ())), preferred_element_type=jnp.float32)

    for c in range(0, TB, 2):
        col_high = high[c : c + 2].reshape(2 * BLOCK, LEAD)
        col_low = low[c : c + 2].reshape(2 * BLOCK, LEAD)
        product = mul(own_high, col_high) + (mul(own_high, col_low) + mul(own_low, col_high))
        for n in range(2):
            block = LB + c + n
            at = slice(block * BLOCK, (block + 1) * BLOCK)
            for local in range(2):
                row_block = local * (FB // 2) + g
                slot = c + n if local == 1 else jnp.minimum(LB + 1 + g + c + n, TSLOTS - 1)
                value = entries[local, :, at] + extra[slot]
                value = value - product[
                    local * BLOCK : (local + 1) * BLOCK, n * BLOCK : (n + 1) * BLOCK
                ]
                inside = (block * BLOCK + col) <= (row_block * BLOCK + row)
                out[local, :, at] = jnp.where(inside, value, 0.0)


def update(position, pieces, entries, lead_rows, extra):
    return pl.pallas_call(
        update_kernel,
        out_shape=jax.ShapeDtypeStruct(entries.shape, jnp.float32),
        in_specs=[SMEM] + [ANY] * 10 + [VMEM] * 3,
        out_specs=VMEM,
        scratch_shapes=[
            pltpu.VMEM((TB, BLOCK, LEAD), jnp.float32),
            pltpu.VMEM((TB, BLOCK, LEAD), jnp.bfloat16),
            pltpu.VMEM((TB, BLOCK, LEAD), jnp.bfloat16),
            pltpu.SemaphoreType.DMA((32,)),
        ],
        compiler_params=pltpu.CompilerParams(vmem_limit_bytes=VMEM_LIMIT),
        name="update",
    )(position, *pieces, entries, lead_rows, extra)


def destination_bins(owners, local_rows, picks):
    front, g = owners // GRID, owners % GRID
    shifted = local_rows + (local_rows * GRID + g < LB).astype(jnp.int32)
    row_block = shifted * GRID + g
    col_block = picks % (row_block + 1)
    panel = (front * TB + row_block - LB) * LB + col_block
    slot = col_block - LB + jnp.where(row_block < GRID, LB + 1 + g, 0)
    trail = PBINS + (g * FRONTS + front) * TSLOTS + slot
    return jnp.where(col_block < LB, panel, trail)


def local(front_entries, child_tiles, tile_owner, tile_rows, tile_picks):
    both = ("grid", "front")
    g = lax.axis_index("grid")
    position = g.astype(jnp.int32).reshape(1)
    entries = front_entries[0, :, 0]
    panel = entries[:, :, :LEAD].reshape(2, GRID, SUB, LEAD)
    panel = lax.all_to_all(panel, "grid", split_axis=1, concat_axis=1)
    panel = panel.reshape(FB, SUB, LEAD)
    bins = destination_bins(tile_owner[0, :, 0], tile_rows[0], tile_picks[0])
    bins = gather_small(gather_small(bins[None], "front", FRONTS), "grid", GRID).reshape(-1)
    tile_rows_in = lax.all_to_all(child_tiles[0], both, split_axis=1, concat_axis=0)
    lead_rows, inverse = factor(position, gather_rings(panel[:LB]))
    panel_sums, trail_sums = combine(bins, tile_rows_in.reshape(DEVICES * TILES, BLOCK))
    panel_sums = lax.all_to_all(
        panel_sums.reshape(FRONTS, TB, LB, BLOCK), "front", split_axis=0, concat_axis=0
    )
    panel_sums = panel_sums.transpose(1, 0, 2, 3).reshape(TB, SUB, LEAD)
    below = (panel[LB:] + panel_sums).reshape(TB * SUB, LEAD)
    solved = lax.dot_general(below, inverse, (((1,), (1,)), ((), ())), precision=highest)
    pieces = gather_rings(solved.reshape(TB, SUB, LEAD))
    extra = lax.all_to_all(
        trail_sums.reshape(DEVICES, TSLOTS, BLOCK), both, split_axis=0, concat_axis=0
    )
    out = update(position, pieces, entries, lead_rows, extra.transpose(1, 0, 2))
    return out[None, :, None]


def solution(mesh):
    return jax.shard_map(
        local,
        mesh=mesh,
        in_specs=(
            P("front", None, "grid", None, None),
            P("front", "grid", None, None),
            P("front", "grid", None),
            P("front", "grid"),
            P("front", "grid"),
        ),
        out_specs=P("front", None, "grid", None, None),
        check_vma=False,
    )
```

time: 1010 us -> 494 us (0.49)
  other arithmetic: 331 us -> 3.58 us
  waiting for transfers between devices: 366 us -> 177 us
  Pallas kernels: 0 us -> 183 us
  local copies, waits for them, and re-layouts: 175 us -> 29.7 us
  matrix products: 92.7 us -> 6.88 us
  starting transfers between devices: 21.6 us -> 83.7 us
  between operations: 19.6 us -> 0.81 us
    another operation x38 -> x8, other arithmetic: 241 us -> 2.76 us  [gather_rings(): line = jnp.stack([own, nxt, jnp.concatenate([far_a, far_b], 0), prv], 0)]
    all_to_all x2 -> x4, waiting for transfers between devices: 226 us -> 6.18 us  [the longest x1 6.17 us: local(): panel = lax.all_to_all(panel, 'grid', split_axis=1, concat_axis=1)]
    pallas_call x0 -> x3, Pallas kernels: none -> 183 us  [the longest x1 142 us: factor(): pl.pallas_call(factor_kernel, out_shape=[jax.ShapeDtypeStruct((BLOCK, LEA...]
    ppermute x0 -> x39, waiting for transfers between devices: none -> 171 us  [the longest x8 94.2 us: ring(): from_next = lax.ppermute(block, 'grid', down)]
    all_gather x2 -> x0, waiting for transfers between devices: 140 us -> none  [local(): lax.all_gather(panel_cols.reshape(blocks_dev, 1, BLOCK, PANEL), 'grid', a...]
    another operation x26 -> x0, matrix products: 68.8 us -> none  [the longest x14 64.6 us: panel_rows(): solved = jax.scipy.linalg.solve_triangular(factor, source.T, lower=True).T]
    ppermute x0 -> x39, starting transfers between devices: none -> 58.1 us  [the longest x8 23.8 us: ring(): far_b = lax.ppermute(from_next[half:], 'grid', down)]
    scatter-add x1 -> x0, other arithmetic: 54.7 us -> none  [extend_add(): blocked = blocked.at[shifted, :, col_block, :].add(tile_data)]
  transfers between devices with their start and end apart: 4 -> 43, of which waited for: 3 -> 14; matrix products, arithmetic and copies ran while one was open for 5% -> 6% of each run, Pallas kernels for 0% -> 34%
where the time goes in v1:
time: 494 us; the launch traced here: 485 us
  Pallas kernels  183 us (37%)
  waiting for transfers between devices  177 us (36%)
  starting transfers between devices  83.7 us (17%)
  local copies, waits for them, and re-layouts  29.7 us (6%)
  matrix products  6.88 us (1%)
    pallas_call x1, Pallas kernels, factor(): pl.pallas_call(factor_kernel, out_shape=[jax.ShapeDtypeStruct((BLOCK, LEA...  142 us
    ppermute x8, waiting for transfers between devices, ring(): from_next = lax.ppermute(block, 'grid', down)  94.2 us
    ppermute x8, waiting for transfers between devices, ring(): from_prev = lax.ppermute(block, 'grid', up)  43.7 us
    ppermute x8, starting transfers between devices, ring(): far_b = lax.ppermute(from_next[half:], 'grid', down)  23.8 us
    pallas_call x1, Pallas kernels, combine(): pl.pallas_call(combine_kernel, out_shape=[jax.ShapeDtypeStruct((PBINS, BL...  23.5 us
    ppermute x8, starting transfers between devices, ring(): from_next = lax.ppermute(block, 'grid', down)  22.6 us
    ppermute x7, waiting for transfers between devices, gather_small(): other = lax.ppermute(values, axis, [(i, i ^ bit) for i in range(size)])  19.9 us
    pallas_call x1, Pallas kernels, update(): pl.pallas_call(update_kernel, out_shape=jax.ShapeDtypeStruct(entries.shap...  17.4 us
  transfers between devices with their start and end apart: 43, of which 14 were waited for; matrix products, arithmetic and copies ran while one was open for 6% of the time, Pallas kernels for 34%

profile of v1, /device:TPU:0, one launch (start us, length us, event | category | flops | bytes accessed | tf_op | source)
XLA Modules:
  0.0 484.5 jit_solution(4107530377151426104)
XLA Ops:
  0.0 1.3 slice_bitcast_fusion
  2.4 7.1 %all-to-all-start = ((f32[2,16,8,1024]{3,2,0,1:T(8,128)}), f32[2,16,8,1024]{3,2,0,1:T(8,128)S(1)}, u32[]{:S(2)}, u32[]{:S(2)}) async-start(f32[2,16,8,1024]{3,2,0,1:T(8,128)} %copy.13), calls=%async_computation | async-start | bytes 2097152 | tf_op jit(solution)/shard_map/all_to_all | solution.py:330
  9.5 11.5 %copy.15 = f32[1,128,128,128]{3,1,0,2:T(8,128)} copy(f32[1,128,128,128]{3,2,1,0:T(8,128)} %param.6) | data formatting | bytes 16777216 | tf_op args[1]
  21.1 6.2 %all-to-all-done = f32[2,16,8,1024]{3,2,0,1:T(8,128)S(1)} async-done(((f32[2,16,8,1024]{3,2,0,1:T(8,128)}), f32[2,16,8,1024]{3,2,0,1:T(8,128)S(1)}, u32[]{:S(2)}, u32[]{:S(2)}) %all-to-all-start) | async-done | bytes 1048608 | tf_op jit(solution)/shard_map/all_to_all | solution.py:330
  27.2 7.8 %all-to-all-start.1 = ((f32[1,128,128,128]{3,1,0,2:T(8,128)}), f32[1,128,128,128]{3,1,0,2:T(8,128)}, u32[]{:S(2)}, u32[]{:S(2)}) async-start(f32[1,128,128,128]{3,1,0,2:T(8,128)} %copy.15), calls=%async_computation.1 | async-start | bytes 16777216 | tf_op jit(solution)/shard_map/all_to_all | solution.py:334
  35.2 2.2 collective-permute-start.7
  37.4 2.8 collective-permute-start.15
  40.2 94.2 %collective-permute-done.7 = f32[4,8,1024]{2,1,0:T(8,128)S(1)} collective-permute-done((f32[4,8,1024]{2,1,0:T(8,128)S(1)}, f32[4,8,1024]{2,1,0:T(8,128)S(1)}, u32[]{:S(2)}, u32[]{:S(2)}) %collective-permute-start.7) | collective-permute-done | bytes 131104 | tf_op jit(solution)/shard_map/ppermute | solution.py:64
  134.4 2.1 collective-permute-start.9
  136.8 6.2 %collective-permute-start.18 = (f32[2,8,1024]{2,1,0:T(8,128)S(1)}, f32[2,8,1024]{2,1,0:T(8,128)S(1)}, u32[]{:S(2)}, u32[]{:S(2)}) collective-permute-start(f32[2,8,1024]{2,1,0:T(8,128)S(1)} %slice.108), channel_id=1, source_target_pairs={{0,3},{1,0},{2,1},{3,2},{4,7},{5,4},{6,5},{7,6},{8,11},{9,8},{10,9... | collective-permute-start | bytes 196616 | tf_op jit(solution)/shard_map/ppermute | solution.py:66
  143.6 3.0 collective-permute-start.11
  146.6 2.7 collective-permute-done.17
  149.4 3.2 collective-permute-start.19
  152.6 3.0 collective-permute-start.1
  155.6 1.5 collective-permute-done.1
  157.6 4.9 %collective-permute-done.2 = s32[4,128]{1,0:T(4,128)S(1)} collective-permute-done((s32[4,128]{1,0:T(4,128)S(1)}, s32[4,128]{1,0:T(4,128)S(1)}, u32[]{:S(2)}, u32[]{:S(2)}) %collective-permute-start.2) | collective-permute-done | bytes 2080 | tf_op jit(solution)/shard_map/ppermute | solution.py:43
  162.5 3.6 collective-permute-done.3
  166.1 5.3 %collective-permute-done.4 = s32[16,128]{1,0:T(8,128)S(1)} collective-permute-done((s32[16,128]{1,0:T(8,128)S(1)}, s32[16,128]{1,0:T(8,128)S(1)}, u32[]{:S(2)}, u32[]{:S(2)}) %collective-permute-start.4) | collective-permute-done | bytes 8224 | tf_op jit(solution)/shard_map/ppermute | solution.py:43
  173.4 3.3 collective-permute-start.14
  177.5 2.0 collective-permute-start.21
  179.5 1.7 slice.110
  183.3 4.6 collective-permute-done.6
  188.5 23.5 %combine.1 = (f32[1536,128]{1,0:T(8,128)}, f32[4096,128]{1,0:T(8,128)}) custom-call(s32[16384]{0:T(1024)} %fusion.5.bins, f32[16384,128]{1,0:T(8,128)} %bitcast.8.x), custom_call_target="tpu_custom_call" | custom-call | tf_op jit(solution)/shard_map/combine/pallas_call | solution.py:141
  212.0 3.5 all-to-all-start.2
  215.6 142.2 %factor.1 = (f32[128,1024]{1,0:T(8,128)}, f32[1024,1024]{1,0:T(8,128)}) custom-call(s32[1]{0:T(128)} %bitcast.position, f32[4,4,8,1024]{3,2,1,0:T(8,128)} %copy-done.1, f32[4,4,8,1024]{3,2,1,0:T(8,128)} %collective-permute-done.11.refs_1_, f32[2,4,8,1024]{3,2,1,0:T(8,128)} %collective-permute-done.13.refs_2_, ...), custom_call_target="tpu_custom_call" | custom-call | flops 120000004096 | bytes 20971520 | tf_op jit(solution)/shard_map/factor/pallas_call | solution.py:226
  357.9 6.9 %fusion.1 = f32[192,1024]{1,0:T(8,128)S(1)} fusion(f32[1024,1024]{1,0:T(8,128)} %get-tuple-element.10, f32[32,8,1024]{2,1,0:T(8,128)S(1)} %bitcast.75, f32[24,8,8,128]{3,2,0,1:T(8,128)S(1)} %bitcast.76), kind=kOutput, calls=%fused_computation.6 | convolution fusion | flops 2416115712 | bytes 6553600 | tf_op jit(solution)/shard_map/dot_general | solution.py:342
  365.0 3.2 collective-permute-start.31
  369.3 2.4 collective-permute-start.23
  371.7 6.0 %collective-permute-done.32 = f32[12,8,1024]{2,1,0:T(8,128)S(1)} collective-permute-done((f32[12,8,1024]{2,1,0:T(8,128)S(1)}, f32[12,8,1024]{2,1,0:T(8,128)S(1)}, u32[]{:S(2)}, u32[]{:S(2)}) %collective-permute-start.32) | collective-permute-done | bytes 393248 | tf_op jit(solution)/shard_map/ppermute | solution.py:63
  377.8 3.3 collective-permute-start.34
  382.0 2.6 collective-permute-start.26
  385.5 1.3 pad_maximum_fusion.1.refs_5_
  387.5 2.6 collective-permute-start.35
  390.1 1.3 pad_maximum_fusion.refs_0_
  391.4 3.2 collective-permute-start.27
  394.6 7.1 %all-to-all-start.3 = ((f32[128,32,128]{2,1,0:T(8,128)}), f32[128,32,128]{2,1,0:T(8,128)S(1)}, u32[]{:S(2)}, u32[]{:S(2)}) async-start(f32[128,32,128]{2,1,0:T(8,128)} %bitcast.77), calls=%async_computation.3 | async-start | bytes 4194304 | tf_op jit(solution)/shard_map/all_to_all | solution.py:344
  401.7 25.5 %collective-permute-done.36.refs_9_ = f32[4,12,8,1024]{3,2,1,0:T(8,128)} collective-permute-done((f32[4,12,8,1024]{3,2,1,0:T(8,128)}, f32[4,12,8,1024]{3,2,1,0:T(8,128)}, u32[]{:S(2)}, u32[]{:S(2)}) %collective-permute-start.36) | collective-permute-done | bytes 1572896 | tf_op jit(solution)/shard_map/ppermute | solution.py:63
  427.3 2.1 slice.119
  429.4 2.1 slice.120
  431.5 3.2 collective-permute-start.38
  434.7 12.2 %collective-permute-done.28.refs_4_ = f32[4,12,8,1024]{3,2,1,0:T(8,128)} collective-permute-done((f32[4,12,8,1024]{3,2,1,0:T(8,128)}, f32[4,12,8,1024]{3,2,1,0:T(8,128)}, u32[]{:S(2)}, u32[]{:S(2)}) %collective-permute-start.28) | collective-permute-done | bytes 1572896 | tf_op jit(solution)/shard_map/ppermute | solution.py:63
  446.9 2.1 slice.114
  449.0 2.1 slice.115
  451.1 4.0 collective-permute-start.30
  455.0 2.6 copy.24
  457.6 5.0 %collective-permute-done.37.refs_7_ = f32[2,12,8,1024]{3,2,1,0:T(8,128)S(1)} collective-permute-done((f32[2,12,8,1024]{3,2,1,0:T(8,128)}, f32[2,12,8,1024]{3,2,1,0:T(8,128)S(1)}, u32[]{:S(2)}, u32[]{:S(2)}) %collective-permute-start.37) | collective-permute-done | bytes 786464 | tf_op jit(solution)/shard_map/ppermute | solution.py:65
  462.6 4.1 collective-permute-done.29.refs_2_
  466.7 17.4 %update.1 = f32[2,128,4096]{2,1,0:T(8,128)} custom-call(s32[1]{0:T(128)} %bitcast.position, f32[4,12,8,1024]{3,2,1,0:T(8,128)} %pad_maximum_fusion.refs_0_, f32[4,12,8,1024]{3,2,1,0:T(8,128)} %collective-permute-done.27.refs_1_, f32[2,12,8,1024]{3,2,1,0:T(8,128)} %collective-permute-done.29.refs_2_, f32[2,12,8,1024]{3,2,1,0:T(8,128)} %collective-permute-done.30.refs_3_, ...), custom_call_target="tpu_custom_call" | custom-call | tf_op jit(solution)/shard_map/update/pallas_call | solution.py:297
  (95 shorter events, 12.1 us)
Async XLA Ops:
  2.4 24.8 %all-to-all-start = ((f32[2,16,8,1024]{3,2,0,1:T(8,128)}), f32[2,16,8,1024]{3,2,0,1:T(8,128)S(1)}, u32[]{:S(2)}, u32[]{:S(2)}) async-start(f32[2,16,8,1024]{3,2,0,1:T(8,128)} %copy.13), calls=%async_computation | async-start | bytes 2097152 | tf_op jit(solution)/shard_map/all_to_all | solution.py:330
  27.2 161.3 %all-to-all-start.1 = ((f32[1,128,128,128]{3,1,0,2:T(8,128)}), f32[1,128,128,128]{3,1,0,2:T(8,128)}, u32[]{:S(2)}, u32[]{:S(2)}) async-start(f32[1,128,128,128]{3,1,0,2:T(8,128)} %copy.15), calls=%async_computation.1 | async-start | bytes 16777216 | tf_op jit(solution)/shard_map/all_to_all | solution.py:334
  35.1 101.4 %copy-start.4 = (s32[1,128]{1,0:T(1,128)S(1)}, s32[1,128]{1,0:T(1,128)}, u32[]{:S(2)}) copy-start(s32[1,128]{1,0:T(1,128)} %param.9) | copy-start | bytes 1540
  35.1 101.4 %copy-start.5 = (s32[1,128,1]{1,2,0:T(1,128)S(1)}, s32[1,128,1]{1,2,0:T(1,128)}, u32[]{:S(2)}) copy-start(s32[1,128,1]{1,2,0:T(1,128)} %param.7) | copy-start | bytes 1540
  35.1 101.4 %copy-start.6 = (s32[1,128]{1,0:T(1,128)S(1)}, s32[1,128]{1,0:T(1,128)}, u32[]{:S(2)}) copy-start(s32[1,128]{1,0:T(1,128)} %param.8) | copy-start | bytes 1540
  35.2 99.2 %collective-permute-start.7 = (f32[4,8,1024]{2,1,0:T(8,128)S(1)}, f32[4,8,1024]{2,1,0:T(8,128)S(1)}, u32[]{:S(2)}, u32[]{:S(2)}) collective-permute-start(f32[4,8,1024]{2,1,0:T(8,128)S(1)} %get-tuple-element.16), channel_id=1, source_target_pairs={{0,12},{1,13},{2,14},{3,15},{4,0},{5,1},{6,2},{7,3},{8,4},{9,5},{1... | collective-permute-start | bytes 393224 | tf_op jit(solution)/shard_map/ppermute | solution.py:64
  37.4 97.0 %collective-permute-start.8 = (f32[4,8,1024]{2,1,0:T(8,128)S(1)}, f32[4,8,1024]{2,1,0:T(8,128)S(1)}, u32[]{:S(2)}, u32[]{:S(2)}) collective-permute-start(f32[4,8,1024]{2,1,0:T(8,128)S(1)} %get-tuple-element.16), channel_id=1, source_target_pairs={{0,4},{1,5},{2,6},{3,7},{4,8},{5,9},{6,10},{7,11},{8,12},{9,13},{1... | collective-permute-start | bytes 393224 | tf_op jit(solution)/shard_map/ppermute | solution.py:63
  37.4 99.4 %collective-permute-start.15 = (f32[4,8,1024]{2,1,0:T(8,128)S(1)}, f32[4,8,1024]{2,1,0:T(8,128)S(1)}, u32[]{:S(2)}, u32[]{:S(2)}) collective-permute-start(f32[4,8,1024]{2,1,0:T(8,128)S(1)} %get-tuple-element.15), channel_id=1, source_target_pairs={{0,3},{1,0},{2,1},{3,2},{4,7},{5,4},{6,5},{7,6},{8,11},{9,8},{10,9... | collective-permute-start | bytes 393224 | tf_op jit(solution)/shard_map/ppermute | solution.py:64
  40.2 102.8 %collective-permute-start.16 = (f32[4,8,1024]{2,1,0:T(8,128)S(1)}, f32[4,8,1024]{2,1,0:T(8,128)S(1)}, u32[]{:S(2)}, u32[]{:S(2)}) collective-permute-start(f32[4,8,1024]{2,1,0:T(8,128)S(1)} %get-tuple-element.15), channel_id=1, source_target_pairs={{0,1},{1,2},{2,3},{3,0},{4,5},{5,6},{6,7},{7,4},{8,9},{9,10},{10,1... | collective-permute-start | bytes 393224 | tf_op jit(solution)/shard_map/ppermute | solution.py:63
  134.4 8.7 %collective-permute-start.10 = (f32[2,8,1024]{2,1,0:T(8,128)S(1)}, f32[2,8,1024]{2,1,0:T(8,128)S(1)}, u32[]{:S(2)}, u32[]{:S(2)}) collective-permute-start(f32[2,8,1024]{2,1,0:T(8,128)S(1)} %slice.103), channel_id=1, source_target_pairs={{0,12},{1,13},{2,14},{3,15},{4,0},{5,1},{6,2},{7,3},{8,4},{9,5},{1... | collective-permute-start | bytes 196616 | tf_op jit(solution)/shard_map/ppermute | solution.py:66
  134.4 8.7 %collective-permute-start.9 = (f32[2,8,1024]{2,1,0:T(8,128)S(1)}, f32[2,8,1024]{2,1,0:T(8,128)S(1)}, u32[]{:S(2)}, u32[]{:S(2)}) collective-permute-start(f32[2,8,1024]{2,1,0:T(8,128)S(1)} %slice.102), channel_id=1, source_target_pairs={{0,4},{1,5},{2,6},{3,7},{4,8},{5,9},{6,10},{7,11},{8,12},{9,13},{1... | collective-permute-start | bytes 196616 | tf_op jit(solution)/shard_map/ppermute | solution.py:65
  136.7 16.0 %collective-permute-start = (s32[1,128]{1,0:T(1,128)S(1)}, s32[1,128]{1,0:T(1,128)S(1)}, u32[]{:S(2)}, u32[]{:S(2)}) collective-permute-start(s32[1,128]{1,0:T(1,128)S(1)} %compare_select_fusion.2), channel_id=1, source_target_pairs={{0,16},{16,0},{32,48},{48,32},{64,80},{80,64},{96,112},{112,96},{1... | collective-permute-start | bytes 1544 | tf_op jit(solution)/shard_map/ppermute | solution.py:43
  136.8 9.8 %collective-permute-start.18 = (f32[2,8,1024]{2,1,0:T(8,128)S(1)}, f32[2,8,1024]{2,1,0:T(8,128)S(1)}, u32[]{:S(2)}, u32[]{:S(2)}) collective-permute-start(f32[2,8,1024]{2,1,0:T(8,128)S(1)} %slice.108), channel_id=1, source_target_pairs={{0,3},{1,0},{2,1},{3,2},{4,7},{5,4},{6,5},{7,6},{8,11},{9,8},{10,9... | collective-permute-start | bytes 196616 | tf_op jit(solution)/shard_map/ppermute | solution.py:66
  143.0 6.2 %collective-permute-start.17 = (f32[2,8,1024]{2,1,0:T(8,128)S(1)}, f32[2,8,1024]{2,1,0:T(8,128)S(1)}, u32[]{:S(2)}, u32[]{:S(2)}) collective-permute-start(f32[2,8,1024]{2,1,0:T(8,128)S(1)} %slice.107), channel_id=1, source_target_pairs={{0,1},{1,2},{2,3},{3,0},{4,5},{5,6},{6,7},{7,4},{8,9},{9,10},{10,1... | collective-permute-start | bytes 196616 | tf_op jit(solution)/shard_map/ppermute | solution.py:65
  143.2 38.0 %copy-start.1 = (f32[4,4,8,1024]{3,2,1,0:T(8,128)}, f32[4,4,8,1024]{3,2,1,0:T(8,128)S(1)}, u32[]{:S(2)}) copy-start(f32[4,4,8,1024]{3,2,1,0:T(8,128)S(1)} %pad_maximum_fusion.2.refs_0_) | copy-start | bytes 1572868
  143.2 28.2 %collective-permute-start.12 = (f32[4,4,8,1024]{3,2,1,0:T(8,128)S(1)}, f32[4,4,8,1024]{3,2,1,0:T(8,128)}, u32[]{:S(2)}, u32[]{:S(2)}) collective-permute-start(f32[4,4,8,1024]{3,2,1,0:T(8,128)S(1)} %pad_maximum_fusion.2.refs_0_), channel_id=1, source_target_pairs={{0,1},{1,2},{2,3},{3,0},{4,5},{5,6},{6,7},{7,4},{8,9},{9,10},{10,1... | collective-permute-start | bytes 1572872 | tf_op jit(solution)/shard_map/ppermute | solution.py:63
  143.6 28.9 %collective-permute-start.11 = (f32[4,4,8,1024]{3,2,1,0:T(8,128)S(1)}, f32[4,4,8,1024]{3,2,1,0:T(8,128)}, u32[]{:S(2)}, u32[]{:S(2)}) collective-permute-start(f32[4,4,8,1024]{3,2,1,0:T(8,128)S(1)} %pad_maximum_fusion.2.refs_0_), channel_id=1, source_target_pairs={{0,3},{1,0},{2,1},{3,2},{4,7},{5,4},{6,5},{7,6},{8,11},{9,8},{10,9... | collective-permute-start | bytes 1572872 | tf_op jit(solution)/shard_map/ppermute | solution.py:64
  149.3 62.7 %copy-start.2 = (f32[4,4,8,1024]{3,2,1,0:T(8,128)}, f32[4,4,8,1024]{3,2,1,0:T(8,128)S(1)}, u32[]{:S(2)}) copy-start(f32[4,4,8,1024]{3,2,1,0:T(8,128)S(1)} %pad_maximum_fusion.3.refs_5_) | copy-start | bytes 1572868
  149.3 27.4 %collective-permute-start.20 = (f32[4,4,8,1024]{3,2,1,0:T(8,128)S(1)}, f32[4,4,8,1024]{3,2,1,0:T(8,128)S(1)}, u32[]{:S(2)}, u32[]{:S(2)}) collective-permute-start(f32[4,4,8,1024]{3,2,1,0:T(8,128)S(1)} %pad_maximum_fusion.3.refs_5_), channel_id=1, source_target_pairs={{0,4},{1,5},{2,6},{3,7},{4,8},{5,9},{6,10},{7,11},{8,12},{9,13},{1... | collective-permute-start | bytes 1572872 | tf_op jit(solution)/shard_map/ppermute | solution.py:63
  149.4 30.1 %collective-permute-start.19 = (f32[4,4,8,1024]{3,2,1,0:T(8,128)S(1)}, f32[4,4,8,1024]{3,2,1,0:T(8,128)}, u32[]{:S(2)}, u32[]{:S(2)}) collective-permute-start(f32[4,4,8,1024]{3,2,1,0:T(8,128)S(1)} %pad_maximum_fusion.3.refs_5_), channel_id=1, source_target_pairs={{0,12},{1,13},{2,14},{3,15},{4,0},{5,1},{6,2},{7,3},{8,4},{9,5},{1... | collective-permute-start | bytes 1572872 | tf_op jit(solution)/shard_map/ppermute | solution.py:64
  152.6 4.6 collective-permute-start.1
  157.2 5.2 %collective-permute-start.2 = (s32[4,128]{1,0:T(4,128)S(1)}, s32[4,128]{1,0:T(4,128)S(1)}, u32[]{:S(2)}, u32[]{:S(2)}) collective-permute-start(s32[4,128]{1,0:T(4,128)S(1)} %add_select_fusion.5), channel_id=1, source_target_pairs={{0,64},{16,80},{32,96},{48,112},{64,0},{80,16},{96,32},{112,48},{1... | collective-permute-start | bytes 6152 | tf_op jit(solution)/shard_map/ppermute | solution.py:43
  162.5 3.6 collective-permute-start.3
  166.1 5.3 %collective-permute-start.4 = (s32[16,128]{1,0:T(8,128)S(1)}, s32[16,128]{1,0:T(8,128)S(1)}, u32[]{:S(2)}, u32[]{:S(2)}) collective-permute-start(s32[16,128]{1,0:T(8,128)S(1)} %add_select_fusion.3), channel_id=1, source_target_pairs={{0,2},{1,3},{2,0},{3,1},{4,6},{5,7},{6,4},{7,5},{8,10},{9,11},{10,... | collective-permute-start | bytes 24584 | tf_op jit(solution)/shard_map/ppermute | solution.py:43
  171.4 11.0 %collective-permute-start.5 = (s32[32,128]{1,0:T(8,128)S(1)}, s32[32,128]{1,0:T(8,128)S(1)}, u32[]{:S(2)}, u32[]{:S(2)}) collective-permute-start(s32[32,128]{1,0:T(8,128)S(1)} %add_select_fusion.2), channel_id=1, source_target_pairs={{0,4},{1,5},{2,6},{3,7},{4,0},{5,1},{6,2},{7,3},{8,12},{9,13},{10,... | collective-permute-start | bytes 49160 | tf_op jit(solution)/shard_map/ppermute | solution.py:43
  172.4 43.2 %collective-permute-start.13 = (f32[2,4,8,1024]{3,2,1,0:T(8,128)S(1)}, f32[2,4,8,1024]{3,2,1,0:T(8,128)}, u32[]{:S(2)}, u32[]{:S(2)}) collective-permute-start(f32[2,4,8,1024]{3,2,1,0:T(8,128)S(1)} %slice.104), channel_id=1, source_target_pairs={{0,1},{1,2},{2,3},{3,0},{4,5},{5,6},{6,7},{7,4},{8,9},{9,10},{10,1... | collective-permute-start | bytes 786440 | tf_op jit(solution)/shard_map/ppermute | solution.py:65
  173.4 42.2 %collective-permute-start.14 = (f32[2,4,8,1024]{3,2,1,0:T(8,128)S(1)}, f32[2,4,8,1024]{3,2,1,0:T(8,128)}, u32[]{:S(2)}, u32[]{:S(2)}) collective-permute-start(f32[2,4,8,1024]{3,2,1,0:T(8,128)S(1)} %slice.105), channel_id=1, source_target_pairs={{0,3},{1,0},{2,1},{3,2},{4,7},{5,4},{6,5},{7,6},{8,11},{9,8},{10,9... | collective-permute-start | bytes 786440 | tf_op jit(solution)/shard_map/ppermute | solution.py:66
  177.5 38.1 %collective-permute-start.21 = (f32[2,4,8,1024]{3,2,1,0:T(8,128)}, f32[2,4,8,1024]{3,2,1,0:T(8,128)}, u32[]{:S(2)}, u32[]{:S(2)}) collective-permute-start(f32[2,4,8,1024]{3,2,1,0:T(8,128)} %slice.109), channel_id=1, source_target_pairs={{0,4},{1,5},{2,6},{3,7},{4,8},{5,9},{6,10},{7,11},{8,12},{9,13},{1... | collective-permute-start | bytes 786440 | tf_op jit(solution)/shard_map/ppermute | solution.py:65
  181.2 34.4 %collective-permute-start.22 = (f32[2,4,8,1024]{3,2,1,0:T(8,128)}, f32[2,4,8,1024]{3,2,1,0:T(8,128)}, u32[]{:S(2)}, u32[]{:S(2)}) collective-permute-start(f32[2,4,8,1024]{3,2,1,0:T(8,128)} %slice.110), channel_id=1, source_target_pairs={{0,12},{1,13},{2,14},{3,15},{4,0},{5,1},{6,2},{7,3},{8,4},{9,5},{1... | collective-permute-start | bytes 786440 | tf_op jit(solution)/shard_map/ppermute | solution.py:66
  182.4 5.5 %collective-permute-start.6 = (s32[64,128]{1,0:T(8,128)S(1)}, s32[64,128]{1,0:T(8,128)S(1)}, u32[]{:S(2)}, u32[]{:S(2)}) collective-permute-start(s32[64,128]{1,0:T(8,128)S(1)} %add_select_fusion.1), channel_id=1, source_target_pairs={{0,8},{1,9},{2,10},{3,11},{4,12},{5,13},{6,14},{7,15},{8,0},{9,1},... | collective-permute-start | bytes 98312 | tf_op jit(solution)/shard_map/ppermute | solution.py:43
  212.0 145.8 %all-to-all-start.2 = ((f32[8,24,8,128]{3,2,1,0:T(8,128)}), f32[8,24,8,128]{3,2,1,0:T(8,128)S(1)}, u32[]{:S(2)}, u32[]{:S(2)}) async-start(f32[8,24,8,128]{3,2,1,0:T(8,128)} %bitcast.82), calls=%async_computation.2 | async-start | bytes 1572864 | tf_op jit(solution)/shard_map/all_to_all | solution.py:337
  364.9 12.7 %collective-permute-start.32 = (f32[12,8,1024]{2,1,0:T(8,128)S(1)}, f32[12,8,1024]{2,1,0:T(8,128)S(1)}, u32[]{:S(2)}, u32[]{:S(2)}) collective-permute-start(f32[12,8,1024]{2,1,0:T(8,128)S(1)} %get-tuple-element.19), channel_id=1, source_target_pairs={{0,1},{1,2},{2,3},{3,0},{4,5},{5,6},{6,7},{7,4},{8,9},{9,10},{10,1... | collective-permute-start | bytes 1179656 | tf_op jit(solution)/shard_map/ppermute | solution.py:63
  365.0 12.8 %collective-permute-start.31 = (f32[12,8,1024]{2,1,0:T(8,128)S(1)}, f32[12,8,1024]{2,1,0:T(8,128)S(1)}, u32[]{:S(2)}, u32[]{:S(2)}) collective-permute-start(f32[12,8,1024]{2,1,0:T(8,128)S(1)} %get-tuple-element.19), channel_id=1, source_target_pairs={{0,3},{1,0},{2,1},{3,2},{4,7},{5,4},{6,5},{7,6},{8,11},{9,8},{10,9... | collective-permute-start | bytes 1179656 | tf_op jit(solution)/shard_map/ppermute | solution.py:64
  368.3 12.9 %collective-permute-start.24 = (f32[12,8,1024]{2,1,0:T(8,128)S(1)}, f32[12,8,1024]{2,1,0:T(8,128)S(1)}, u32[]{:S(2)}, u32[]{:S(2)}) collective-permute-start(f32[12,8,1024]{2,1,0:T(8,128)S(1)} %get-tuple-element.18), channel_id=1, source_target_pairs={{0,4},{1,5},{2,6},{3,7},{4,8},{5,9},{6,10},{7,11},{8,12},{9,13},{1... | collective-permute-start | bytes 1179656 | tf_op jit(solution)/shard_map/ppermute | solution.py:63
  369.3 12.7 %collective-permute-start.23 = (f32[12,8,1024]{2,1,0:T(8,128)S(1)}, f32[12,8,1024]{2,1,0:T(8,128)S(1)}, u32[]{:S(2)}, u32[]{:S(2)}) collective-permute-start(f32[12,8,1024]{2,1,0:T(8,128)S(1)} %get-tuple-element.18), channel_id=1, source_target_pairs={{0,12},{1,13},{2,14},{3,15},{4,0},{5,1},{6,2},{7,3},{8,4},{9,5},{1... | collective-permute-start | bytes 1179656 | tf_op jit(solution)/shard_map/ppermute | solution.py:64
  377.7 7.7 %collective-permute-start.33 = (f32[6,8,1024]{2,1,0:T(8,128)S(1)}, f32[6,8,1024]{2,1,0:T(8,128)S(1)}, u32[]{:S(2)}, u32[]{:S(2)}) collective-permute-start(f32[6,8,1024]{2,1,0:T(8,128)S(1)} %slice.117), channel_id=1, source_target_pairs={{0,1},{1,2},{2,3},{3,0},{4,5},{5,6},{6,7},{7,4},{8,9},{9,10},{10,1... | collective-permute-start | bytes 589832 | tf_op jit(solution)/shard_map/ppermute | solution.py:65
  377.8 7.6 %collective-permute-start.34 = (f32[6,8,1024]{2,1,0:T(8,128)S(1)}, f32[6,8,1024]{2,1,0:T(8,128)S(1)}, u32[]{:S(2)}, u32[]{:S(2)}) collective-permute-start(f32[6,8,1024]{2,1,0:T(8,128)S(1)} %slice.118), channel_id=1, source_target_pairs={{0,3},{1,0},{2,1},{3,2},{4,7},{5,4},{6,5},{7,6},{8,11},{9,8},{10,9... | collective-permute-start | bytes 589832 | tf_op jit(solution)/shard_map/ppermute | solution.py:66
  381.1 8.9 %collective-permute-start.25 = (f32[6,8,1024]{2,1,0:T(8,128)S(1)}, f32[6,8,1024]{2,1,0:T(8,128)S(1)}, u32[]{:S(2)}, u32[]{:S(2)}) collective-permute-start(f32[6,8,1024]{2,1,0:T(8,128)S(1)} %slice.112), channel_id=1, source_target_pairs={{0,4},{1,5},{2,6},{3,7},{4,8},{5,9},{6,10},{7,11},{8,12},{9,13},{1... | collective-permute-start | bytes 589832 | tf_op jit(solution)/shard_map/ppermute | solution.py:65
  382.0 8.1 %collective-permute-start.26 = (f32[6,8,1024]{2,1,0:T(8,128)S(1)}, f32[6,8,1024]{2,1,0:T(8,128)S(1)}, u32[]{:S(2)}, u32[]{:S(2)}) collective-permute-start(f32[6,8,1024]{2,1,0:T(8,128)S(1)} %slice.113), channel_id=1, source_target_pairs={{0,12},{1,13},{2,14},{3,15},{4,0},{5,1},{6,2},{7,3},{8,4},{9,5},{1... | collective-permute-start | bytes 589832 | tf_op jit(solution)/shard_map/ppermute | solution.py:66
  386.8 40.4 %collective-permute-start.36 = (f32[4,12,8,1024]{3,2,1,0:T(8,128)}, f32[4,12,8,1024]{3,2,1,0:T(8,128)}, u32[]{:S(2)}, u32[]{:S(2)}) collective-permute-start(f32[4,12,8,1024]{3,2,1,0:T(8,128)} %pad_maximum_fusion.1.refs_5_), channel_id=1, source_target_pairs={{0,4},{1,5},{2,6},{3,7},{4,8},{5,9},{6,10},{7,11},{8,12},{9,13},{1... | collective-permute-start | bytes 4718600 | tf_op jit(solution)/shard_map/ppermute | solution.py:63
  387.5 41.9 %collective-permute-start.35 = (f32[4,12,8,1024]{3,2,1,0:T(8,128)}, f32[4,12,8,1024]{3,2,1,0:T(8,128)}, u32[]{:S(2)}, u32[]{:S(2)}) collective-permute-start(f32[4,12,8,1024]{3,2,1,0:T(8,128)} %pad_maximum_fusion.1.refs_5_), channel_id=1, source_target_pairs={{0,12},{1,13},{2,14},{3,15},{4,0},{5,1},{6,2},{7,3},{8,4},{9,5},{1... | collective-permute-start | bytes 4718600 | tf_op jit(solution)/shard_map/ppermute | solution.py:64
  391.4 55.5 %collective-permute-start.28 = (f32[4,12,8,1024]{3,2,1,0:T(8,128)}, f32[4,12,8,1024]{3,2,1,0:T(8,128)}, u32[]{:S(2)}, u32[]{:S(2)}) collective-permute-start(f32[4,12,8,1024]{3,2,1,0:T(8,128)} %pad_maximum_fusion.refs_0_), channel_id=1, source_target_pairs={{0,1},{1,2},{2,3},{3,0},{4,5},{5,6},{6,7},{7,4},{8,9},{9,10},{10,1... | collective-permute-start | bytes 4718600 | tf_op jit(solution)/shard_map/ppermute | solution.py:63
  391.4 57.6 %collective-permute-start.27 = (f32[4,12,8,1024]{3,2,1,0:T(8,128)}, f32[4,12,8,1024]{3,2,1,0:T(8,128)}, u32[]{:S(2)}, u32[]{:S(2)}) collective-permute-start(f32[4,12,8,1024]{3,2,1,0:T(8,128)} %pad_maximum_fusion.refs_0_), channel_id=1, source_target_pairs={{0,3},{1,0},{2,1},{3,2},{4,7},{5,4},{6,5},{7,6},{8,11},{9,8},{10,9... | collective-permute-start | bytes 4718600 | tf_op jit(solution)/shard_map/ppermute | solution.py:64
  394.6 60.4 %all-to-all-start.3 = ((f32[128,32,128]{2,1,0:T(8,128)}), f32[128,32,128]{2,1,0:T(8,128)S(1)}, u32[]{:S(2)}, u32[]{:S(2)}) async-start(f32[128,32,128]{2,1,0:T(8,128)} %bitcast.77), calls=%async_computation.3 | async-start | bytes 4194304 | tf_op jit(solution)/shard_map/all_to_all | solution.py:344
  429.4 33.2 %collective-permute-start.37 = (f32[2,12,8,1024]{3,2,1,0:T(8,128)}, f32[2,12,8,1024]{3,2,1,0:T(8,128)S(1)}, u32[]{:S(2)}, u32[]{:S(2)}) collective-permute-start(f32[2,12,8,1024]{3,2,1,0:T(8,128)} %slice.119), channel_id=1, source_target_pairs={{0,4},{1,5},{2,6},{3,7},{4,8},{5,9},{6,10},{7,11},{8,12},{9,13},{1... | collective-permute-start | bytes 2359304 | tf_op jit(solution)/shard_map/ppermute | solution.py:65
  431.5 31.2 %collective-permute-start.38 = (f32[2,12,8,1024]{3,2,1,0:T(8,128)}, f32[2,12,8,1024]{3,2,1,0:T(8,128)}, u32[]{:S(2)}, u32[]{:S(2)}) collective-permute-start(f32[2,12,8,1024]{3,2,1,0:T(8,128)} %slice.120), channel_id=1, source_target_pairs={{0,12},{1,13},{2,14},{3,15},{4,0},{5,1},{6,2},{7,3},{8,4},{9,5},{1... | collective-permute-start | bytes 2359304 | tf_op jit(solution)/shard_map/ppermute | solution.py:66
  449.0 17.8 %collective-permute-start.29 = (f32[2,12,8,1024]{3,2,1,0:T(8,128)}, f32[2,12,8,1024]{3,2,1,0:T(8,128)}, u32[]{:S(2)}, u32[]{:S(2)}) collective-permute-start(f32[2,12,8,1024]{3,2,1,0:T(8,128)} %slice.114), channel_id=1, source_target_pairs={{0,1},{1,2},{2,3},{3,0},{4,5},{5,6},{6,7},{7,4},{8,9},{9,10},{10,1... | collective-permute-start | bytes 2359304 | tf_op jit(solution)/shard_map/ppermute | solution.py:65
  451.1 15.7 %collective-permute-start.30 = (f32[2,12,8,1024]{3,2,1,0:T(8,128)}, f32[2,12,8,1024]{3,2,1,0:T(8,128)}, u32[]{:S(2)}, u32[]{:S(2)}) collective-permute-start(f32[2,12,8,1024]{3,2,1,0:T(8,128)} %slice.115), channel_id=1, source_target_pairs={{0,3},{1,0},{2,1},{3,2},{4,7},{5,4},{6,5},{7,6},{8,11},{9,8},{10,9... | collective-permute-start | bytes 2359304 | tf_op jit(solution)/shard_map/ppermute | solution.py:66
  (2 other events, 39.4 us)

commit v2 on v1

v2 whole, which is shorter than its diff:
```python
import functools
import jax
import jax.numpy as jnp
from jax import lax
from jax.experimental import pallas as pl
from jax.experimental.pallas import tpu as pltpu
from jax.sharding import Mesh
from jax.sharding import PartitionSpec as P

BLOCK = 128
LEAD = 1024
LB = LEAD // BLOCK
FRONTS = 8
GRID = 16
SIDE = 4
DEVICES = FRONTS * GRID
FB = 32
TB = FB - LB
TILES = 128
LINES = TB // SIDE
SLICE = BLOCK // SIDE
PSLOTS = LINES * LB
TSLOTS = 88
SLOTS = PSLOTS + TSLOTS
BINS = SIDE * FRONTS * SLOTS
OUT_SLOTS = 2 + LINES
SUB = 8
SLABS = BLOCK // SUB
ACCS = 8
VMEM_LIMIT = 60 << 20

highest = lax.Precision.HIGHEST
ANY = pl.BlockSpec(memory_space=pl.ANY)
VMEM = pl.BlockSpec(memory_space=pltpu.VMEM)
SMEM = pl.BlockSpec(memory_space=pltpu.SMEM)


def split(values):
    high = values.astype(jnp.bfloat16)
    return high, (values - high.astype(jnp.float32)).astype(jnp.bfloat16)


def mul(a, b):
    return lax.dot_general(a, b, (((1,), (1,)), ((), ())), preferred_element_type=jnp.float32)


def tdot(a, b):
    return lax.dot_general(
        a, b, (((0,), (0,)), ((), ())), precision=highest, preferred_element_type=jnp.float32
    )


def shift(block, axis, step):
    return lax.ppermute(block, axis, [(i, (i + step) % SIDE) for i in range(SIDE)])


def ring(block, axis):
    half = block.shape[0] // 2
    from_prev = shift(block, axis, 1)
    from_next = shift(block, axis, -1)
    far_a = shift(from_prev[:half], axis, 1)
    far_b = shift(from_next[half:], axis, -1)
    return block, from_next, far_a, far_b, from_prev


def ring_copies(pieces, here, place, sem, first_sem):
    own, nxt, far_a, far_b, prv = pieces
    parts = [(own, 0, None), (nxt, 1, None), (far_a, 2, 0), (far_b, 2, 1), (prv, 3, None)]
    return [
        pltpu.make_async_copy(src, place((here + step) % SIDE, part), sem.at[first_sem + n])
        for n, (src, step, part) in enumerate(parts)
    ]


def gather_lines(first, second, tied):
    lines = []
    for part, axis in ((first, "x"), (second, "y")):
        lines.append(jnp.stack([part, *(shift(part, axis, -n) for n in range(1, SIDE))]))
    *lines, tied = lax.optimization_barrier((*lines, tied))
    return [*ring(lines[0], "y"), *ring(lines[1], "x")], tied


def line_copies(pieces, place, sem, x, y):
    copies = []
    for h in range(2):
        own, nxt, far_a, far_b, prv = pieces[5 * h : 5 * h + 5]
        for outer in range(SIDE):
            for inner in range(SIDE):
                if outer == 2:
                    src = (far_a if inner < 2 else far_b).at[inner % 2]
                else:
                    src = (own, nxt, None, prv)[outer].at[inner]
                dx, dy = (inner, outer) if h == 0 else (outer, inner)
                dst = place(h, (x + dx) % SIDE, (y + dy) % SIDE)
                copies.append(pltpu.make_async_copy(src, dst, sem.at[len(copies)]))
    return copies


def combine_kernel(bins, x, out, *accs):
    sources = x.shape[0] // TILES

    @pl.when(pl.program_id(0) == 0)
    def _():
        for acc in accs:
            acc[...] = jnp.zeros_like(acc)

    group = 32

    def body(q, carry):
        base = pl.multiple_of(q * group, group)
        labels = pl.program_id(0) * (sources * TILES) + base
        for first in range(0, group, ACCS):
            at = [bins[labels + first + m] for m in range(ACCS)]
            rows = [x[pl.ds(base + first + m, 1), :] for m in range(ACCS)]
            sums = [accs[m][pl.ds(at[m], 1), :] + rows[m] for m in range(ACCS)]
            for m in range(ACCS):
                accs[m][pl.ds(at[m], 1), :] = sums[m]
        return carry

    lax.fori_loop(0, x.shape[0] // group, body, 0)
    step = 256

    @pl.when(pl.program_id(0) == pl.num_programs(0) - 1)
    def _():
        def add(b, carry):
            at = pl.ds(pl.multiple_of(b * step, step), step)
            total = accs[0][at, :]
            for acc in accs[1:]:
                total = total + acc[at, :]
            out[at, :] = total
            return carry

        lax.fori_loop(0, BINS // step, add, 0)


def combine(bins, rows):
    steps = 4
    return pl.pallas_call(
        combine_kernel,
        grid=(steps,),
        out_shape=jax.ShapeDtypeStruct((BINS, BLOCK), jnp.float32),
        in_specs=[SMEM, pl.BlockSpec((rows.shape[0] // steps, BLOCK), lambda i: (i, 0))],
        out_specs=pl.BlockSpec((BINS, BLOCK), lambda i: (0, 0)),
        scratch_shapes=[pltpu.VMEM((BINS, BLOCK), jnp.float32)] * ACCS,
        compiler_params=pltpu.CompilerParams(vmem_limit_bytes=VMEM_LIMIT),
        cost_estimate=pl.CostEstimate(flops=20 * 10**9, bytes_accessed=20 << 20, transcendentals=0),
        name="combine",
    )(bins, rows)


def factor_rows(rows, first, sub):
    def spread(values, j):
        return jnp.broadcast_to(values[j : j + 1, :], values.shape)

    columns = [
        jnp.broadcast_to(rows[:, first + j : first + j + 1], (SUB, BLOCK)) for j in range(SUB)
    ]
    parts = [rows[:, :BLOCK], rows[:, BLOCK:]]
    for j in range(SUB):
        scale = lax.rsqrt(spread(columns[j], j))
        weight = jnp.where(sub > j, columns[j] * scale, 0.0)
        for m in range(j + 1, SUB):
            columns[m] = columns[m] - weight * (spread(columns[m], j) * scale)
        for n in range(2):
            pivot = spread(parts[n], j) * scale
            parts[n] = jnp.where(sub == j, pivot, parts[n] - weight * pivot)
    return jnp.concatenate(parts, 1)


def factor_kernel(position, *refs):
    pieces, (own_rows, inverse_high, inverse_low, entries, work, diag, pair, sem) = refs[:10], refs[10:]
    px, py = position[0], position[1]

    def place(h, x, y):
        block = (x % 2) * SIDE + y
        slab = block * SLABS + (x // 2) * (SLABS // 2) + h * (SLABS // 4)
        return entries.at[pl.ds(slab, SLABS // 4)]

    copies = line_copies(pieces, place, sem, px, py)
    for copy in copies:
        copy.start()
    for copy in copies:
        copy.wait()
    sub = lax.broadcasted_iota(jnp.int32, (SUB, 1), 0)
    row = lax.broadcasted_iota(jnp.int32, (BLOCK, BLOCK), 0)
    col = lax.broadcasted_iota(jnp.int32, (BLOCK, BLOCK), 1)
    eye = jnp.where(row == col, 1.0, 0.0)
    for r in range(LB):
        for c in range(r + 1):
            block = entries[r * SLABS : (r + 1) * SLABS, :, c * BLOCK : (c + 1) * BLOCK]
            block = block.reshape(BLOCK, BLOCK)
            if r == c:
                block = jnp.where(col <= row, block, 0.0)
                block = block + jnp.where(col < row, block, 0.0).T
                work[r * BLOCK : (r + 1) * BLOCK, r * BLOCK : (r + 1) * BLOCK] = block
            else:
                work[c * BLOCK : (c + 1) * BLOCK, r * BLOCK : (r + 1) * BLOCK] = block.T

    def step(k, carry):
        at = pl.ds(pl.multiple_of(k * BLOCK, BLOCK), BLOCK)
        pair[:, :BLOCK] = work[at, at]
        pair[:, BLOCK:] = eye
        for q in range(BLOCK // SUB):
            first = SUB * q
            rows = pair[first : first + SUB, :]
            if q > 0:
                rows = rows - tdot(pair[0:first, first : first + SUB], pair[0:first, :])
            pair[first : first + SUB, :] = factor_rows(rows, first, sub)
        block_inverse = pair[:, BLOCK:]
        diag[k] = pair[:, :BLOCK]
        work[at, :] = jnp.dot(
            block_inverse, work[at, :], precision=highest, preferred_element_type=jnp.float32
        )
        work[at, at] = block_inverse

        def update(i, inner):
            below = pl.ds(pl.multiple_of(i * BLOCK, BLOCK), BLOCK)
            work[below, at] = jnp.zeros((BLOCK, BLOCK), jnp.float32)
            work[below, :] = work[below, :] - tdot(work[at, below], work[at, :])
            return inner

        lax.fori_loop(k + 1, LB, update, 0)
        return carry

    lax.fori_loop(0, LB, step, 0)
    for k in range(LB):
        at = slice(k * BLOCK, (k + 1) * BLOCK)
        done = slice(0, (k + 1) * BLOCK)
        inverse_high[at, done], inverse_low[at, done] = split(work[at, done])
        if k + 1 < LB:
            rest = jnp.zeros((BLOCK, LEAD - (k + 1) * BLOCK), jnp.bfloat16)
            inverse_high[at, (k + 1) * BLOCK :] = rest
            inverse_low[at, (k + 1) * BLOCK :] = rest
    mine = jnp.minimum(px * SIDE + py, LB - 1)
    mine_at = pl.ds(pl.multiple_of(mine * BLOCK, BLOCK), BLOCK)
    for k in range(LB):
        at = slice(k * BLOCK, (k + 1) * BLOCK)
        block = jnp.where(k == mine, jnp.where(row <= col, diag[k], 0.0), work[at, mine_at])
        own_rows[:, at] = jnp.where(k <= mine, block, 0.0).T


def factor(position, pieces):
    return pl.pallas_call(
        factor_kernel,
        out_shape=[
            jax.ShapeDtypeStruct((BLOCK, LEAD), jnp.float32),
            jax.ShapeDtypeStruct((LEAD, LEAD), jnp.bfloat16),
            jax.ShapeDtypeStruct((LEAD, LEAD), jnp.bfloat16),
        ],
        in_specs=[SMEM] + [ANY] * 10,
        out_specs=[VMEM] * 3,
        scratch_shapes=[
            pltpu.VMEM((LB * SLABS, SUB, LEAD), jnp.float32),
            pltpu.VMEM((LEAD, LEAD), jnp.float32),
            pltpu.VMEM((LB, BLOCK, BLOCK), jnp.float32),
            pltpu.VMEM((BLOCK, 2 * BLOCK), jnp.float32),
            pltpu.SemaphoreType.DMA((32,)),
        ],
        compiler_params=pltpu.CompilerParams(vmem_limit_bytes=VMEM_LIMIT),
        cost_estimate=pl.CostEstimate(flops=120 * 10**9, bytes_accessed=20 << 20, transcendentals=1024),
        name="factor",
    )(position, *pieces)


def solve_kernel(position, own, part1, part2, part3, sums, inverse_high, inverse_low, out, rows):
    x = position[0]
    for step, part in enumerate((own, part1, part2, part3)):
        source = (x + SIDE - step) % SIDE
        for l in range(2):
            rows[SIDE * l + source] = part[l]
    for m in range(LINES):
        for c in range(LB):
            at = slice(c * BLOCK, (c + 1) * BLOCK)
            values = sums[pl.ds(m * LB + c, SLICE, stride=SLOTS), :]
            rows[LB // SIDE + m, :, at] = rows[LB // SIDE + m, :, at] + values
    high, low = split(rows[LB // SIDE :].reshape(LINES * SLICE, LEAD))
    wide = 2 * BLOCK
    for c in range(LEAD // wide):
        end = (c + 1) * wide
        inv_high = inverse_high[end - wide : end, :end]
        inv_low = inverse_low[end - wide : end, :end]
        value = mul(high[:, :end], inv_high) + (
            mul(high[:, :end], inv_low) + mul(low[:, :end], inv_high)
        )
        out[:, :, end - wide : end] = value.reshape(LINES, SLICE, wide)


def solve(position, parts, sums, inverse_high, inverse_low):
    return pl.pallas_call(
        solve_kernel,
        out_shape=jax.ShapeDtypeStruct((LINES, SLICE, LEAD), jnp.float32),
        in_specs=[SMEM] + [VMEM] * 7,
        out_specs=VMEM,
        scratch_shapes=[pltpu.VMEM((2 * SIDE, SLICE, LEAD), jnp.float32)],
        compiler_params=pltpu.CompilerParams(vmem_limit_bytes=VMEM_LIMIT),
        name="solve",
    )(position, *parts, sums, inverse_high, inverse_low)


def product_kernel(position, *refs):
    along_x, along_y, (sums, out, own, cols, rows, high, low, sem) = refs[:5], refs[5:10], refs[10:]
    x, y = position[0], position[1]
    half = LINES // 2

    def place_cols(index, part):
        at = pl.ds(pl.multiple_of(index * SLICE, SLICE), SLICE)
        span = pl.ds(0, LINES) if part is None else pl.ds(part * half, half)
        return cols.at[span, at, :]

    def place_rows(index, part):
        start, count = (0, LINES) if part is None else (part * half, half)
        return rows.at[index, pl.ds(start, count)]

    copies = ring_copies(along_x, x, place_cols, sem, 0)
    copies += ring_copies(along_y, y, place_rows, sem, 5)
    for copy in copies:
        copy.start()
    for copy in copies[:5]:
        copy.wait()
    for m in range(LINES):
        at = slice(m * BLOCK, (m + 1) * BLOCK)
        high[at], low[at] = split(cols[m])
    own[0] = cols[jnp.maximum(x - 2, 0)]
    own[1] = cols[x + 2]
    for copy in copies[5:]:
        copy.wait()
    for z in range(SIDE):
        row_high, row_low = split(rows[z].reshape(LINES * SLICE, LEAD))
        value = mul(row_high, high[...]) + (mul(row_high, low[...]) + mul(row_low, high[...]))
        for m in range(LINES):
            row_block = LB + z + SIDE * m
            owner, first = row_block % GRID, 2 if row_block >= GRID else 0
            for n in range(LINES if first else 2):
                below = jnp.maximum(row_block - LB - y - SIDE * n, 0)
                slot = (TB - y) * n - 2 * n * (n - 1) + below
                out[owner, first + n] = sums[pl.ds(PSLOTS + slot, SLICE, stride=SLOTS), :] - value[
                    m * SLICE : (m + 1) * SLICE, n * BLOCK : (n + 1) * BLOCK
                ]
    for owner in range(LB):
        for n in range(2):
            out[owner, n] = jnp.zeros((SLICE, BLOCK), jnp.float32)


def product(position, along_x, along_y, sums):
    return pl.pallas_call(
        product_kernel,
        out_shape=[
            jax.ShapeDtypeStruct((GRID, OUT_SLOTS, SLICE, BLOCK), jnp.float32),
            jax.ShapeDtypeStruct((2, BLOCK, LEAD), jnp.float32),
        ],
        in_specs=[SMEM] + [ANY] * 10 + [VMEM],
        out_specs=[VMEM] * 2,
        scratch_shapes=[
            pltpu.VMEM((LINES, BLOCK, LEAD), jnp.float32),
            pltpu.VMEM((SIDE, LINES, SLICE, LEAD), jnp.float32),
            pltpu.VMEM((LINES * BLOCK, LEAD), jnp.bfloat16),
            pltpu.VMEM((LINES * BLOCK, LEAD), jnp.bfloat16),
            pltpu.SemaphoreType.DMA((10,)),
        ],
        compiler_params=pltpu.CompilerParams(vmem_limit_bytes=VMEM_LIMIT),
        name="product",
    )(position, *along_x, *along_y, sums)


def finish_kernel(position, entries, lead_rows, own, change, out):
    g = position[0] * SIDE + position[1]
    row = lax.broadcasted_iota(jnp.int32, (SLICE, BLOCK), 0)
    col = lax.broadcasted_iota(jnp.int32, (SLICE, BLOCK), 1)
    out[0, :, :LEAD] = jnp.where(g < LB, lead_rows[...], own[0])
    out[1, :, :LEAD] = own[1]
    for local in range(2):
        row_block = local * GRID + g
        for block in range(LB, FB):
            at = slice(block * BLOCK, (block + 1) * BLOCK)
            y, n = block % SIDE, (block - LB) // SIDE
            if local == 0 and n >= 2:
                out[local, :, at] = jnp.zeros((BLOCK, BLOCK), jnp.float32)
                continue
            for x in range(SIDE):
                span = slice(x * SLICE, (x + 1) * SLICE)
                value = entries[local, span, at] + change[x * SIDE + y, 2 * local + n]
                inside = (block * BLOCK + col) <= (row_block * BLOCK + x * SLICE + row)
                out[local, span, at] = jnp.where(inside, value, 0.0)


def finish(position, entries, lead_rows, own, change):
    return pl.pallas_call(
        finish_kernel,
        out_shape=jax.ShapeDtypeStruct(entries.shape, jnp.float32),
        in_specs=[SMEM] + [VMEM] * 4,
        out_specs=VMEM,
        compiler_params=pltpu.CompilerParams(vmem_limit_bytes=VMEM_LIMIT),
        name="finish",
    )(position, entries, lead_rows, own, change)


def destination_bins(owners, local_rows, picks):
    front, g = owners // GRID, owners % GRID
    shifted = local_rows + (local_rows * GRID + g < LB).astype(jnp.int32)
    row_block = shifted * GRID + g
    col_block = picks % (row_block + 1)
    panel = (row_block % SIDE * FRONTS + front) * SLOTS + (row_block - LB) // SIDE * LB + col_block
    y, n = col_block % SIDE, (col_block - LB) // SIDE
    slot = (TB - y) * n - 2 * n * (n - 1) + row_block - col_block
    trail = (y * FRONTS + front) * SLOTS + PSLOTS + slot
    return jnp.where(col_block < LB, panel, trail)


def across(values, axes):
    return lax.all_to_all(values, axes, split_axis=0, concat_axis=0)


def local(front_entries, child_tiles, tile_owner, tile_rows, tile_picks):
    x, y = lax.axis_index("x"), lax.axis_index("y")
    position = jnp.stack([x, y]).astype(jnp.int32)
    entries = front_entries[0, :, 0]
    half = BLOCK // 2
    lead = entries[0, :, :LEAD]
    other = lax.ppermute(lead[half:], "x", [(0, 2), (1, 3)])
    lead = jnp.where(x < 2, lead[:half], other).reshape(SLABS // 2, SUB, LEAD)
    bins = destination_bins(tile_owner[0, :, 0], tile_rows[0], tile_picks[0])
    bins = across(jnp.broadcast_to(bins, (DEVICES, 1, TILES)), ("x", "y", "front")).reshape(-1)
    lead, bins, tiles = lax.optimization_barrier((lead, bins, child_tiles))
    half = SLABS // 4
    lead, tiles = gather_lines(lead[:half], lead[half:], tiles[0].transpose(1, 0, 2))
    tiles, lead, entries = lax.optimization_barrier((tiles, lead, entries))
    rows = across(tiles, ("x", "y", "front")).reshape(-1, BLOCK)
    panel = entries[:, :, :LEAD].reshape(2, SIDE, SLICE, LEAD)
    panel = [
        lax.dynamic_index_in_dim(panel, (x + n) % SIDE, 1, keepdims=False) for n in range(SIDE)
    ]
    panel = [part if n == 0 else shift(part, "x", n) for n, part in enumerate(panel)]
    lead_rows, *inverse = factor(position, lead)
    bins, lead_rows, panel = lax.optimization_barrier((bins, lead_rows, panel))
    sums = combine(bins, rows).reshape(SLICE, SLOTS, BLOCK)
    sums = across(sums, ("y", "front")).reshape(-1, BLOCK)
    solved = solve(position, panel, sums, *inverse)
    change, own = product(position, ring(solved, "x"), ring(solved, "y"), sums)
    change = across(change, ("x", "y"))
    out = finish(position, entries, lead_rows, own, change)
    return out[None, :, None]


def solution(mesh):
    mesh = Mesh(mesh.devices.reshape(FRONTS, SIDE, SIDE), ("front", "x", "y"))
    grid = ("x", "y")
    return jax.shard_map(
        local,
        mesh=mesh,
        in_specs=(
            P("front", None, grid, None, None),
            P("front", grid, None, None),
            P("front", grid, None),
            P("front", grid),
            P("front", grid),
        ),
        out_specs=P("front", None, grid, None, None),
        check_vma=False,
    )
```

time: 494 us -> 338 us (0.68); the launches traced: 485 us -> 338 us
  waiting for transfers between devices: 177 us -> 54.3 us
  blocking collectives: 0 us -> 74.2 us
  Pallas kernels: 183 us -> 131 us
  starting transfers between devices: 83.7 us -> 58.6 us
  local copies, waits for them, and re-layouts: 29.7 us -> 16.4 us
  matrix products: 6.88 us -> 0 us
    ppermute x39 -> x26, waiting for transfers between devices: 171 us -> 45.8 us  [the longest x25 45.8 us: shift(): lax.ppermute(block, axis, [(i, (i + step) % SIDE) for i in range(SIDE)])]
    all_to_all x0 -> x2, blocking collectives: none -> 74.2 us  [across(): return lax.all_to_all(values, axes, split_axis=0, concat_axis=0)]
    pallas_call x1, Pallas kernels: 142 us -> 86.4 us  [factor(): pl.pallas_call(factor_kernel, out_shape=[jax.ShapeDtypeStruct((BLOCK, LEA...]
    ppermute x39 -> x26, starting transfers between devices: 58.1 us -> 42.8 us  [the longest x25 37.8 us: shift(): lax.ppermute(block, axis, [(i, (i + step) % SIDE) for i in range(SIDE)])]
    optimization_barrier x0 -> x1, local copies, waits for them, and re-layouts: none -> 11.5 us  [local(): lead, bins, tiles = lax.optimization_barrier((lead, bins, child_tiles))]
    unnamed x15 -> x34, local copies, waits for them, and re-layouts: 11.6 us -> 0.83 us
    slice x16 -> x10, local copies, waits for them, and re-layouts: 12.8 us -> 2.47 us  [the longest x1 1.33 us: local(): panel = entries[:, :, :LEAD].reshape(2, SIDE, SLICE, LEAD)]
    all_to_all x4 -> x2, starting transfers between devices: 25.6 us -> 15.8 us  [across(): return lax.all_to_all(values, axes, split_axis=0, concat_axis=0)]
  transfers between devices with their start and end apart: 43 -> 28, of which waited for: 14 -> 11; matrix products, arithmetic and copies ran while one was open for 6% -> 5% of each run, Pallas kernels for 34% -> 26%
where the time goes in v2:
time: 338 us
  Pallas kernels  131 us (39%)
  blocking collectives  74.2 us (22%)
  starting transfers between devices  58.6 us (17%)
  waiting for transfers between devices  54.3 us (16%)
  local copies, waits for them, and re-layouts  16.4 us (5%)
    pallas_call x1, Pallas kernels, factor(): pl.pallas_call(factor_kernel, out_shape=[jax.ShapeDtypeStruct((BLOCK, LEA...  86.4 us
    all_to_all x2, blocking collectives, across(): return lax.all_to_all(values, axes, split_axis=0, concat_axis=0)  74.2 us
    ppermute x25, waiting for transfers between devices, shift(): lax.ppermute(block, axis, [(i, (i + step) % SIDE) for i in range(SIDE)])  45.8 us
    ppermute x25, starting transfers between devices, shift(): lax.ppermute(block, axis, [(i, (i + step) % SIDE) for i in range(SIDE)])  37.8 us
    pallas_call x1, Pallas kernels, combine(): pl.pallas_call(combine_kernel, grid=(steps,), out_shape=jax.ShapeDtypeStr...  21 us
    all_to_all x2, starting transfers between devices, across(): return lax.all_to_all(values, axes, split_axis=0, concat_axis=0)  15.8 us
    pallas_call x1, Pallas kernels, product(): pl.pallas_call(product_kernel, out_shape=[jax.ShapeDtypeStruct((GRID, OUT...  12.3 us
    optimization_barrier x1, local copies, waits for them, and re-layouts, local(): lead, bins, tiles = lax.optimization_barrier((lead, bins, child_tiles))  11.5 us
  transfers between devices with their start and end apart: 28, of which 11 were waited for; matrix products, arithmetic and copies ran while one was open for 5% of the time, Pallas kernels for 26%

profile of v2, /device:TPU:0, one launch (start us, length us, event | category | flops | bytes accessed | tf_op | source)
XLA Modules:
  0.0 337.5 jit_solution(6299126987832415866)
XLA Ops:
  0.0 1.0 slice_bitcast_fusion
  1.0 5.0 %collective-permute-start = (f32[64,1024]{1,0:T(8,128)S(1)}, f32[64,1024]{1,0:T(8,128)S(1)}, u32[]{:S(2)}, u32[]{:S(2)}) collective-permute-start(f32[64,1024]{1,0:T(8,128)S(1)} %slice_bitcast_fusion), channel_id=1, source_target_pairs={{0,8},{4,12},{1,9},{5,13},{2,10},{6,14},{3,11},{7,15},{16,24},{20,... | collective-permute-start | bytes 786440 | tf_op jit(solution)/shard_map/ppermute | solution.py:419
  6.0 0.8 compare_select_fusion.5
  6.8 0.7 broadcast_in_dim.8
  7.5 8.6 %all-to-all-start = ((s32[128,1,128]{2,1,0:T(1,128)}), s32[128,1,128]{2,1,0:T(1,128)S(1)}, u32[]{:S(2)}, u32[]{:S(2)}) async-start(s32[128,1,128]{2,1,0:T(1,128)} %broadcast_in_dim.8), calls=%async_computation | async-start | bytes 131072 | tf_op jit(solution)/shard_map/all_to_all | solution.py:410
  16.2 1.0 fusion.1
  17.2 8.4 %all-to-all-done = s32[128,1,128]{2,1,0:T(1,128)S(1)} async-done(((s32[128,1,128]{2,1,0:T(1,128)}), s32[128,1,128]{2,1,0:T(1,128)S(1)}, u32[]{:S(2)}, u32[]{:S(2)}) %all-to-all-start) | async-done | bytes 65568 | tf_op jit(solution)/shard_map/all_to_all | solution.py:410
  25.6 1.1 collective-permute-start.5
  26.8 2.3 collective-permute-start.4
  29.0 0.9 collective-permute-start.2
  29.9 2.4 collective-permute-start.1
  32.3 1.2 collective-permute-done.5
  34.1 11.5 %copy.11 = f32[1,128,128,128]{3,1,2,0:T(8,128)} copy(f32[1,128,128,128]{3,2,1,0:T(8,128)} %param.6) | data formatting | bytes 16777216 | tf_op jit(solution)/shard_map/optimization_barrier | solution.py:423
  45.8 0.6 collective-permute-start.8
  46.4 2.7 collective-permute-start.7
  49.5 2.9 collective-permute-start.11
  52.3 5.5 %collective-permute-done.8.refs_4_ = f32[4,4,8,1024]{3,2,1,0:T(8,128)S(1)} collective-permute-done((f32[4,4,8,1024]{3,2,1,0:T(8,128)S(1)}, f32[4,4,8,1024]{3,2,1,0:T(8,128)S(1)}, u32[]{:S(2)}, u32[]{:S(2)}) %collective-permute-start.8) | collective-permute-done | bytes 524320 | tf_op jit(solution)/shard_map/ppermute | solution.py:54
  58.0 3.3 collective-permute-start.10
  61.3 1.2 collective-permute-start.13
  62.5 0.8 copy-done.14
  63.3 2.3 collective-permute-start.14
  66.1 2.9 collective-permute-done.13.refs_7_
  69.0 0.7 collective-permute-done.14.refs_8_
  69.8 7.2 %all-to-all-start.1 = ((f32[128,128,128]{2,1,0:T(8,128)}), f32[128,128,128]{2,1,0:T(8,128)}, u32[]{:S(2)}, u32[]{:S(2)}) async-start(f32[128,128,128]{2,1,0:T(8,128)} %bitcast.70), calls=%async_computation.1 | async-start | bytes 16777216 | tf_op jit(solution)/shard_map/all_to_all | solution.py:410
  77.0 1.3 slice.58
  78.3 0.8 dynamic-slice_bitcast_fusion
  79.2 2.1 collective-permute-start.17
  81.3 0.9 collective-permute-start.16
  82.1 0.9 collective-permute-start.15
  83.0 86.4 %factor.1 = (f32[128,1024]{1,0:T(8,128)}, bf16[1024,1024]{1,0:T(8,128)(2,1)}, bf16[1024,1024]{1,0:T(8,128)(2,1)}) custom-call(s32[2]{0:T(128)} %pad_add_fusion.position, f32[4,4,8,1024]{3,2,1,0:T(8,128)} %copy-done.5, f32[4,4,8,1024]{3,2,1,0:T(8,128)} %copy-done.12, f32[2,4,8,1024]{3,2,1,0:T(8,128)} %copy-done.16, ...), custom_call_target="tpu_custom_call" | custom-call | flops 120000004096 | bytes 20971520 | tf_op jit(solution)/shard_map/factor/pallas_call | solution.py:243
  169.4 10.2 %collective-permute-done.17.part3 = f32[2,32,1024]{2,1,0:T(8,128)S(1)} collective-permute-done((f32[2,32,1024]{2,1,0:T(8,128)S(1)}, f32[2,32,1024]{2,1,0:T(8,128)S(1)}, u32[]{:S(2)}, u32[]{:S(2)}) %collective-permute-start.17) | collective-permute-done | bytes 262176 | tf_op jit(solution)/shard_map/ppermute | solution.py:54
  179.6 2.0 collective-permute-done.16.part2
  181.5 21.0 %combine.1 = f32[4352,128]{1,0:T(8,128)} custom-call(s32[16384]{0:T(1024)} %bitcast.85, f32[16384,128]{1,0:T(8,128)} %bitcast.25.x), custom_call_target="tpu_custom_call" | custom-call | flops 20000000000 | bytes 20971520 | tf_op jit(solution)/shard_map/combine/pallas_call | solution.py:138
  202.6 43.4 %all_to_all.20 = f32[32,136,128]{2,1,0:T(8,128)} all-to-all(f32[32,136,128]{2,1,0:T(8,128)} %bitcast.78), channel_id=1, replica_groups=mesh['front'=8,'x'=4,'y'=4] {'y','front'}, dimensions={0} | all-to-all | bytes 4456448 | tf_op jit(solution)/shard_map/all_to_all | solution.py:410
  246.0 5.6 %solve.1.refs_0_.refs_5_ = f32[6,32,1024]{2,1,0:T(8,128)} custom-call(s32[2]{0:T(128)} %pad_add_fusion.position, f32[2,32,1024]{2,1,0:T(8,128)} %get-tuple-element.53.own, f32[2,32,1024]{2,1,0:T(8,128)} %copy-done.10, f32[2,32,1024]{2,1,0:T(8,128)} %copy-done.9, f32[2,32,1024]{2,1,0:T(8,128)} %copy-done.8, f32[4352,128]{1,0:T(8,128)} %bitcast.71, ...), custom_call_target="tpu_custom_call" | custom-call | tf_op jit(solution)/shard_map/solve/pallas_call | solution.py:289
  252.2 2.7 collective-permute-start.22
  254.8 2.5 collective-permute-start.19
  257.3 0.7 collective-permute-start.18
  258.1 14.5 %collective-permute-done.23.refs_9_ = f32[6,32,1024]{2,1,0:T(8,128)S(1)} collective-permute-done((f32[6,32,1024]{2,1,0:T(8,128)}, f32[6,32,1024]{2,1,0:T(8,128)S(1)}, u32[]{:S(2)}, u32[]{:S(2)}) %collective-permute-start.23) | collective-permute-done | bytes 786464 | tf_op jit(solution)/shard_map/ppermute | solution.py:54
  272.7 3.3 collective-permute-start.25
  276.1 2.6 collective-permute-start.20
  278.7 1.0 collective-permute-start.21
  279.7 4.5 %collective-permute-done.24.refs_7_ = f32[3,32,1024]{2,1,0:T(8,128)S(1)} collective-permute-done((f32[3,32,1024]{2,1,0:T(8,128)S(1)}, f32[3,32,1024]{2,1,0:T(8,128)S(1)}, u32[]{:S(2)}, u32[]{:S(2)}) %collective-permute-start.24) | collective-permute-done | bytes 393248 | tf_op jit(solution)/shard_map/ppermute | solution.py:54
  284.2 3.2 collective-permute-done.20.refs_2_
  287.4 1.1 collective-permute-done.21.refs_3_
  288.6 12.3 %product.1 = (f32[16,8,32,128]{3,2,1,0:T(8,128)}, f32[2,128,1024]{2,1,0:T(8,128)}) custom-call(s32[2]{0:T(128)} %pad_add_fusion.position, f32[6,32,1024]{2,1,0:T(8,128)} %solve.1.refs_0_.refs_5_, f32[6,32,1024]{2,1,0:T(8,128)} %copy-done.3, f32[3,32,1024]{2,1,0:T(8,128)} %collective-permute-done.20.refs_2_, f32[3,32,1024]{2,1,0:T(8,128)} %collective-permute-done.21.refs_3_, ...), custom_call_target="tpu_custom_call" | custom-call | tf_op jit(solution)/shard_map/product/pallas_call | solution.py:345
  300.9 30.7 %all_to_all.21.change = f32[16,8,32,128]{3,2,1,0:T(8,128)} all-to-all(f32[16,8,32,128]{3,2,1,0:T(8,128)} %get-tuple-element.62), channel_id=1, replica_groups=mesh['front'=8,'x'=4,'y'=4] {'x','y'}, dimensions={0} | all-to-all | bytes 4194304 | tf_op jit(solution)/shard_map/all_to_all | solution.py:410
  331.6 5.9 %finish.1 = f32[2,128,4096]{2,1,0:T(8,128)} custom-call(s32[2]{0:T(128)} %pad_add_fusion.position, f32[2,128,4096]{2,1,0:T(8,128)} %bitcast.76, f32[128,1024]{1,0:T(8,128)} %get-tuple-element.52.lead_rows, f32[2,128,1024]{2,1,0:T(8,128)} %get-tuple-element.61.own, f32[16,8,32,128]{3,2,1,0:T(8,128)} %all_to_all.21.change), custom_call_target="tpu_custom_call" | custom-call | tf_op jit(solution)/shard_map/finish/pallas_call | solution.py:387
  (68 shorter events, 2.7 us)
Async XLA Ops:
  1.0 15.2 %collective-permute-start = (f32[64,1024]{1,0:T(8,128)S(1)}, f32[64,1024]{1,0:T(8,128)S(1)}, u32[]{:S(2)}, u32[]{:S(2)}) collective-permute-start(f32[64,1024]{1,0:T(8,128)S(1)} %slice_bitcast_fusion), channel_id=1, source_target_pairs={{0,8},{4,12},{1,9},{5,13},{2,10},{6,14},{3,11},{7,15},{16,24},{20,... | collective-permute-start | bytes 786440 | tf_op jit(solution)/shard_map/ppermute | solution.py:419
  7.5 18.1 %all-to-all-start = ((s32[128,1,128]{2,1,0:T(1,128)}), s32[128,1,128]{2,1,0:T(1,128)S(1)}, u32[]{:S(2)}, u32[]{:S(2)}) async-start(s32[128,1,128]{2,1,0:T(1,128)} %broadcast_in_dim.8), calls=%async_computation | async-start | bytes 131072 | tf_op jit(solution)/shard_map/all_to_all | solution.py:410
  25.6 20.0 %copy-start.15 = (s32[128,1,128]{2,1,0:T(1,128)}, s32[128,1,128]{2,1,0:T(1,128)S(1)}, u32[]{:S(2)}) copy-start(s32[128,1,128]{2,1,0:T(1,128)S(1)} %all-to-all-done) | copy-start | bytes 196612
  25.6 7.8 %collective-permute-start.5 = (f32[4,8,1024]{2,1,0:T(8,128)S(1)}, f32[4,8,1024]{2,1,0:T(8,128)S(1)}, u32[]{:S(2)}, u32[]{:S(2)}) collective-permute-start(f32[4,8,1024]{2,1,0:T(8,128)S(1)} %get-tuple-element.69), channel_id=1, source_target_pairs={{0,2},{1,3},{2,0},{3,1},{4,6},{5,7},{6,4},{7,5},{8,10},{9,11},{10,... | collective-permute-start | bytes 393224 | tf_op jit(solution)/shard_map/ppermute | solution.py:54
  26.8 18.8 %collective-permute-start.4 = (f32[4,8,1024]{2,1,0:T(8,128)S(1)}, f32[4,8,1024]{2,1,0:T(8,128)S(1)}, u32[]{:S(2)}, u32[]{:S(2)}) collective-permute-start(f32[4,8,1024]{2,1,0:T(8,128)S(1)} %get-tuple-element.69), channel_id=1, source_target_pairs={{0,3},{1,0},{2,1},{3,2},{4,7},{5,4},{6,5},{7,6},{8,11},{9,8},{10,9... | collective-permute-start | bytes 393224 | tf_op jit(solution)/shard_map/ppermute | solution.py:54
  29.0 16.6 %collective-permute-start.6 = (f32[4,8,1024]{2,1,0:T(8,128)S(1)}, f32[4,8,1024]{2,1,0:T(8,128)S(1)}, u32[]{:S(2)}, u32[]{:S(2)}) collective-permute-start(f32[4,8,1024]{2,1,0:T(8,128)S(1)} %get-tuple-element.69), channel_id=1, source_target_pairs={{0,1},{1,2},{2,3},{3,0},{4,5},{5,6},{6,7},{7,4},{8,9},{9,10},{10,1... | collective-permute-start | bytes 393224 | tf_op jit(solution)/shard_map/ppermute | solution.py:54
  29.0 16.7 %collective-permute-start.2 = (f32[4,8,1024]{2,1,0:T(8,128)S(1)}, f32[4,8,1024]{2,1,0:T(8,128)S(1)}, u32[]{:S(2)}, u32[]{:S(2)}) collective-permute-start(f32[4,8,1024]{2,1,0:T(8,128)S(1)} %get-tuple-element.70), channel_id=1, source_target_pairs={{0,8},{4,12},{8,0},{12,4},{1,9},{5,13},{9,1},{13,5},{2,10},{6,14},... | collective-permute-start | bytes 393224 | tf_op jit(solution)/shard_map/ppermute | solution.py:54
  29.9 15.8 %collective-permute-start.1 = (f32[4,8,1024]{2,1,0:T(8,128)S(1)}, f32[4,8,1024]{2,1,0:T(8,128)S(1)}, u32[]{:S(2)}, u32[]{:S(2)}) collective-permute-start(f32[4,8,1024]{2,1,0:T(8,128)S(1)} %get-tuple-element.70), channel_id=1, source_target_pairs={{0,12},{4,0},{8,4},{12,8},{1,13},{5,1},{9,5},{13,9},{2,14},{6,2},{... | collective-permute-start | bytes 393224 | tf_op jit(solution)/shard_map/ppermute | solution.py:54
  33.5 12.2 %collective-permute-start.3 = (f32[4,8,1024]{2,1,0:T(8,128)S(1)}, f32[4,8,1024]{2,1,0:T(8,128)S(1)}, u32[]{:S(2)}, u32[]{:S(2)}) collective-permute-start(f32[4,8,1024]{2,1,0:T(8,128)S(1)} %get-tuple-element.70), channel_id=1, source_target_pairs={{0,4},{4,8},{8,12},{12,0},{1,5},{5,9},{9,13},{13,1},{2,6},{6,10},{... | collective-permute-start | bytes 393224 | tf_op jit(solution)/shard_map/ppermute | solution.py:54
  45.7 24.1 %copy-start.4 = (f32[4,4,8,1024]{3,2,1,0:T(8,128)}, f32[4,4,8,1024]{3,2,1,0:T(8,128)S(1)}, u32[]{:S(2)}) copy-start(f32[4,4,8,1024]{3,2,1,0:T(8,128)S(1)} %pad_maximum_fusion.1.refs_5_) | copy-start | bytes 1572868
  45.8 24.0 %copy-start.5 = (f32[4,4,8,1024]{3,2,1,0:T(8,128)}, f32[4,4,8,1024]{3,2,1,0:T(8,128)S(1)}, u32[]{:S(2)}) copy-start(f32[4,4,8,1024]{3,2,1,0:T(8,128)S(1)} %pad_maximum_fusion.refs_0_) | copy-start | bytes 1572868
  45.8 12.1 %collective-permute-start.8 = (f32[4,4,8,1024]{3,2,1,0:T(8,128)S(1)}, f32[4,4,8,1024]{3,2,1,0:T(8,128)S(1)}, u32[]{:S(2)}, u32[]{:S(2)}) collective-permute-start(f32[4,4,8,1024]{3,2,1,0:T(8,128)S(1)} %pad_maximum_fusion.refs_0_), channel_id=1, source_target_pairs={{0,1},{1,2},{2,3},{3,0},{4,5},{5,6},{6,7},{7,4},{8,9},{9,10},{10,1... | collective-permute-start | bytes 1572872 | tf_op jit(solution)/shard_map/ppermute | solution.py:54
  46.4 11.6 %collective-permute-start.7 = (f32[4,4,8,1024]{3,2,1,0:T(8,128)S(1)}, f32[4,4,8,1024]{3,2,1,0:T(8,128)S(1)}, u32[]{:S(2)}, u32[]{:S(2)}) collective-permute-start(f32[4,4,8,1024]{3,2,1,0:T(8,128)S(1)} %pad_maximum_fusion.refs_0_), channel_id=1, source_target_pairs={{0,3},{1,0},{2,1},{3,2},{4,7},{5,4},{6,5},{7,6},{8,11},{9,8},{10,9... | collective-permute-start | bytes 1572872 | tf_op jit(solution)/shard_map/ppermute | solution.py:54
  49.1 12.2 %collective-permute-start.12 = (f32[4,4,8,1024]{3,2,1,0:T(8,128)S(1)}, f32[4,4,8,1024]{3,2,1,0:T(8,128)S(1)}, u32[]{:S(2)}, u32[]{:S(2)}) collective-permute-start(f32[4,4,8,1024]{3,2,1,0:T(8,128)S(1)} %pad_maximum_fusion.1.refs_5_), channel_id=1, source_target_pairs={{0,4},{4,8},{8,12},{12,0},{1,5},{5,9},{9,13},{13,1},{2,6},{6,10},{... | collective-permute-start | bytes 1572872 | tf_op jit(solution)/shard_map/ppermute | solution.py:54
  49.5 13.0 %collective-permute-start.11 = (f32[4,4,8,1024]{3,2,1,0:T(8,128)S(1)}, f32[4,4,8,1024]{3,2,1,0:T(8,128)S(1)}, u32[]{:S(2)}, u32[]{:S(2)}) collective-permute-start(f32[4,4,8,1024]{3,2,1,0:T(8,128)S(1)} %pad_maximum_fusion.1.refs_5_), channel_id=1, source_target_pairs={{0,12},{4,0},{8,4},{12,8},{1,13},{5,1},{9,5},{13,9},{2,14},{6,2},{... | collective-permute-start | bytes 1572872 | tf_op jit(solution)/shard_map/ppermute | solution.py:54
  57.8 11.9 %copy-start.11 = (f32[4,4,8,1024]{3,2,1,0:T(8,128)}, f32[4,4,8,1024]{3,2,1,0:T(8,128)S(1)}, u32[]{:S(2)}) copy-start(f32[4,4,8,1024]{3,2,1,0:T(8,128)S(1)} %collective-permute-done.8.refs_4_) | copy-start | bytes 1572868
  57.9 8.2 %collective-permute-start.9 = (f32[2,4,8,1024]{3,2,1,0:T(8,128)S(1)}, f32[2,4,8,1024]{3,2,1,0:T(8,128)S(1)}, u32[]{:S(2)}, u32[]{:S(2)}) collective-permute-start(f32[2,4,8,1024]{3,2,1,0:T(8,128)S(1)} %slice.65), channel_id=1, source_target_pairs={{0,1},{1,2},{2,3},{3,0},{4,5},{5,6},{6,7},{7,4},{8,9},{9,10},{10,1... | collective-permute-start | bytes 786440 | tf_op jit(solution)/shard_map/ppermute | solution.py:54
  58.0 11.8 %copy-start.12 = (f32[4,4,8,1024]{3,2,1,0:T(8,128)}, f32[4,4,8,1024]{3,2,1,0:T(8,128)S(1)}, u32[]{:S(2)}) copy-start(f32[4,4,8,1024]{3,2,1,0:T(8,128)S(1)} %collective-permute-done.7.refs_1_) | copy-start | bytes 1572868
  58.0 8.1 %collective-permute-start.10 = (f32[2,4,8,1024]{3,2,1,0:T(8,128)S(1)}, f32[2,4,8,1024]{3,2,1,0:T(8,128)}, u32[]{:S(2)}, u32[]{:S(2)}) collective-permute-start(f32[2,4,8,1024]{3,2,1,0:T(8,128)S(1)} %slice.66), channel_id=1, source_target_pairs={{0,3},{1,0},{2,1},{3,2},{4,7},{5,4},{6,5},{7,6},{8,11},{9,8},{10,9... | collective-permute-start | bytes 786440 | tf_op jit(solution)/shard_map/ppermute | solution.py:54
  61.3 1.2 copy-start.13
  61.3 7.8 %collective-permute-start.13 = (f32[2,4,8,1024]{3,2,1,0:T(8,128)S(1)}, f32[2,4,8,1024]{3,2,1,0:T(8,128)}, u32[]{:S(2)}, u32[]{:S(2)}) collective-permute-start(f32[2,4,8,1024]{3,2,1,0:T(8,128)S(1)} %slice.67), channel_id=1, source_target_pairs={{0,4},{4,8},{8,12},{12,0},{1,5},{5,9},{9,13},{13,1},{2,6},{6,10},{... | collective-permute-start | bytes 786440 | tf_op jit(solution)/shard_map/ppermute | solution.py:54
  62.5 0.8 copy-start.14
  63.3 6.5 %collective-permute-start.14 = (f32[2,4,8,1024]{3,2,1,0:T(8,128)S(1)}, f32[2,4,8,1024]{3,2,1,0:T(8,128)}, u32[]{:S(2)}, u32[]{:S(2)}) collective-permute-start(f32[2,4,8,1024]{3,2,1,0:T(8,128)S(1)} %slice.68), channel_id=1, source_target_pairs={{0,12},{4,0},{8,4},{12,8},{1,13},{5,1},{9,5},{13,9},{2,14},{6,2},{... | collective-permute-start | bytes 786440 | tf_op jit(solution)/shard_map/ppermute | solution.py:54
  66.1 3.6 %copy-start.16 = (f32[2,4,8,1024]{3,2,1,0:T(8,128)}, f32[2,4,8,1024]{3,2,1,0:T(8,128)S(1)}, u32[]{:S(2)}) copy-start(f32[2,4,8,1024]{3,2,1,0:T(8,128)S(1)} %collective-permute-done.9.refs_2_) | copy-start | bytes 786436
  69.8 111.8 %all-to-all-start.1 = ((f32[128,128,128]{2,1,0:T(8,128)}), f32[128,128,128]{2,1,0:T(8,128)}, u32[]{:S(2)}, u32[]{:S(2)}) async-start(f32[128,128,128]{2,1,0:T(8,128)} %bitcast.70), calls=%async_computation.1 | async-start | bytes 16777216 | tf_op jit(solution)/shard_map/all_to_all | solution.py:410
  79.2 100.4 %collective-permute-start.17 = (f32[2,32,1024]{2,1,0:T(8,128)S(1)}, f32[2,32,1024]{2,1,0:T(8,128)S(1)}, u32[]{:S(2)}, u32[]{:S(2)}) collective-permute-start(f32[2,32,1024]{2,1,0:T(8,128)S(1)} %get-tuple-element.63), channel_id=1, source_target_pairs={{0,12},{4,0},{8,4},{12,8},{1,13},{5,1},{9,5},{13,9},{2,14},{6,2},{... | collective-permute-start | bytes 786440 | tf_op jit(solution)/shard_map/ppermute | solution.py:54
  81.3 100.3 %collective-permute-start.16 = (f32[2,32,1024]{2,1,0:T(8,128)S(1)}, f32[2,32,1024]{2,1,0:T(8,128)S(1)}, u32[]{:S(2)}, u32[]{:S(2)}) collective-permute-start(f32[2,32,1024]{2,1,0:T(8,128)S(1)} %get-tuple-element.64), channel_id=1, source_target_pairs={{0,8},{4,12},{8,0},{12,4},{1,9},{5,13},{9,1},{13,5},{2,10},{6,14},... | collective-permute-start | bytes 786440 | tf_op jit(solution)/shard_map/ppermute | solution.py:54
  82.1 99.4 %collective-permute-start.15 = (f32[2,32,1024]{2,1,0:T(8,128)S(1)}, f32[2,32,1024]{2,1,0:T(8,128)S(1)}, u32[]{:S(2)}, u32[]{:S(2)}) collective-permute-start(f32[2,32,1024]{2,1,0:T(8,128)S(1)} %get-tuple-element.65), channel_id=1, source_target_pairs={{0,4},{4,8},{8,12},{12,0},{1,5},{5,9},{9,13},{13,1},{2,6},{6,10},{... | collective-permute-start | bytes 786440 | tf_op jit(solution)/shard_map/ppermute | solution.py:54
  179.6 23.0 %copy-start.8 = (f32[2,32,1024]{2,1,0:T(8,128)}, f32[2,32,1024]{2,1,0:T(8,128)S(1)}, u32[]{:S(2)}) copy-start(f32[2,32,1024]{2,1,0:T(8,128)S(1)} %collective-permute-done.17.part3) | copy-start | bytes 786436
  181.5 21.0 %copy-start.9 = (f32[2,32,1024]{2,1,0:T(8,128)}, f32[2,32,1024]{2,1,0:T(8,128)S(1)}, u32[]{:S(2)}) copy-start(f32[2,32,1024]{2,1,0:T(8,128)S(1)} %collective-permute-done.16.part2) | copy-start | bytes 786436
  181.5 21.0 %copy-start.10 = (f32[2,32,1024]{2,1,0:T(8,128)}, f32[2,32,1024]{2,1,0:T(8,128)S(1)}, u32[]{:S(2)}) copy-start(f32[2,32,1024]{2,1,0:T(8,128)S(1)} %collective-permute-done.15.part1) | copy-start | bytes 786436
  251.6 21.0 %collective-permute-start.23 = (f32[6,32,1024]{2,1,0:T(8,128)}, f32[6,32,1024]{2,1,0:T(8,128)S(1)}, u32[]{:S(2)}, u32[]{:S(2)}) collective-permute-start(f32[6,32,1024]{2,1,0:T(8,128)} %solve.1.refs_0_.refs_5_), channel_id=1, source_target_pairs={{0,1},{1,2},{2,3},{3,0},{4,5},{5,6},{6,7},{7,4},{8,9},{9,10},{10,1... | collective-permute-start | bytes 2359304 | tf_op jit(solution)/shard_map/ppermute | solution.py:54
  252.2 20.5 %collective-permute-start.22 = (f32[6,32,1024]{2,1,0:T(8,128)}, f32[6,32,1024]{2,1,0:T(8,128)S(1)}, u32[]{:S(2)}, u32[]{:S(2)}) collective-permute-start(f32[6,32,1024]{2,1,0:T(8,128)} %solve.1.refs_0_.refs_5_), channel_id=1, source_target_pairs={{0,3},{1,0},{2,1},{3,2},{4,7},{5,4},{6,5},{7,6},{8,11},{9,8},{10,9... | collective-permute-start | bytes 2359304 | tf_op jit(solution)/shard_map/ppermute | solution.py:54
  254.8 21.2 %collective-permute-start.19 = (f32[6,32,1024]{2,1,0:T(8,128)}, f32[6,32,1024]{2,1,0:T(8,128)S(1)}, u32[]{:S(2)}, u32[]{:S(2)}) collective-permute-start(f32[6,32,1024]{2,1,0:T(8,128)} %solve.1.refs_0_.refs_5_), channel_id=1, source_target_pairs={{0,4},{4,8},{8,12},{12,0},{1,5},{5,9},{9,13},{13,1},{2,6},{6,10},{... | collective-permute-start | bytes 2359304 | tf_op jit(solution)/shard_map/ppermute | solution.py:54
  257.3 21.3 %collective-permute-start.18 = (f32[6,32,1024]{2,1,0:T(8,128)}, f32[6,32,1024]{2,1,0:T(8,128)S(1)}, u32[]{:S(2)}, u32[]{:S(2)}) collective-permute-start(f32[6,32,1024]{2,1,0:T(8,128)} %solve.1.refs_0_.refs_5_), channel_id=1, source_target_pairs={{0,12},{4,0},{8,4},{12,8},{1,13},{5,1},{9,5},{13,9},{2,14},{6,2},{... | collective-permute-start | bytes 2359304 | tf_op jit(solution)/shard_map/ppermute | solution.py:54
  272.6 15.9 %copy-start = (f32[6,32,1024]{2,1,0:T(8,128)}, f32[6,32,1024]{2,1,0:T(8,128)S(1)}, u32[]{:S(2)}) copy-start(f32[6,32,1024]{2,1,0:T(8,128)S(1)} %collective-permute-done.23.refs_9_) | copy-start | bytes 2359300
  272.6 11.6 %collective-permute-start.24 = (f32[3,32,1024]{2,1,0:T(8,128)S(1)}, f32[3,32,1024]{2,1,0:T(8,128)S(1)}, u32[]{:S(2)}, u32[]{:S(2)}) collective-permute-start(f32[3,32,1024]{2,1,0:T(8,128)S(1)} %slice.71), channel_id=1, source_target_pairs={{0,1},{1,2},{2,3},{3,0},{4,5},{5,6},{6,7},{7,4},{8,9},{9,10},{10,1... | collective-permute-start | bytes 1179656 | tf_op jit(solution)/shard_map/ppermute | solution.py:54
  272.7 15.8 %copy-start.1 = (f32[6,32,1024]{2,1,0:T(8,128)}, f32[6,32,1024]{2,1,0:T(8,128)S(1)}, u32[]{:S(2)}) copy-start(f32[6,32,1024]{2,1,0:T(8,128)S(1)} %collective-permute-done.22.refs_6_) | copy-start | bytes 2359300
  272.7 11.4 %collective-permute-start.25 = (f32[3,32,1024]{2,1,0:T(8,128)S(1)}, f32[3,32,1024]{2,1,0:T(8,128)S(1)}, u32[]{:S(2)}, u32[]{:S(2)}) collective-permute-start(f32[3,32,1024]{2,1,0:T(8,128)S(1)} %slice.72), channel_id=1, source_target_pairs={{0,3},{1,0},{2,1},{3,2},{4,7},{5,4},{6,5},{7,6},{8,11},{9,8},{10,9... | collective-permute-start | bytes 1179656 | tf_op jit(solution)/shard_map/ppermute | solution.py:54
  276.0 12.5 %copy-start.2 = (f32[6,32,1024]{2,1,0:T(8,128)}, f32[6,32,1024]{2,1,0:T(8,128)S(1)}, u32[]{:S(2)}) copy-start(f32[6,32,1024]{2,1,0:T(8,128)S(1)} %collective-permute-done.19.refs_4_) | copy-start | bytes 2359300
  276.1 11.3 %collective-permute-start.20 = (f32[3,32,1024]{2,1,0:T(8,128)S(1)}, f32[3,32,1024]{2,1,0:T(8,128)}, u32[]{:S(2)}, u32[]{:S(2)}) collective-permute-start(f32[3,32,1024]{2,1,0:T(8,128)S(1)} %slice.69), channel_id=1, source_target_pairs={{0,4},{4,8},{8,12},{12,0},{1,5},{5,9},{9,13},{13,1},{2,6},{6,10},{... | collective-permute-start | bytes 1179656 | tf_op jit(solution)/shard_map/ppermute | solution.py:54
  278.6 9.9 %copy-start.3 = (f32[6,32,1024]{2,1,0:T(8,128)}, f32[6,32,1024]{2,1,0:T(8,128)S(1)}, u32[]{:S(2)}) copy-start(f32[6,32,1024]{2,1,0:T(8,128)S(1)} %collective-permute-done.18.refs_1_) | copy-start | bytes 2359300
  278.7 9.9 %collective-permute-start.21 = (f32[3,32,1024]{2,1,0:T(8,128)S(1)}, f32[3,32,1024]{2,1,0:T(8,128)}, u32[]{:S(2)}, u32[]{:S(2)}) collective-permute-start(f32[3,32,1024]{2,1,0:T(8,128)S(1)} %slice.70), channel_id=1, source_target_pairs={{0,12},{4,0},{8,4},{12,8},{1,13},{5,1},{9,5},{13,9},{2,14},{6,2},{... | collective-permute-start | bytes 1179656 | tf_op jit(solution)/shard_map/ppermute | solution.py:54
  284.2 4.4 %copy-start.6 = (f32[3,32,1024]{2,1,0:T(8,128)}, f32[3,32,1024]{2,1,0:T(8,128)S(1)}, u32[]{:S(2)}) copy-start(f32[3,32,1024]{2,1,0:T(8,128)S(1)} %collective-permute-done.24.refs_7_) | copy-start | bytes 1179652
  284.2 4.4 %copy-start.7 = (f32[3,32,1024]{2,1,0:T(8,128)}, f32[3,32,1024]{2,1,0:T(8,128)S(1)}, u32[]{:S(2)}) copy-start(f32[3,32,1024]{2,1,0:T(8,128)S(1)} %collective-permute-done.25.refs_8_) | copy-start | bytes 1179652

commit v3 on v2

v3 whole, which is shorter than its diff:
```python
import functools
import jax
import jax.numpy as jnp
from jax import lax
from jax.experimental import pallas as pl
from jax.experimental.pallas import tpu as pltpu
from jax.sharding import Mesh
from jax.sharding import PartitionSpec as P

BLOCK = 128
LEAD = 1024
LB = LEAD // BLOCK
FRONTS = 8
GRID = 16
SIDE = 4
DEVICES = FRONTS * GRID
FB = 32
TB = FB - LB
TILES = 128
LINES = TB // SIDE
SLICE = BLOCK // SIDE
PSLOTS = LINES * LB
TSLOTS = 88
PBINS = SIDE * FRONTS * PSLOTS
TBINS = SIDE * FRONTS * TSLOTS
BINS = PBINS + TBINS
OUT_SLOTS = 2 + LINES
SUB = 8
SLABS = BLOCK // SUB
ACCS = 8
VMEM_LIMIT = 60 << 20

highest = lax.Precision.HIGHEST
ANY = pl.BlockSpec(memory_space=pl.ANY)
VMEM = pl.BlockSpec(memory_space=pltpu.VMEM)
SMEM = pl.BlockSpec(memory_space=pltpu.SMEM)


def split(values):
    high = values.astype(jnp.bfloat16)
    return high, (values - high.astype(jnp.float32)).astype(jnp.bfloat16)


def mul(a, b):
    return lax.dot_general(a, b, (((1,), (1,)), ((), ())), preferred_element_type=jnp.float32)


def tdot(a, b):
    return lax.dot_general(
        a, b, (((0,), (0,)), ((), ())), precision=highest, preferred_element_type=jnp.float32
    )


def shift(block, axis, step):
    return lax.ppermute(block, axis, [(i, (i + step) % SIDE) for i in range(SIDE)])


def gather_front(values):
    others = [
        lax.ppermute(values, "front", [(i, i ^ k) for i in range(FRONTS)]) for k in range(1, FRONTS)
    ]
    return jnp.stack([values, *others])


def ring_near(block, axis):
    return shift(block, axis, -1), shift(block, axis, 1)


def ring_far(near, axis):
    from_next, from_prev = near
    half = from_prev.shape[0] // 2
    return shift(from_prev[:half], axis, 1), shift(from_next[half:], axis, -1)


def ring_pieces(block, near, far):
    return [block, near[0], *far, near[1]]


def gather_lines(first, second, given, work):
    lines = []
    for part, axis in ((first, "x"), (second, "y")):
        lines.append(jnp.stack([part, *(shift(part, axis, -n) for n in range(1, SIDE))]))
    lines, given = lax.optimization_barrier((lines, given))
    near = [ring_near(line, axis) for line, axis in zip(lines, ("y", "x"))]
    near, done = lax.optimization_barrier((near, work(given)))
    far = [ring_far(pair, axis) for pair, axis in zip(near, ("y", "x"))]
    return lines, near, far, done


def line_copies(pieces, place, sem, x, y):
    copies = []
    for h in range(2):
        own, nxt, far_a, far_b, prv = pieces[5 * h : 5 * h + 5]
        for outer in range(SIDE):
            for inner in range(SIDE):
                if outer == 2:
                    src = (far_a if inner < 2 else far_b).at[inner % 2]
                else:
                    src = (own, nxt, None, prv)[outer].at[inner]
                dx, dy = (inner, outer) if h == 0 else (outer, inner)
                for start, count, dst in place(h, (x + dx) % SIDE, (y + dy) % SIDE):
                    copies.append(
                        pltpu.make_async_copy(src.at[pl.ds(start, count)], dst, sem.at[len(copies)])
                    )
    return copies


def turn_kernel(x, out):
    tiles = out.shape[1]

    def body(i, carry):
        for first in range(0, tiles, SUB):
            rows = x[pl.ds(first * BLOCK + i, SUB, stride=BLOCK), :]
            out[i, first : first + SUB, :] = rows
        return carry

    lax.fori_loop(0, BLOCK, body, 0, unroll=4)


def turn(tiles):
    step = 64
    return pl.pallas_call(
        turn_kernel,
        grid=(TILES // step,),
        out_shape=jax.ShapeDtypeStruct((BLOCK, TILES, BLOCK), jnp.float32),
        in_specs=[pl.BlockSpec((step * BLOCK, BLOCK), lambda n: (n, 0))],
        out_specs=pl.BlockSpec((BLOCK, step, BLOCK), lambda n: (0, n, 0)),
        compiler_params=pltpu.CompilerParams(vmem_limit_bytes=VMEM_LIMIT),
        cost_estimate=pl.CostEstimate(flops=0, bytes_accessed=16 << 20, transcendentals=0),
        name="turn",
    )(tiles.reshape(TILES * BLOCK, BLOCK))


def combine_kernel(position, bins, x, panel, trail, *accs):
    sources = x.shape[0] // TILES

    @pl.when(pl.program_id(0) == 0)
    def _():
        for acc in accs:
            acc[...] = jnp.zeros_like(acc)

    def body(q, carry):
        source = (q // FRONTS) * FRONTS + jnp.bitwise_xor(q % FRONTS, position[2])
        base = pl.multiple_of(source * TILES, TILES)
        labels = (pl.program_id(0) * sources + q) * TILES
        for first in range(0, TILES, ACCS):
            at = [bins[labels + first + m] for m in range(ACCS)]
            rows = [x[pl.ds(base + first + m, 1), :] for m in range(ACCS)]
            sums = [accs[m][pl.ds(at[m], 1), :] + rows[m] for m in range(ACCS)]
            for m in range(ACCS):
                accs[m][pl.ds(at[m], 1), :] = sums[m]
        return carry

    lax.fori_loop(0, sources, body, 0)
    step = 256

    @pl.when(pl.program_id(0) == pl.num_programs(0) - 1)
    def _():
        for out, offset in ((panel, 0), (trail, PBINS)):

            def add(b, carry, out=out, offset=offset):
                first = pl.multiple_of(b * step, step)
                total = accs[0][pl.ds(offset + first, step), :]
                for acc in accs[1:]:
                    total = total + acc[pl.ds(offset + first, step), :]
                out[pl.ds(first, step), :] = total
                return carry

            lax.fori_loop(0, out.shape[0] // step, add, 0)


def combine(position, bins, rows):
    steps = 4
    sizes = [PBINS, TBINS]
    return pl.pallas_call(
        combine_kernel,
        grid=(steps,),
        out_shape=[jax.ShapeDtypeStruct((size, BLOCK), jnp.float32) for size in sizes],
        in_specs=[SMEM, SMEM, pl.BlockSpec((rows.shape[0] // steps, BLOCK), lambda i: (i, 0))],
        out_specs=[pl.BlockSpec((size, BLOCK), lambda i: (0, 0)) for size in sizes],
        scratch_shapes=[pltpu.VMEM((BINS, BLOCK), jnp.float32)] * ACCS,
        compiler_params=pltpu.CompilerParams(vmem_limit_bytes=VMEM_LIMIT),
        cost_estimate=pl.CostEstimate(flops=20 * 10**9, bytes_accessed=20 << 20, transcendentals=0),
        name="combine",
    )(position, bins, rows)


def factor_rows(rows, first, sub):
    def spread(values, j):
        return jnp.broadcast_to(values[j : j + 1, :], values.shape)

    columns = [
        jnp.broadcast_to(rows[:, first + j : first + j + 1], (SUB, BLOCK)) for j in range(SUB)
    ]
    parts = [rows[:, :BLOCK], rows[:, BLOCK:]]
    for j in range(SUB):
        scale = lax.rsqrt(spread(columns[j], j))
        weight = jnp.where(sub > j, columns[j] * scale, 0.0)
        for m in range(j + 1, SUB):
            columns[m] = columns[m] - weight * (spread(columns[m], j) * scale)
        for n in range(2):
            pivot = spread(parts[n], j) * scale
            parts[n] = jnp.where(sub == j, pivot, parts[n] - weight * pivot)
    return jnp.concatenate(parts, 1)


def factor_kernel(position, *refs):
    pieces, outs, scratch = refs[:10], refs[10:14], refs[14:]
    own_rows, inverse_high, inverse_low, labels = outs
    (entries, labels_in, work, diag, pair, sem) = scratch
    px, py = position[0], position[1]

    def place(h, x, y):
        block = (x % 2) * SIDE + y
        slab = block * SLABS + (x // 2) * (SLABS // 2) + h * (SLABS // 4)
        spans = [(0, SLABS // 4, entries.at[pl.ds(slab, SLABS // 4)])]
        if h == 0:
            spans.append((SLABS // 4, 1, labels_in.at[pl.ds(x * SIDE + y, 1)]))
        return spans

    copies = line_copies(pieces, place, sem, px, py)
    for copy in copies:
        copy.start()
    for copy in copies:
        copy.wait()
    for g in range(GRID):
        labels[g : g + 1, :] = labels_in[g, 0:1, :].astype(jnp.int32)
    sub = lax.broadcasted_iota(jnp.int32, (SUB, 1), 0)
    row = lax.broadcasted_iota(jnp.int32, (BLOCK, BLOCK), 0)
    col = lax.broadcasted_iota(jnp.int32, (BLOCK, BLOCK), 1)
    eye = jnp.where(row == col, 1.0, 0.0)
    for r in range(LB):
        for c in range(r + 1):
            block = entries[r * SLABS : (r + 1) * SLABS, :, c * BLOCK : (c + 1) * BLOCK]
            block = block.reshape(BLOCK, BLOCK)
            if r == c:
                block = jnp.where(col <= row, block, 0.0)
                block = block + jnp.where(col < row, block, 0.0).T
                work[r * BLOCK : (r + 1) * BLOCK, r * BLOCK : (r + 1) * BLOCK] = block
            else:
                work[c * BLOCK : (c + 1) * BLOCK, r * BLOCK : (r + 1) * BLOCK] = block.T

    def step(k, carry):
        at = pl.ds(pl.multiple_of(k * BLOCK, BLOCK), BLOCK)
        pair[:, :BLOCK] = work[at, at]
        pair[:, BLOCK:] = eye
        for q in range(BLOCK // SUB):
            first = SUB * q
            rows = pair[first : first + SUB, :]
            if q > 0:
                rows = rows - tdot(pair[0:first, first : first + SUB], pair[0:first, :])
            pair[first : first + SUB, :] = factor_rows(rows, first, sub)
        block_inverse = pair[:, BLOCK:]
        diag[k] = pair[:, :BLOCK]
        work[at, :] = jnp.dot(
            block_inverse, work[at, :], precision=highest, preferred_element_type=jnp.float32
        )
        work[at, at] = block_inverse

        def update(i, inner):
            below = pl.ds(pl.multiple_of(i * BLOCK, BLOCK), BLOCK)
            work[below, at] = jnp.zeros((BLOCK, BLOCK), jnp.float32)
            work[below, :] = work[below, :] - tdot(work[at, below], work[at, :])
            return inner

        lax.fori_loop(k + 1, LB, update, 0)
        return carry

    lax.fori_loop(0, LB, step, 0)
    for k in range(LB):
        at = slice(k * BLOCK, (k + 1) * BLOCK)
        done = slice(0, (k + 1) * BLOCK)
        inverse_high[at, done], inverse_low[at, done] = split(work[at, done])
        if k + 1 < LB:
            rest = jnp.zeros((BLOCK, LEAD - (k + 1) * BLOCK), jnp.bfloat16)
            inverse_high[at, (k + 1) * BLOCK :] = rest
            inverse_low[at, (k + 1) * BLOCK :] = rest
    mine = jnp.minimum(px * SIDE + py, LB - 1)
    mine_at = pl.ds(pl.multiple_of(mine * BLOCK, BLOCK), BLOCK)
    for k in range(LB):
        at = slice(k * BLOCK, (k + 1) * BLOCK)
        block = jnp.where(k == mine, jnp.where(row <= col, diag[k], 0.0), work[at, mine_at])
        own_rows[:, at] = jnp.where(k <= mine, block, 0.0).T


def factor(position, pieces):
    return pl.pallas_call(
        factor_kernel,
        out_shape=[
            jax.ShapeDtypeStruct((BLOCK, LEAD), jnp.float32),
            jax.ShapeDtypeStruct((LEAD, LEAD), jnp.bfloat16),
            jax.ShapeDtypeStruct((LEAD, LEAD), jnp.bfloat16),
            jax.ShapeDtypeStruct((GRID, LEAD), jnp.int32),
        ],
        in_specs=[SMEM] + [ANY] * 10,
        out_specs=[VMEM] * 4,
        scratch_shapes=[
            pltpu.VMEM((LB * SLABS, SUB, LEAD), jnp.float32),
            pltpu.VMEM((GRID, SUB, LEAD), jnp.float32),
            pltpu.VMEM((LEAD, LEAD), jnp.float32),
            pltpu.VMEM((LB, BLOCK, BLOCK), jnp.float32),
            pltpu.VMEM((BLOCK, 2 * BLOCK), jnp.float32),
            pltpu.SemaphoreType.DMA((48,)),
        ],
        compiler_params=pltpu.CompilerParams(vmem_limit_bytes=VMEM_LIMIT),
        cost_estimate=pl.CostEstimate(flops=120 * 10**9, bytes_accessed=20 << 20, transcendentals=1024),
        name="factor",
    )(position, *pieces)


def solve_kernel(position, own, part1, part2, part3, sums, inverse_high, inverse_low, out, rows):
    x = position[0]
    for step, part in enumerate((own, part1, part2, part3)):
        source = (x + SIDE - step) % SIDE
        for l in range(2):
            rows[SIDE * l + source] = part[l]
    for m in range(LINES):
        for c in range(LB):
            at = slice(c * BLOCK, (c + 1) * BLOCK)
            values = sums[pl.ds(m * LB + c, SLICE, stride=PSLOTS), :]
            rows[LB // SIDE + m, :, at] = rows[LB // SIDE + m, :, at] + values
    high, low = split(rows[LB // SIDE :].reshape(LINES * SLICE, LEAD))
    wide = 2 * BLOCK
    for c in range(LEAD // wide):
        end = (c + 1) * wide
        inv_high = inverse_high[end - wide : end, :end]
        inv_low = inverse_low[end - wide : end, :end]
        value = mul(high[:, :end], inv_high) + (
            mul(high[:, :end], inv_low) + mul(low[:, :end], inv_high)
        )
        out[:, :, end - wide : end] = value.reshape(LINES, SLICE, wide)


def solve(position, parts, sums, inverse_high, inverse_low):
    return pl.pallas_call(
        solve_kernel,
        out_shape=jax.ShapeDtypeStruct((LINES, SLICE, LEAD), jnp.float32),
        in_specs=[SMEM] + [VMEM] * 7,
        out_specs=VMEM,
        scratch_shapes=[pltpu.VMEM((2 * SIDE, SLICE, LEAD), jnp.float32)],
        compiler_params=pltpu.CompilerParams(vmem_limit_bytes=VMEM_LIMIT),
        name="solve",
    )(position, *parts, sums, inverse_high, inverse_low)


def product_kernel(position, *refs):
    along_x, along_y, scratch = refs[:5], refs[5:10], refs[10:]
    sums, out, own, high, low, row_high, row_low = scratch
    x, y = position[0], position[1]
    half = LINES // 2
    out[...] = jnp.zeros_like(out)

    def blocks(pieces, here):
        nearby, nxt, far_a, far_b, prv = pieces
        for step, piece, first in (
            (0, nearby, 0),
            (1, nxt, 0),
            (2, far_a, 0),
            (2, far_b, half),
            (3, prv, 0),
        ):
            for m in range(piece.shape[0]):
                yield (here + step) % SIDE, first + m, piece[m]

    for index, m, values in blocks(along_x, x):
        at = pl.ds(pl.multiple_of(m * BLOCK + index * SLICE, SLICE), SLICE)
        high[at, :], low[at, :] = split(values)
    for l in range(2):
        m = jnp.maximum(x - 2, 0) if l == 0 else x + 2
        nearby, nxt, far_a, far_b, prv = along_x
        for step in range(SIDE):
            at = pl.ds(pl.multiple_of((x + step) % SIDE * SLICE, SLICE), SLICE)
            if step == 2:
                first = far_a[jnp.minimum(m, half - 1)]
                second = far_b[jnp.maximum(m - half, 0)]
                own[l, at, :] = jnp.where(m < half, first, second)
            else:
                own[l, at, :] = (nearby, nxt, None, prv)[step][m]
    for z, m, values in blocks(along_y, y):
        at = pl.ds(pl.multiple_of(m * BLOCK + z * SLICE, SLICE), SLICE)
        row_high[at, :], row_low[at, :] = split(values)
    for pair in range(LINES // 2):
        start = pair * 2 * BLOCK
        rows_high, rows_low = row_high[start:], row_low[start:]
        cols_high, cols_low = high[start : start + 2 * BLOCK], low[start : start + 2 * BLOCK]
        value = mul(rows_high, cols_high) + (mul(rows_high, cols_low) + mul(rows_low, cols_high))
        for row_block in range(LB + 2 * pair * SIDE, FB):
            owner, first = row_block % GRID, 2 if row_block >= GRID else 0
            line = (row_block - LB) * SLICE - start
            for n in range(2 * pair, 2 * pair + 2):
                if first + n >= OUT_SLOTS or (first == 0 and n >= 2):
                    continue
                below = jnp.maximum(row_block - LB - y - SIDE * n, 0)
                slot = (TB - y) * n - 2 * n * (n - 1) + below
                tiles = sums[pl.ds(slot, SLICE, stride=TSLOTS), :]
                col = (n - 2 * pair) * BLOCK
                out[owner, first + n] = tiles - value[line : line + SLICE, col : col + BLOCK]


def product(position, along_x, along_y, sums):
    return pl.pallas_call(
        product_kernel,
        out_shape=[
            jax.ShapeDtypeStruct((GRID, OUT_SLOTS, SLICE, BLOCK), jnp.float32),
            jax.ShapeDtypeStruct((2, BLOCK, LEAD), jnp.float32),
        ],
        in_specs=[SMEM] + [VMEM] * 11,
        out_specs=[VMEM] * 2,
        scratch_shapes=[
            pltpu.VMEM((LINES * BLOCK, LEAD), jnp.bfloat16),
            pltpu.VMEM((LINES * BLOCK, LEAD), jnp.bfloat16),
            pltpu.VMEM((LINES * BLOCK, LEAD), jnp.bfloat16),
            pltpu.VMEM((LINES * BLOCK, LEAD), jnp.bfloat16),
        ],
        compiler_params=pltpu.CompilerParams(vmem_limit_bytes=VMEM_LIMIT),
        cost_estimate=pl.CostEstimate(flops=11 * 10**9, bytes_accessed=8 << 20, transcendentals=0),
        name="product",
    )(position, *along_x, *along_y, sums)


def lower(values, row_block, block, first_row):
    row = lax.broadcasted_iota(jnp.int32, values.shape, 0)
    col = lax.broadcasted_iota(jnp.int32, values.shape, 1)
    inside = block * BLOCK + col <= row_block * BLOCK + first_row + row
    return jnp.where(inside, values, 0.0)


def base_kernel(position, entries, lead_rows, own, out):
    g = position[0] * SIDE + position[1]
    out[0, :, :LEAD] = jnp.where(g < LB, lead_rows[...], own[0])
    out[1, :, :LEAD] = own[1]
    for local in range(2):
        for block in range(LB, FB):
            at = slice(block * BLOCK, (block + 1) * BLOCK)
            out[local, :, at] = lower(entries[local, :, at], local * GRID + g, block, 0)


def base(position, entries, lead_rows, own):
    return pl.pallas_call(
        base_kernel,
        out_shape=jax.ShapeDtypeStruct(entries.shape, jnp.float32),
        in_specs=[SMEM] + [VMEM] * 3,
        out_specs=VMEM,
        compiler_params=pltpu.CompilerParams(vmem_limit_bytes=VMEM_LIMIT),
        cost_estimate=pl.CostEstimate(flops=0, bytes_accessed=32 << 20, transcendentals=0),
        name="base",
    )(position, entries, lead_rows, own)


def finish_kernel(position, before, change, out):
    g = position[0] * SIDE + position[1]
    out[...] = before[...]
    for local in range(2):
        for block in range(LB, FB if local else GRID):
            at = slice(block * BLOCK, (block + 1) * BLOCK)
            y, n = block % SIDE, (block - LB) // SIDE
            for x in range(SIDE):
                span = slice(x * SLICE, (x + 1) * SLICE)
                value = lower(
                    change[x * SIDE + y, 2 * local + n], local * GRID + g, block, x * SLICE
                )
                out[local, span, at] = before[local, span, at] + value


def finish(position, before, change):
    return pl.pallas_call(
        finish_kernel,
        out_shape=jax.ShapeDtypeStruct(before.shape, jnp.float32),
        in_specs=[SMEM, VMEM, VMEM],
        out_specs=VMEM,
        compiler_params=pltpu.CompilerParams(vmem_limit_bytes=VMEM_LIMIT),
        name="finish",
    )(position, before, change)


def destination_bins(owners, local_rows, picks):
    front, g = owners // GRID, owners % GRID
    shifted = local_rows + (local_rows * GRID + g < LB).astype(jnp.int32)
    row_block = shifted * GRID + g
    col_block = picks % (row_block + 1)
    panel = (row_block % SIDE * FRONTS + front) * PSLOTS + (row_block - LB) // SIDE * LB + col_block
    y, n = col_block % SIDE, (col_block - LB) // SIDE
    slot = (TB - y) * n - 2 * n * (n - 1) + row_block - col_block
    trail = PBINS + (y * FRONTS + front) * TSLOTS + slot
    return jnp.where(col_block < LB, panel, trail)


def across(values, axes):
    return lax.all_to_all(values, axes, split_axis=0, concat_axis=0)


def local(front_entries, child_tiles, tile_owner, tile_rows, tile_picks):
    x, y, f = lax.axis_index("x"), lax.axis_index("y"), lax.axis_index("front")
    position = jnp.stack([x, y, f]).astype(jnp.int32)
    entries = front_entries[0, :, 0]
    half = BLOCK // 2
    lead = entries[0, :, :LEAD]
    other = lax.ppermute(lead[half:], "x", [(0, 2), (1, 3)])
    lead = jnp.where(x < 2, lead[:half], other).reshape(SLABS // 2, SUB, LEAD)
    bins = destination_bins(tile_owner[0, :, 0], tile_rows[0], tile_picks[0])
    bins = gather_front(bins).reshape(1, 1, LEAD).astype(jnp.float32)
    bins = jnp.pad(bins, ((0, 0), (0, SUB - 1), (0, 0)))
    lead, bins, tiles = lax.optimization_barrier((lead, bins, child_tiles))
    half = SLABS // 4
    lines, near, far, tiles = gather_lines(
        jnp.concatenate([lead[:half], bins], 0), lead[half:], tiles, turn
    )
    tiles, near, entries = lax.optimization_barrier((tiles, near, entries))
    lead = [piece for ring in zip(lines, near, far) for piece in ring_pieces(*ring)]
    rows = across(tiles, ("x", "y", "front")).reshape(-1, BLOCK)
    panel = entries[:, :, :LEAD].reshape(2, SIDE, SLICE, LEAD)
    panel = [
        lax.dynamic_index_in_dim(panel, (x + n) % SIDE, 1, keepdims=False) for n in range(SIDE)
    ]
    panel = [part if n == 0 else shift(part, "x", n) for n, part in enumerate(panel)]
    lead_rows, *inverse, bins = factor(position, lead)
    panel_sums, trail_sums = combine(position, bins.reshape(-1), rows)
    panel_sums = across(panel_sums.reshape(SLICE, PSLOTS, BLOCK), ("y", "front"))
    panel_sums, trail_sums = lax.optimization_barrier((panel_sums, trail_sums))
    trail_sums = across(trail_sums.reshape(SLICE, TSLOTS, BLOCK), ("y", "front"))
    solved = solve(position, panel, panel_sums.reshape(-1, BLOCK), *inverse)
    near = [ring_near(solved, axis) for axis in ("x", "y")]
    far = [ring_far(pair, axis) for pair, axis in zip(near, ("x", "y"))]
    along = [ring_pieces(solved, *pair) for pair in zip(near, far)]
    change, own = product(position, *along, trail_sums.reshape(-1, BLOCK))
    change = across(change, ("x", "y"))
    out = finish(position, base(position, entries, lead_rows, own), change)
    return out[None, :, None]


def solution(mesh):
    mesh = Mesh(mesh.devices.reshape(FRONTS, SIDE, SIDE), ("front", "x", "y"))
    grid = ("x", "y")
    return jax.shard_map(
        local,
        mesh=mesh,
        in_specs=(
            P("front", None, grid, None, None),
            P("front", grid, None, None),
            P("front", grid, None),
            P("front", grid),
            P("front", grid),
        ),
        out_specs=P("front", None, grid, None, None),
        check_vma=False,
    )
```

time: 338 us -> 317 us (0.938)
  blocking collectives: 74.2 us -> 0 us
  waiting for transfers between devices: 54.3 us -> 87 us
  starting transfers between devices: 58.6 us -> 75.3 us
  Pallas kernels: 131 us -> 142 us
  local copies, waits for them, and re-layouts: 16.4 us -> 8.71 us
    all_to_all x2 -> x0, blocking collectives: 74.2 us -> none  [across(): return lax.all_to_all(values, axes, split_axis=0, concat_axis=0)]
    all_to_all x2 -> x4, waiting for transfers between devices: 8.43 us -> 45.4 us  [across(): return lax.all_to_all(values, axes, split_axis=0, concat_axis=0)]
    pallas_call x2 -> x4, Pallas kernels: 26.9 us -> 40.6 us  [the longest x1 20 us: combine(): pl.pallas_call(combine_kernel, grid=(steps,), out_shape=[jax.ShapeDtypeSt...]
    optimization_barrier x1 -> x0, local copies, waits for them, and re-layouts: 11.5 us -> none  [local(): lead, bins, tiles = lax.optimization_barrier((lead, bins, child_tiles))]
    ppermute x0 -> x7, starting transfers between devices: none -> 9.31 us  [gather_front(): lax.ppermute(values, 'front', [(i, i ^ k) for i in range(FRONTS)])]
    all_to_all x2 -> x4, starting transfers between devices: 15.8 us -> 23.4 us  [across(): return lax.all_to_all(values, axes, split_axis=0, concat_axis=0)]
    ppermute x25, waiting for transfers between devices: 45.8 us -> 39.8 us  [shift(): lax.ppermute(block, axis, [(i, (i + step) % SIDE) for i in range(SIDE)])]
    unnamed x34 -> x37, local copies, waits for them, and re-layouts: 0.83 us -> 5.36 us
  transfers between devices with their start and end apart: 28 -> 37, of which waited for: 11 -> 14; matrix products, arithmetic and copies ran while one was open for 5% -> 2% of each run, Pallas kernels for 26% -> 34%
where the time goes in v3:
time: 317 us; the launch traced here: 316 us
  Pallas kernels  142 us (45%)
  waiting for transfers between devices  87 us (27%)
  starting transfers between devices  75.3 us (24%)
  local copies, waits for them, and re-layouts  8.71 us (3%)
  other arithmetic  3.34 us (1%)
    pallas_call x1, Pallas kernels, factor(): pl.pallas_call(factor_kernel, out_shape=[jax.ShapeDtypeStruct((BLOCK, LEA...  86.9 us
    all_to_all x4, waiting for transfers between devices, across(): return lax.all_to_all(values, axes, split_axis=0, concat_axis=0)  45.4 us
    ppermute x25, waiting for transfers between devices, shift(): lax.ppermute(block, axis, [(i, (i + step) % SIDE) for i in range(SIDE)])  39.8 us
    ppermute x25, starting transfers between devices, shift(): lax.ppermute(block, axis, [(i, (i + step) % SIDE) for i in range(SIDE)])  37.5 us
    all_to_all x4, starting transfers between devices, across(): return lax.all_to_all(values, axes, split_axis=0, concat_axis=0)  23.4 us
    pallas_call x1, Pallas kernels, combine(): pl.pallas_call(combine_kernel, grid=(steps,), out_shape=[jax.ShapeDtypeSt...  20 us
    pallas_call x1, Pallas kernels, turn(): pl.pallas_call(turn_kernel, grid=(TILES // step,), out_shape=jax.ShapeDty...  10.1 us
    ppermute x7, starting transfers between devices, gather_front(): lax.ppermute(values, 'front', [(i, i ^ k) for i in range(FRONTS)])  9.31 us
  transfers between devices with their start and end apart: 37, of which 14 were waited for; matrix products, arithmetic and copies ran while one was open for 2% of the time, Pallas kernels for 34%

profile of v3, /device:TPU:0, one launch (start us, length us, event | category | flops | bytes accessed | tf_op | source)
XLA Modules:
  0.0 316.4 jit_solution(15229067967673137930)
XLA Ops:
  0.0 1.0 slice_bitcast_fusion
  1.0 5.0 %collective-permute-start = (f32[64,1024]{1,0:T(8,128)S(1)}, f32[64,1024]{1,0:T(8,128)S(1)}, u32[]{:S(2)}, u32[]{:S(2)}) collective-permute-start(f32[64,1024]{1,0:T(8,128)S(1)} %slice_bitcast_fusion), channel_id=1, source_target_pairs={{0,8},{4,12},{1,9},{5,13},{2,10},{6,14},{3,11},{7,15},{16,24},{20,... | collective-permute-start | bytes 786440 | tf_op jit(solution)/shard_map/ppermute | solution.py:498
  6.8 3.3 %collective-permute-start.7 = (s32[128]{0:T(128)S(1)}, s32[128]{0:T(128)S(1)}, u32[]{:S(2)}, u32[]{:S(2)}) collective-permute-start(s32[128]{0:T(128)S(1)} %compare_select_fusion.10), channel_id=1, source_target_pairs={{0,112},{16,96},{32,80},{48,64},{64,48},{80,32},{96,16},{112,0},{1... | collective-permute-start | bytes 1544 | tf_op jit(solution)/shard_map/ppermute | solution.py:60
  10.1 0.9 collective-permute-start.6
  11.1 1.2 collective-permute-start.5
  12.3 1.9 collective-permute-start.4
  15.2 1.8 collective-permute-start.2
  18.9 1.0 fusion.1
  19.9 3.3 %collective-permute-start.12 = (f32[4,8,1024]{2,1,0:T(8,128)S(1)}, f32[4,8,1024]{2,1,0:T(8,128)S(1)}, u32[]{:S(2)}, u32[]{:S(2)}) collective-permute-start(f32[4,8,1024]{2,1,0:T(8,128)S(1)} %get-tuple-element.64), channel_id=1, source_target_pairs={{0,2},{1,3},{2,0},{3,1},{4,6},{5,7},{6,4},{7,5},{8,10},{9,11},{10,... | collective-permute-start | bytes 393224 | tf_op jit(solution)/shard_map/ppermute | solution.py:55
  23.2 1.1 collective-permute-start.11
  24.2 1.0 collective-permute-start.13
  25.3 3.3 %collective-permute-start.8 = (f32[5,8,1024]{2,1,0:T(8,128)S(1)}, f32[5,8,1024]{2,1,0:T(8,128)S(1)}, u32[]{:S(2)}, u32[]{:S(2)}) collective-permute-start(f32[5,8,1024]{2,1,0:T(8,128)S(1)} %get-tuple-element.67), channel_id=1, source_target_pairs={{0,12},{4,0},{8,4},{12,8},{1,13},{5,1},{9,5},{13,9},{2,14},{6,2},{... | collective-permute-start | bytes 491528 | tf_op jit(solution)/shard_map/ppermute | solution.py:55
  28.6 1.0 collective-permute-done.11
  30.4 3.0 collective-permute-done.9
  33.5 2.3 collective-permute-done.10
  36.5 2.6 collective-permute-start.14
  39.1 3.2 %collective-permute-start.16 = (f32[4,4,8,1024]{3,2,1,0:T(8,128)S(1)}, f32[4,4,8,1024]{3,2,1,0:T(8,128)S(1)}, u32[]{:S(2)}, u32[]{:S(2)}) collective-permute-start(f32[4,4,8,1024]{3,2,1,0:T(8,128)S(1)} %pad_maximum_fusion.1.refs_5_), channel_id=1, source_target_pairs={{0,12},{4,0},{8,4},{12,8},{1,13},{5,1},{9,5},{13,9},{2,14},{6,2},{... | collective-permute-start | bytes 1572872 | tf_op jit(solution)/shard_map/ppermute | solution.py:55
  42.3 10.1 %turn.1 = f32[128,128,128]{2,1,0:T(8,128)} custom-call(f32[16384,128]{1,0:T(8,128)} %bitcast.91), custom_call_target="tpu_custom_call" | custom-call | bytes 16777216 | tf_op jit(solution)/shard_map/turn/pallas_call | solution.py:122
  53.1 2.8 collective-permute-start.19
  56.0 3.2 %collective-permute-start.21 = (f32[2,4,8,1024]{3,2,1,0:T(8,128)S(1)}, f32[2,4,8,1024]{3,2,1,0:T(8,128)}, u32[]{:S(2)}, u32[]{:S(2)}) collective-permute-start(f32[2,4,8,1024]{3,2,1,0:T(8,128)S(1)} %slice.57), channel_id=1, source_target_pairs={{0,12},{4,0},{8,4},{12,8},{1,13},{5,1},{9,5},{13,9},{2,14},{6,2},{... | collective-permute-start | bytes 786440 | tf_op jit(solution)/shard_map/ppermute | solution.py:55
  59.8 7.4 %all-to-all-start = ((f32[128,128,128]{2,1,0:T(8,128)}), f32[128,128,128]{2,1,0:T(8,128)}, u32[]{:S(2)}, u32[]{:S(2)}) async-start(f32[128,128,128]{2,1,0:T(8,128)} %turn.1), calls=%async_computation | async-start | bytes 16777216 | tf_op jit(solution)/shard_map/all_to_all | solution.py:489
  67.3 86.9 %factor.1 = (f32[128,1024]{1,0:T(8,128)}, bf16[1024,1024]{1,0:T(8,128)(2,1)}, bf16[1024,1024]{1,0:T(8,128)(2,1)}, s32[16,1024]{1,0:T(8,128)}) custom-call(s32[3]{0:T(128)} %pad_add_fusion.position, f32[4,5,8,1024]{3,2,1,0:T(8,128)} %copy-done.3, f32[4,5,8,1024]{3,2,1,0:T(8,128)} %copy-done.12, f32[2,5,8,1024]{3,2,1,0:T(8,128)} %collective-permute-done.18.refs_2_, ...), custom_call_target="tpu_custom_call" | custom-call | flops 120000004096 | bytes 20971520 | tf_op jit(solution)/shard_map/factor/pallas_call | solution.py:287
  154.1 1.5 copy.7
  155.6 13.7 %all-to-all-done = f32[128,128,128]{2,1,0:T(8,128)} async-done(((f32[128,128,128]{2,1,0:T(8,128)}), f32[128,128,128]{2,1,0:T(8,128)}, u32[]{:S(2)}, u32[]{:S(2)}) %all-to-all-start) | async-done | bytes 8388640 | tf_op jit(solution)/shard_map/all_to_all | solution.py:489
  169.3 20.0 %combine.1 = (f32[1536,128]{1,0:T(8,128)}, f32[2816,128]{1,0:T(8,128)}) custom-call(s32[3]{0:T(128)} %pad_add_fusion.position, s32[16384]{0:T(1024)} %bitcast.107, f32[16384,128]{1,0:T(8,128)} %bitcast.33.x), custom_call_target="tpu_custom_call" | custom-call | flops 20000000000 | bytes 20971520 | tf_op jit(solution)/shard_map/combine/pallas_call | solution.py:175
  189.3 8.1 %all-to-all-start.1 = ((f32[32,48,128]{2,1,0:T(8,128)}), f32[32,48,128]{2,1,0:T(8,128)S(1)}, u32[]{:S(2)}, u32[]{:S(2)}) async-start(f32[32,48,128]{2,1,0:T(8,128)} %bitcast.99), calls=%async_computation.1 | async-start | bytes 1572864 | tf_op jit(solution)/shard_map/all_to_all | solution.py:489
  197.4 1.3 slice.58
  199.5 2.1 collective-permute-start.24
  201.6 0.9 collective-permute-start.22
  202.4 8.7 %all-to-all-done.1 = f32[32,48,128]{2,1,0:T(8,128)S(1)} async-done(((f32[32,48,128]{2,1,0:T(8,128)}), f32[32,48,128]{2,1,0:T(8,128)S(1)}, u32[]{:S(2)}, u32[]{:S(2)}) %all-to-all-start.1) | async-done | bytes 786464 | tf_op jit(solution)/shard_map/all_to_all | solution.py:489
  211.2 4.2 %all-to-all-start.2 = ((f32[32,88,128]{2,1,0:T(8,128)}), f32[32,88,128]{2,1,0:T(8,128)S(1)}, u32[]{:S(2)}, u32[]{:S(2)}) async-start(f32[32,88,128]{2,1,0:T(8,128)} %bitcast.36), calls=%async_computation.2 | async-start | bytes 2883584 | tf_op jit(solution)/shard_map/all_to_all | solution.py:489
  215.4 1.3 collective-permute-done.22.part1
  216.7 5.2 %solve.1.refs_0_.refs_5_ = f32[6,32,1024]{2,1,0:T(8,128)} custom-call(s32[3]{0:T(128)} %pad_add_fusion.position, f32[2,32,1024]{2,1,0:T(8,128)} %get-tuple-element.62.own, f32[2,32,1024]{2,1,0:T(8,128)} %collective-permute-done.22.part1, f32[2,32,1024]{2,1,0:T(8,128)} %copy-done.6, f32[2,32,1024]{2,1,0:T(8,128)} %copy-done.5, f32[1536,128]{1,0:T(8,128)} %bitcast.97, ...), custom_call_target="tpu_custom_call" | custom-call | tf_op jit(solution)/shard_map/solve/pallas_call | solution.py:335
  222.0 1.7 collective-permute-start.30
  223.6 1.6 collective-permute-start.29
  225.2 3.2 %collective-permute-start.25 = (f32[6,32,1024]{2,1,0:T(8,128)}, f32[6,32,1024]{2,1,0:T(8,128)S(1)}, u32[]{:S(2)}, u32[]{:S(2)}) collective-permute-start(f32[6,32,1024]{2,1,0:T(8,128)} %solve.1.refs_0_.refs_5_), channel_id=1, source_target_pairs={{0,12},{4,0},{8,4},{12,8},{1,13},{5,1},{9,5},{13,9},{2,14},{6,2},{... | collective-permute-start | bytes 2359304 | tf_op jit(solution)/shard_map/ppermute | solution.py:55
  228.4 23.4 %collective-permute-done.30.refs_9_ = f32[6,32,1024]{2,1,0:T(8,128)S(1)} collective-permute-done((f32[6,32,1024]{2,1,0:T(8,128)}, f32[6,32,1024]{2,1,0:T(8,128)S(1)}, u32[]{:S(2)}, u32[]{:S(2)}) %collective-permute-start.30) | collective-permute-done | bytes 786464 | tf_op jit(solution)/shard_map/ppermute | solution.py:55
  252.0 3.3 %collective-permute-start.32 = (f32[3,32,1024]{2,1,0:T(8,128)S(1)}, f32[3,32,1024]{2,1,0:T(8,128)S(1)}, u32[]{:S(2)}, u32[]{:S(2)}) collective-permute-start(f32[3,32,1024]{2,1,0:T(8,128)S(1)} %slice.68), channel_id=1, source_target_pairs={{0,3},{1,0},{2,1},{3,2},{4,7},{5,4},{6,5},{7,6},{8,11},{9,8},{10,9... | collective-permute-start | bytes 1179656 | tf_op jit(solution)/shard_map/ppermute | solution.py:55
  256.2 2.7 collective-permute-start.28
  259.0 4.9 %collective-permute-done.31.refs_7_ = f32[3,32,1024]{2,1,0:T(8,128)S(1)} collective-permute-done((f32[3,32,1024]{2,1,0:T(8,128)S(1)}, f32[3,32,1024]{2,1,0:T(8,128)S(1)}, u32[]{:S(2)}, u32[]{:S(2)}) %collective-permute-start.31) | collective-permute-done | bytes 393248 | tf_op jit(solution)/shard_map/ppermute | solution.py:55
  263.8 3.1 collective-permute-done.27.refs_2_
  267.7 1.1 copy-done.2
  268.9 8.8 %product.1 = (f32[16,8,32,128]{3,2,1,0:T(8,128)}, f32[2,128,1024]{2,1,0:T(8,128)}) custom-call(s32[3]{0:T(128)} %pad_add_fusion.position, f32[6,32,1024]{2,1,0:T(8,128)} %solve.1.refs_0_.refs_5_, f32[6,32,1024]{2,1,0:T(8,128)} %copy-done.10, f32[3,32,1024]{2,1,0:T(8,128)} %copy-done.17, f32[3,32,1024]{2,1,0:T(8,128)} %collective-permute-done.28.refs_3_, ...), custom_call_target="tpu_custom_call" | custom-call | flops 11000000512 | bytes 8388608 | tf_op jit(solution)/shard_map/product/pallas_call | solution.py:401
  277.6 3.8 %all-to-all-start.3 = ((f32[16,8,32,128]{3,2,1,0:T(8,128)}), f32[16,8,32,128]{3,2,1,0:T(8,128)S(1)}, u32[]{:S(2)}, u32[]{:S(2)}) async-start(f32[16,8,32,128]{3,2,1,0:T(8,128)} %get-tuple-element.58), calls=%async_computation.3 | async-start | bytes 4194304 | tf_op jit(solution)/shard_map/all_to_all | solution.py:489
  281.4 5.2 %base.1.before = f32[2,128,4096]{2,1,0:T(8,128)} custom-call(s32[3]{0:T(128)} %pad_add_fusion.position, f32[2,128,4096]{2,1,0:T(8,128)} %bitcast.95, f32[128,1024]{1,0:T(8,128)} %get-tuple-element.48.lead_rows, f32[2,128,1024]{2,1,0:T(8,128)} %get-tuple-element.57.own), custom_call_target="tpu_custom_call" | custom-call | bytes 33554432 | tf_op jit(solution)/shard_map/base/pallas_call | solution.py:439
  286.6 23.0 %all-to-all-done.3.change = f32[16,8,32,128]{3,2,1,0:T(8,128)S(1)} async-done(((f32[16,8,32,128]{3,2,1,0:T(8,128)}), f32[16,8,32,128]{3,2,1,0:T(8,128)S(1)}, u32[]{:S(2)}, u32[]{:S(2)}) %all-to-all-start.3) | async-done | bytes 2097184 | tf_op jit(solution)/shard_map/all_to_all | solution.py:489
  309.7 1.4 copy-done
  311.0 5.3 %finish.1 = f32[2,128,4096]{2,1,0:T(8,128)} custom-call(s32[3]{0:T(128)} %pad_add_fusion.position, f32[2,128,4096]{2,1,0:T(8,128)} %base.1.before, f32[16,8,32,128]{3,2,1,0:T(8,128)} %copy-done), custom_call_target="tpu_custom_call" | custom-call | tf_op jit(solution)/shard_map/finish/pallas_call | solution.py:466
  (92 shorter events, 9.5 us)
Async XLA Ops:
  1.0 17.9 %collective-permute-start = (f32[64,1024]{1,0:T(8,128)S(1)}, f32[64,1024]{1,0:T(8,128)S(1)}, u32[]{:S(2)}, u32[]{:S(2)}) collective-permute-start(f32[64,1024]{1,0:T(8,128)S(1)} %slice_bitcast_fusion), channel_id=1, source_target_pairs={{0,8},{4,12},{1,9},{5,13},{2,10},{6,14},{3,11},{7,15},{16,24},{20,... | collective-permute-start | bytes 786440 | tf_op jit(solution)/shard_map/ppermute | solution.py:498
  6.8 8.2 %collective-permute-start.7 = (s32[128]{0:T(128)S(1)}, s32[128]{0:T(128)S(1)}, u32[]{:S(2)}, u32[]{:S(2)}) collective-permute-start(s32[128]{0:T(128)S(1)} %compare_select_fusion.10), channel_id=1, source_target_pairs={{0,112},{16,96},{32,80},{48,64},{64,48},{80,32},{96,16},{112,0},{1... | collective-permute-start | bytes 1544 | tf_op jit(solution)/shard_map/ppermute | solution.py:60
  10.1 5.1 %collective-permute-start.6 = (s32[128]{0:T(128)S(1)}, s32[128]{0:T(128)S(1)}, u32[]{:S(2)}, u32[]{:S(2)}) collective-permute-start(s32[128]{0:T(128)S(1)} %compare_select_fusion.10), channel_id=1, source_target_pairs={{0,96},{16,112},{32,64},{48,80},{64,32},{80,48},{96,0},{112,16},{1... | collective-permute-start | bytes 1544 | tf_op jit(solution)/shard_map/ppermute | solution.py:60
  11.1 5.9 %collective-permute-start.5 = (s32[128]{0:T(128)S(1)}, s32[128]{0:T(128)S(1)}, u32[]{:S(2)}, u32[]{:S(2)}) collective-permute-start(s32[128]{0:T(128)S(1)} %compare_select_fusion.10), channel_id=1, source_target_pairs={{0,80},{16,64},{32,112},{48,96},{64,16},{80,0},{96,48},{112,32},{1... | collective-permute-start | bytes 1544 | tf_op jit(solution)/shard_map/ppermute | solution.py:60
  12.3 5.0 %collective-permute-start.4 = (s32[128]{0:T(128)S(1)}, s32[128]{0:T(128)S(1)}, u32[]{:S(2)}, u32[]{:S(2)}) collective-permute-start(s32[128]{0:T(128)S(1)} %compare_select_fusion.10), channel_id=1, source_target_pairs={{0,64},{16,80},{32,96},{48,112},{64,0},{80,16},{96,32},{112,48},{1... | collective-permute-start | bytes 1544 | tf_op jit(solution)/shard_map/ppermute | solution.py:60
  15.1 3.0 collective-permute-start.3
  15.2 3.6 %collective-permute-start.2 = (s32[128]{0:T(128)S(1)}, s32[128]{0:T(128)S(1)}, u32[]{:S(2)}, u32[]{:S(2)}) collective-permute-start(s32[128]{0:T(128)S(1)} %compare_select_fusion.10), channel_id=1, source_target_pairs={{0,32},{16,48},{32,0},{48,16},{64,96},{80,112},{96,64},{112,80},{1... | collective-permute-start | bytes 1544 | tf_op jit(solution)/shard_map/ppermute | solution.py:60
  17.0 1.8 collective-permute-start.1
  19.9 8.7 %collective-permute-start.12 = (f32[4,8,1024]{2,1,0:T(8,128)S(1)}, f32[4,8,1024]{2,1,0:T(8,128)S(1)}, u32[]{:S(2)}, u32[]{:S(2)}) collective-permute-start(f32[4,8,1024]{2,1,0:T(8,128)S(1)} %get-tuple-element.64), channel_id=1, source_target_pairs={{0,2},{1,3},{2,0},{3,1},{4,6},{5,7},{6,4},{7,5},{8,10},{9,11},{10,... | collective-permute-start | bytes 393224 | tf_op jit(solution)/shard_map/ppermute | solution.py:55
  23.2 6.4 %collective-permute-start.11 = (f32[4,8,1024]{2,1,0:T(8,128)S(1)}, f32[4,8,1024]{2,1,0:T(8,128)S(1)}, u32[]{:S(2)}, u32[]{:S(2)}) collective-permute-start(f32[4,8,1024]{2,1,0:T(8,128)S(1)} %get-tuple-element.64), channel_id=1, source_target_pairs={{0,3},{1,0},{2,1},{3,2},{4,7},{5,4},{6,5},{7,6},{8,11},{9,8},{10,9... | collective-permute-start | bytes 393224 | tf_op jit(solution)/shard_map/ppermute | solution.py:55
  24.2 6.2 %collective-permute-start.13 = (f32[4,8,1024]{2,1,0:T(8,128)S(1)}, f32[4,8,1024]{2,1,0:T(8,128)S(1)}, u32[]{:S(2)}, u32[]{:S(2)}) collective-permute-start(f32[4,8,1024]{2,1,0:T(8,128)S(1)} %get-tuple-element.64), channel_id=1, source_target_pairs={{0,1},{1,2},{2,3},{3,0},{4,5},{5,6},{6,7},{7,4},{8,9},{9,10},{10,1... | collective-permute-start | bytes 393224 | tf_op jit(solution)/shard_map/ppermute | solution.py:55
  25.2 8.2 %collective-permute-start.9 = (f32[5,8,1024]{2,1,0:T(8,128)S(1)}, f32[5,8,1024]{2,1,0:T(8,128)S(1)}, u32[]{:S(2)}, u32[]{:S(2)}) collective-permute-start(f32[5,8,1024]{2,1,0:T(8,128)S(1)} %get-tuple-element.67), channel_id=1, source_target_pairs={{0,8},{4,12},{8,0},{12,4},{1,9},{5,13},{9,1},{13,5},{2,10},{6,14},... | collective-permute-start | bytes 491528 | tf_op jit(solution)/shard_map/ppermute | solution.py:55
  25.3 8.1 %collective-permute-start.8 = (f32[5,8,1024]{2,1,0:T(8,128)S(1)}, f32[5,8,1024]{2,1,0:T(8,128)S(1)}, u32[]{:S(2)}, u32[]{:S(2)}) collective-permute-start(f32[5,8,1024]{2,1,0:T(8,128)S(1)} %get-tuple-element.67), channel_id=1, source_target_pairs={{0,12},{4,0},{8,4},{12,8},{1,13},{5,1},{9,5},{13,9},{2,14},{6,2},{... | collective-permute-start | bytes 491528 | tf_op jit(solution)/shard_map/ppermute | solution.py:55
  28.6 7.2 %collective-permute-start.10 = (f32[5,8,1024]{2,1,0:T(8,128)S(1)}, f32[5,8,1024]{2,1,0:T(8,128)S(1)}, u32[]{:S(2)}, u32[]{:S(2)}) collective-permute-start(f32[5,8,1024]{2,1,0:T(8,128)S(1)} %get-tuple-element.67), channel_id=1, source_target_pairs={{0,4},{4,8},{8,12},{12,0},{1,5},{5,9},{9,13},{13,1},{2,6},{6,10},{... | collective-permute-start | bytes 491528 | tf_op jit(solution)/shard_map/ppermute | solution.py:55
  30.4 22.0 %copy-start.4 = (f32[4,4,8,1024]{3,2,1,0:T(8,128)}, f32[4,4,8,1024]{3,2,1,0:T(8,128)S(1)}, u32[]{:S(2)}) copy-start(f32[4,4,8,1024]{3,2,1,0:T(8,128)S(1)} %pad_maximum_fusion.1.refs_5_) | copy-start | bytes 1572868
  35.8 16.7 %copy-start.3 = (f32[4,5,8,1024]{3,2,1,0:T(8,128)}, f32[4,5,8,1024]{3,2,1,0:T(8,128)S(1)}, u32[]{:S(2)}) copy-start(f32[4,5,8,1024]{3,2,1,0:T(8,128)S(1)} %pad_maximum_fusion.refs_0_) | copy-start | bytes 1966084
  35.8 16.7 %collective-permute-start.15 = (f32[4,5,8,1024]{3,2,1,0:T(8,128)S(1)}, f32[4,5,8,1024]{3,2,1,0:T(8,128)S(1)}, u32[]{:S(2)}, u32[]{:S(2)}) collective-permute-start(f32[4,5,8,1024]{3,2,1,0:T(8,128)S(1)} %pad_maximum_fusion.refs_0_), channel_id=1, source_target_pairs={{0,1},{1,2},{2,3},{3,0},{4,5},{5,6},{6,7},{7,4},{8,9},{9,10},{10,1... | collective-permute-start | bytes 1966088 | tf_op jit(solution)/shard_map/ppermute | solution.py:55
  36.5 16.0 %collective-permute-start.14 = (f32[4,5,8,1024]{3,2,1,0:T(8,128)S(1)}, f32[4,5,8,1024]{3,2,1,0:T(8,128)S(1)}, u32[]{:S(2)}, u32[]{:S(2)}) collective-permute-start(f32[4,5,8,1024]{3,2,1,0:T(8,128)S(1)} %pad_maximum_fusion.refs_0_), channel_id=1, source_target_pairs={{0,3},{1,0},{2,1},{3,2},{4,7},{5,4},{6,5},{7,6},{8,11},{9,8},{10,9... | collective-permute-start | bytes 1966088 | tf_op jit(solution)/shard_map/ppermute | solution.py:55
  39.1 13.4 %collective-permute-start.17 = (f32[4,4,8,1024]{3,2,1,0:T(8,128)S(1)}, f32[4,4,8,1024]{3,2,1,0:T(8,128)S(1)}, u32[]{:S(2)}, u32[]{:S(2)}) collective-permute-start(f32[4,4,8,1024]{3,2,1,0:T(8,128)S(1)} %pad_maximum_fusion.1.refs_5_), channel_id=1, source_target_pairs={{0,4},{4,8},{8,12},{12,0},{1,5},{5,9},{9,13},{13,1},{2,6},{6,10},{... | collective-permute-start | bytes 1572872 | tf_op jit(solution)/shard_map/ppermute | solution.py:55
  39.1 13.4 %collective-permute-start.16 = (f32[4,4,8,1024]{3,2,1,0:T(8,128)S(1)}, f32[4,4,8,1024]{3,2,1,0:T(8,128)S(1)}, u32[]{:S(2)}, u32[]{:S(2)}) collective-permute-start(f32[4,4,8,1024]{3,2,1,0:T(8,128)S(1)} %pad_maximum_fusion.1.refs_5_), channel_id=1, source_target_pairs={{0,12},{4,0},{8,4},{12,8},{1,13},{5,1},{9,5},{13,9},{2,14},{6,2},{... | collective-permute-start | bytes 1572872 | tf_op jit(solution)/shard_map/ppermute | solution.py:55
  52.5 7.4 %copy-start.13 = (f32[4,4,8,1024]{3,2,1,0:T(8,128)}, f32[4,4,8,1024]{3,2,1,0:T(8,128)S(1)}, u32[]{:S(2)}) copy-start(f32[4,4,8,1024]{3,2,1,0:T(8,128)S(1)} %collective-permute-done.17.refs_9_) | copy-start | bytes 1572868
  52.5 7.3 %copy-start.14 = (f32[4,4,8,1024]{3,2,1,0:T(8,128)}, f32[4,4,8,1024]{3,2,1,0:T(8,128)S(1)}, u32[]{:S(2)}) copy-start(f32[4,4,8,1024]{3,2,1,0:T(8,128)S(1)} %collective-permute-done.16.refs_6_) | copy-start | bytes 1572868
  52.5 7.3 %copy-start.11 = (f32[4,5,8,1024]{3,2,1,0:T(8,128)}, f32[4,5,8,1024]{3,2,1,0:T(8,128)S(1)}, u32[]{:S(2)}) copy-start(f32[4,5,8,1024]{3,2,1,0:T(8,128)S(1)} %collective-permute-done.15.refs_4_) | copy-start | bytes 1966084
  52.5 7.3 %copy-start.12 = (f32[4,5,8,1024]{3,2,1,0:T(8,128)}, f32[4,5,8,1024]{3,2,1,0:T(8,128)S(1)}, u32[]{:S(2)}) copy-start(f32[4,5,8,1024]{3,2,1,0:T(8,128)S(1)} %collective-permute-done.14.refs_1_) | copy-start | bytes 1966084
  52.6 14.6 %collective-permute-start.18 = (f32[2,5,8,1024]{3,2,1,0:T(8,128)S(1)}, f32[2,5,8,1024]{3,2,1,0:T(8,128)}, u32[]{:S(2)}, u32[]{:S(2)}) collective-permute-start(f32[2,5,8,1024]{3,2,1,0:T(8,128)S(1)} %slice.54), channel_id=1, source_target_pairs={{0,1},{1,2},{2,3},{3,0},{4,5},{5,6},{6,7},{7,4},{8,9},{9,10},{10,1... | collective-permute-start | bytes 983048 | tf_op jit(solution)/shard_map/ppermute | solution.py:55
  53.1 14.1 %collective-permute-start.19 = (f32[2,5,8,1024]{3,2,1,0:T(8,128)S(1)}, f32[2,5,8,1024]{3,2,1,0:T(8,128)}, u32[]{:S(2)}, u32[]{:S(2)}) collective-permute-start(f32[2,5,8,1024]{3,2,1,0:T(8,128)S(1)} %slice.55), channel_id=1, source_target_pairs={{0,3},{1,0},{2,1},{3,2},{4,7},{5,4},{6,5},{7,6},{8,11},{9,8},{10,9... | collective-permute-start | bytes 983048 | tf_op jit(solution)/shard_map/ppermute | solution.py:55
  56.0 11.3 %collective-permute-start.20 = (f32[2,4,8,1024]{3,2,1,0:T(8,128)S(1)}, f32[2,4,8,1024]{3,2,1,0:T(8,128)}, u32[]{:S(2)}, u32[]{:S(2)}) collective-permute-start(f32[2,4,8,1024]{3,2,1,0:T(8,128)S(1)} %slice.56), channel_id=1, source_target_pairs={{0,4},{4,8},{8,12},{12,0},{1,5},{5,9},{9,13},{13,1},{2,6},{6,10},{... | collective-permute-start | bytes 786440 | tf_op jit(solution)/shard_map/ppermute | solution.py:55
  56.0 11.2 %collective-permute-start.21 = (f32[2,4,8,1024]{3,2,1,0:T(8,128)S(1)}, f32[2,4,8,1024]{3,2,1,0:T(8,128)}, u32[]{:S(2)}, u32[]{:S(2)}) collective-permute-start(f32[2,4,8,1024]{3,2,1,0:T(8,128)S(1)} %slice.57), channel_id=1, source_target_pairs={{0,12},{4,0},{8,4},{12,8},{1,13},{5,1},{9,5},{13,9},{2,14},{6,2},{... | collective-permute-start | bytes 786440 | tf_op jit(solution)/shard_map/ppermute | solution.py:55
  59.8 109.4 %all-to-all-start = ((f32[128,128,128]{2,1,0:T(8,128)}), f32[128,128,128]{2,1,0:T(8,128)}, u32[]{:S(2)}, u32[]{:S(2)}) async-start(f32[128,128,128]{2,1,0:T(8,128)} %turn.1), calls=%async_computation | async-start | bytes 16777216 | tf_op jit(solution)/shard_map/all_to_all | solution.py:489
  189.3 21.9 %all-to-all-start.1 = ((f32[32,48,128]{2,1,0:T(8,128)}), f32[32,48,128]{2,1,0:T(8,128)S(1)}, u32[]{:S(2)}, u32[]{:S(2)}) async-start(f32[32,48,128]{2,1,0:T(8,128)} %bitcast.99), calls=%async_computation.1 | async-start | bytes 1572864 | tf_op jit(solution)/shard_map/all_to_all | solution.py:489
  199.5 15.9 %collective-permute-start.24 = (f32[2,32,1024]{2,1,0:T(8,128)S(1)}, f32[2,32,1024]{2,1,0:T(8,128)S(1)}, u32[]{:S(2)}, u32[]{:S(2)}) collective-permute-start(f32[2,32,1024]{2,1,0:T(8,128)S(1)} %get-tuple-element.59), channel_id=1, source_target_pairs={{0,12},{4,0},{8,4},{12,8},{1,13},{5,1},{9,5},{13,9},{2,14},{6,2},{... | collective-permute-start | bytes 786440 | tf_op jit(solution)/shard_map/ppermute | solution.py:55
  201.6 13.8 %collective-permute-start.23 = (f32[2,32,1024]{2,1,0:T(8,128)S(1)}, f32[2,32,1024]{2,1,0:T(8,128)S(1)}, u32[]{:S(2)}, u32[]{:S(2)}) collective-permute-start(f32[2,32,1024]{2,1,0:T(8,128)S(1)} %get-tuple-element.60), channel_id=1, source_target_pairs={{0,8},{4,12},{8,0},{12,4},{1,9},{5,13},{9,1},{13,5},{2,10},{6,14},... | collective-permute-start | bytes 786440 | tf_op jit(solution)/shard_map/ppermute | solution.py:55
  201.6 15.1 %collective-permute-start.22 = (f32[2,32,1024]{2,1,0:T(8,128)S(1)}, f32[2,32,1024]{2,1,0:T(8,128)}, u32[]{:S(2)}, u32[]{:S(2)}) collective-permute-start(f32[2,32,1024]{2,1,0:T(8,128)S(1)} %get-tuple-element.61), channel_id=1, source_target_pairs={{0,4},{4,8},{8,12},{12,0},{1,5},{5,9},{9,13},{13,1},{2,6},{6,10},{... | collective-permute-start | bytes 786440 | tf_op jit(solution)/shard_map/ppermute | solution.py:55
  211.2 5.6 %copy-start.1 = (f32[32,48,128]{2,1,0:T(8,128)}, f32[32,48,128]{2,1,0:T(8,128)S(1)}, u32[]{:S(2)}) copy-start(f32[32,48,128]{2,1,0:T(8,128)S(1)} %all-to-all-done.1) | copy-start | bytes 2359300
  211.2 56.5 %all-to-all-start.2 = ((f32[32,88,128]{2,1,0:T(8,128)}), f32[32,88,128]{2,1,0:T(8,128)S(1)}, u32[]{:S(2)}, u32[]{:S(2)}) async-start(f32[32,88,128]{2,1,0:T(8,128)} %bitcast.36), calls=%async_computation.2 | async-start | bytes 2883584 | tf_op jit(solution)/shard_map/all_to_all | solution.py:489
  222.0 29.9 %collective-permute-start.30 = (f32[6,32,1024]{2,1,0:T(8,128)}, f32[6,32,1024]{2,1,0:T(8,128)S(1)}, u32[]{:S(2)}, u32[]{:S(2)}) collective-permute-start(f32[6,32,1024]{2,1,0:T(8,128)} %solve.1.refs_0_.refs_5_), channel_id=1, source_target_pairs={{0,1},{1,2},{2,3},{3,0},{4,5},{5,6},{6,7},{7,4},{8,9},{9,10},{10,1... | collective-permute-start | bytes 2359304 | tf_op jit(solution)/shard_map/ppermute | solution.py:55
  223.6 28.3 %collective-permute-start.29 = (f32[6,32,1024]{2,1,0:T(8,128)}, f32[6,32,1024]{2,1,0:T(8,128)S(1)}, u32[]{:S(2)}, u32[]{:S(2)}) collective-permute-start(f32[6,32,1024]{2,1,0:T(8,128)} %solve.1.refs_0_.refs_5_), channel_id=1, source_target_pairs={{0,3},{1,0},{2,1},{3,2},{4,7},{5,4},{6,5},{7,6},{8,11},{9,8},{10,9... | collective-permute-start | bytes 2359304 | tf_op jit(solution)/shard_map/ppermute | solution.py:55
  225.2 30.1 %collective-permute-start.26 = (f32[6,32,1024]{2,1,0:T(8,128)}, f32[6,32,1024]{2,1,0:T(8,128)S(1)}, u32[]{:S(2)}, u32[]{:S(2)}) collective-permute-start(f32[6,32,1024]{2,1,0:T(8,128)} %solve.1.refs_0_.refs_5_), channel_id=1, source_target_pairs={{0,4},{4,8},{8,12},{12,0},{1,5},{5,9},{9,13},{13,1},{2,6},{6,10},{... | collective-permute-start | bytes 2359304 | tf_op jit(solution)/shard_map/ppermute | solution.py:55
  225.2 31.0 %collective-permute-start.25 = (f32[6,32,1024]{2,1,0:T(8,128)}, f32[6,32,1024]{2,1,0:T(8,128)S(1)}, u32[]{:S(2)}, u32[]{:S(2)}) collective-permute-start(f32[6,32,1024]{2,1,0:T(8,128)} %solve.1.refs_0_.refs_5_), channel_id=1, source_target_pairs={{0,12},{4,0},{8,4},{12,8},{1,13},{5,1},{9,5},{13,9},{2,14},{6,2},{... | collective-permute-start | bytes 2359304 | tf_op jit(solution)/shard_map/ppermute | solution.py:55
  251.8 15.9 %copy-start.7 = (f32[6,32,1024]{2,1,0:T(8,128)}, f32[6,32,1024]{2,1,0:T(8,128)S(1)}, u32[]{:S(2)}) copy-start(f32[6,32,1024]{2,1,0:T(8,128)S(1)} %collective-permute-done.30.refs_9_) | copy-start | bytes 2359300
  251.9 11.9 %collective-permute-start.31 = (f32[3,32,1024]{2,1,0:T(8,128)S(1)}, f32[3,32,1024]{2,1,0:T(8,128)S(1)}, u32[]{:S(2)}, u32[]{:S(2)}) collective-permute-start(f32[3,32,1024]{2,1,0:T(8,128)S(1)} %slice.67), channel_id=1, source_target_pairs={{0,1},{1,2},{2,3},{3,0},{4,5},{5,6},{6,7},{7,4},{8,9},{9,10},{10,1... | collective-permute-start | bytes 1179656 | tf_op jit(solution)/shard_map/ppermute | solution.py:55
  252.0 15.8 %copy-start.8 = (f32[6,32,1024]{2,1,0:T(8,128)}, f32[6,32,1024]{2,1,0:T(8,128)S(1)}, u32[]{:S(2)}) copy-start(f32[6,32,1024]{2,1,0:T(8,128)S(1)} %collective-permute-done.29.refs_6_) | copy-start | bytes 2359300
  252.0 11.8 %collective-permute-start.32 = (f32[3,32,1024]{2,1,0:T(8,128)S(1)}, f32[3,32,1024]{2,1,0:T(8,128)S(1)}, u32[]{:S(2)}, u32[]{:S(2)}) collective-permute-start(f32[3,32,1024]{2,1,0:T(8,128)S(1)} %slice.68), channel_id=1, source_target_pairs={{0,3},{1,0},{2,1},{3,2},{4,7},{5,4},{6,5},{7,6},{8,11},{9,8},{10,9... | collective-permute-start | bytes 1179656 | tf_op jit(solution)/shard_map/ppermute | solution.py:55
  255.3 11.6 %collective-permute-start.27 = (f32[3,32,1024]{2,1,0:T(8,128)S(1)}, f32[3,32,1024]{2,1,0:T(8,128)S(1)}, u32[]{:S(2)}, u32[]{:S(2)}) collective-permute-start(f32[3,32,1024]{2,1,0:T(8,128)S(1)} %slice.65), channel_id=1, source_target_pairs={{0,4},{4,8},{8,12},{12,0},{1,5},{5,9},{9,13},{13,1},{2,6},{6,10},{... | collective-permute-start | bytes 1179656 | tf_op jit(solution)/shard_map/ppermute | solution.py:55
  256.2 10.7 %copy-start.10 = (f32[6,32,1024]{2,1,0:T(8,128)}, f32[6,32,1024]{2,1,0:T(8,128)S(1)}, u32[]{:S(2)}) copy-start(f32[6,32,1024]{2,1,0:T(8,128)S(1)} %collective-permute-done.25.refs_1_) | copy-start | bytes 2359300
  256.2 11.5 %collective-permute-start.28 = (f32[3,32,1024]{2,1,0:T(8,128)S(1)}, f32[3,32,1024]{2,1,0:T(8,128)}, u32[]{:S(2)}, u32[]{:S(2)}) collective-permute-start(f32[3,32,1024]{2,1,0:T(8,128)S(1)} %slice.66), channel_id=1, source_target_pairs={{0,12},{4,0},{8,4},{12,8},{1,13},{5,1},{9,5},{13,9},{2,14},{6,2},{... | collective-permute-start | bytes 1179656 | tf_op jit(solution)/shard_map/ppermute | solution.py:55
  263.8 3.9 %copy-start.15 = (f32[3,32,1024]{2,1,0:T(8,128)}, f32[3,32,1024]{2,1,0:T(8,128)S(1)}, u32[]{:S(2)}) copy-start(f32[3,32,1024]{2,1,0:T(8,128)S(1)} %collective-permute-done.31.refs_7_) | copy-start | bytes 1179652
  277.6 32.0 %all-to-all-start.3 = ((f32[16,8,32,128]{3,2,1,0:T(8,128)}), f32[16,8,32,128]{3,2,1,0:T(8,128)S(1)}, u32[]{:S(2)}, u32[]{:S(2)}) async-start(f32[16,8,32,128]{3,2,1,0:T(8,128)} %get-tuple-element.58), calls=%async_computation.3 | async-start | bytes 4194304 | tf_op jit(solution)/shard_map/all_to_all | solution.py:489
  (7 other events, 9.9 us)

commit v4 on v3

--- a/solution.py
+++ b/solution.py
@@ -21,10 +21,11 @@
 SLICE = BLOCK // SIDE
 PSLOTS = LINES * LB
 TSLOTS = 88
-PBINS = SIDE * FRONTS * PSLOTS
-TBINS = SIDE * FRONTS * TSLOTS
-BINS = PBINS + TBINS
+SLOTS = PSLOTS + TSLOTS
+BINS = SIDE * FRONTS * SLOTS
 OUT_SLOTS = 2 + LINES
+WIDE = 2 * BLOCK
+PACKED = [WIDE * (c * (c + 1) // 2) for c in range(LEAD // WIDE + 1)]
 SUB = 8
 SLABS = BLOCK // SUB
 ACCS = 8
@@ -131,7 +132,7 @@
     )(tiles.reshape(TILES * BLOCK, BLOCK))
 
 
-def combine_kernel(position, bins, x, panel, trail, *accs):
+def combine_kernel(position, bins, x, out, *accs):
     sources = x.shape[0] // TILES
 
     @pl.when(pl.program_id(0) == 0)
@@ -156,28 +157,25 @@
 
     @pl.when(pl.program_id(0) == pl.num_programs(0) - 1)
     def _():
-        for out, offset in ((panel, 0), (trail, PBINS)):
-
-            def add(b, carry, out=out, offset=offset):
-                first = pl.multiple_of(b * step, step)
-                total = accs[0][pl.ds(offset + first, step), :]
-                for acc in accs[1:]:
-                    total = total + acc[pl.ds(offset + first, step), :]
-                out[pl.ds(first, step), :] = total
-                return carry
-
-            lax.fori_loop(0, out.shape[0] // step, add, 0)
+        def add(b, carry):
+            at = pl.ds(pl.multiple_of(b * step, step), step)
+            total = accs[0][at, :]
+            for acc in accs[1:]:
+                total = total + acc[at, :]
+            out[at, :] = total
+            return carry
+
+        lax.fori_loop(0, BINS // step, add, 0)
 
 
 def combine(position, bins, rows):
     steps = 4
-    sizes = [PBINS, TBINS]
     return pl.pallas_call(
         combine_kernel,
         grid=(steps,),
-        out_shape=[jax.ShapeDtypeStruct((size, BLOCK), jnp.float32) for size in sizes],
+        out_shape=jax.ShapeDtypeStruct((BINS, BLOCK), jnp.float32),
         in_specs=[SMEM, SMEM, pl.BlockSpec((rows.shape[0] // steps, BLOCK), lambda i: (i, 0))],
-        out_specs=[pl.BlockSpec((size, BLOCK), lambda i: (0, 0)) for size in sizes],
+        out_specs=pl.BlockSpec((BINS, BLOCK), lambda i: (0, 0)),
         scratch_shapes=[pltpu.VMEM((BINS, BLOCK), jnp.float32)] * ACCS,
         compiler_params=pltpu.CompilerParams(vmem_limit_bytes=VMEM_LIMIT),
         cost_estimate=pl.CostEstimate(flops=20 * 10**9, bytes_accessed=20 << 20, transcendentals=0),
@@ -205,8 +203,8 @@
 
 
 def factor_kernel(position, *refs):
-    pieces, outs, scratch = refs[:10], refs[10:14], refs[14:]
-    own_rows, inverse_high, inverse_low, labels = outs
+    pieces, outs, scratch = refs[:10], refs[10:13], refs[13:]
+    own_rows, inverse, labels = outs
     (entries, labels_in, work, diag, pair, sem) = scratch
     px, py = position[0], position[1]
 
@@ -269,12 +267,14 @@
     lax.fori_loop(0, LB, step, 0)
     for k in range(LB):
         at = slice(k * BLOCK, (k + 1) * BLOCK)
-        done = slice(0, (k + 1) * BLOCK)
-        inverse_high[at, done], inverse_low[at, done] = split(work[at, done])
-        if k + 1 < LB:
-            rest = jnp.zeros((BLOCK, LEAD - (k + 1) * BLOCK), jnp.bfloat16)
-            inverse_high[at, (k + 1) * BLOCK :] = rest
-            inverse_low[at, (k + 1) * BLOCK :] = rest
+        start, width = PACKED[k // 2], (k + 1) * BLOCK
+        part = slice(k % 2 * BLOCK, (k % 2 + 1) * BLOCK)
+        high, low = split(work[at, :width])
+        inverse[0, part, start : start + width] = high
+        inverse[1, part, start : start + width] = low
+        if k % 2 == 0:
+            rest = jnp.zeros((2, BLOCK, BLOCK), jnp.bfloat16)
+            inverse[:, part, start + width : start + width + BLOCK] = rest
     mine = jnp.minimum(px * SIDE + py, LB - 1)
     mine_at = pl.ds(pl.multiple_of(mine * BLOCK, BLOCK), BLOCK)
     for k in range(LB):
@@ -288,12 +288,11 @@
         factor_kernel,
         out_shape=[
             jax.ShapeDtypeStruct((BLOCK, LEAD), jnp.float32),
-            jax.ShapeDtypeStruct((LEAD, LEAD), jnp.bfloat16),
-            jax.ShapeDtypeStruct((LEAD, LEAD), jnp.bfloat16),
+            jax.ShapeDtypeStruct((2, WIDE, PACKED[-1]), jnp.bfloat16),
             jax.ShapeDtypeStruct((GRID, LEAD), jnp.int32),
         ],
         in_specs=[SMEM] + [ANY] * 10,
-        out_specs=[VMEM] * 4,
+        out_specs=[VMEM] * 3,
         scratch_shapes=[
             pltpu.VMEM((LB * SLABS, SUB, LEAD), jnp.float32),
             pltpu.VMEM((GRID, SUB, LEAD), jnp.float32),
@@ -308,7 +307,7 @@
     )(position, *pieces)
 
 
-def solve_kernel(position, own, part1, part2, part3, sums, inverse_high, inverse_low, out, rows):
+def solve_kernel(position, own, part1, part2, part3, sums, inverse, out, rows):
     x = position[0]
     for step, part in enumerate((own, part1, part2, part3)):
         source = (x + SIDE - step) % SIDE
@@ -317,30 +316,28 @@
     for m in range(LINES):
         for c in range(LB):
             at = slice(c * BLOCK, (c + 1) * BLOCK)
-            values = sums[pl.ds(m * LB + c, SLICE, stride=PSLOTS), :]
+            values = sums[pl.ds(m * LB + c, SLICE, stride=SLOTS), :]
             rows[LB // SIDE + m, :, at] = rows[LB // SIDE + m, :, at] + values
     high, low = split(rows[LB // SIDE :].reshape(LINES * SLICE, LEAD))
-    wide = 2 * BLOCK
-    for c in range(LEAD // wide):
-        end = (c + 1) * wide
-        inv_high = inverse_high[end - wide : end, :end]
-        inv_low = inverse_low[end - wide : end, :end]
+    for c in range(LEAD // WIDE):
+        end = (c + 1) * WIDE
+        inv_high, inv_low = inverse[:, :, PACKED[c] : PACKED[c + 1]]
         value = mul(high[:, :end], inv_high) + (
             mul(high[:, :end], inv_low) + mul(low[:, :end], inv_high)
         )
-        out[:, :, end - wide : end] = value.reshape(LINES, SLICE, wide)
-
-
-def solve(position, parts, sums, inverse_high, inverse_low):
+        out[:, :, end - WIDE : end] = value.reshape(LINES, SLICE, WIDE)
+
+
+def solve(position, parts, sums, inverse):
     return pl.pallas_call(
         solve_kernel,
         out_shape=jax.ShapeDtypeStruct((LINES, SLICE, LEAD), jnp.float32),
-        in_specs=[SMEM] + [VMEM] * 7,
+        in_specs=[SMEM] + [VMEM] * 6,
         out_specs=VMEM,
         scratch_shapes=[pltpu.VMEM((2 * SIDE, SLICE, LEAD), jnp.float32)],
-        compiler_params=pltpu.CompilerParams(vmem_limit_bytes=VMEM_LIMIT),
+        compiler_params=pltpu.CompilerParams(vmem_limit_bytes=20 << 20),
         name="solve",
-    )(position, *parts, sums, inverse_high, inverse_low)
+    )(position, *parts, sums, inverse)
 
 
 def product_kernel(position, *refs):
@@ -392,7 +389,7 @@
                     continue
                 below = jnp.maximum(row_block - LB - y - SIDE * n, 0)
                 slot = (TB - y) * n - 2 * n * (n - 1) + below
-                tiles = sums[pl.ds(slot, SLICE, stride=TSLOTS), :]
+                tiles = sums[pl.ds(PSLOTS + slot, SLICE, stride=SLOTS), :]
                 col = (n - 2 * pair) * BLOCK
                 out[owner, first + n] = tiles - value[line : line + SLICE, col : col + BLOCK]
 
@@ -412,7 +409,7 @@
             pltpu.VMEM((LINES * BLOCK, LEAD), jnp.bfloat16),
             pltpu.VMEM((LINES * BLOCK, LEAD), jnp.bfloat16),
         ],
-        compiler_params=pltpu.CompilerParams(vmem_limit_bytes=VMEM_LIMIT),
+        compiler_params=pltpu.CompilerParams(vmem_limit_bytes=32 << 20),
         cost_estimate=pl.CostEstimate(flops=11 * 10**9, bytes_accessed=8 << 20, transcendentals=0),
         name="product",
     )(position, *along_x, *along_y, sums)
@@ -425,52 +422,73 @@
     return jnp.where(inside, values, 0.0)
 
 
-def base_kernel(position, entries, lead_rows, own, out):
+def base_kernel(position, lead_rows, own, out):
     g = position[0] * SIDE + position[1]
     out[0, :, :LEAD] = jnp.where(g < LB, lead_rows[...], own[0])
     out[1, :, :LEAD] = own[1]
-    for local in range(2):
-        for block in range(LB, FB):
-            at = slice(block * BLOCK, (block + 1) * BLOCK)
-            out[local, :, at] = lower(entries[local, :, at], local * GRID + g, block, 0)
-
-
-def base(position, entries, lead_rows, own):
+    out[:, :, LEAD:] = jnp.zeros((2, BLOCK, TB * BLOCK), jnp.float32)
+
+
+def base(position, shape, lead_rows, own):
     return pl.pallas_call(
         base_kernel,
-        out_shape=jax.ShapeDtypeStruct(entries.shape, jnp.float32),
-        in_specs=[SMEM] + [VMEM] * 3,
+        out_shape=jax.ShapeDtypeStruct(shape, jnp.float32),
+        in_specs=[SMEM, VMEM, VMEM],
         out_specs=VMEM,
-        compiler_params=pltpu.CompilerParams(vmem_limit_bytes=VMEM_LIMIT),
+        compiler_params=pltpu.CompilerParams(vmem_limit_bytes=16 << 20),
         cost_estimate=pl.CostEstimate(flops=0, bytes_accessed=32 << 20, transcendentals=0),
         name="base",
-    )(position, entries, lead_rows, own)
-
-
-def finish_kernel(position, before, change, out):
+    )(position, lead_rows, own)
+
+
+def finish_kernel(position, before, entries_in, change_in, out, entries, change, values, sem):
     g = position[0] * SIDE + position[1]
-    out[...] = before[...]
-    for local in range(2):
-        for block in range(LB, FB if local else GRID):
-            at = slice(block * BLOCK, (block + 1) * BLOCK)
-            y, n = block % SIDE, (block - LB) // SIDE
+    wide = SIDE * BLOCK
+    steps = [(0, n) for n in range(2)] + [(1, n) for n in range(LINES)]
+    arriving, leaving = [], []
+    for i, (local, n) in enumerate(steps):
+        at = pl.ds(LEAD + n * wide, wide)
+        arriving.append(
+            (
+                pltpu.make_async_copy(entries_in.at[local, :, at], entries.at[i], sem.at[0, i]),
+                pltpu.make_async_copy(change_in.at[:, i], change.at[i], sem.at[1, i]),
+            )
+        )
+        leaving.append(pltpu.make_async_copy(values.at[i], out.at[local, :, at], sem.at[2, i]))
+    for pair in arriving:
+        for copy in pair:
+            copy.start()
+    for i, (local, n) in enumerate(steps):
+        for copy in arriving[i]:
+            copy.wait()
+        for y in range(SIDE):
+            at = slice(y * BLOCK, (y + 1) * BLOCK)
             for x in range(SIDE):
                 span = slice(x * SLICE, (x + 1) * SLICE)
-                value = lower(
-                    change[x * SIDE + y, 2 * local + n], local * GRID + g, block, x * SLICE
-                )
-                out[local, span, at] = before[local, span, at] + value
-
-
-def finish(position, before, change):
+                value = entries[i, span, at] + change[i, x * SIDE + y]
+                block = LB + n * SIDE + y
+                values[i, span, at] = lower(value, local * GRID + g, block, x * SLICE)
+        leaving[i].start()
+    for copy in leaving:
+        copy.wait()
+
+
+def finish(position, before, entries, change):
     return pl.pallas_call(
         finish_kernel,
         out_shape=jax.ShapeDtypeStruct(before.shape, jnp.float32),
-        in_specs=[SMEM, VMEM, VMEM],
-        out_specs=VMEM,
+        in_specs=[SMEM, ANY, ANY, ANY],
+        out_specs=ANY,
+        input_output_aliases={1: 0},
+        scratch_shapes=[
+            pltpu.VMEM((OUT_SLOTS, BLOCK, SIDE * BLOCK), jnp.float32),
+            pltpu.VMEM((OUT_SLOTS, GRID, SLICE, BLOCK), jnp.float32),
+            pltpu.VMEM((OUT_SLOTS, BLOCK, SIDE * BLOCK), jnp.float32),
+            pltpu.SemaphoreType.DMA((3, OUT_SLOTS)),
+        ],
         compiler_params=pltpu.CompilerParams(vmem_limit_bytes=VMEM_LIMIT),
         name="finish",
-    )(position, before, change)
+    )(position, before, entries, change)
 
 
 def destination_bins(owners, local_rows, picks):
@@ -478,10 +496,10 @@
     shifted = local_rows + (local_rows * GRID + g < LB).astype(jnp.int32)
     row_block = shifted * GRID + g
     col_block = picks % (row_block + 1)
-    panel = (row_block % SIDE * FRONTS + front) * PSLOTS + (row_block - LB) // SIDE * LB + col_block
+    panel = (row_block % SIDE * FRONTS + front) * SLOTS + (row_block - LB) // SIDE * LB + col_block
     y, n = col_block % SIDE, (col_block - LB) // SIDE
     slot = (TB - y) * n - 2 * n * (n - 1) + row_block - col_block
-    trail = PBINS + (y * FRONTS + front) * TSLOTS + slot
+    trail = (y * FRONTS + front) * SLOTS + PSLOTS + slot
     return jnp.where(col_block < LB, panel, trail)
 
 
@@ -513,18 +531,16 @@
         lax.dynamic_index_in_dim(panel, (x + n) % SIDE, 1, keepdims=False) for n in range(SIDE)
     ]
     panel = [part if n == 0 else shift(part, "x", n) for n, part in enumerate(panel)]
-    lead_rows, *inverse, bins = factor(position, lead)
-    panel_sums, trail_sums = combine(position, bins.reshape(-1), rows)
-    panel_sums = across(panel_sums.reshape(SLICE, PSLOTS, BLOCK), ("y", "front"))
-    panel_sums, trail_sums = lax.optimization_barrier((panel_sums, trail_sums))
-    trail_sums = across(trail_sums.reshape(SLICE, TSLOTS, BLOCK), ("y", "front"))
-    solved = solve(position, panel, panel_sums.reshape(-1, BLOCK), *inverse)
+    lead_rows, inverse, bins = factor(position, lead)
+    sums = combine(position, bins.reshape(-1), rows).reshape(SLICE, SLOTS, BLOCK)
+    sums = across(sums, ("y", "front")).reshape(-1, BLOCK)
+    solved = solve(position, panel, sums, inverse)
     near = [ring_near(solved, axis) for axis in ("x", "y")]
     far = [ring_far(pair, axis) for pair, axis in zip(near, ("x", "y"))]
     along = [ring_pieces(solved, *pair) for pair in zip(near, far)]
-    change, own = product(position, *along, trail_sums.reshape(-1, BLOCK))
+    change, own = product(position, *along, sums)
     change = across(change, ("x", "y"))
-    out = finish(position, base(position, entries, lead_rows, own), change)
+    out = finish(position, base(position, entries.shape, lead_rows, own), entries, change)
     return out[None, :, None]
 
 

time: 317 us -> 313 us (0.987)
  waiting for transfers between devices: 87 us -> 101 us
  Pallas kernels: 142 us -> 129 us
  starting transfers between devices: 75.3 us -> 70.8 us
    all_to_all x4 -> x3, waiting for transfers between devices: 45.4 us -> 51.8 us  [across(): return lax.all_to_all(values, axes, split_axis=0, concat_axis=0)]
    ppermute x25, waiting for transfers between devices: 39.8 us -> 45.3 us  [shift(): lax.ppermute(block, axis, [(i, (i + step) % SIDE) for i in range(SIDE)])]
    pallas_call x1, Pallas kernels: 8.77 us -> 4.35 us  [product(): pl.pallas_call(product_kernel, out_shape=[jax.ShapeDtypeStruct((GRID, OUT...]
    all_to_all x4 -> x3, starting transfers between devices: 23.4 us -> 19.6 us  [across(): return lax.all_to_all(values, axes, split_axis=0, concat_axis=0)]
    pallas_call x1, Pallas kernels: 5.23 us -> 2.02 us  [solve(): pl.pallas_call(solve_kernel, out_shape=jax.ShapeDtypeStruct((LINES, SLICE...]
  transfers between devices with their start and end apart: 37 -> 36, of which waited for: 14 -> 18; matrix products, arithmetic and copies ran while one was open for 2% -> 2% of each run, Pallas kernels for 34% -> 32%
where the time goes in v4:
time: 313 us
  Pallas kernels  129 us (41%)
  waiting for transfers between devices  101 us (32%)
  starting transfers between devices  70.8 us (23%)
  local copies, waits for them, and re-layouts  7.23 us (2%)
  other arithmetic  3.34 us (1%)
    pallas_call x1, Pallas kernels, factor(): pl.pallas_call(factor_kernel, out_shape=[jax.ShapeDtypeStruct((BLOCK, LEA...  86.2 us
    all_to_all x3, waiting for transfers between devices, across(): return lax.all_to_all(values, axes, split_axis=0, concat_axis=0)  51.8 us
    ppermute x25, waiting for transfers between devices, shift(): lax.ppermute(block, axis, [(i, (i + step) % SIDE) for i in range(SIDE)])  45.3 us
    ppermute x25, starting transfers between devices, shift(): lax.ppermute(block, axis, [(i, (i + step) % SIDE) for i in range(SIDE)])  36.8 us
    pallas_call x1, Pallas kernels, combine(): pl.pallas_call(combine_kernel, grid=(steps,), out_shape=jax.ShapeDtypeStr...  20 us
    all_to_all x3, starting transfers between devices, across(): return lax.all_to_all(values, axes, split_axis=0, concat_axis=0)  19.6 us
    pallas_call x1, Pallas kernels, turn(): pl.pallas_call(turn_kernel, grid=(TILES // step,), out_shape=jax.ShapeDty...  10 us
    ppermute x7, starting transfers between devices, gather_front(): lax.ppermute(values, 'front', [(i, i ^ k) for i in range(FRONTS)])  9.4 us
  transfers between devices with their start and end apart: 36, of which 18 were waited for; matrix products, arithmetic and copies ran while one was open for 2% of the time, Pallas kernels for 32%

profile of v4, /device:TPU:0, one launch (start us, length us, event | category | flops | bytes accessed | tf_op | source)
XLA Modules:
  0.0 312.6 jit_solution(2801796434242387674)
XLA Ops:
  0.0 1.0 slice_bitcast_fusion
  1.0 5.0 %collective-permute-start = (f32[64,1024]{1,0:T(8,128)S(1)}, f32[64,1024]{1,0:T(8,128)S(1)}, u32[]{:S(2)}, u32[]{:S(2)}) collective-permute-start(f32[64,1024]{1,0:T(8,128)S(1)} %slice_bitcast_fusion), channel_id=1, source_target_pairs={{0,8},{4,12},{1,9},{5,13},{2,10},{6,14},{3,11},{7,15},{16,24},{20,... | collective-permute-start | bytes 786440 | tf_op jit(solution)/shard_map/ppermute | solution.py:516
  6.9 2.0 collective-permute-start.2
  9.0 3.7 %collective-permute-start.4 = (s32[128]{0:T(128)S(1)}, s32[128]{0:T(128)S(1)}, u32[]{:S(2)}, u32[]{:S(2)}) collective-permute-start(s32[128]{0:T(128)S(1)} %compare_select_fusion.10), channel_id=1, source_target_pairs={{0,64},{16,80},{32,96},{48,112},{64,0},{80,16},{96,32},{112,48},{1... | collective-permute-start | bytes 1544 | tf_op jit(solution)/shard_map/ppermute | solution.py:61
  13.7 3.3 %collective-permute-start.6 = (s32[128]{0:T(128)S(1)}, s32[128]{0:T(128)S(1)}, u32[]{:S(2)}, u32[]{:S(2)}) collective-permute-start(s32[128]{0:T(128)S(1)} %compare_select_fusion.10), channel_id=1, source_target_pairs={{0,96},{16,112},{32,64},{48,80},{64,32},{80,48},{96,0},{112,16},{1... | collective-permute-start | bytes 1544 | tf_op jit(solution)/shard_map/ppermute | solution.py:61
  17.1 1.0 collective-permute-done.5
  18.5 2.7 collective-permute-done.7
  21.2 1.0 fusion.1
  22.3 3.1 collective-permute-start.11
  26.0 1.0 collective-permute-start.13
  27.1 2.6 collective-permute-start.9
  29.7 1.5 collective-permute-done.11
  31.8 1.4 collective-permute-done.12
  33.2 1.7 collective-permute-done.13
  35.6 2.8 collective-permute-done.10
  38.5 3.2 %collective-permute-start.14 = (f32[4,5,8,1024]{3,2,1,0:T(8,128)S(1)}, f32[4,5,8,1024]{3,2,1,0:T(8,128)S(1)}, u32[]{:S(2)}, u32[]{:S(2)}) collective-permute-start(f32[4,5,8,1024]{3,2,1,0:T(8,128)S(1)} %pad_maximum_fusion.refs_0_), channel_id=1, source_target_pairs={{0,3},{1,0},{2,1},{3,2},{4,7},{5,4},{6,5},{7,6},{8,11},{9,8},{10,9... | collective-permute-start | bytes 1966088 | tf_op jit(solution)/shard_map/ppermute | solution.py:56
  41.7 2.0 collective-permute-start.17
  43.7 10.0 %turn.1 = f32[128,128,128]{2,1,0:T(8,128)} custom-call(f32[16384,128]{1,0:T(8,128)} %bitcast.91), custom_call_target="tpu_custom_call" | custom-call | bytes 16777216 | tf_op jit(solution)/shard_map/turn/pallas_call | solution.py:123
  53.8 1.1 collective-permute-done.17.refs_9_
  54.9 2.8 collective-permute-done.15.refs_4_
  57.8 3.3 %collective-permute-start.19 = (f32[2,5,8,1024]{3,2,1,0:T(8,128)S(1)}, f32[2,5,8,1024]{3,2,1,0:T(8,128)}, u32[]{:S(2)}, u32[]{:S(2)}) collective-permute-start(f32[2,5,8,1024]{3,2,1,0:T(8,128)S(1)} %slice.55), channel_id=1, source_target_pairs={{0,3},{1,0},{2,1},{3,2},{4,7},{5,4},{6,5},{7,6},{8,11},{9,8},{10,9... | collective-permute-start | bytes 983048 | tf_op jit(solution)/shard_map/ppermute | solution.py:56
  61.3 3.3 %collective-permute-start.21 = (f32[2,4,8,1024]{3,2,1,0:T(8,128)S(1)}, f32[2,4,8,1024]{3,2,1,0:T(8,128)}, u32[]{:S(2)}, u32[]{:S(2)}) collective-permute-start(f32[2,4,8,1024]{3,2,1,0:T(8,128)S(1)} %slice.57), channel_id=1, source_target_pairs={{0,12},{4,0},{8,4},{12,8},{1,13},{5,1},{9,5},{13,9},{2,14},{6,2},{... | collective-permute-start | bytes 786440 | tf_op jit(solution)/shard_map/ppermute | solution.py:56
  65.1 6.1 %all-to-all-start = ((f32[128,128,128]{2,1,0:T(8,128)}), f32[128,128,128]{2,1,0:T(8,128)}, u32[]{:S(2)}, u32[]{:S(2)}) async-start(f32[128,128,128]{2,1,0:T(8,128)} %turn.1), calls=%async_computation | async-start | bytes 16777216 | tf_op jit(solution)/shard_map/all_to_all | solution.py:507
  71.3 86.2 %factor.1 = (f32[128,1024]{1,0:T(8,128)}, bf16[2,256,2560]{2,1,0:T(8,128)(2,1)}, s32[16,1024]{1,0:T(8,128)}) custom-call(s32[3]{0:T(128)} %pad_add_fusion.position, f32[4,5,8,1024]{3,2,1,0:T(8,128)} %copy-done.4, f32[4,5,8,1024]{3,2,1,0:T(8,128)} %copy-done.6, f32[2,5,8,1024]{3,2,1,0:T(8,128)} %collective-permute-done.18.refs_2_, ...), custom_call_target="tpu_custom_call" | custom-call | flops 120000004096 | bytes 20971520 | tf_op jit(solution)/shard_map/factor/pallas_call | solution.py:287
  157.5 1.5 copy.8
  159.0 14.3 %all-to-all-done = f32[128,128,128]{2,1,0:T(8,128)} async-done(((f32[128,128,128]{2,1,0:T(8,128)}), f32[128,128,128]{2,1,0:T(8,128)}, u32[]{:S(2)}, u32[]{:S(2)}) %all-to-all-start) | async-done | bytes 8388640 | tf_op jit(solution)/shard_map/all_to_all | solution.py:507
  173.3 20.0 %combine.1 = f32[4352,128]{1,0:T(8,128)} custom-call(s32[3]{0:T(128)} %pad_add_fusion.position, s32[16384]{0:T(1024)} %bitcast.105, f32[16384,128]{1,0:T(8,128)} %bitcast.33.x), custom_call_target="tpu_custom_call" | custom-call | flops 20000000000 | bytes 20971520 | tf_op jit(solution)/shard_map/combine/pallas_call | solution.py:173
  193.3 8.6 %all-to-all-start.1 = ((f32[32,136,128]{2,1,0:T(8,128)}), f32[32,136,128]{2,1,0:T(8,128)S(1)}, u32[]{:S(2)}, u32[]{:S(2)}) async-start(f32[32,136,128]{2,1,0:T(8,128)} %bitcast.97), calls=%async_computation.1 | async-start | bytes 4456448 | tf_op jit(solution)/shard_map/all_to_all | solution.py:507
  202.0 1.3 slice.58
  203.5 1.8 collective-permute-start.23
  205.3 1.5 collective-permute-start.24
  206.8 12.1 %collective-permute-done.22.part1 = f32[2,32,1024]{2,1,0:T(8,128)S(1)} collective-permute-done((f32[2,32,1024]{2,1,0:T(8,128)S(1)}, f32[2,32,1024]{2,1,0:T(8,128)S(1)}, u32[]{:S(2)}, u32[]{:S(2)}) %collective-permute-start.22) | collective-permute-done | bytes 262176 | tf_op jit(solution)/shard_map/ppermute | solution.py:56
  219.5 12.9 %all-to-all-done.1 = f32[32,136,128]{2,1,0:T(8,128)S(1)} async-done(((f32[32,136,128]{2,1,0:T(8,128)}), f32[32,136,128]{2,1,0:T(8,128)S(1)}, u32[]{:S(2)}, u32[]{:S(2)}) %all-to-all-start.1) | async-done | bytes 2228256 | tf_op jit(solution)/shard_map/all_to_all | solution.py:507
  232.3 1.7 copy-done
  234.1 2.0 solve.1.refs_0_.refs_5_
  236.2 3.2 %collective-permute-start.25 = (f32[6,32,1024]{2,1,0:T(8,128)S(1)}, f32[6,32,1024]{2,1,0:T(8,128)S(1)}, u32[]{:S(2)}, u32[]{:S(2)}) collective-permute-start(f32[6,32,1024]{2,1,0:T(8,128)S(1)} %solve.1.refs_0_.refs_5_), channel_id=1, source_target_pairs={{0,12},{4,0},{8,4},{12,8},{1,13},{5,1},{9,5},{13,9},{2,14},{6,2},{... | collective-permute-start | bytes 2359304 | tf_op jit(solution)/shard_map/ppermute | solution.py:56
  239.4 3.2 %collective-permute-start.29 = (f32[6,32,1024]{2,1,0:T(8,128)S(1)}, f32[6,32,1024]{2,1,0:T(8,128)S(1)}, u32[]{:S(2)}, u32[]{:S(2)}) collective-permute-start(f32[6,32,1024]{2,1,0:T(8,128)S(1)} %solve.1.refs_0_.refs_5_), channel_id=1, source_target_pairs={{0,3},{1,0},{2,1},{3,2},{4,7},{5,4},{6,5},{7,6},{8,11},{9,8},{10,9... | collective-permute-start | bytes 2359304 | tf_op jit(solution)/shard_map/ppermute | solution.py:56
  242.7 13.8 %collective-permute-done.26.refs_4_ = f32[6,32,1024]{2,1,0:T(8,128)S(1)} collective-permute-done((f32[6,32,1024]{2,1,0:T(8,128)S(1)}, f32[6,32,1024]{2,1,0:T(8,128)S(1)}, u32[]{:S(2)}, u32[]{:S(2)}) %collective-permute-start.26) | collective-permute-done | bytes 786464 | tf_op jit(solution)/shard_map/ppermute | solution.py:56
  256.6 3.3 %collective-permute-start.28 = (f32[3,32,1024]{2,1,0:T(8,128)S(1)}, f32[3,32,1024]{2,1,0:T(8,128)S(1)}, u32[]{:S(2)}, u32[]{:S(2)}) collective-permute-start(f32[3,32,1024]{2,1,0:T(8,128)S(1)} %slice.66), channel_id=1, source_target_pairs={{0,12},{4,0},{8,4},{12,8},{1,13},{5,1},{9,5},{13,9},{2,14},{6,2},{... | collective-permute-start | bytes 1179656 | tf_op jit(solution)/shard_map/ppermute | solution.py:56
  260.1 3.5 %collective-permute-start.32 = (f32[3,32,1024]{2,1,0:T(8,128)S(1)}, f32[3,32,1024]{2,1,0:T(8,128)S(1)}, u32[]{:S(2)}, u32[]{:S(2)}) collective-permute-start(f32[3,32,1024]{2,1,0:T(8,128)S(1)} %slice.68), channel_id=1, source_target_pairs={{0,3},{1,0},{2,1},{3,2},{4,7},{5,4},{6,5},{7,6},{8,11},{9,8},{10,9... | collective-permute-start | bytes 1179656 | tf_op jit(solution)/shard_map/ppermute | solution.py:56
  263.6 3.9 %collective-permute-done.27.refs_2_ = f32[3,32,1024]{2,1,0:T(8,128)S(1)} collective-permute-done((f32[3,32,1024]{2,1,0:T(8,128)S(1)}, f32[3,32,1024]{2,1,0:T(8,128)S(1)}, u32[]{:S(2)}, u32[]{:S(2)}) %collective-permute-start.27) | collective-permute-done | bytes 393248 | tf_op jit(solution)/shard_map/ppermute | solution.py:56
  267.5 2.9 collective-permute-done.31.refs_7_
  270.4 4.3 %product.1 = (f32[16,8,32,128]{3,2,1,0:T(8,128)S(1)}, f32[2,128,1024]{2,1,0:T(8,128)S(1)}) custom-call(s32[3]{0:T(128)S(1)} %copy-done.3, f32[6,32,1024]{2,1,0:T(8,128)S(1)} %solve.1.refs_0_.refs_5_, f32[6,32,1024]{2,1,0:T(8,128)S(1)} %collective-permute-done.25.refs_1_, f32[3,32,1024]{2,1,0:T(8,128)S(1)} %collective-permute-done.27.refs_2_, ...), custom_call_target="tpu_custom_call" | custom-call | flops 11000000512 | bytes 8388608 | tf_op jit(solution)/shard_map/product/pallas_call | solution.py:398
  274.7 1.3 copy-done.1
  276.1 4.8 %all-to-all-start.2 = ((f32[16,8,32,128]{3,2,1,0:T(8,128)}), f32[16,8,32,128]{3,2,1,0:T(8,128)}, u32[]{:S(2)}, u32[]{:S(2)}) async-start(f32[16,8,32,128]{3,2,1,0:T(8,128)} %copy-done.1), calls=%async_computation.2 | async-start | bytes 4194304 | tf_op jit(solution)/shard_map/all_to_all | solution.py:507
  280.9 2.8 base.1.before
  283.8 24.6 %all-to-all-done.2.change_in = f32[16,8,32,128]{3,2,1,0:T(8,128)} async-done(((f32[16,8,32,128]{3,2,1,0:T(8,128)}), f32[16,8,32,128]{3,2,1,0:T(8,128)}, u32[]{:S(2)}, u32[]{:S(2)}) %all-to-all-start.2) | async-done | bytes 2097184 | tf_op jit(solution)/shard_map/all_to_all | solution.py:507
  308.4 4.0 %finish.1 = f32[2,128,4096]{2,1,0:T(8,128)} custom-call(s32[3]{0:T(128)} %pad_add_fusion.position, f32[2,128,4096]{2,1,0:T(8,128)} %base.1.before, f32[2,128,4096]{2,1,0:T(8,128)} %bitcast.95, f32[16,8,32,128]{3,2,1,0:T(8,128)} %all-to-all-done.2.change_in), custom_call_target="tpu_custom_call", output_to_operand_aliasing={{}: (1, {})} | custom-call | tf_op jit(solution)/shard_map/finish/pallas_call | solution.py:477
  (74 shorter events, 6.5 us)
Async XLA Ops:
  1.0 20.3 %collective-permute-start = (f32[64,1024]{1,0:T(8,128)S(1)}, f32[64,1024]{1,0:T(8,128)S(1)}, u32[]{:S(2)}, u32[]{:S(2)}) collective-permute-start(f32[64,1024]{1,0:T(8,128)S(1)} %slice_bitcast_fusion), channel_id=1, source_target_pairs={{0,8},{4,12},{1,9},{5,13},{2,10},{6,14},{3,11},{7,15},{16,24},{20,... | collective-permute-start | bytes 786440 | tf_op jit(solution)/shard_map/ppermute | solution.py:516
  6.8 6.7 %collective-permute-start.1 = (s32[128]{0:T(128)S(1)}, s32[128]{0:T(128)S(1)}, u32[]{:S(2)}, u32[]{:S(2)}) collective-permute-start(s32[128]{0:T(128)S(1)} %compare_select_fusion.10), channel_id=1, source_target_pairs={{0,16},{16,0},{32,48},{48,32},{64,80},{80,64},{96,112},{112,96},{1... | collective-permute-start | bytes 1544 | tf_op jit(solution)/shard_map/ppermute | solution.py:61
  6.9 6.7 %collective-permute-start.2 = (s32[128]{0:T(128)S(1)}, s32[128]{0:T(128)S(1)}, u32[]{:S(2)}, u32[]{:S(2)}) collective-permute-start(s32[128]{0:T(128)S(1)} %compare_select_fusion.10), channel_id=1, source_target_pairs={{0,32},{16,48},{32,0},{48,16},{64,96},{80,112},{96,64},{112,80},{1... | collective-permute-start | bytes 1544 | tf_op jit(solution)/shard_map/ppermute | solution.py:61
  8.9 8.1 %collective-permute-start.3 = (s32[128]{0:T(128)S(1)}, s32[128]{0:T(128)S(1)}, u32[]{:S(2)}, u32[]{:S(2)}) collective-permute-start(s32[128]{0:T(128)S(1)} %compare_select_fusion.10), channel_id=1, source_target_pairs={{0,48},{16,32},{32,16},{48,0},{64,112},{80,96},{96,80},{112,64},{1... | collective-permute-start | bytes 1544 | tf_op jit(solution)/shard_map/ppermute | solution.py:61
  9.0 8.1 %collective-permute-start.4 = (s32[128]{0:T(128)S(1)}, s32[128]{0:T(128)S(1)}, u32[]{:S(2)}, u32[]{:S(2)}) collective-permute-start(s32[128]{0:T(128)S(1)} %compare_select_fusion.10), channel_id=1, source_target_pairs={{0,64},{16,80},{32,96},{48,112},{64,0},{80,16},{96,32},{112,48},{1... | collective-permute-start | bytes 1544 | tf_op jit(solution)/shard_map/ppermute | solution.py:61
  13.5 4.5 %collective-permute-start.5 = (s32[128]{0:T(128)S(1)}, s32[128]{0:T(128)S(1)}, u32[]{:S(2)}, u32[]{:S(2)}) collective-permute-start(s32[128]{0:T(128)S(1)} %compare_select_fusion.10), channel_id=1, source_target_pairs={{0,80},{16,64},{32,112},{48,96},{64,16},{80,0},{96,48},{112,32},{1... | collective-permute-start | bytes 1544 | tf_op jit(solution)/shard_map/ppermute | solution.py:61
  13.7 4.9 %collective-permute-start.6 = (s32[128]{0:T(128)S(1)}, s32[128]{0:T(128)S(1)}, u32[]{:S(2)}, u32[]{:S(2)}) collective-permute-start(s32[128]{0:T(128)S(1)} %compare_select_fusion.10), channel_id=1, source_target_pairs={{0,96},{16,112},{32,64},{48,80},{64,32},{80,48},{96,0},{112,16},{1... | collective-permute-start | bytes 1544 | tf_op jit(solution)/shard_map/ppermute | solution.py:61
  17.0 4.2 %collective-permute-start.7 = (s32[128]{0:T(128)S(1)}, s32[128]{0:T(128)S(1)}, u32[]{:S(2)}, u32[]{:S(2)}) collective-permute-start(s32[128]{0:T(128)S(1)} %compare_select_fusion.10), channel_id=1, source_target_pairs={{0,112},{16,96},{32,80},{48,64},{64,48},{80,32},{96,16},{112,0},{1... | collective-permute-start | bytes 1544 | tf_op jit(solution)/shard_map/ppermute | solution.py:61
  22.3 9.0 %collective-permute-start.11 = (f32[4,8,1024]{2,1,0:T(8,128)S(1)}, f32[4,8,1024]{2,1,0:T(8,128)S(1)}, u32[]{:S(2)}, u32[]{:S(2)}) collective-permute-start(f32[4,8,1024]{2,1,0:T(8,128)S(1)} %get-tuple-element.54), channel_id=1, source_target_pairs={{0,3},{1,0},{2,1},{3,2},{4,7},{5,4},{6,5},{7,6},{8,11},{9,8},{10,9... | collective-permute-start | bytes 393224 | tf_op jit(solution)/shard_map/ppermute | solution.py:56
  25.3 7.9 %collective-permute-start.12 = (f32[4,8,1024]{2,1,0:T(8,128)S(1)}, f32[4,8,1024]{2,1,0:T(8,128)S(1)}, u32[]{:S(2)}, u32[]{:S(2)}) collective-permute-start(f32[4,8,1024]{2,1,0:T(8,128)S(1)} %get-tuple-element.54), channel_id=1, source_target_pairs={{0,2},{1,3},{2,0},{3,1},{4,6},{5,7},{6,4},{7,5},{8,10},{9,11},{10,... | collective-permute-start | bytes 393224 | tf_op jit(solution)/shard_map/ppermute | solution.py:56
  26.0 9.0 %collective-permute-start.13 = (f32[4,8,1024]{2,1,0:T(8,128)S(1)}, f32[4,8,1024]{2,1,0:T(8,128)S(1)}, u32[]{:S(2)}, u32[]{:S(2)}) collective-permute-start(f32[4,8,1024]{2,1,0:T(8,128)S(1)} %get-tuple-element.54), channel_id=1, source_target_pairs={{0,1},{1,2},{2,3},{3,0},{4,5},{5,6},{6,7},{7,4},{8,9},{9,10},{10,1... | collective-permute-start | bytes 393224 | tf_op jit(solution)/shard_map/ppermute | solution.py:56
  27.0 8.0 %collective-permute-start.8 = (f32[5,8,1024]{2,1,0:T(8,128)S(1)}, f32[5,8,1024]{2,1,0:T(8,128)S(1)}, u32[]{:S(2)}, u32[]{:S(2)}) collective-permute-start(f32[5,8,1024]{2,1,0:T(8,128)S(1)} %get-tuple-element.57), channel_id=1, source_target_pairs={{0,12},{4,0},{8,4},{12,8},{1,13},{5,1},{9,5},{13,9},{2,14},{6,2},{... | collective-permute-start | bytes 491528 | tf_op jit(solution)/shard_map/ppermute | solution.py:56
  27.1 8.5 %collective-permute-start.9 = (f32[5,8,1024]{2,1,0:T(8,128)S(1)}, f32[5,8,1024]{2,1,0:T(8,128)S(1)}, u32[]{:S(2)}, u32[]{:S(2)}) collective-permute-start(f32[5,8,1024]{2,1,0:T(8,128)S(1)} %get-tuple-element.57), channel_id=1, source_target_pairs={{0,8},{4,12},{8,0},{12,4},{1,9},{5,13},{9,1},{13,5},{2,10},{6,14},... | collective-permute-start | bytes 491528 | tf_op jit(solution)/shard_map/ppermute | solution.py:56
  31.2 7.2 %collective-permute-start.10 = (f32[5,8,1024]{2,1,0:T(8,128)S(1)}, f32[5,8,1024]{2,1,0:T(8,128)S(1)}, u32[]{:S(2)}, u32[]{:S(2)}) collective-permute-start(f32[5,8,1024]{2,1,0:T(8,128)S(1)} %get-tuple-element.57), channel_id=1, source_target_pairs={{0,4},{4,8},{8,12},{12,0},{1,5},{5,9},{9,13},{13,1},{2,6},{6,10},{... | collective-permute-start | bytes 491528 | tf_op jit(solution)/shard_map/ppermute | solution.py:56
  35.0 18.8 %copy-start.5 = (f32[4,4,8,1024]{3,2,1,0:T(8,128)}, f32[4,4,8,1024]{3,2,1,0:T(8,128)S(1)}, u32[]{:S(2)}) copy-start(f32[4,4,8,1024]{3,2,1,0:T(8,128)S(1)} %pad_maximum_fusion.1.refs_5_) | copy-start | bytes 1572868
  38.5 15.3 %copy-start.4 = (f32[4,5,8,1024]{3,2,1,0:T(8,128)}, f32[4,5,8,1024]{3,2,1,0:T(8,128)S(1)}, u32[]{:S(2)}) copy-start(f32[4,5,8,1024]{3,2,1,0:T(8,128)S(1)} %pad_maximum_fusion.refs_0_) | copy-start | bytes 1966084
  38.5 16.4 %collective-permute-start.14 = (f32[4,5,8,1024]{3,2,1,0:T(8,128)S(1)}, f32[4,5,8,1024]{3,2,1,0:T(8,128)S(1)}, u32[]{:S(2)}, u32[]{:S(2)}) collective-permute-start(f32[4,5,8,1024]{3,2,1,0:T(8,128)S(1)} %pad_maximum_fusion.refs_0_), channel_id=1, source_target_pairs={{0,3},{1,0},{2,1},{3,2},{4,7},{5,4},{6,5},{7,6},{8,11},{9,8},{10,9... | collective-permute-start | bytes 1966088 | tf_op jit(solution)/shard_map/ppermute | solution.py:56
  41.7 16.0 %collective-permute-start.15 = (f32[4,5,8,1024]{3,2,1,0:T(8,128)S(1)}, f32[4,5,8,1024]{3,2,1,0:T(8,128)S(1)}, u32[]{:S(2)}, u32[]{:S(2)}) collective-permute-start(f32[4,5,8,1024]{3,2,1,0:T(8,128)S(1)} %pad_maximum_fusion.refs_0_), channel_id=1, source_target_pairs={{0,1},{1,2},{2,3},{3,0},{4,5},{5,6},{6,7},{7,4},{8,9},{9,10},{10,1... | collective-permute-start | bytes 1966088 | tf_op jit(solution)/shard_map/ppermute | solution.py:56
  41.7 12.1 %collective-permute-start.16 = (f32[4,4,8,1024]{3,2,1,0:T(8,128)S(1)}, f32[4,4,8,1024]{3,2,1,0:T(8,128)S(1)}, u32[]{:S(2)}, u32[]{:S(2)}) collective-permute-start(f32[4,4,8,1024]{3,2,1,0:T(8,128)S(1)} %pad_maximum_fusion.1.refs_5_), channel_id=1, source_target_pairs={{0,12},{4,0},{8,4},{12,8},{1,13},{5,1},{9,5},{13,9},{2,14},{6,2},{... | collective-permute-start | bytes 1572872 | tf_op jit(solution)/shard_map/ppermute | solution.py:56
  41.7 13.2 %collective-permute-start.17 = (f32[4,4,8,1024]{3,2,1,0:T(8,128)S(1)}, f32[4,4,8,1024]{3,2,1,0:T(8,128)S(1)}, u32[]{:S(2)}, u32[]{:S(2)}) collective-permute-start(f32[4,4,8,1024]{3,2,1,0:T(8,128)S(1)} %pad_maximum_fusion.1.refs_5_), channel_id=1, source_target_pairs={{0,4},{4,8},{8,12},{12,0},{1,5},{5,9},{9,13},{13,1},{2,6},{6,10},{... | collective-permute-start | bytes 1572872 | tf_op jit(solution)/shard_map/ppermute | solution.py:56
  53.8 11.4 %copy-start.8 = (f32[4,4,8,1024]{3,2,1,0:T(8,128)}, f32[4,4,8,1024]{3,2,1,0:T(8,128)S(1)}, u32[]{:S(2)}) copy-start(f32[4,4,8,1024]{3,2,1,0:T(8,128)S(1)} %collective-permute-done.16.refs_6_) | copy-start | bytes 1572868
  54.9 10.2 %copy-start.9 = (f32[4,4,8,1024]{3,2,1,0:T(8,128)}, f32[4,4,8,1024]{3,2,1,0:T(8,128)S(1)}, u32[]{:S(2)}) copy-start(f32[4,4,8,1024]{3,2,1,0:T(8,128)S(1)} %collective-permute-done.17.refs_9_) | copy-start | bytes 1572868
  54.9 10.2 %copy-start.6 = (f32[4,5,8,1024]{3,2,1,0:T(8,128)}, f32[4,5,8,1024]{3,2,1,0:T(8,128)S(1)}, u32[]{:S(2)}) copy-start(f32[4,5,8,1024]{3,2,1,0:T(8,128)S(1)} %collective-permute-done.14.refs_1_) | copy-start | bytes 1966084
  57.7 7.4 %copy-start.7 = (f32[4,5,8,1024]{3,2,1,0:T(8,128)}, f32[4,5,8,1024]{3,2,1,0:T(8,128)S(1)}, u32[]{:S(2)}) copy-start(f32[4,5,8,1024]{3,2,1,0:T(8,128)S(1)} %collective-permute-done.15.refs_4_) | copy-start | bytes 1966084
  57.7 13.6 %collective-permute-start.18 = (f32[2,5,8,1024]{3,2,1,0:T(8,128)S(1)}, f32[2,5,8,1024]{3,2,1,0:T(8,128)}, u32[]{:S(2)}, u32[]{:S(2)}) collective-permute-start(f32[2,5,8,1024]{3,2,1,0:T(8,128)S(1)} %slice.54), channel_id=1, source_target_pairs={{0,1},{1,2},{2,3},{3,0},{4,5},{5,6},{6,7},{7,4},{8,9},{9,10},{10,1... | collective-permute-start | bytes 983048 | tf_op jit(solution)/shard_map/ppermute | solution.py:56
  57.8 13.5 %collective-permute-start.19 = (f32[2,5,8,1024]{3,2,1,0:T(8,128)S(1)}, f32[2,5,8,1024]{3,2,1,0:T(8,128)}, u32[]{:S(2)}, u32[]{:S(2)}) collective-permute-start(f32[2,5,8,1024]{3,2,1,0:T(8,128)S(1)} %slice.55), channel_id=1, source_target_pairs={{0,3},{1,0},{2,1},{3,2},{4,7},{5,4},{6,5},{7,6},{8,11},{9,8},{10,9... | collective-permute-start | bytes 983048 | tf_op jit(solution)/shard_map/ppermute | solution.py:56
  61.2 10.1 %collective-permute-start.20 = (f32[2,4,8,1024]{3,2,1,0:T(8,128)S(1)}, f32[2,4,8,1024]{3,2,1,0:T(8,128)}, u32[]{:S(2)}, u32[]{:S(2)}) collective-permute-start(f32[2,4,8,1024]{3,2,1,0:T(8,128)S(1)} %slice.56), channel_id=1, source_target_pairs={{0,4},{4,8},{8,12},{12,0},{1,5},{5,9},{9,13},{13,1},{2,6},{6,10},{... | collective-permute-start | bytes 786440 | tf_op jit(solution)/shard_map/ppermute | solution.py:56
  61.3 10.0 %collective-permute-start.21 = (f32[2,4,8,1024]{3,2,1,0:T(8,128)S(1)}, f32[2,4,8,1024]{3,2,1,0:T(8,128)}, u32[]{:S(2)}, u32[]{:S(2)}) collective-permute-start(f32[2,4,8,1024]{3,2,1,0:T(8,128)S(1)} %slice.57), channel_id=1, source_target_pairs={{0,12},{4,0},{8,4},{12,8},{1,13},{5,1},{9,5},{13,9},{2,14},{6,2},{... | collective-permute-start | bytes 786440 | tf_op jit(solution)/shard_map/ppermute | solution.py:56
  65.1 108.2 %all-to-all-start = ((f32[128,128,128]{2,1,0:T(8,128)}), f32[128,128,128]{2,1,0:T(8,128)}, u32[]{:S(2)}, u32[]{:S(2)}) async-start(f32[128,128,128]{2,1,0:T(8,128)} %turn.1), calls=%async_computation | async-start | bytes 16777216 | tf_op jit(solution)/shard_map/all_to_all | solution.py:507
  193.3 39.0 %copy-start.3 = (s32[3]{0:T(128)S(1)}, s32[3]{0:T(128)}, u32[]{:S(2)}) copy-start(s32[3]{0:T(128)} %pad_add_fusion.position) | copy-start | bytes 40
  193.3 39.0 %all-to-all-start.1 = ((f32[32,136,128]{2,1,0:T(8,128)}), f32[32,136,128]{2,1,0:T(8,128)S(1)}, u32[]{:S(2)}, u32[]{:S(2)}) async-start(f32[32,136,128]{2,1,0:T(8,128)} %bitcast.97), calls=%async_computation.1 | async-start | bytes 4456448 | tf_op jit(solution)/shard_map/all_to_all | solution.py:507
  203.5 15.4 %collective-permute-start.22 = (f32[2,32,1024]{2,1,0:T(8,128)S(1)}, f32[2,32,1024]{2,1,0:T(8,128)S(1)}, u32[]{:S(2)}, u32[]{:S(2)}) collective-permute-start(f32[2,32,1024]{2,1,0:T(8,128)S(1)} %get-tuple-element.51), channel_id=1, source_target_pairs={{0,4},{4,8},{8,12},{12,0},{1,5},{5,9},{9,13},{13,1},{2,6},{6,10},{... | collective-permute-start | bytes 786440 | tf_op jit(solution)/shard_map/ppermute | solution.py:56
  203.5 15.3 %collective-permute-start.23 = (f32[2,32,1024]{2,1,0:T(8,128)S(1)}, f32[2,32,1024]{2,1,0:T(8,128)S(1)}, u32[]{:S(2)}, u32[]{:S(2)}) collective-permute-start(f32[2,32,1024]{2,1,0:T(8,128)S(1)} %get-tuple-element.50), channel_id=1, source_target_pairs={{0,8},{4,12},{8,0},{12,4},{1,9},{5,13},{9,1},{13,5},{2,10},{6,14},... | collective-permute-start | bytes 786440 | tf_op jit(solution)/shard_map/ppermute | solution.py:56
  205.3 14.2 %collective-permute-start.24 = (f32[2,32,1024]{2,1,0:T(8,128)S(1)}, f32[2,32,1024]{2,1,0:T(8,128)S(1)}, u32[]{:S(2)}, u32[]{:S(2)}) collective-permute-start(f32[2,32,1024]{2,1,0:T(8,128)S(1)} %get-tuple-element.49), channel_id=1, source_target_pairs={{0,12},{4,0},{8,4},{12,8},{1,13},{5,1},{9,5},{13,9},{2,14},{6,2},{... | collective-permute-start | bytes 786440 | tf_op jit(solution)/shard_map/ppermute | solution.py:56
  232.3 1.7 copy-start
  236.1 20.3 %collective-permute-start.26 = (f32[6,32,1024]{2,1,0:T(8,128)S(1)}, f32[6,32,1024]{2,1,0:T(8,128)S(1)}, u32[]{:S(2)}, u32[]{:S(2)}) collective-permute-start(f32[6,32,1024]{2,1,0:T(8,128)S(1)} %solve.1.refs_0_.refs_5_), channel_id=1, source_target_pairs={{0,4},{4,8},{8,12},{12,0},{1,5},{5,9},{9,13},{13,1},{2,6},{6,10},{... | collective-permute-start | bytes 2359304 | tf_op jit(solution)/shard_map/ppermute | solution.py:56
  236.2 20.4 %collective-permute-start.25 = (f32[6,32,1024]{2,1,0:T(8,128)S(1)}, f32[6,32,1024]{2,1,0:T(8,128)S(1)}, u32[]{:S(2)}, u32[]{:S(2)}) collective-permute-start(f32[6,32,1024]{2,1,0:T(8,128)S(1)} %solve.1.refs_0_.refs_5_), channel_id=1, source_target_pairs={{0,12},{4,0},{8,4},{12,8},{1,13},{5,1},{9,5},{13,9},{2,14},{6,2},{... | collective-permute-start | bytes 2359304 | tf_op jit(solution)/shard_map/ppermute | solution.py:56
  239.4 20.5 %collective-permute-start.30 = (f32[6,32,1024]{2,1,0:T(8,128)S(1)}, f32[6,32,1024]{2,1,0:T(8,128)S(1)}, u32[]{:S(2)}, u32[]{:S(2)}) collective-permute-start(f32[6,32,1024]{2,1,0:T(8,128)S(1)} %solve.1.refs_0_.refs_5_), channel_id=1, source_target_pairs={{0,1},{1,2},{2,3},{3,0},{4,5},{5,6},{6,7},{7,4},{8,9},{9,10},{10,1... | collective-permute-start | bytes 2359304 | tf_op jit(solution)/shard_map/ppermute | solution.py:56
  239.4 20.6 %collective-permute-start.29 = (f32[6,32,1024]{2,1,0:T(8,128)S(1)}, f32[6,32,1024]{2,1,0:T(8,128)S(1)}, u32[]{:S(2)}, u32[]{:S(2)}) collective-permute-start(f32[6,32,1024]{2,1,0:T(8,128)S(1)} %solve.1.refs_0_.refs_5_), channel_id=1, source_target_pairs={{0,3},{1,0},{2,1},{3,2},{4,7},{5,4},{6,5},{7,6},{8,11},{9,8},{10,9... | collective-permute-start | bytes 2359304 | tf_op jit(solution)/shard_map/ppermute | solution.py:56
  256.5 11.0 %collective-permute-start.27 = (f32[3,32,1024]{2,1,0:T(8,128)S(1)}, f32[3,32,1024]{2,1,0:T(8,128)S(1)}, u32[]{:S(2)}, u32[]{:S(2)}) collective-permute-start(f32[3,32,1024]{2,1,0:T(8,128)S(1)} %slice.65), channel_id=1, source_target_pairs={{0,4},{4,8},{8,12},{12,0},{1,5},{5,9},{9,13},{13,1},{2,6},{6,10},{... | collective-permute-start | bytes 1179656 | tf_op jit(solution)/shard_map/ppermute | solution.py:56
  256.6 10.9 %collective-permute-start.28 = (f32[3,32,1024]{2,1,0:T(8,128)S(1)}, f32[3,32,1024]{2,1,0:T(8,128)S(1)}, u32[]{:S(2)}, u32[]{:S(2)}) collective-permute-start(f32[3,32,1024]{2,1,0:T(8,128)S(1)} %slice.66), channel_id=1, source_target_pairs={{0,12},{4,0},{8,4},{12,8},{1,13},{5,1},{9,5},{13,9},{2,14},{6,2},{... | collective-permute-start | bytes 1179656 | tf_op jit(solution)/shard_map/ppermute | solution.py:56
  259.9 10.4 %collective-permute-start.31 = (f32[3,32,1024]{2,1,0:T(8,128)S(1)}, f32[3,32,1024]{2,1,0:T(8,128)S(1)}, u32[]{:S(2)}, u32[]{:S(2)}) collective-permute-start(f32[3,32,1024]{2,1,0:T(8,128)S(1)} %slice.67), channel_id=1, source_target_pairs={{0,1},{1,2},{2,3},{3,0},{4,5},{5,6},{6,7},{7,4},{8,9},{9,10},{10,1... | collective-permute-start | bytes 1179656 | tf_op jit(solution)/shard_map/ppermute | solution.py:56
  260.1 10.3 %collective-permute-start.32 = (f32[3,32,1024]{2,1,0:T(8,128)S(1)}, f32[3,32,1024]{2,1,0:T(8,128)S(1)}, u32[]{:S(2)}, u32[]{:S(2)}) collective-permute-start(f32[3,32,1024]{2,1,0:T(8,128)S(1)} %slice.68), channel_id=1, source_target_pairs={{0,3},{1,0},{2,1},{3,2},{4,7},{5,4},{6,5},{7,6},{8,11},{9,8},{10,9... | collective-permute-start | bytes 1179656 | tf_op jit(solution)/shard_map/ppermute | solution.py:56
  274.7 1.4 copy-start.1
  276.1 4.9 %copy-start.2 = (f32[128,1024]{1,0:T(8,128)S(1)}, f32[128,1024]{1,0:T(8,128)}, u32[]{:S(2)}) copy-start(f32[128,1024]{1,0:T(8,128)} %get-tuple-element.42.lead_rows) | copy-start | bytes 1572868
  276.1 32.3 %all-to-all-start.2 = ((f32[16,8,32,128]{3,2,1,0:T(8,128)}), f32[16,8,32,128]{3,2,1,0:T(8,128)}, u32[]{:S(2)}, u32[]{:S(2)}) async-start(f32[16,8,32,128]{3,2,1,0:T(8,128)} %copy-done.1), calls=%async_computation.2 | async-start | bytes 4194304 | tf_op jit(solution)/shard_map/all_to_all | solution.py:507

commit v5 on v4

--- a/solution.py
+++ b/solution.py
@@ -141,9 +141,10 @@
             acc[...] = jnp.zeros_like(acc)
 
     def body(q, carry):
-        source = (q // FRONTS) * FRONTS + jnp.bitwise_xor(q % FRONTS, position[2])
+        line, k = q // FRONTS, q % FRONTS
+        source = line * FRONTS + jnp.bitwise_xor(k, position[2])
         base = pl.multiple_of(source * TILES, TILES)
-        labels = (pl.program_id(0) * sources + q) * TILES
+        labels = (k * GRID + pl.program_id(0) * (sources // FRONTS) + line) * TILES
         for first in range(0, TILES, ACCS):
             at = [bins[labels + first + m] for m in range(ACCS)]
             rows = [x[pl.ds(base + first + m, 1), :] for m in range(ACCS)]
@@ -222,7 +223,7 @@
     for copy in copies:
         copy.wait()
     for g in range(GRID):
-        labels[g : g + 1, :] = labels_in[g, 0:1, :].astype(jnp.int32)
+        labels[g : g + 1, :] = labels_in[g, 0:1, :TILES].astype(jnp.int32)
     sub = lax.broadcasted_iota(jnp.int32, (SUB, 1), 0)
     row = lax.broadcasted_iota(jnp.int32, (BLOCK, BLOCK), 0)
     col = lax.broadcasted_iota(jnp.int32, (BLOCK, BLOCK), 1)
@@ -289,7 +290,7 @@
         out_shape=[
             jax.ShapeDtypeStruct((BLOCK, LEAD), jnp.float32),
             jax.ShapeDtypeStruct((2, WIDE, PACKED[-1]), jnp.bfloat16),
-            jax.ShapeDtypeStruct((GRID, LEAD), jnp.int32),
+            jax.ShapeDtypeStruct((GRID, TILES), jnp.int32),
         ],
         in_specs=[SMEM] + [ANY] * 10,
         out_specs=[VMEM] * 3,
@@ -516,8 +517,7 @@
     other = lax.ppermute(lead[half:], "x", [(0, 2), (1, 3)])
     lead = jnp.where(x < 2, lead[:half], other).reshape(SLABS // 2, SUB, LEAD)
     bins = destination_bins(tile_owner[0, :, 0], tile_rows[0], tile_picks[0])
-    bins = gather_front(bins).reshape(1, 1, LEAD).astype(jnp.float32)
-    bins = jnp.pad(bins, ((0, 0), (0, SUB - 1), (0, 0)))
+    bins = jnp.pad(bins.astype(jnp.float32).reshape(1, 1, TILES), ((0, 0), (0, SUB - 1), (0, LEAD - TILES)))
     lead, bins, tiles = lax.optimization_barrier((lead, bins, child_tiles))
     half = SLABS // 4
     lines, near, far, tiles = gather_lines(
@@ -532,7 +532,8 @@
     ]
     panel = [part if n == 0 else shift(part, "x", n) for n, part in enumerate(panel)]
     lead_rows, inverse, bins = factor(position, lead)
-    sums = combine(position, bins.reshape(-1), rows).reshape(SLICE, SLOTS, BLOCK)
+    bins = gather_front(bins).reshape(-1)
+    sums = combine(position, bins, rows).reshape(SLICE, SLOTS, BLOCK)
     sums = across(sums, ("y", "front")).reshape(-1, BLOCK)
     solved = solve(position, panel, sums, inverse)
     near = [ring_near(solved, axis) for axis in ("x", "y")]

time: 313 us -> 303 us (0.968)
  waiting for transfers between devices: 101 us -> 86.6 us
  starting transfers between devices: 70.8 us -> 76.7 us
    all_to_all x3, waiting for transfers between devices: 51.8 us -> 39.8 us  [across(): return lax.all_to_all(values, axes, split_axis=0, concat_axis=0)]
    ppermute x25, waiting for transfers between devices: 45.3 us -> 39.4 us  [shift(): lax.ppermute(block, axis, [(i, (i + step) % SIDE) for i in range(SIDE)])]
    ppermute x25, starting transfers between devices: 36.8 us -> 41.5 us  [shift(): lax.ppermute(block, axis, [(i, (i + step) % SIDE) for i in range(SIDE)])]
    ppermute x1, waiting for transfers between devices: 0.01 us -> 4.67 us  [local(): other = lax.ppermute(lead[half:], 'x', [(0, 2), (1, 3)])]
  transfers between devices with their start and end apart: 36 -> 36, of which waited for: 18 -> 18; matrix products, arithmetic and copies ran while one was open for 2% -> 1% of each run, Pallas kernels for 32% -> 33%
where the time goes in v5:
time: 303 us
  Pallas kernels  130 us (43%)
  waiting for transfers between devices  86.6 us (29%)
  starting transfers between devices  76.7 us (25%)
  local copies, waits for them, and re-layouts  6.46 us (2%)
    pallas_call x1, Pallas kernels, factor(): pl.pallas_call(factor_kernel, out_shape=[jax.ShapeDtypeStruct((BLOCK, LEA...  86.2 us
    ppermute x25, starting transfers between devices, shift(): lax.ppermute(block, axis, [(i, (i + step) % SIDE) for i in range(SIDE)])  41.5 us
    all_to_all x3, waiting for transfers between devices, across(): return lax.all_to_all(values, axes, split_axis=0, concat_axis=0)  39.8 us
    ppermute x25, waiting for transfers between devices, shift(): lax.ppermute(block, axis, [(i, (i + step) % SIDE) for i in range(SIDE)])  39.4 us
    all_to_all x3, starting transfers between devices, across(): return lax.all_to_all(values, axes, split_axis=0, concat_axis=0)  20.2 us
    pallas_call x1, Pallas kernels, combine(): pl.pallas_call(combine_kernel, grid=(steps,), out_shape=jax.ShapeDtypeStr...  20 us
    pallas_call x1, Pallas kernels, turn(): pl.pallas_call(turn_kernel, grid=(TILES // step,), out_shape=jax.ShapeDty...  10.1 us
    ppermute x7, starting transfers between devices, gather_front(): lax.ppermute(values, 'front', [(i, i ^ k) for i in range(FRONTS)])  10 us
  transfers between devices with their start and end apart: 36, of which 18 were waited for; matrix products, arithmetic and copies ran while one was open for 1% of the time, Pallas kernels for 33%

profile of v5, /device:TPU:0, one launch (start us, length us, event | category | flops | bytes accessed | tf_op | source)
XLA Modules:
  0.0 302.5 jit_solution(14825057557708995974)
XLA Ops:
  1.0 5.0 %collective-permute-start = (f32[64,1024]{1,0:T(8,128)S(1)}, f32[64,1024]{1,0:T(8,128)S(1)}, u32[]{:S(2)}, u32[]{:S(2)}) collective-permute-start(f32[64,1024]{1,0:T(8,128)S(1)} %slice_bitcast_fusion), channel_id=1, source_target_pairs={{0,8},{4,12},{1,9},{5,13},{2,10},{6,14},{3,11},{7,15},{16,24},{20,... | collective-permute-start | bytes 786440 | tf_op jit(solution)/shard_map/ppermute | solution.py:517
  6.9 4.7 %collective-permute-done = f32[64,1024]{1,0:T(8,128)S(1)} collective-permute-done((f32[64,1024]{1,0:T(8,128)S(1)}, f32[64,1024]{1,0:T(8,128)S(1)}, u32[]{:S(2)}, u32[]{:S(2)}) %collective-permute-start) | collective-permute-done | bytes 262176 | tf_op jit(solution)/shard_map/ppermute | solution.py:517
  12.6 3.1 %collective-permute-start.4 = (f32[4,8,1024]{2,1,0:T(8,128)S(1)}, f32[4,8,1024]{2,1,0:T(8,128)S(1)}, u32[]{:S(2)}, u32[]{:S(2)}) collective-permute-start(f32[4,8,1024]{2,1,0:T(8,128)S(1)} %get-tuple-element.54), channel_id=1, source_target_pairs={{0,3},{1,0},{2,1},{3,2},{4,7},{5,4},{6,5},{7,6},{8,11},{9,8},{10,9... | collective-permute-start | bytes 393224 | tf_op jit(solution)/shard_map/ppermute | solution.py:56
  17.3 3.8 %collective-permute-start.1 = (f32[5,8,1024]{2,1,0:T(8,128)S(1)}, f32[5,8,1024]{2,1,0:T(8,128)S(1)}, u32[]{:S(2)}, u32[]{:S(2)}) collective-permute-start(f32[5,8,1024]{2,1,0:T(8,128)S(1)} %get-tuple-element.57), channel_id=1, source_target_pairs={{0,12},{4,0},{8,4},{12,8},{1,13},{5,1},{9,5},{13,9},{2,14},{6,2},{... | collective-permute-start | bytes 491528 | tf_op jit(solution)/shard_map/ppermute | solution.py:56
  21.4 1.3 collective-permute-start.3
  22.8 1.3 collective-permute-done.6
  24.1 2.3 collective-permute-done.1
  26.4 2.0 collective-permute-done.2
  28.4 1.6 collective-permute-done.3
  30.1 2.4 collective-permute-start.7
  32.5 3.2 %collective-permute-start.9 = (f32[4,4,8,1024]{3,2,1,0:T(8,128)S(1)}, f32[4,4,8,1024]{3,2,1,0:T(8,128)S(1)}, u32[]{:S(2)}, u32[]{:S(2)}) collective-permute-start(f32[4,4,8,1024]{3,2,1,0:T(8,128)S(1)} %pad_maximum_fusion.1.refs_5_), channel_id=1, source_target_pairs={{0,12},{4,0},{8,4},{12,8},{1,13},{5,1},{9,5},{13,9},{2,14},{6,2},{... | collective-permute-start | bytes 1572872 | tf_op jit(solution)/shard_map/ppermute | solution.py:56
  35.7 10.1 %turn.1 = f32[128,128,128]{2,1,0:T(8,128)} custom-call(f32[16384,128]{1,0:T(8,128)} %bitcast.85), custom_call_target="tpu_custom_call" | custom-call | bytes 16777216 | tf_op jit(solution)/shard_map/turn/pallas_call | solution.py:123
  45.9 1.0 collective-permute-done.8.refs_4_
  47.7 2.7 collective-permute-start.12
  50.5 3.3 %collective-permute-start.14 = (f32[2,4,8,1024]{3,2,1,0:T(8,128)S(1)}, f32[2,4,8,1024]{3,2,1,0:T(8,128)}, u32[]{:S(2)}, u32[]{:S(2)}) collective-permute-start(f32[2,4,8,1024]{3,2,1,0:T(8,128)S(1)} %slice.57), channel_id=1, source_target_pairs={{0,12},{4,0},{8,4},{12,8},{1,13},{5,1},{9,5},{13,9},{2,14},{6,2},{... | collective-permute-start | bytes 786440 | tf_op jit(solution)/shard_map/ppermute | solution.py:56
  54.4 7.0 %all-to-all-start = ((f32[128,128,128]{2,1,0:T(8,128)}), f32[128,128,128]{2,1,0:T(8,128)}, u32[]{:S(2)}, u32[]{:S(2)}) async-start(f32[128,128,128]{2,1,0:T(8,128)} %turn.1), calls=%async_computation | async-start | bytes 16777216 | tf_op jit(solution)/shard_map/all_to_all | solution.py:508
  61.4 86.2 %factor.1 = (f32[128,1024]{1,0:T(8,128)}, bf16[2,256,2560]{2,1,0:T(8,128)(2,1)}, s32[16,128]{1,0:T(8,128)}) custom-call(s32[3]{0:T(128)} %pad_add_fusion.position, f32[4,5,8,1024]{3,2,1,0:T(8,128)} %copy-done.4, f32[4,5,8,1024]{3,2,1,0:T(8,128)} %copy-done.6, f32[2,5,8,1024]{3,2,1,0:T(8,128)} %collective-permute-done.11.refs_2_, ...), custom_call_target="tpu_custom_call" | custom-call | flops 120000004096 | bytes 20971520 | tf_op jit(solution)/shard_map/factor/pallas_call | solution.py:288
  148.4 1.2 collective-permute-start.19
  150.3 2.8 collective-permute-start.21
  153.4 2.9 collective-permute-start.23
  156.7 2.0 collective-permute-start.24
  158.9 2.3 collective-permute-done.24
  161.2 2.6 all-to-all-done
  163.8 20.0 %combine.1 = f32[4352,128]{1,0:T(8,128)} custom-call(s32[3]{0:T(128)} %pad_add_fusion.position, s32[16384]{0:T(1024)} %bitcast.98, f32[16384,128]{1,0:T(8,128)} %bitcast.33.x), custom_call_target="tpu_custom_call" | custom-call | flops 20000000000 | bytes 20971520 | tf_op jit(solution)/shard_map/combine/pallas_call | solution.py:174
  183.8 8.1 %all-to-all-start.1 = ((f32[32,136,128]{2,1,0:T(8,128)}), f32[32,136,128]{2,1,0:T(8,128)S(1)}, u32[]{:S(2)}, u32[]{:S(2)}) async-start(f32[32,136,128]{2,1,0:T(8,128)} %bitcast.91), calls=%async_computation.1 | async-start | bytes 4456448 | tf_op jit(solution)/shard_map/all_to_all | solution.py:508
  192.0 1.3 slice.58
  193.4 1.6 collective-permute-start.15
  195.0 2.0 collective-permute-start.16
  197.0 2.2 collective-permute-start.17
  199.2 4.4 %collective-permute-done.15.part1 = f32[2,32,1024]{2,1,0:T(8,128)S(1)} collective-permute-done((f32[2,32,1024]{2,1,0:T(8,128)S(1)}, f32[2,32,1024]{2,1,0:T(8,128)S(1)}, u32[]{:S(2)}, u32[]{:S(2)}) %collective-permute-start.15) | collective-permute-done | bytes 262176 | tf_op jit(solution)/shard_map/ppermute | solution.py:56
  203.6 5.5 %collective-permute-done.16.part2 = f32[2,32,1024]{2,1,0:T(8,128)S(1)} collective-permute-done((f32[2,32,1024]{2,1,0:T(8,128)S(1)}, f32[2,32,1024]{2,1,0:T(8,128)S(1)}, u32[]{:S(2)}, u32[]{:S(2)}) %collective-permute-start.16) | collective-permute-done | bytes 262176 | tf_op jit(solution)/shard_map/ppermute | solution.py:56
  209.4 12.9 %all-to-all-done.1 = f32[32,136,128]{2,1,0:T(8,128)S(1)} async-done(((f32[32,136,128]{2,1,0:T(8,128)}), f32[32,136,128]{2,1,0:T(8,128)S(1)}, u32[]{:S(2)}, u32[]{:S(2)}) %all-to-all-start.1) | async-done | bytes 2228256 | tf_op jit(solution)/shard_map/all_to_all | solution.py:508
  222.3 1.7 copy-done
  224.0 2.0 solve.1.refs_0_.refs_5_
  226.1 1.6 collective-permute-start.26
  227.6 1.7 collective-permute-start.25
  229.4 3.2 %collective-permute-start.29 = (f32[6,32,1024]{2,1,0:T(8,128)S(1)}, f32[6,32,1024]{2,1,0:T(8,128)S(1)}, u32[]{:S(2)}, u32[]{:S(2)}) collective-permute-start(f32[6,32,1024]{2,1,0:T(8,128)S(1)} %solve.1.refs_0_.refs_5_), channel_id=1, source_target_pairs={{0,3},{1,0},{2,1},{3,2},{4,7},{5,4},{6,5},{7,6},{8,11},{9,8},{10,9... | collective-permute-start | bytes 2359304 | tf_op jit(solution)/shard_map/ppermute | solution.py:56
  232.6 13.8 %collective-permute-done.26.refs_4_ = f32[6,32,1024]{2,1,0:T(8,128)S(1)} collective-permute-done((f32[6,32,1024]{2,1,0:T(8,128)S(1)}, f32[6,32,1024]{2,1,0:T(8,128)S(1)}, u32[]{:S(2)}, u32[]{:S(2)}) %collective-permute-start.26) | collective-permute-done | bytes 786464 | tf_op jit(solution)/shard_map/ppermute | solution.py:56
  246.8 3.0 %collective-permute-start.28 = (f32[3,32,1024]{2,1,0:T(8,128)S(1)}, f32[3,32,1024]{2,1,0:T(8,128)S(1)}, u32[]{:S(2)}, u32[]{:S(2)}) collective-permute-start(f32[3,32,1024]{2,1,0:T(8,128)S(1)} %slice.66), channel_id=1, source_target_pairs={{0,12},{4,0},{8,4},{12,8},{1,13},{5,1},{9,5},{13,9},{2,14},{6,2},{... | collective-permute-start | bytes 1179656 | tf_op jit(solution)/shard_map/ppermute | solution.py:56
  250.0 3.3 %collective-permute-start.32 = (f32[3,32,1024]{2,1,0:T(8,128)S(1)}, f32[3,32,1024]{2,1,0:T(8,128)S(1)}, u32[]{:S(2)}, u32[]{:S(2)}) collective-permute-start(f32[3,32,1024]{2,1,0:T(8,128)S(1)} %slice.68), channel_id=1, source_target_pairs={{0,3},{1,0},{2,1},{3,2},{4,7},{5,4},{6,5},{7,6},{8,11},{9,8},{10,9... | collective-permute-start | bytes 1179656 | tf_op jit(solution)/shard_map/ppermute | solution.py:56
  253.3 4.2 %collective-permute-done.27.refs_2_ = f32[3,32,1024]{2,1,0:T(8,128)S(1)} collective-permute-done((f32[3,32,1024]{2,1,0:T(8,128)S(1)}, f32[3,32,1024]{2,1,0:T(8,128)S(1)}, u32[]{:S(2)}, u32[]{:S(2)}) %collective-permute-start.27) | collective-permute-done | bytes 393248 | tf_op jit(solution)/shard_map/ppermute | solution.py:56
  257.5 2.9 collective-permute-done.31.refs_7_
  260.3 4.3 %product.1 = (f32[16,8,32,128]{3,2,1,0:T(8,128)S(1)}, f32[2,128,1024]{2,1,0:T(8,128)S(1)}) custom-call(s32[3]{0:T(128)S(1)} %copy-done.3, f32[6,32,1024]{2,1,0:T(8,128)S(1)} %solve.1.refs_0_.refs_5_, f32[6,32,1024]{2,1,0:T(8,128)S(1)} %collective-permute-done.25.refs_1_, f32[3,32,1024]{2,1,0:T(8,128)S(1)} %collective-permute-done.27.refs_2_, ...), custom_call_target="tpu_custom_call" | custom-call | flops 11000000512 | bytes 8388608 | tf_op jit(solution)/shard_map/product/pallas_call | solution.py:399
  264.7 1.4 copy-done.1
  266.0 5.1 %all-to-all-start.2 = ((f32[16,8,32,128]{3,2,1,0:T(8,128)}), f32[16,8,32,128]{3,2,1,0:T(8,128)}, u32[]{:S(2)}, u32[]{:S(2)}) async-start(f32[16,8,32,128]{3,2,1,0:T(8,128)} %copy-done.1), calls=%async_computation.2 | async-start | bytes 4194304 | tf_op jit(solution)/shard_map/all_to_all | solution.py:508
  271.2 2.8 base.1.before
  274.0 24.3 %all-to-all-done.2.change_in = f32[16,8,32,128]{3,2,1,0:T(8,128)} async-done(((f32[16,8,32,128]{3,2,1,0:T(8,128)}), f32[16,8,32,128]{3,2,1,0:T(8,128)}, u32[]{:S(2)}, u32[]{:S(2)}) %all-to-all-start.2) | async-done | bytes 2097184 | tf_op jit(solution)/shard_map/all_to_all | solution.py:508
  298.3 4.0 %finish.1 = f32[2,128,4096]{2,1,0:T(8,128)} custom-call(s32[3]{0:T(128)} %pad_add_fusion.position, f32[2,128,4096]{2,1,0:T(8,128)} %base.1.before, f32[2,128,4096]{2,1,0:T(8,128)} %bitcast.89, f32[16,8,32,128]{3,2,1,0:T(8,128)} %all-to-all-done.2.change_in), custom_call_target="tpu_custom_call", output_to_operand_aliasing={{}: (1, {})} | custom-call | tf_op jit(solution)/shard_map/finish/pallas_call | solution.py:478
  (80 shorter events, 9.8 us)
Async XLA Ops:
  1.0 10.6 %collective-permute-start = (f32[64,1024]{1,0:T(8,128)S(1)}, f32[64,1024]{1,0:T(8,128)S(1)}, u32[]{:S(2)}, u32[]{:S(2)}) collective-permute-start(f32[64,1024]{1,0:T(8,128)S(1)} %slice_bitcast_fusion), channel_id=1, source_target_pairs={{0,8},{4,12},{1,9},{5,13},{2,10},{6,14},{3,11},{7,15},{16,24},{20,... | collective-permute-start | bytes 786440 | tf_op jit(solution)/shard_map/ppermute | solution.py:517
  12.6 8.9 %collective-permute-start.4 = (f32[4,8,1024]{2,1,0:T(8,128)S(1)}, f32[4,8,1024]{2,1,0:T(8,128)S(1)}, u32[]{:S(2)}, u32[]{:S(2)}) collective-permute-start(f32[4,8,1024]{2,1,0:T(8,128)S(1)} %get-tuple-element.54), channel_id=1, source_target_pairs={{0,3},{1,0},{2,1},{3,2},{4,7},{5,4},{6,5},{7,6},{8,11},{9,8},{10,9... | collective-permute-start | bytes 393224 | tf_op jit(solution)/shard_map/ppermute | solution.py:56
  15.6 7.1 %collective-permute-start.5 = (f32[4,8,1024]{2,1,0:T(8,128)S(1)}, f32[4,8,1024]{2,1,0:T(8,128)S(1)}, u32[]{:S(2)}, u32[]{:S(2)}) collective-permute-start(f32[4,8,1024]{2,1,0:T(8,128)S(1)} %get-tuple-element.54), channel_id=1, source_target_pairs={{0,2},{1,3},{2,0},{3,1},{4,6},{5,7},{6,4},{7,5},{8,10},{9,11},{10,... | collective-permute-start | bytes 393224 | tf_op jit(solution)/shard_map/ppermute | solution.py:56
  16.3 7.8 %collective-permute-start.6 = (f32[4,8,1024]{2,1,0:T(8,128)S(1)}, f32[4,8,1024]{2,1,0:T(8,128)S(1)}, u32[]{:S(2)}, u32[]{:S(2)}) collective-permute-start(f32[4,8,1024]{2,1,0:T(8,128)S(1)} %get-tuple-element.54), channel_id=1, source_target_pairs={{0,1},{1,2},{2,3},{3,0},{4,5},{5,6},{6,7},{7,4},{8,9},{9,10},{10,1... | collective-permute-start | bytes 393224 | tf_op jit(solution)/shard_map/ppermute | solution.py:56
  17.3 9.2 %collective-permute-start.1 = (f32[5,8,1024]{2,1,0:T(8,128)S(1)}, f32[5,8,1024]{2,1,0:T(8,128)S(1)}, u32[]{:S(2)}, u32[]{:S(2)}) collective-permute-start(f32[5,8,1024]{2,1,0:T(8,128)S(1)} %get-tuple-element.57), channel_id=1, source_target_pairs={{0,12},{4,0},{8,4},{12,8},{1,13},{5,1},{9,5},{13,9},{2,14},{6,2},{... | collective-permute-start | bytes 491528 | tf_op jit(solution)/shard_map/ppermute | solution.py:56
  21.1 7.3 %collective-permute-start.2 = (f32[5,8,1024]{2,1,0:T(8,128)S(1)}, f32[5,8,1024]{2,1,0:T(8,128)S(1)}, u32[]{:S(2)}, u32[]{:S(2)}) collective-permute-start(f32[5,8,1024]{2,1,0:T(8,128)S(1)} %get-tuple-element.57), channel_id=1, source_target_pairs={{0,8},{4,12},{8,0},{12,4},{1,9},{5,13},{9,1},{13,5},{2,10},{6,14},... | collective-permute-start | bytes 491528 | tf_op jit(solution)/shard_map/ppermute | solution.py:56
  21.4 8.6 %collective-permute-start.3 = (f32[5,8,1024]{2,1,0:T(8,128)S(1)}, f32[5,8,1024]{2,1,0:T(8,128)S(1)}, u32[]{:S(2)}, u32[]{:S(2)}) collective-permute-start(f32[5,8,1024]{2,1,0:T(8,128)S(1)} %get-tuple-element.57), channel_id=1, source_target_pairs={{0,4},{4,8},{8,12},{12,0},{1,5},{5,9},{9,13},{13,1},{2,6},{6,10},{... | collective-permute-start | bytes 491528 | tf_op jit(solution)/shard_map/ppermute | solution.py:56
  24.1 21.7 %copy-start.5 = (f32[4,4,8,1024]{3,2,1,0:T(8,128)}, f32[4,4,8,1024]{3,2,1,0:T(8,128)S(1)}, u32[]{:S(2)}) copy-start(f32[4,4,8,1024]{3,2,1,0:T(8,128)S(1)} %pad_maximum_fusion.1.refs_5_) | copy-start | bytes 1572868
  30.1 15.7 %copy-start.4 = (f32[4,5,8,1024]{3,2,1,0:T(8,128)}, f32[4,5,8,1024]{3,2,1,0:T(8,128)S(1)}, u32[]{:S(2)}) copy-start(f32[4,5,8,1024]{3,2,1,0:T(8,128)S(1)} %pad_maximum_fusion.refs_0_) | copy-start | bytes 1966084
  30.1 15.8 %collective-permute-start.7 = (f32[4,5,8,1024]{3,2,1,0:T(8,128)S(1)}, f32[4,5,8,1024]{3,2,1,0:T(8,128)S(1)}, u32[]{:S(2)}, u32[]{:S(2)}) collective-permute-start(f32[4,5,8,1024]{3,2,1,0:T(8,128)S(1)} %pad_maximum_fusion.refs_0_), channel_id=1, source_target_pairs={{0,3},{1,0},{2,1},{3,2},{4,7},{5,4},{6,5},{7,6},{8,11},{9,8},{10,9... | collective-permute-start | bytes 1966088 | tf_op jit(solution)/shard_map/ppermute | solution.py:56
  32.5 14.5 %collective-permute-start.8 = (f32[4,5,8,1024]{3,2,1,0:T(8,128)S(1)}, f32[4,5,8,1024]{3,2,1,0:T(8,128)S(1)}, u32[]{:S(2)}, u32[]{:S(2)}) collective-permute-start(f32[4,5,8,1024]{3,2,1,0:T(8,128)S(1)} %pad_maximum_fusion.refs_0_), channel_id=1, source_target_pairs={{0,1},{1,2},{2,3},{3,0},{4,5},{5,6},{6,7},{7,4},{8,9},{9,10},{10,1... | collective-permute-start | bytes 1966088 | tf_op jit(solution)/shard_map/ppermute | solution.py:56
  32.5 13.4 %collective-permute-start.10 = (f32[4,4,8,1024]{3,2,1,0:T(8,128)S(1)}, f32[4,4,8,1024]{3,2,1,0:T(8,128)S(1)}, u32[]{:S(2)}, u32[]{:S(2)}) collective-permute-start(f32[4,4,8,1024]{3,2,1,0:T(8,128)S(1)} %pad_maximum_fusion.1.refs_5_), channel_id=1, source_target_pairs={{0,4},{4,8},{8,12},{12,0},{1,5},{5,9},{9,13},{13,1},{2,6},{6,10},{... | collective-permute-start | bytes 1572872 | tf_op jit(solution)/shard_map/ppermute | solution.py:56
  32.5 13.4 %collective-permute-start.9 = (f32[4,4,8,1024]{3,2,1,0:T(8,128)S(1)}, f32[4,4,8,1024]{3,2,1,0:T(8,128)S(1)}, u32[]{:S(2)}, u32[]{:S(2)}) collective-permute-start(f32[4,4,8,1024]{3,2,1,0:T(8,128)S(1)} %pad_maximum_fusion.1.refs_5_), channel_id=1, source_target_pairs={{0,12},{4,0},{8,4},{12,8},{1,13},{5,1},{9,5},{13,9},{2,14},{6,2},{... | collective-permute-start | bytes 1572872 | tf_op jit(solution)/shard_map/ppermute | solution.py:56
  45.8 8.6 %copy-start.8 = (f32[4,4,8,1024]{3,2,1,0:T(8,128)}, f32[4,4,8,1024]{3,2,1,0:T(8,128)S(1)}, u32[]{:S(2)}) copy-start(f32[4,4,8,1024]{3,2,1,0:T(8,128)S(1)} %collective-permute-done.10.refs_9_) | copy-start | bytes 1572868
  45.9 8.6 %copy-start.9 = (f32[4,4,8,1024]{3,2,1,0:T(8,128)}, f32[4,4,8,1024]{3,2,1,0:T(8,128)S(1)}, u32[]{:S(2)}) copy-start(f32[4,4,8,1024]{3,2,1,0:T(8,128)S(1)} %collective-permute-done.9.refs_6_) | copy-start | bytes 1572868
  45.9 8.6 %copy-start.6 = (f32[4,5,8,1024]{3,2,1,0:T(8,128)}, f32[4,5,8,1024]{3,2,1,0:T(8,128)S(1)}, u32[]{:S(2)}) copy-start(f32[4,5,8,1024]{3,2,1,0:T(8,128)S(1)} %collective-permute-done.7.refs_1_) | copy-start | bytes 1966084
  46.9 7.5 %copy-start.7 = (f32[4,5,8,1024]{3,2,1,0:T(8,128)}, f32[4,5,8,1024]{3,2,1,0:T(8,128)S(1)}, u32[]{:S(2)}) copy-start(f32[4,5,8,1024]{3,2,1,0:T(8,128)S(1)} %collective-permute-done.8.refs_4_) | copy-start | bytes 1966084
  46.9 14.5 %collective-permute-start.11 = (f32[2,5,8,1024]{3,2,1,0:T(8,128)S(1)}, f32[2,5,8,1024]{3,2,1,0:T(8,128)}, u32[]{:S(2)}, u32[]{:S(2)}) collective-permute-start(f32[2,5,8,1024]{3,2,1,0:T(8,128)S(1)} %slice.54), channel_id=1, source_target_pairs={{0,1},{1,2},{2,3},{3,0},{4,5},{5,6},{6,7},{7,4},{8,9},{9,10},{10,1... | collective-permute-start | bytes 983048 | tf_op jit(solution)/shard_map/ppermute | solution.py:56
  47.7 13.8 %collective-permute-start.12 = (f32[2,5,8,1024]{3,2,1,0:T(8,128)S(1)}, f32[2,5,8,1024]{3,2,1,0:T(8,128)}, u32[]{:S(2)}, u32[]{:S(2)}) collective-permute-start(f32[2,5,8,1024]{3,2,1,0:T(8,128)S(1)} %slice.55), channel_id=1, source_target_pairs={{0,3},{1,0},{2,1},{3,2},{4,7},{5,4},{6,5},{7,6},{8,11},{9,8},{10,9... | collective-permute-start | bytes 983048 | tf_op jit(solution)/shard_map/ppermute | solution.py:56
  50.4 11.0 %collective-permute-start.13 = (f32[2,4,8,1024]{3,2,1,0:T(8,128)S(1)}, f32[2,4,8,1024]{3,2,1,0:T(8,128)}, u32[]{:S(2)}, u32[]{:S(2)}) collective-permute-start(f32[2,4,8,1024]{3,2,1,0:T(8,128)S(1)} %slice.56), channel_id=1, source_target_pairs={{0,4},{4,8},{8,12},{12,0},{1,5},{5,9},{9,13},{13,1},{2,6},{6,10},{... | collective-permute-start | bytes 786440 | tf_op jit(solution)/shard_map/ppermute | solution.py:56
  50.5 10.9 %collective-permute-start.14 = (f32[2,4,8,1024]{3,2,1,0:T(8,128)S(1)}, f32[2,4,8,1024]{3,2,1,0:T(8,128)}, u32[]{:S(2)}, u32[]{:S(2)}) collective-permute-start(f32[2,4,8,1024]{3,2,1,0:T(8,128)S(1)} %slice.57), channel_id=1, source_target_pairs={{0,12},{4,0},{8,4},{12,8},{1,13},{5,1},{9,5},{13,9},{2,14},{6,2},{... | collective-permute-start | bytes 786440 | tf_op jit(solution)/shard_map/ppermute | solution.py:56
  54.4 109.3 %all-to-all-start = ((f32[128,128,128]{2,1,0:T(8,128)}), f32[128,128,128]{2,1,0:T(8,128)}, u32[]{:S(2)}, u32[]{:S(2)}) async-start(f32[128,128,128]{2,1,0:T(8,128)} %turn.1), calls=%async_computation | async-start | bytes 16777216 | tf_op jit(solution)/shard_map/all_to_all | solution.py:508
  147.6 5.8 %collective-permute-start.18 = (s32[16,128]{1,0:T(8,128)}, s32[16,128]{1,0:T(8,128)S(1)}, u32[]{:S(2)}, u32[]{:S(2)}) collective-permute-start(s32[16,128]{1,0:T(8,128)} %get-tuple-element.44), channel_id=1, source_target_pairs={{0,16},{16,0},{32,48},{48,32},{64,80},{80,64},{96,112},{112,96},{1... | collective-permute-start | bytes 24584 | tf_op jit(solution)/shard_map/ppermute | solution.py:61
  148.4 8.2 %collective-permute-start.19 = (s32[16,128]{1,0:T(8,128)}, s32[16,128]{1,0:T(8,128)S(1)}, u32[]{:S(2)}, u32[]{:S(2)}) collective-permute-start(s32[16,128]{1,0:T(8,128)} %get-tuple-element.44), channel_id=1, source_target_pairs={{0,32},{16,48},{32,0},{48,16},{64,96},{80,112},{96,64},{112,80},{1... | collective-permute-start | bytes 24584 | tf_op jit(solution)/shard_map/ppermute | solution.py:61
  149.6 9.1 %collective-permute-start.20 = (s32[16,128]{1,0:T(8,128)}, s32[16,128]{1,0:T(8,128)S(1)}, u32[]{:S(2)}, u32[]{:S(2)}) collective-permute-start(s32[16,128]{1,0:T(8,128)} %get-tuple-element.44), channel_id=1, source_target_pairs={{0,48},{16,32},{32,16},{48,0},{64,112},{80,96},{96,80},{112,64},{1... | collective-permute-start | bytes 24584 | tf_op jit(solution)/shard_map/ppermute | solution.py:61
  150.3 8.4 %collective-permute-start.21 = (s32[16,128]{1,0:T(8,128)}, s32[16,128]{1,0:T(8,128)S(1)}, u32[]{:S(2)}, u32[]{:S(2)}) collective-permute-start(s32[16,128]{1,0:T(8,128)} %get-tuple-element.44), channel_id=1, source_target_pairs={{0,64},{16,80},{32,96},{48,112},{64,0},{80,16},{96,32},{112,48},{1... | collective-permute-start | bytes 24584 | tf_op jit(solution)/shard_map/ppermute | solution.py:61
  153.1 5.8 %collective-permute-start.22 = (s32[16,128]{1,0:T(8,128)}, s32[16,128]{1,0:T(8,128)S(1)}, u32[]{:S(2)}, u32[]{:S(2)}) collective-permute-start(s32[16,128]{1,0:T(8,128)} %get-tuple-element.44), channel_id=1, source_target_pairs={{0,80},{16,64},{32,112},{48,96},{64,16},{80,0},{96,48},{112,32},{1... | collective-permute-start | bytes 24584 | tf_op jit(solution)/shard_map/ppermute | solution.py:61
  153.4 5.4 %collective-permute-start.23 = (s32[16,128]{1,0:T(8,128)}, s32[16,128]{1,0:T(8,128)S(1)}, u32[]{:S(2)}, u32[]{:S(2)}) collective-permute-start(s32[16,128]{1,0:T(8,128)} %get-tuple-element.44), channel_id=1, source_target_pairs={{0,96},{16,112},{32,64},{48,80},{64,32},{80,48},{96,0},{112,16},{1... | collective-permute-start | bytes 24584 | tf_op jit(solution)/shard_map/ppermute | solution.py:61
  156.7 4.5 %collective-permute-start.24 = (s32[16,128]{1,0:T(8,128)}, s32[16,128]{1,0:T(8,128)S(1)}, u32[]{:S(2)}, u32[]{:S(2)}) collective-permute-start(s32[16,128]{1,0:T(8,128)} %get-tuple-element.44), channel_id=1, source_target_pairs={{0,112},{16,96},{32,80},{48,64},{64,48},{80,32},{96,16},{112,0},{1... | collective-permute-start | bytes 24584 | tf_op jit(solution)/shard_map/ppermute | solution.py:61
  161.2 2.6 copy-start.10
  183.8 38.5 %copy-start.3 = (s32[3]{0:T(128)S(1)}, s32[3]{0:T(128)}, u32[]{:S(2)}) copy-start(s32[3]{0:T(128)} %pad_add_fusion.position) | copy-start | bytes 40
  183.8 38.5 %all-to-all-start.1 = ((f32[32,136,128]{2,1,0:T(8,128)}), f32[32,136,128]{2,1,0:T(8,128)S(1)}, u32[]{:S(2)}, u32[]{:S(2)}) async-start(f32[32,136,128]{2,1,0:T(8,128)} %bitcast.91), calls=%async_computation.1 | async-start | bytes 4456448 | tf_op jit(solution)/shard_map/all_to_all | solution.py:508
  193.4 10.2 %collective-permute-start.15 = (f32[2,32,1024]{2,1,0:T(8,128)S(1)}, f32[2,32,1024]{2,1,0:T(8,128)S(1)}, u32[]{:S(2)}, u32[]{:S(2)}) collective-permute-start(f32[2,32,1024]{2,1,0:T(8,128)S(1)} %get-tuple-element.51), channel_id=1, source_target_pairs={{0,4},{4,8},{8,12},{12,0},{1,5},{5,9},{9,13},{13,1},{2,6},{6,10},{... | collective-permute-start | bytes 786440 | tf_op jit(solution)/shard_map/ppermute | solution.py:56
  195.0 14.1 %collective-permute-start.16 = (f32[2,32,1024]{2,1,0:T(8,128)S(1)}, f32[2,32,1024]{2,1,0:T(8,128)S(1)}, u32[]{:S(2)}, u32[]{:S(2)}) collective-permute-start(f32[2,32,1024]{2,1,0:T(8,128)S(1)} %get-tuple-element.50), channel_id=1, source_target_pairs={{0,8},{4,12},{8,0},{12,4},{1,9},{5,13},{9,1},{13,5},{2,10},{6,14},... | collective-permute-start | bytes 786440 | tf_op jit(solution)/shard_map/ppermute | solution.py:56
  197.0 12.4 %collective-permute-start.17 = (f32[2,32,1024]{2,1,0:T(8,128)S(1)}, f32[2,32,1024]{2,1,0:T(8,128)S(1)}, u32[]{:S(2)}, u32[]{:S(2)}) collective-permute-start(f32[2,32,1024]{2,1,0:T(8,128)S(1)} %get-tuple-element.49), channel_id=1, source_target_pairs={{0,12},{4,0},{8,4},{12,8},{1,13},{5,1},{9,5},{13,9},{2,14},{6,2},{... | collective-permute-start | bytes 786440 | tf_op jit(solution)/shard_map/ppermute | solution.py:56
  222.3 1.7 copy-start
  226.1 20.3 %collective-permute-start.26 = (f32[6,32,1024]{2,1,0:T(8,128)S(1)}, f32[6,32,1024]{2,1,0:T(8,128)S(1)}, u32[]{:S(2)}, u32[]{:S(2)}) collective-permute-start(f32[6,32,1024]{2,1,0:T(8,128)S(1)} %solve.1.refs_0_.refs_5_), channel_id=1, source_target_pairs={{0,4},{4,8},{8,12},{12,0},{1,5},{5,9},{9,13},{13,1},{2,6},{6,10},{... | collective-permute-start | bytes 2359304 | tf_op jit(solution)/shard_map/ppermute | solution.py:56
  227.6 19.2 %collective-permute-start.25 = (f32[6,32,1024]{2,1,0:T(8,128)S(1)}, f32[6,32,1024]{2,1,0:T(8,128)S(1)}, u32[]{:S(2)}, u32[]{:S(2)}) collective-permute-start(f32[6,32,1024]{2,1,0:T(8,128)S(1)} %solve.1.refs_0_.refs_5_), channel_id=1, source_target_pairs={{0,12},{4,0},{8,4},{12,8},{1,13},{5,1},{9,5},{13,9},{2,14},{6,2},{... | collective-permute-start | bytes 2359304 | tf_op jit(solution)/shard_map/ppermute | solution.py:56
  229.4 20.5 %collective-permute-start.30 = (f32[6,32,1024]{2,1,0:T(8,128)S(1)}, f32[6,32,1024]{2,1,0:T(8,128)S(1)}, u32[]{:S(2)}, u32[]{:S(2)}) collective-permute-start(f32[6,32,1024]{2,1,0:T(8,128)S(1)} %solve.1.refs_0_.refs_5_), channel_id=1, source_target_pairs={{0,1},{1,2},{2,3},{3,0},{4,5},{5,6},{6,7},{7,4},{8,9},{9,10},{10,1... | collective-permute-start | bytes 2359304 | tf_op jit(solution)/shard_map/ppermute | solution.py:56
  229.4 20.6 %collective-permute-start.29 = (f32[6,32,1024]{2,1,0:T(8,128)S(1)}, f32[6,32,1024]{2,1,0:T(8,128)S(1)}, u32[]{:S(2)}, u32[]{:S(2)}) collective-permute-start(f32[6,32,1024]{2,1,0:T(8,128)S(1)} %solve.1.refs_0_.refs_5_), channel_id=1, source_target_pairs={{0,3},{1,0},{2,1},{3,2},{4,7},{5,4},{6,5},{7,6},{8,11},{9,8},{10,9... | collective-permute-start | bytes 2359304 | tf_op jit(solution)/shard_map/ppermute | solution.py:56
  246.4 11.0 %collective-permute-start.27 = (f32[3,32,1024]{2,1,0:T(8,128)S(1)}, f32[3,32,1024]{2,1,0:T(8,128)S(1)}, u32[]{:S(2)}, u32[]{:S(2)}) collective-permute-start(f32[3,32,1024]{2,1,0:T(8,128)S(1)} %slice.65), channel_id=1, source_target_pairs={{0,4},{4,8},{8,12},{12,0},{1,5},{5,9},{9,13},{13,1},{2,6},{6,10},{... | collective-permute-start | bytes 1179656 | tf_op jit(solution)/shard_map/ppermute | solution.py:56
  246.8 10.6 %collective-permute-start.28 = (f32[3,32,1024]{2,1,0:T(8,128)S(1)}, f32[3,32,1024]{2,1,0:T(8,128)S(1)}, u32[]{:S(2)}, u32[]{:S(2)}) collective-permute-start(f32[3,32,1024]{2,1,0:T(8,128)S(1)} %slice.66), channel_id=1, source_target_pairs={{0,12},{4,0},{8,4},{12,8},{1,13},{5,1},{9,5},{13,9},{2,14},{6,2},{... | collective-permute-start | bytes 1179656 | tf_op jit(solution)/shard_map/ppermute | solution.py:56
  249.9 10.5 %collective-permute-start.31 = (f32[3,32,1024]{2,1,0:T(8,128)S(1)}, f32[3,32,1024]{2,1,0:T(8,128)S(1)}, u32[]{:S(2)}, u32[]{:S(2)}) collective-permute-start(f32[3,32,1024]{2,1,0:T(8,128)S(1)} %slice.67), channel_id=1, source_target_pairs={{0,1},{1,2},{2,3},{3,0},{4,5},{5,6},{6,7},{7,4},{8,9},{9,10},{10,1... | collective-permute-start | bytes 1179656 | tf_op jit(solution)/shard_map/ppermute | solution.py:56
  250.0 10.3 %collective-permute-start.32 = (f32[3,32,1024]{2,1,0:T(8,128)S(1)}, f32[3,32,1024]{2,1,0:T(8,128)S(1)}, u32[]{:S(2)}, u32[]{:S(2)}) collective-permute-start(f32[3,32,1024]{2,1,0:T(8,128)S(1)} %slice.68), channel_id=1, source_target_pairs={{0,3},{1,0},{2,1},{3,2},{4,7},{5,4},{6,5},{7,6},{8,11},{9,8},{10,9... | collective-permute-start | bytes 1179656 | tf_op jit(solution)/shard_map/ppermute | solution.py:56
  264.7 1.4 copy-start.1
  266.0 5.1 %copy-start.2 = (f32[128,1024]{1,0:T(8,128)S(1)}, f32[128,1024]{1,0:T(8,128)}, u32[]{:S(2)}) copy-start(f32[128,1024]{1,0:T(8,128)} %get-tuple-element.42.lead_rows) | copy-start | bytes 1572868
  266.0 32.3 %all-to-all-start.2 = ((f32[16,8,32,128]{3,2,1,0:T(8,128)}), f32[16,8,32,128]{3,2,1,0:T(8,128)}, u32[]{:S(2)}, u32[]{:S(2)}) async-start(f32[16,8,32,128]{3,2,1,0:T(8,128)} %copy-done.1), calls=%async_computation.2 | async-start | bytes 4194304 | tf_op jit(solution)/shard_map/all_to_all | solution.py:508

commit v6 on v5

--- a/solution.py
+++ b/solution.py
@@ -17,6 +17,8 @@
 FB = 32
 TB = FB - LB
 TILES = 128
+LABEL_ROWS = 4
+LABEL_LANES = TILES // LABEL_ROWS
 LINES = TB // SIDE
 SLICE = BLOCK // SIDE
 PSLOTS = LINES * LB
@@ -99,10 +101,8 @@
                 else:
                     src = (own, nxt, None, prv)[outer].at[inner]
                 dx, dy = (inner, outer) if h == 0 else (outer, inner)
-                for start, count, dst in place(h, (x + dx) % SIDE, (y + dy) % SIDE):
-                    copies.append(
-                        pltpu.make_async_copy(src.at[pl.ds(start, count)], dst, sem.at[len(copies)])
-                    )
+                dst = place(h, (x + dx) % SIDE, (y + dy) % SIDE)
+                copies.append(pltpu.make_async_copy(src, dst, sem.at[len(copies)]))
     return copies
 
 
@@ -206,24 +206,27 @@
 def factor_kernel(position, *refs):
     pieces, outs, scratch = refs[:10], refs[10:13], refs[13:]
     own_rows, inverse, labels = outs
-    (entries, labels_in, work, diag, pair, sem) = scratch
+    (entries, work, diag, pair, sem) = scratch
     px, py = position[0], position[1]
 
     def place(h, x, y):
         block = (x % 2) * SIDE + y
         slab = block * SLABS + (x // 2) * (SLABS // 2) + h * (SLABS // 4)
-        spans = [(0, SLABS // 4, entries.at[pl.ds(slab, SLABS // 4)])]
-        if h == 0:
-            spans.append((SLABS // 4, 1, labels_in.at[pl.ds(x * SIDE + y, 1)]))
-        return spans
+        return entries.at[pl.ds(slab, SLABS // 4)]
 
     copies = line_copies(pieces, place, sem, px, py)
     for copy in copies:
         copy.start()
     for copy in copies:
         copy.wait()
+    lane = lax.broadcasted_iota(jnp.int32, (1, TILES), 1)
     for g in range(GRID):
-        labels[g : g + 1, :] = labels_in[g, 0:1, :TILES].astype(jnp.int32)
+        slab = entries[(g % LB) * SLABS + (g // LB) * (SLABS // 2), :, LEAD - TILES :]
+        found = jnp.zeros((1, TILES), jnp.float32)
+        for n in range(LABEL_ROWS):
+            turned = pltpu.roll(slab[n : n + 1], (n + 1) * LABEL_LANES % TILES, 1)
+            found = jnp.where(lane // LABEL_LANES == n, turned, found)
+        labels[g : g + 1, :] = found.astype(jnp.int32)
     sub = lax.broadcasted_iota(jnp.int32, (SUB, 1), 0)
     row = lax.broadcasted_iota(jnp.int32, (BLOCK, BLOCK), 0)
     col = lax.broadcasted_iota(jnp.int32, (BLOCK, BLOCK), 1)
@@ -296,11 +299,10 @@
         out_specs=[VMEM] * 3,
         scratch_shapes=[
             pltpu.VMEM((LB * SLABS, SUB, LEAD), jnp.float32),
-            pltpu.VMEM((GRID, SUB, LEAD), jnp.float32),
             pltpu.VMEM((LEAD, LEAD), jnp.float32),
             pltpu.VMEM((LB, BLOCK, BLOCK), jnp.float32),
             pltpu.VMEM((BLOCK, 2 * BLOCK), jnp.float32),
-            pltpu.SemaphoreType.DMA((48,)),
+            pltpu.SemaphoreType.DMA((32,)),
         ],
         compiler_params=pltpu.CompilerParams(vmem_limit_bytes=VMEM_LIMIT),
         cost_estimate=pl.CostEstimate(flops=120 * 10**9, bytes_accessed=20 << 20, transcendentals=1024),
@@ -515,13 +517,14 @@
     half = BLOCK // 2
     lead = entries[0, :, :LEAD]
     other = lax.ppermute(lead[half:], "x", [(0, 2), (1, 3)])
-    lead = jnp.where(x < 2, lead[:half], other).reshape(SLABS // 2, SUB, LEAD)
+    lead = jnp.where(x < 2, lead[:half], other)
     bins = destination_bins(tile_owner[0, :, 0], tile_rows[0], tile_picks[0])
-    bins = jnp.pad(bins.astype(jnp.float32).reshape(1, 1, TILES), ((0, 0), (0, SUB - 1), (0, LEAD - TILES)))
-    lead, bins, tiles = lax.optimization_barrier((lead, bins, child_tiles))
+    bins = bins.astype(jnp.float32).reshape(LABEL_ROWS, LABEL_LANES)
+    lead = lax.dynamic_update_slice(lead, bins, (0, LEAD - LABEL_LANES))
+    lead, tiles = lax.optimization_barrier((lead.reshape(SLABS // 2, SUB, LEAD), child_tiles))
     half = SLABS // 4
     lines, near, far, tiles = gather_lines(
-        jnp.concatenate([lead[:half], bins], 0), lead[half:], tiles, turn
+        lead[:half], lead[half:], tiles, turn
     )
     tiles, near, entries = lax.optimization_barrier((tiles, near, entries))
     lead = [piece for ring in zip(lines, near, far) for piece in ring_pieces(*ring)]

time: 303 us -> 302 us (level)
  starting transfers between devices: 76.7 us -> 72.1 us
  other arithmetic: 2.6 us -> 5.72 us
    ppermute x7, waiting for transfers between devices: 2.74 us -> 9.06 us  [gather_front(): lax.ppermute(values, 'front', [(i, i ^ k) for i in range(FRONTS)])]
    all_to_all x3, waiting for transfers between devices: 39.8 us -> 35.6 us  [across(): return lax.all_to_all(values, axes, split_axis=0, concat_axis=0)]
    ppermute x1, waiting for transfers between devices: 4.67 us -> 0.65 us  [local(): other = lax.ppermute(lead[half:], 'x', [(0, 2), (1, 3)])]
    unnamed x0 -> x3, other arithmetic: none -> 3.95 us
    ppermute x7, starting transfers between devices: 10 us -> 6.92 us  [gather_front(): lax.ppermute(values, 'front', [(i, i ^ k) for i in range(FRONTS)])]
  transfers between devices with their start and end apart: 36 -> 36, of which waited for: 18 -> 15; matrix products, arithmetic and copies ran while one was open for 1% -> 3% of each run, Pallas kernels for 33% -> 33%
where the time goes in v6:
time: 302 us; the launch traced here: 301 us
  Pallas kernels  129 us (43%)
  waiting for transfers between devices  84.5 us (28%)
  starting transfers between devices  72.1 us (24%)
  local copies, waits for them, and re-layouts  9.02 us (3%)
  other arithmetic  5.72 us (2%)
    pallas_call x1, Pallas kernels, factor(): pl.pallas_call(factor_kernel, out_shape=[jax.ShapeDtypeStruct((BLOCK, LEA...  85.9 us
    ppermute x25, starting transfers between devices, shift(): lax.ppermute(block, axis, [(i, (i + step) % SIDE) for i in range(SIDE)])  42.3 us
    ppermute x25, waiting for transfers between devices, shift(): lax.ppermute(block, axis, [(i, (i + step) % SIDE) for i in range(SIDE)])  39.2 us
    all_to_all x3, waiting for transfers between devices, across(): return lax.all_to_all(values, axes, split_axis=0, concat_axis=0)  35.6 us
    pallas_call x1, Pallas kernels, combine(): pl.pallas_call(combine_kernel, grid=(steps,), out_shape=jax.ShapeDtypeStr...  20 us
    all_to_all x3, starting transfers between devices, across(): return lax.all_to_all(values, axes, split_axis=0, concat_axis=0)  17.9 us
    pallas_call x1, Pallas kernels, turn(): pl.pallas_call(turn_kernel, grid=(TILES // step,), out_shape=jax.ShapeDty...  10.1 us
    ppermute x7, waiting for transfers between devices, gather_front(): lax.ppermute(values, 'front', [(i, i ^ k) for i in range(FRONTS)])  9.06 us
  transfers between devices with their start and end apart: 36, of which 15 were waited for; matrix products, arithmetic and copies ran while one was open for 3% of the time, Pallas kernels for 33%

profile of v6, /device:TPU:0, one launch (start us, length us, event | category | flops | bytes accessed | tf_op | source)
XLA Modules:
  0.0 301.3 jit_solution(3223065971933270569)
XLA Ops:
  1.0 5.0 %collective-permute-start = (f32[64,1024]{1,0:T(8,128)S(1)}, f32[64,1024]{1,0:T(8,128)S(1)}, u32[]{:S(2)}, u32[]{:S(2)}) collective-permute-start(f32[64,1024]{1,0:T(8,128)S(1)} %slice_bitcast_fusion), channel_id=1, source_target_pairs={{0,8},{4,12},{1,9},{5,13},{2,10},{6,14},{3,11},{7,15},{16,24},{20,... | collective-permute-start | bytes 786440 | tf_op jit(solution)/shard_map/ppermute | solution.py:519
  6.5 1.3 reduce.9
  7.8 1.3 reduce.11
  9.2 1.3 reduce.10
  11.5 1.0 fusion
  13.1 3.3 %collective-permute-start.5 = (f32[4,8,1024]{2,1,0:T(8,128)S(1)}, f32[4,8,1024]{2,1,0:T(8,128)S(1)}, u32[]{:S(2)}, u32[]{:S(2)}) collective-permute-start(f32[4,8,1024]{2,1,0:T(8,128)S(1)} %get-tuple-element.53), channel_id=1, source_target_pairs={{0,2},{1,3},{2,0},{3,1},{4,6},{5,7},{6,4},{7,5},{8,10},{9,11},{10,... | collective-permute-start | bytes 393224 | tf_op jit(solution)/shard_map/ppermute | solution.py:58
  16.4 1.1 collective-permute-start.4
  18.4 4.0 %collective-permute-start.2 = (f32[4,8,1024]{2,1,0:T(8,128)S(1)}, f32[4,8,1024]{2,1,0:T(8,128)S(1)}, u32[]{:S(2)}, u32[]{:S(2)}) collective-permute-start(f32[4,8,1024]{2,1,0:T(8,128)S(1)} %get-tuple-element.54), channel_id=1, source_target_pairs={{0,8},{4,12},{8,0},{12,4},{1,9},{5,13},{9,1},{13,5},{2,10},{6,14},... | collective-permute-start | bytes 393224 | tf_op jit(solution)/shard_map/ppermute | solution.py:58
  22.4 2.0 collective-permute-start.3
  24.5 1.9 collective-permute-done.2
  26.4 1.0 collective-permute-done.1
  27.4 1.2 collective-permute-done.3
  29.4 2.6 collective-permute-start.7
  32.8 2.4 collective-permute-start.9
  35.2 10.1 %turn.1 = f32[128,128,128]{2,1,0:T(8,128)} custom-call(f32[16384,128]{1,0:T(8,128)} %bitcast.57), custom_call_target="tpu_custom_call" | custom-call | bytes 16777216 | tf_op jit(solution)/shard_map/turn/pallas_call | solution.py:123
  45.6 3.2 %collective-permute-start.14 = (f32[2,4,8,1024]{3,2,1,0:T(8,128)S(1)}, f32[2,4,8,1024]{3,2,1,0:T(8,128)}, u32[]{:S(2)}, u32[]{:S(2)}) collective-permute-start(f32[2,4,8,1024]{3,2,1,0:T(8,128)S(1)} %slice.57), channel_id=1, source_target_pairs={{0,12},{4,0},{8,4},{12,8},{1,13},{5,1},{9,5},{13,9},{2,14},{6,2},{... | collective-permute-start | bytes 786440 | tf_op jit(solution)/shard_map/ppermute | solution.py:58
  48.8 3.2 %collective-permute-start.12 = (f32[2,4,8,1024]{3,2,1,0:T(8,128)S(1)}, f32[2,4,8,1024]{3,2,1,0:T(8,128)}, u32[]{:S(2)}, u32[]{:S(2)}) collective-permute-start(f32[2,4,8,1024]{3,2,1,0:T(8,128)S(1)} %slice.55), channel_id=1, source_target_pairs={{0,3},{1,0},{2,1},{3,2},{4,7},{5,4},{6,5},{7,6},{8,11},{9,8},{10,9... | collective-permute-start | bytes 786440 | tf_op jit(solution)/shard_map/ppermute | solution.py:58
  52.7 6.7 %all-to-all-start = ((f32[128,128,128]{2,1,0:T(8,128)}), f32[128,128,128]{2,1,0:T(8,128)}, u32[]{:S(2)}, u32[]{:S(2)}) async-start(f32[128,128,128]{2,1,0:T(8,128)} %turn.1), calls=%async_computation | async-start | bytes 16777216 | tf_op jit(solution)/shard_map/all_to_all | solution.py:510
  60.1 85.9 %factor.1 = (f32[128,1024]{1,0:T(8,128)}, bf16[2,256,2560]{2,1,0:T(8,128)(2,1)}, s32[16,128]{1,0:T(8,128)}) custom-call(s32[3]{0:T(128)} %pad_add_fusion.position, f32[4,4,8,1024]{3,2,1,0:T(8,128)} %copy-done.5, f32[4,4,8,1024]{3,2,1,0:T(8,128)} %copy-done.7, f32[2,4,8,1024]{3,2,1,0:T(8,128)} %collective-permute-done.11.refs_2_, ...), custom_call_target="tpu_custom_call" | custom-call | flops 120000004096 | bytes 20971520 | tf_op jit(solution)/shard_map/factor/pallas_call | solution.py:291
  146.0 2.6 collective-permute-start.24
  149.1 1.2 collective-permute-start.22
  150.3 2.0 collective-permute-start.21
  154.1 5.3 %collective-permute-done.19 = s32[16,128]{1,0:T(8,128)S(1)} collective-permute-done((s32[16,128]{1,0:T(8,128)}, s32[16,128]{1,0:T(8,128)S(1)}, u32[]{:S(2)}, u32[]{:S(2)}) %collective-permute-start.19) | collective-permute-done | bytes 8224 | tf_op jit(solution)/shard_map/ppermute | solution.py:63
  159.4 3.3 %collective-permute-done.20 = s32[16,128]{1,0:T(8,128)S(1)} collective-permute-done((s32[16,128]{1,0:T(8,128)}, s32[16,128]{1,0:T(8,128)S(1)}, u32[]{:S(2)}, u32[]{:S(2)}) %collective-permute-start.20) | collective-permute-done | bytes 8224 | tf_op jit(solution)/shard_map/ppermute | solution.py:63
  163.4 20.0 %combine.1 = f32[4352,128]{1,0:T(8,128)} custom-call(s32[3]{0:T(128)} %pad_add_fusion.position, s32[16384]{0:T(1024)} %bitcast.71, f32[16384,128]{1,0:T(8,128)} %bitcast.30.x), custom_call_target="tpu_custom_call" | custom-call | flops 20000000000 | bytes 20971520 | tf_op jit(solution)/shard_map/combine/pallas_call | solution.py:174
  183.4 6.5 %all-to-all-start.1 = ((f32[32,136,128]{2,1,0:T(8,128)}), f32[32,136,128]{2,1,0:T(8,128)S(1)}, u32[]{:S(2)}, u32[]{:S(2)}) async-start(f32[32,136,128]{2,1,0:T(8,128)} %bitcast.63), calls=%async_computation.1 | async-start | bytes 4456448 | tf_op jit(solution)/shard_map/all_to_all | solution.py:510
  189.9 1.3 slice.58
  191.4 3.3 %collective-permute-start.17 = (f32[2,32,1024]{2,1,0:T(8,128)S(1)}, f32[2,32,1024]{2,1,0:T(8,128)S(1)}, u32[]{:S(2)}, u32[]{:S(2)}) collective-permute-start(f32[2,32,1024]{2,1,0:T(8,128)S(1)} %get-tuple-element.47), channel_id=1, source_target_pairs={{0,12},{4,0},{8,4},{12,8},{1,13},{5,1},{9,5},{13,9},{2,14},{6,2},{... | collective-permute-start | bytes 786440 | tf_op jit(solution)/shard_map/ppermute | solution.py:58
  195.7 10.7 %collective-permute-done.17.part3 = f32[2,32,1024]{2,1,0:T(8,128)S(1)} collective-permute-done((f32[2,32,1024]{2,1,0:T(8,128)S(1)}, f32[2,32,1024]{2,1,0:T(8,128)S(1)}, u32[]{:S(2)}, u32[]{:S(2)}) %collective-permute-start.17) | collective-permute-done | bytes 262176 | tf_op jit(solution)/shard_map/ppermute | solution.py:58
  206.3 3.5 %collective-permute-done.15.part1 = f32[2,32,1024]{2,1,0:T(8,128)S(1)} collective-permute-done((f32[2,32,1024]{2,1,0:T(8,128)S(1)}, f32[2,32,1024]{2,1,0:T(8,128)S(1)}, u32[]{:S(2)}, u32[]{:S(2)}) %collective-permute-start.15) | collective-permute-done | bytes 262176 | tf_op jit(solution)/shard_map/ppermute | solution.py:58
  209.8 10.4 %all-to-all-done.1 = f32[32,136,128]{2,1,0:T(8,128)S(1)} async-done(((f32[32,136,128]{2,1,0:T(8,128)}), f32[32,136,128]{2,1,0:T(8,128)S(1)}, u32[]{:S(2)}, u32[]{:S(2)}) %all-to-all-start.1) | async-done | bytes 2228256 | tf_op jit(solution)/shard_map/all_to_all | solution.py:510
  220.3 1.7 copy-done
  222.0 2.0 solve.1.refs_0_.refs_5_
  224.1 3.2 %collective-permute-start.29 = (f32[6,32,1024]{2,1,0:T(8,128)S(1)}, f32[6,32,1024]{2,1,0:T(8,128)S(1)}, u32[]{:S(2)}, u32[]{:S(2)}) collective-permute-start(f32[6,32,1024]{2,1,0:T(8,128)S(1)} %solve.1.refs_0_.refs_5_), channel_id=1, source_target_pairs={{0,3},{1,0},{2,1},{3,2},{4,7},{5,4},{6,5},{7,6},{8,11},{9,8},{10,9... | collective-permute-start | bytes 2359304 | tf_op jit(solution)/shard_map/ppermute | solution.py:58
  227.3 1.6 collective-permute-start.26
  228.9 1.7 collective-permute-start.25
  230.6 13.7 %collective-permute-done.30.refs_9_ = f32[6,32,1024]{2,1,0:T(8,128)S(1)} collective-permute-done((f32[6,32,1024]{2,1,0:T(8,128)S(1)}, f32[6,32,1024]{2,1,0:T(8,128)S(1)}, u32[]{:S(2)}, u32[]{:S(2)}) %collective-permute-start.30) | collective-permute-done | bytes 786464 | tf_op jit(solution)/shard_map/ppermute | solution.py:58
  244.5 3.3 %collective-permute-start.32 = (f32[3,32,1024]{2,1,0:T(8,128)S(1)}, f32[3,32,1024]{2,1,0:T(8,128)S(1)}, u32[]{:S(2)}, u32[]{:S(2)}) collective-permute-start(f32[3,32,1024]{2,1,0:T(8,128)S(1)} %slice.68), channel_id=1, source_target_pairs={{0,3},{1,0},{2,1},{3,2},{4,7},{5,4},{6,5},{7,6},{8,11},{9,8},{10,9... | collective-permute-start | bytes 1179656 | tf_op jit(solution)/shard_map/ppermute | solution.py:58
  247.8 1.6 collective-permute-start.27
  249.5 2.0 collective-permute-start.28
  251.5 3.9 %collective-permute-done.31.refs_7_ = f32[3,32,1024]{2,1,0:T(8,128)S(1)} collective-permute-done((f32[3,32,1024]{2,1,0:T(8,128)S(1)}, f32[3,32,1024]{2,1,0:T(8,128)S(1)}, u32[]{:S(2)}, u32[]{:S(2)}) %collective-permute-start.31) | collective-permute-done | bytes 393248 | tf_op jit(solution)/shard_map/ppermute | solution.py:58
  255.4 3.2 %collective-permute-done.27.refs_2_ = f32[3,32,1024]{2,1,0:T(8,128)S(1)} collective-permute-done((f32[3,32,1024]{2,1,0:T(8,128)S(1)}, f32[3,32,1024]{2,1,0:T(8,128)S(1)}, u32[]{:S(2)}, u32[]{:S(2)}) %collective-permute-start.27) | collective-permute-done | bytes 393248 | tf_op jit(solution)/shard_map/ppermute | solution.py:58
  258.7 4.3 %product.1 = (f32[16,8,32,128]{3,2,1,0:T(8,128)S(1)}, f32[2,128,1024]{2,1,0:T(8,128)S(1)}) custom-call(s32[3]{0:T(128)S(1)} %copy-done.3, f32[6,32,1024]{2,1,0:T(8,128)S(1)} %solve.1.refs_0_.refs_5_, f32[6,32,1024]{2,1,0:T(8,128)S(1)} %collective-permute-done.25.refs_1_, f32[3,32,1024]{2,1,0:T(8,128)S(1)} %collective-permute-done.27.refs_2_, ...), custom_call_target="tpu_custom_call" | custom-call | flops 11000000512 | bytes 8388608 | tf_op jit(solution)/shard_map/product/pallas_call | solution.py:401
  263.0 1.3 copy-done.1
  264.3 4.8 %all-to-all-start.2 = ((f32[16,8,32,128]{3,2,1,0:T(8,128)}), f32[16,8,32,128]{3,2,1,0:T(8,128)}, u32[]{:S(2)}, u32[]{:S(2)}) async-start(f32[16,8,32,128]{3,2,1,0:T(8,128)} %copy-done.1), calls=%async_computation.2 | async-start | bytes 4194304 | tf_op jit(solution)/shard_map/all_to_all | solution.py:510
  269.1 2.8 base.1.before
  272.0 25.2 %all-to-all-done.2.change_in = f32[16,8,32,128]{3,2,1,0:T(8,128)} async-done(((f32[16,8,32,128]{3,2,1,0:T(8,128)}), f32[16,8,32,128]{3,2,1,0:T(8,128)}, u32[]{:S(2)}, u32[]{:S(2)}) %all-to-all-start.2) | async-done | bytes 2097184 | tf_op jit(solution)/shard_map/all_to_all | solution.py:510
  297.1 4.0 %finish.1 = f32[2,128,4096]{2,1,0:T(8,128)} custom-call(s32[3]{0:T(128)} %pad_add_fusion.position, f32[2,128,4096]{2,1,0:T(8,128)} %base.1.before, f32[2,128,4096]{2,1,0:T(8,128)} %bitcast.61, f32[16,8,32,128]{3,2,1,0:T(8,128)} %all-to-all-done.2.change_in), custom_call_target="tpu_custom_call", output_to_operand_aliasing={{}: (1, {})} | custom-call | tf_op jit(solution)/shard_map/finish/pallas_call | solution.py:480
  (88 shorter events, 11.6 us)
Async XLA Ops:
  1.0 10.6 %collective-permute-start = (f32[64,1024]{1,0:T(8,128)S(1)}, f32[64,1024]{1,0:T(8,128)S(1)}, u32[]{:S(2)}, u32[]{:S(2)}) collective-permute-start(f32[64,1024]{1,0:T(8,128)S(1)} %slice_bitcast_fusion), channel_id=1, source_target_pairs={{0,8},{4,12},{1,9},{5,13},{2,10},{6,14},{3,11},{7,15},{16,24},{20,... | collective-permute-start | bytes 786440 | tf_op jit(solution)/shard_map/ppermute | solution.py:519
  13.1 9.3 %collective-permute-start.5 = (f32[4,8,1024]{2,1,0:T(8,128)S(1)}, f32[4,8,1024]{2,1,0:T(8,128)S(1)}, u32[]{:S(2)}, u32[]{:S(2)}) collective-permute-start(f32[4,8,1024]{2,1,0:T(8,128)S(1)} %get-tuple-element.53), channel_id=1, source_target_pairs={{0,2},{1,3},{2,0},{3,1},{4,6},{5,7},{6,4},{7,5},{8,10},{9,11},{10,... | collective-permute-start | bytes 393224 | tf_op jit(solution)/shard_map/ppermute | solution.py:58
  16.4 8.0 %collective-permute-start.4 = (f32[4,8,1024]{2,1,0:T(8,128)S(1)}, f32[4,8,1024]{2,1,0:T(8,128)S(1)}, u32[]{:S(2)}, u32[]{:S(2)}) collective-permute-start(f32[4,8,1024]{2,1,0:T(8,128)S(1)} %get-tuple-element.53), channel_id=1, source_target_pairs={{0,3},{1,0},{2,1},{3,2},{4,7},{5,4},{6,5},{7,6},{8,11},{9,8},{10,9... | collective-permute-start | bytes 393224 | tf_op jit(solution)/shard_map/ppermute | solution.py:58
  17.5 7.0 %collective-permute-start.6 = (f32[4,8,1024]{2,1,0:T(8,128)S(1)}, f32[4,8,1024]{2,1,0:T(8,128)S(1)}, u32[]{:S(2)}, u32[]{:S(2)}) collective-permute-start(f32[4,8,1024]{2,1,0:T(8,128)S(1)} %get-tuple-element.53), channel_id=1, source_target_pairs={{0,1},{1,2},{2,3},{3,0},{4,5},{5,6},{6,7},{7,4},{8,9},{9,10},{10,1... | collective-permute-start | bytes 393224 | tf_op jit(solution)/shard_map/ppermute | solution.py:58
  18.4 8.0 %collective-permute-start.2 = (f32[4,8,1024]{2,1,0:T(8,128)S(1)}, f32[4,8,1024]{2,1,0:T(8,128)S(1)}, u32[]{:S(2)}, u32[]{:S(2)}) collective-permute-start(f32[4,8,1024]{2,1,0:T(8,128)S(1)} %get-tuple-element.54), channel_id=1, source_target_pairs={{0,8},{4,12},{8,0},{12,4},{1,9},{5,13},{9,1},{13,5},{2,10},{6,14},... | collective-permute-start | bytes 393224 | tf_op jit(solution)/shard_map/ppermute | solution.py:58
  22.4 5.0 %collective-permute-start.1 = (f32[4,8,1024]{2,1,0:T(8,128)S(1)}, f32[4,8,1024]{2,1,0:T(8,128)S(1)}, u32[]{:S(2)}, u32[]{:S(2)}) collective-permute-start(f32[4,8,1024]{2,1,0:T(8,128)S(1)} %get-tuple-element.54), channel_id=1, source_target_pairs={{0,12},{4,0},{8,4},{12,8},{1,13},{5,1},{9,5},{13,9},{2,14},{6,2},{... | collective-permute-start | bytes 393224 | tf_op jit(solution)/shard_map/ppermute | solution.py:58
  22.4 6.2 %collective-permute-start.3 = (f32[4,8,1024]{2,1,0:T(8,128)S(1)}, f32[4,8,1024]{2,1,0:T(8,128)S(1)}, u32[]{:S(2)}, u32[]{:S(2)}) collective-permute-start(f32[4,8,1024]{2,1,0:T(8,128)S(1)} %get-tuple-element.54), channel_id=1, source_target_pairs={{0,4},{4,8},{8,12},{12,0},{1,5},{5,9},{9,13},{13,1},{2,6},{6,10},{... | collective-permute-start | bytes 393224 | tf_op jit(solution)/shard_map/ppermute | solution.py:58
  24.5 20.8 %copy-start.4 = (f32[4,4,8,1024]{3,2,1,0:T(8,128)}, f32[4,4,8,1024]{3,2,1,0:T(8,128)S(1)}, u32[]{:S(2)}) copy-start(f32[4,4,8,1024]{3,2,1,0:T(8,128)S(1)} %pad_maximum_fusion.1.refs_5_) | copy-start | bytes 1572868
  28.6 16.7 %copy-start.5 = (f32[4,4,8,1024]{3,2,1,0:T(8,128)}, f32[4,4,8,1024]{3,2,1,0:T(8,128)S(1)}, u32[]{:S(2)}) copy-start(f32[4,4,8,1024]{3,2,1,0:T(8,128)S(1)} %pad_maximum_fusion.refs_0_) | copy-start | bytes 1572868
  28.7 16.7 %collective-permute-start.8 = (f32[4,4,8,1024]{3,2,1,0:T(8,128)S(1)}, f32[4,4,8,1024]{3,2,1,0:T(8,128)S(1)}, u32[]{:S(2)}, u32[]{:S(2)}) collective-permute-start(f32[4,4,8,1024]{3,2,1,0:T(8,128)S(1)} %pad_maximum_fusion.refs_0_), channel_id=1, source_target_pairs={{0,1},{1,2},{2,3},{3,0},{4,5},{5,6},{6,7},{7,4},{8,9},{9,10},{10,1... | collective-permute-start | bytes 1572872 | tf_op jit(solution)/shard_map/ppermute | solution.py:58
  29.4 16.0 %collective-permute-start.7 = (f32[4,4,8,1024]{3,2,1,0:T(8,128)S(1)}, f32[4,4,8,1024]{3,2,1,0:T(8,128)S(1)}, u32[]{:S(2)}, u32[]{:S(2)}) collective-permute-start(f32[4,4,8,1024]{3,2,1,0:T(8,128)S(1)} %pad_maximum_fusion.refs_0_), channel_id=1, source_target_pairs={{0,3},{1,0},{2,1},{3,2},{4,7},{5,4},{6,5},{7,6},{8,11},{9,8},{10,9... | collective-permute-start | bytes 1572872 | tf_op jit(solution)/shard_map/ppermute | solution.py:58
  32.0 13.4 %collective-permute-start.10 = (f32[4,4,8,1024]{3,2,1,0:T(8,128)S(1)}, f32[4,4,8,1024]{3,2,1,0:T(8,128)S(1)}, u32[]{:S(2)}, u32[]{:S(2)}) collective-permute-start(f32[4,4,8,1024]{3,2,1,0:T(8,128)S(1)} %pad_maximum_fusion.1.refs_5_), channel_id=1, source_target_pairs={{0,4},{4,8},{8,12},{12,0},{1,5},{5,9},{9,13},{13,1},{2,6},{6,10},{... | collective-permute-start | bytes 1572872 | tf_op jit(solution)/shard_map/ppermute | solution.py:58
  32.8 12.6 %collective-permute-start.9 = (f32[4,4,8,1024]{3,2,1,0:T(8,128)S(1)}, f32[4,4,8,1024]{3,2,1,0:T(8,128)S(1)}, u32[]{:S(2)}, u32[]{:S(2)}) collective-permute-start(f32[4,4,8,1024]{3,2,1,0:T(8,128)S(1)} %pad_maximum_fusion.1.refs_5_), channel_id=1, source_target_pairs={{0,12},{4,0},{8,4},{12,8},{1,13},{5,1},{9,5},{13,9},{2,14},{6,2},{... | collective-permute-start | bytes 1572872 | tf_op jit(solution)/shard_map/ppermute | solution.py:58
  45.4 7.3 %copy-start.6 = (f32[4,4,8,1024]{3,2,1,0:T(8,128)}, f32[4,4,8,1024]{3,2,1,0:T(8,128)S(1)}, u32[]{:S(2)}) copy-start(f32[4,4,8,1024]{3,2,1,0:T(8,128)S(1)} %collective-permute-done.8.refs_4_) | copy-start | bytes 1572868
  45.4 7.3 %copy-start.7 = (f32[4,4,8,1024]{3,2,1,0:T(8,128)}, f32[4,4,8,1024]{3,2,1,0:T(8,128)S(1)}, u32[]{:S(2)}) copy-start(f32[4,4,8,1024]{3,2,1,0:T(8,128)S(1)} %collective-permute-done.7.refs_1_) | copy-start | bytes 1572868
  45.4 7.2 %copy-start.8 = (f32[4,4,8,1024]{3,2,1,0:T(8,128)}, f32[4,4,8,1024]{3,2,1,0:T(8,128)S(1)}, u32[]{:S(2)}) copy-start(f32[4,4,8,1024]{3,2,1,0:T(8,128)S(1)} %collective-permute-done.10.refs_9_) | copy-start | bytes 1572868
  45.4 7.2 %copy-start.9 = (f32[4,4,8,1024]{3,2,1,0:T(8,128)}, f32[4,4,8,1024]{3,2,1,0:T(8,128)S(1)}, u32[]{:S(2)}) copy-start(f32[4,4,8,1024]{3,2,1,0:T(8,128)S(1)} %collective-permute-done.9.refs_6_) | copy-start | bytes 1572868
  45.5 13.8 %collective-permute-start.13 = (f32[2,4,8,1024]{3,2,1,0:T(8,128)S(1)}, f32[2,4,8,1024]{3,2,1,0:T(8,128)S(1)}, u32[]{:S(2)}, u32[]{:S(2)}) collective-permute-start(f32[2,4,8,1024]{3,2,1,0:T(8,128)S(1)} %slice.56), channel_id=1, source_target_pairs={{0,4},{4,8},{8,12},{12,0},{1,5},{5,9},{9,13},{13,1},{2,6},{6,10},{... | collective-permute-start | bytes 786440 | tf_op jit(solution)/shard_map/ppermute | solution.py:58
  45.6 13.8 %collective-permute-start.14 = (f32[2,4,8,1024]{3,2,1,0:T(8,128)S(1)}, f32[2,4,8,1024]{3,2,1,0:T(8,128)}, u32[]{:S(2)}, u32[]{:S(2)}) collective-permute-start(f32[2,4,8,1024]{3,2,1,0:T(8,128)S(1)} %slice.57), channel_id=1, source_target_pairs={{0,12},{4,0},{8,4},{12,8},{1,13},{5,1},{9,5},{13,9},{2,14},{6,2},{... | collective-permute-start | bytes 786440 | tf_op jit(solution)/shard_map/ppermute | solution.py:58
  48.8 10.6 %collective-permute-start.11 = (f32[2,4,8,1024]{3,2,1,0:T(8,128)S(1)}, f32[2,4,8,1024]{3,2,1,0:T(8,128)}, u32[]{:S(2)}, u32[]{:S(2)}) collective-permute-start(f32[2,4,8,1024]{3,2,1,0:T(8,128)S(1)} %slice.54), channel_id=1, source_target_pairs={{0,1},{1,2},{2,3},{3,0},{4,5},{5,6},{6,7},{7,4},{8,9},{9,10},{10,1... | collective-permute-start | bytes 786440 | tf_op jit(solution)/shard_map/ppermute | solution.py:58
  48.8 10.6 %collective-permute-start.12 = (f32[2,4,8,1024]{3,2,1,0:T(8,128)S(1)}, f32[2,4,8,1024]{3,2,1,0:T(8,128)}, u32[]{:S(2)}, u32[]{:S(2)}) collective-permute-start(f32[2,4,8,1024]{3,2,1,0:T(8,128)S(1)} %slice.55), channel_id=1, source_target_pairs={{0,3},{1,0},{2,1},{3,2},{4,7},{5,4},{6,5},{7,6},{8,11},{9,8},{10,9... | collective-permute-start | bytes 786440 | tf_op jit(solution)/shard_map/ppermute | solution.py:58
  52.7 110.1 %all-to-all-start = ((f32[128,128,128]{2,1,0:T(8,128)}), f32[128,128,128]{2,1,0:T(8,128)}, u32[]{:S(2)}, u32[]{:S(2)}) async-start(f32[128,128,128]{2,1,0:T(8,128)} %turn.1), calls=%async_computation | async-start | bytes 16777216 | tf_op jit(solution)/shard_map/all_to_all | solution.py:510
  59.4 0.7 copy-start.11
  146.0 16.7 %collective-permute-start.24 = (s32[16,128]{1,0:T(8,128)}, s32[16,128]{1,0:T(8,128)S(1)}, u32[]{:S(2)}, u32[]{:S(2)}) collective-permute-start(s32[16,128]{1,0:T(8,128)} %get-tuple-element.42), channel_id=1, source_target_pairs={{0,112},{16,96},{32,80},{48,64},{64,48},{80,32},{96,16},{112,0},{1... | collective-permute-start | bytes 24584 | tf_op jit(solution)/shard_map/ppermute | solution.py:63
  148.6 14.1 %collective-permute-start.23 = (s32[16,128]{1,0:T(8,128)}, s32[16,128]{1,0:T(8,128)S(1)}, u32[]{:S(2)}, u32[]{:S(2)}) collective-permute-start(s32[16,128]{1,0:T(8,128)} %get-tuple-element.42), channel_id=1, source_target_pairs={{0,96},{16,112},{32,64},{48,80},{64,32},{80,48},{96,0},{112,16},{1... | collective-permute-start | bytes 24584 | tf_op jit(solution)/shard_map/ppermute | solution.py:63
  149.1 13.6 %collective-permute-start.22 = (s32[16,128]{1,0:T(8,128)}, s32[16,128]{1,0:T(8,128)S(1)}, u32[]{:S(2)}, u32[]{:S(2)}) collective-permute-start(s32[16,128]{1,0:T(8,128)} %get-tuple-element.42), channel_id=1, source_target_pairs={{0,80},{16,64},{32,112},{48,96},{64,16},{80,0},{96,48},{112,32},{1... | collective-permute-start | bytes 24584 | tf_op jit(solution)/shard_map/ppermute | solution.py:63
  150.3 12.4 %collective-permute-start.21 = (s32[16,128]{1,0:T(8,128)}, s32[16,128]{1,0:T(8,128)S(1)}, u32[]{:S(2)}, u32[]{:S(2)}) collective-permute-start(s32[16,128]{1,0:T(8,128)} %get-tuple-element.42), channel_id=1, source_target_pairs={{0,64},{16,80},{32,96},{48,112},{64,0},{80,16},{96,32},{112,48},{1... | collective-permute-start | bytes 24584 | tf_op jit(solution)/shard_map/ppermute | solution.py:63
  152.3 1.4 collective-permute-start.18
  153.7 5.7 %collective-permute-start.19 = (s32[16,128]{1,0:T(8,128)}, s32[16,128]{1,0:T(8,128)S(1)}, u32[]{:S(2)}, u32[]{:S(2)}) collective-permute-start(s32[16,128]{1,0:T(8,128)} %get-tuple-element.42), channel_id=1, source_target_pairs={{0,32},{16,48},{32,0},{48,16},{64,96},{80,112},{96,64},{112,80},{1... | collective-permute-start | bytes 24584 | tf_op jit(solution)/shard_map/ppermute | solution.py:63
  159.4 3.3 %collective-permute-start.20 = (s32[16,128]{1,0:T(8,128)}, s32[16,128]{1,0:T(8,128)S(1)}, u32[]{:S(2)}, u32[]{:S(2)}) collective-permute-start(s32[16,128]{1,0:T(8,128)} %get-tuple-element.42), channel_id=1, source_target_pairs={{0,48},{16,32},{32,16},{48,0},{64,112},{80,96},{96,80},{112,64},{1... | collective-permute-start | bytes 24584 | tf_op jit(solution)/shard_map/ppermute | solution.py:63
  162.8 0.6 copy-start.10
  183.4 36.8 %copy-start.3 = (s32[3]{0:T(128)S(1)}, s32[3]{0:T(128)}, u32[]{:S(2)}) copy-start(s32[3]{0:T(128)} %pad_add_fusion.position) | copy-start | bytes 40
  183.4 36.8 %all-to-all-start.1 = ((f32[32,136,128]{2,1,0:T(8,128)}), f32[32,136,128]{2,1,0:T(8,128)S(1)}, u32[]{:S(2)}, u32[]{:S(2)}) async-start(f32[32,136,128]{2,1,0:T(8,128)} %bitcast.63), calls=%async_computation.1 | async-start | bytes 4456448 | tf_op jit(solution)/shard_map/all_to_all | solution.py:510
  191.4 15.0 %collective-permute-start.17 = (f32[2,32,1024]{2,1,0:T(8,128)S(1)}, f32[2,32,1024]{2,1,0:T(8,128)S(1)}, u32[]{:S(2)}, u32[]{:S(2)}) collective-permute-start(f32[2,32,1024]{2,1,0:T(8,128)S(1)} %get-tuple-element.47), channel_id=1, source_target_pairs={{0,12},{4,0},{8,4},{12,8},{1,13},{5,1},{9,5},{13,9},{2,14},{6,2},{... | collective-permute-start | bytes 786440 | tf_op jit(solution)/shard_map/ppermute | solution.py:58
  194.7 11.6 %collective-permute-start.16 = (f32[2,32,1024]{2,1,0:T(8,128)S(1)}, f32[2,32,1024]{2,1,0:T(8,128)S(1)}, u32[]{:S(2)}, u32[]{:S(2)}) collective-permute-start(f32[2,32,1024]{2,1,0:T(8,128)S(1)} %get-tuple-element.48), channel_id=1, source_target_pairs={{0,8},{4,12},{8,0},{12,4},{1,9},{5,13},{9,1},{13,5},{2,10},{6,14},... | collective-permute-start | bytes 786440 | tf_op jit(solution)/shard_map/ppermute | solution.py:58
  195.1 14.8 %collective-permute-start.15 = (f32[2,32,1024]{2,1,0:T(8,128)S(1)}, f32[2,32,1024]{2,1,0:T(8,128)S(1)}, u32[]{:S(2)}, u32[]{:S(2)}) collective-permute-start(f32[2,32,1024]{2,1,0:T(8,128)S(1)} %get-tuple-element.49), channel_id=1, source_target_pairs={{0,4},{4,8},{8,12},{12,0},{1,5},{5,9},{9,13},{13,1},{2,6},{6,10},{... | collective-permute-start | bytes 786440 | tf_op jit(solution)/shard_map/ppermute | solution.py:58
  220.3 1.7 copy-start
  224.0 20.3 %collective-permute-start.30 = (f32[6,32,1024]{2,1,0:T(8,128)S(1)}, f32[6,32,1024]{2,1,0:T(8,128)S(1)}, u32[]{:S(2)}, u32[]{:S(2)}) collective-permute-start(f32[6,32,1024]{2,1,0:T(8,128)S(1)} %solve.1.refs_0_.refs_5_), channel_id=1, source_target_pairs={{0,1},{1,2},{2,3},{3,0},{4,5},{5,6},{6,7},{7,4},{8,9},{9,10},{10,1... | collective-permute-start | bytes 2359304 | tf_op jit(solution)/shard_map/ppermute | solution.py:58
  224.1 20.4 %collective-permute-start.29 = (f32[6,32,1024]{2,1,0:T(8,128)S(1)}, f32[6,32,1024]{2,1,0:T(8,128)S(1)}, u32[]{:S(2)}, u32[]{:S(2)}) collective-permute-start(f32[6,32,1024]{2,1,0:T(8,128)S(1)} %solve.1.refs_0_.refs_5_), channel_id=1, source_target_pairs={{0,3},{1,0},{2,1},{3,2},{4,7},{5,4},{6,5},{7,6},{8,11},{9,8},{10,9... | collective-permute-start | bytes 2359304 | tf_op jit(solution)/shard_map/ppermute | solution.py:58
  227.3 20.5 %collective-permute-start.26 = (f32[6,32,1024]{2,1,0:T(8,128)S(1)}, f32[6,32,1024]{2,1,0:T(8,128)S(1)}, u32[]{:S(2)}, u32[]{:S(2)}) collective-permute-start(f32[6,32,1024]{2,1,0:T(8,128)S(1)} %solve.1.refs_0_.refs_5_), channel_id=1, source_target_pairs={{0,4},{4,8},{8,12},{12,0},{1,5},{5,9},{9,13},{13,1},{2,6},{6,10},{... | collective-permute-start | bytes 2359304 | tf_op jit(solution)/shard_map/ppermute | solution.py:58
  228.9 20.6 %collective-permute-start.25 = (f32[6,32,1024]{2,1,0:T(8,128)S(1)}, f32[6,32,1024]{2,1,0:T(8,128)S(1)}, u32[]{:S(2)}, u32[]{:S(2)}) collective-permute-start(f32[6,32,1024]{2,1,0:T(8,128)S(1)} %solve.1.refs_0_.refs_5_), channel_id=1, source_target_pairs={{0,12},{4,0},{8,4},{12,8},{1,13},{5,1},{9,5},{13,9},{2,14},{6,2},{... | collective-permute-start | bytes 2359304 | tf_op jit(solution)/shard_map/ppermute | solution.py:58
  244.4 11.0 %collective-permute-start.31 = (f32[3,32,1024]{2,1,0:T(8,128)S(1)}, f32[3,32,1024]{2,1,0:T(8,128)S(1)}, u32[]{:S(2)}, u32[]{:S(2)}) collective-permute-start(f32[3,32,1024]{2,1,0:T(8,128)S(1)} %slice.67), channel_id=1, source_target_pairs={{0,1},{1,2},{2,3},{3,0},{4,5},{5,6},{6,7},{7,4},{8,9},{9,10},{10,1... | collective-permute-start | bytes 1179656 | tf_op jit(solution)/shard_map/ppermute | solution.py:58
  244.5 10.9 %collective-permute-start.32 = (f32[3,32,1024]{2,1,0:T(8,128)S(1)}, f32[3,32,1024]{2,1,0:T(8,128)S(1)}, u32[]{:S(2)}, u32[]{:S(2)}) collective-permute-start(f32[3,32,1024]{2,1,0:T(8,128)S(1)} %slice.68), channel_id=1, source_target_pairs={{0,3},{1,0},{2,1},{3,2},{4,7},{5,4},{6,5},{7,6},{8,11},{9,8},{10,9... | collective-permute-start | bytes 1179656 | tf_op jit(solution)/shard_map/ppermute | solution.py:58
  247.8 10.7 %collective-permute-start.27 = (f32[3,32,1024]{2,1,0:T(8,128)S(1)}, f32[3,32,1024]{2,1,0:T(8,128)S(1)}, u32[]{:S(2)}, u32[]{:S(2)}) collective-permute-start(f32[3,32,1024]{2,1,0:T(8,128)S(1)} %slice.65), channel_id=1, source_target_pairs={{0,4},{4,8},{8,12},{12,0},{1,5},{5,9},{9,13},{13,1},{2,6},{6,10},{... | collective-permute-start | bytes 1179656 | tf_op jit(solution)/shard_map/ppermute | solution.py:58
  249.5 9.2 %collective-permute-start.28 = (f32[3,32,1024]{2,1,0:T(8,128)S(1)}, f32[3,32,1024]{2,1,0:T(8,128)S(1)}, u32[]{:S(2)}, u32[]{:S(2)}) collective-permute-start(f32[3,32,1024]{2,1,0:T(8,128)S(1)} %slice.66), channel_id=1, source_target_pairs={{0,12},{4,0},{8,4},{12,8},{1,13},{5,1},{9,5},{13,9},{2,14},{6,2},{... | collective-permute-start | bytes 1179656 | tf_op jit(solution)/shard_map/ppermute | solution.py:58
  263.0 1.3 copy-start.1
  264.3 4.8 %copy-start.2 = (f32[128,1024]{1,0:T(8,128)S(1)}, f32[128,1024]{1,0:T(8,128)}, u32[]{:S(2)}) copy-start(f32[128,1024]{1,0:T(8,128)} %get-tuple-element.40.lead_rows) | copy-start | bytes 1572868
  264.3 32.8 %all-to-all-start.2 = ((f32[16,8,32,128]{3,2,1,0:T(8,128)}), f32[16,8,32,128]{3,2,1,0:T(8,128)}, u32[]{:S(2)}, u32[]{:S(2)}) async-start(f32[16,8,32,128]{3,2,1,0:T(8,128)} %copy-done.1), calls=%async_computation.2 | async-start | bytes 4194304 | tf_op jit(solution)/shard_map/all_to_all | solution.py:510

commit v7 on v6

--- a/solution.py
+++ b/solution.py
@@ -119,7 +119,7 @@
 
 
 def turn(tiles):
-    step = 64
+    step = 32
     return pl.pallas_call(
         turn_kernel,
         grid=(TILES // step,),
@@ -310,7 +310,7 @@
     )(position, *pieces)
 
 
-def solve_kernel(position, own, part1, part2, part3, sums, inverse, out, rows):
+def solve_kernel(position, own, part1, part2, part3, sums, inverse, first, second, rows):
     x = position[0]
     for step, part in enumerate((own, part1, part2, part3)):
         source = (x + SIDE - step) % SIDE
@@ -328,15 +328,17 @@
         value = mul(high[:, :end], inv_high) + (
             mul(high[:, :end], inv_low) + mul(low[:, :end], inv_high)
         )
-        out[:, :, end - WIDE : end] = value.reshape(LINES, SLICE, WIDE)
+        value = value.reshape(2, LINES // 2, SLICE, WIDE)
+        first[:, :, end - WIDE : end] = value[0]
+        second[:, :, end - WIDE : end] = value[1]
 
 
 def solve(position, parts, sums, inverse):
     return pl.pallas_call(
         solve_kernel,
-        out_shape=jax.ShapeDtypeStruct((LINES, SLICE, LEAD), jnp.float32),
+        out_shape=[jax.ShapeDtypeStruct((LINES // 2, SLICE, LEAD), jnp.float32)] * 2,
         in_specs=[SMEM] + [VMEM] * 6,
-        out_specs=VMEM,
+        out_specs=[VMEM] * 2,
         scratch_shapes=[pltpu.VMEM((2 * SIDE, SLICE, LEAD), jnp.float32)],
         compiler_params=pltpu.CompilerParams(vmem_limit_bytes=20 << 20),
         name="solve",
@@ -344,38 +346,27 @@
 
 
 def product_kernel(position, *refs):
-    along_x, along_y, scratch = refs[:5], refs[5:10], refs[10:]
+    along_x, along_y, scratch = refs[:8], refs[8:16], refs[16:]
     sums, out, own, high, low, row_high, row_low = scratch
     x, y = position[0], position[1]
     half = LINES // 2
     out[...] = jnp.zeros_like(out)
 
     def blocks(pieces, here):
-        nearby, nxt, far_a, far_b, prv = pieces
-        for step, piece, first in (
-            (0, nearby, 0),
-            (1, nxt, 0),
-            (2, far_a, 0),
-            (2, far_b, half),
-            (3, prv, 0),
-        ):
-            for m in range(piece.shape[0]):
-                yield (here + step) % SIDE, first + m, piece[m]
+        for n, piece in enumerate(pieces):
+            for m in range(half):
+                yield (here + n // 2) % SIDE, n % 2 * half + m, piece[m]
 
     for index, m, values in blocks(along_x, x):
         at = pl.ds(pl.multiple_of(m * BLOCK + index * SLICE, SLICE), SLICE)
         high[at, :], low[at, :] = split(values)
     for l in range(2):
         m = jnp.maximum(x - 2, 0) if l == 0 else x + 2
-        nearby, nxt, far_a, far_b, prv = along_x
         for step in range(SIDE):
             at = pl.ds(pl.multiple_of((x + step) % SIDE * SLICE, SLICE), SLICE)
-            if step == 2:
-                first = far_a[jnp.minimum(m, half - 1)]
-                second = far_b[jnp.maximum(m - half, 0)]
-                own[l, at, :] = jnp.where(m < half, first, second)
-            else:
-                own[l, at, :] = (nearby, nxt, None, prv)[step][m]
+            first = along_x[2 * step][jnp.minimum(m, half - 1)]
+            second = along_x[2 * step + 1][jnp.maximum(m - half, 0)]
+            own[l, at, :] = jnp.where(m < half, first, second)
     for z, m, values in blocks(along_y, y):
         at = pl.ds(pl.multiple_of(m * BLOCK + z * SLICE, SLICE), SLICE)
         row_high[at, :], row_low[at, :] = split(values)
@@ -404,7 +395,7 @@
             jax.ShapeDtypeStruct((GRID, OUT_SLOTS, SLICE, BLOCK), jnp.float32),
             jax.ShapeDtypeStruct((2, BLOCK, LEAD), jnp.float32),
         ],
-        in_specs=[SMEM] + [VMEM] * 11,
+        in_specs=[SMEM] + [VMEM] * 17,
         out_specs=[VMEM] * 2,
         scratch_shapes=[
             pltpu.VMEM((LINES * BLOCK, LEAD), jnp.bfloat16),
@@ -539,9 +530,12 @@
     sums = combine(position, bins, rows).reshape(SLICE, SLOTS, BLOCK)
     sums = across(sums, ("y", "front")).reshape(-1, BLOCK)
     solved = solve(position, panel, sums, inverse)
-    near = [ring_near(solved, axis) for axis in ("x", "y")]
-    far = [ring_far(pair, axis) for pair, axis in zip(near, ("x", "y"))]
-    along = [ring_pieces(solved, *pair) for pair in zip(near, far)]
+    along = []
+    for axis in ("x", "y"):
+        nxt = [shift(part, axis, -1) for part in solved]
+        prv = [shift(part, axis, 1) for part in solved]
+        far = [shift(prv[0], axis, 1), shift(nxt[1], axis, -1)]
+        along.append([*solved, *nxt, *far, *prv])
     change, own = product(position, *along, sums)
     change = across(change, ("x", "y"))
     out = finish(position, base(position, entries.shape, lead_rows, own), entries, change)

time: 302 us -> 302 us (level)
  starting transfers between devices: 72.1 us -> 76.2 us
  waiting for transfers between devices: 84.5 us -> 80.5 us
    ppermute x25 -> x29, waiting for transfers between devices: 39.2 us -> 35.8 us  [shift(): lax.ppermute(block, axis, [(i, (i + step) % SIDE) for i in range(SIDE)])]
    ppermute x25 -> x29, starting transfers between devices: 42.3 us -> 45.4 us  [shift(): lax.ppermute(block, axis, [(i, (i + step) % SIDE) for i in range(SIDE)])]
  transfers between devices with their start and end apart: 36 -> 40, of which waited for: 15 -> 16; matrix products, arithmetic and copies ran while one was open for 3% -> 3% of each run, Pallas kernels for 33% -> 33%
where the time goes in v7:
time: 302 us; the launch traced here: 301 us
  Pallas kernels  129 us (43%)
  waiting for transfers between devices  80.5 us (27%)
  starting transfers between devices  76.2 us (25%)
  local copies, waits for them, and re-layouts  8.91 us (3%)
  other arithmetic  5.78 us (2%)
    pallas_call x1, Pallas kernels, factor(): pl.pallas_call(factor_kernel, out_shape=[jax.ShapeDtypeStruct((BLOCK, LEA...  85.9 us
    ppermute x29, starting transfers between devices, shift(): lax.ppermute(block, axis, [(i, (i + step) % SIDE) for i in range(SIDE)])  45.4 us
    ppermute x29, waiting for transfers between devices, shift(): lax.ppermute(block, axis, [(i, (i + step) % SIDE) for i in range(SIDE)])  35.8 us
    all_to_all x3, waiting for transfers between devices, across(): return lax.all_to_all(values, axes, split_axis=0, concat_axis=0)  35 us
    pallas_call x1, Pallas kernels, combine(): pl.pallas_call(combine_kernel, grid=(steps,), out_shape=jax.ShapeDtypeStr...  20 us
    all_to_all x3, starting transfers between devices, across(): return lax.all_to_all(values, axes, split_axis=0, concat_axis=0)  18.8 us
    pallas_call x1, Pallas kernels, turn(): pl.pallas_call(turn_kernel, grid=(TILES // step,), out_shape=jax.ShapeDty...  9.57 us
    ppermute x7, waiting for transfers between devices, gather_front(): lax.ppermute(values, 'front', [(i, i ^ k) for i in range(FRONTS)])  9.1 us
  transfers between devices with their start and end apart: 40, of which 16 were waited for; matrix products, arithmetic and copies ran while one was open for 3% of the time, Pallas kernels for 33%

profile of v7, /device:TPU:0, one launch (start us, length us, event | category | flops | bytes accessed | tf_op | source)
XLA Modules:
  0.0 300.9 jit_solution(11528741898611865401)
XLA Ops:
  1.0 5.0 %collective-permute-start = (f32[64,1024]{1,0:T(8,128)S(1)}, f32[64,1024]{1,0:T(8,128)S(1)}, u32[]{:S(2)}, u32[]{:S(2)}) collective-permute-start(f32[64,1024]{1,0:T(8,128)S(1)} %slice_bitcast_fusion), channel_id=1, source_target_pairs={{0,8},{4,12},{1,9},{5,13},{2,10},{6,14},{3,11},{7,15},{16,24},{20,... | collective-permute-start | bytes 786440 | tf_op jit(solution)/shard_map/ppermute | solution.py:510
  6.5 1.3 reduce.9
  7.8 1.3 reduce.11
  9.2 1.3 reduce.10
  13.1 3.3 %collective-permute-start.5 = (f32[4,8,1024]{2,1,0:T(8,128)S(1)}, f32[4,8,1024]{2,1,0:T(8,128)S(1)}, u32[]{:S(2)}, u32[]{:S(2)}) collective-permute-start(f32[4,8,1024]{2,1,0:T(8,128)S(1)} %get-tuple-element.57), channel_id=1, source_target_pairs={{0,2},{1,3},{2,0},{3,1},{4,6},{5,7},{6,4},{7,5},{8,10},{9,11},{10,... | collective-permute-start | bytes 393224 | tf_op jit(solution)/shard_map/ppermute | solution.py:58
  16.4 1.1 collective-permute-start.4
  18.4 4.0 %collective-permute-start.2 = (f32[4,8,1024]{2,1,0:T(8,128)S(1)}, f32[4,8,1024]{2,1,0:T(8,128)S(1)}, u32[]{:S(2)}, u32[]{:S(2)}) collective-permute-start(f32[4,8,1024]{2,1,0:T(8,128)S(1)} %get-tuple-element.58), channel_id=1, source_target_pairs={{0,8},{4,12},{8,0},{12,4},{1,9},{5,13},{9,1},{13,5},{2,10},{6,14},... | collective-permute-start | bytes 393224 | tf_op jit(solution)/shard_map/ppermute | solution.py:58
  22.4 2.0 collective-permute-start.3
  24.5 1.9 collective-permute-done.2
  27.4 1.2 collective-permute-done.3
  29.4 2.6 collective-permute-start.7
  32.8 2.4 collective-permute-start.9
  35.2 9.6 %turn.1 = f32[128,128,128]{2,1,0:T(8,128)} custom-call(f32[16384,128]{1,0:T(8,128)} %bitcast.57), custom_call_target="tpu_custom_call" | custom-call | bytes 16777216 | tf_op jit(solution)/shard_map/turn/pallas_call | solution.py:123
  45.0 3.2 %collective-permute-start.14 = (f32[2,4,8,1024]{3,2,1,0:T(8,128)S(1)}, f32[2,4,8,1024]{3,2,1,0:T(8,128)}, u32[]{:S(2)}, u32[]{:S(2)}) collective-permute-start(f32[2,4,8,1024]{3,2,1,0:T(8,128)S(1)} %slice.45), channel_id=1, source_target_pairs={{0,12},{4,0},{8,4},{12,8},{1,13},{5,1},{9,5},{13,9},{2,14},{6,2},{... | collective-permute-start | bytes 786440 | tf_op jit(solution)/shard_map/ppermute | solution.py:58
  48.3 3.2 %collective-permute-start.12 = (f32[2,4,8,1024]{3,2,1,0:T(8,128)S(1)}, f32[2,4,8,1024]{3,2,1,0:T(8,128)}, u32[]{:S(2)}, u32[]{:S(2)}) collective-permute-start(f32[2,4,8,1024]{3,2,1,0:T(8,128)S(1)} %slice.43), channel_id=1, source_target_pairs={{0,3},{1,0},{2,1},{3,2},{4,7},{5,4},{6,5},{7,6},{8,11},{9,8},{10,9... | collective-permute-start | bytes 786440 | tf_op jit(solution)/shard_map/ppermute | solution.py:58
  52.1 7.3 %all-to-all-start = ((f32[128,128,128]{2,1,0:T(8,128)}), f32[128,128,128]{2,1,0:T(8,128)}, u32[]{:S(2)}, u32[]{:S(2)}) async-start(f32[128,128,128]{2,1,0:T(8,128)} %turn.1), calls=%async_computation | async-start | bytes 16777216 | tf_op jit(solution)/shard_map/all_to_all | solution.py:501
  60.1 85.9 %factor.1 = (f32[128,1024]{1,0:T(8,128)}, bf16[2,256,2560]{2,1,0:T(8,128)(2,1)}, s32[16,128]{1,0:T(8,128)}) custom-call(s32[3]{0:T(128)} %pad_add_fusion.position, f32[4,4,8,1024]{3,2,1,0:T(8,128)} %copy-done.5, f32[4,4,8,1024]{3,2,1,0:T(8,128)} %copy-done.7, f32[2,4,8,1024]{3,2,1,0:T(8,128)} %collective-permute-done.11.refs_2_, ...), custom_call_target="tpu_custom_call" | custom-call | flops 120000004096 | bytes 20971520 | tf_op jit(solution)/shard_map/factor/pallas_call | solution.py:291
  146.0 2.6 collective-permute-start.24
  149.2 1.2 collective-permute-start.22
  150.4 2.0 collective-permute-start.21
  154.2 5.3 %collective-permute-done.19 = s32[16,128]{1,0:T(8,128)S(1)} collective-permute-done((s32[16,128]{1,0:T(8,128)}, s32[16,128]{1,0:T(8,128)S(1)}, u32[]{:S(2)}, u32[]{:S(2)}) %collective-permute-start.19) | collective-permute-done | bytes 8224 | tf_op jit(solution)/shard_map/ppermute | solution.py:63
  159.5 3.3 %collective-permute-done.20 = s32[16,128]{1,0:T(8,128)S(1)} collective-permute-done((s32[16,128]{1,0:T(8,128)}, s32[16,128]{1,0:T(8,128)S(1)}, u32[]{:S(2)}, u32[]{:S(2)}) %collective-permute-start.20) | collective-permute-done | bytes 8224 | tf_op jit(solution)/shard_map/ppermute | solution.py:63
  163.4 20.0 %combine.1 = f32[4352,128]{1,0:T(8,128)} custom-call(s32[3]{0:T(128)} %pad_add_fusion.position, s32[16384]{0:T(1024)} %bitcast.71, f32[16384,128]{1,0:T(8,128)} %bitcast.30.x), custom_call_target="tpu_custom_call" | custom-call | flops 20000000000 | bytes 20971520 | tf_op jit(solution)/shard_map/combine/pallas_call | solution.py:174
  183.5 6.5 %all-to-all-start.1 = ((f32[32,136,128]{2,1,0:T(8,128)}), f32[32,136,128]{2,1,0:T(8,128)S(1)}, u32[]{:S(2)}, u32[]{:S(2)}) async-start(f32[32,136,128]{2,1,0:T(8,128)} %bitcast.63), calls=%async_computation.1 | async-start | bytes 4456448 | tf_op jit(solution)/shard_map/all_to_all | solution.py:501
  190.0 1.3 slice.46
  191.4 3.3 %collective-permute-start.17 = (f32[2,32,1024]{2,1,0:T(8,128)S(1)}, f32[2,32,1024]{2,1,0:T(8,128)S(1)}, u32[]{:S(2)}, u32[]{:S(2)}) collective-permute-start(f32[2,32,1024]{2,1,0:T(8,128)S(1)} %get-tuple-element.51), channel_id=1, source_target_pairs={{0,12},{4,0},{8,4},{12,8},{1,13},{5,1},{9,5},{13,9},{2,14},{6,2},{... | collective-permute-start | bytes 786440 | tf_op jit(solution)/shard_map/ppermute | solution.py:58
  195.7 10.7 %collective-permute-done.17.part3 = f32[2,32,1024]{2,1,0:T(8,128)S(1)} collective-permute-done((f32[2,32,1024]{2,1,0:T(8,128)S(1)}, f32[2,32,1024]{2,1,0:T(8,128)S(1)}, u32[]{:S(2)}, u32[]{:S(2)}) %collective-permute-start.17) | collective-permute-done | bytes 262176 | tf_op jit(solution)/shard_map/ppermute | solution.py:58
  206.4 3.5 %collective-permute-done.15.part1 = f32[2,32,1024]{2,1,0:T(8,128)S(1)} collective-permute-done((f32[2,32,1024]{2,1,0:T(8,128)S(1)}, f32[2,32,1024]{2,1,0:T(8,128)S(1)}, u32[]{:S(2)}, u32[]{:S(2)}) %collective-permute-start.15) | collective-permute-done | bytes 262176 | tf_op jit(solution)/shard_map/ppermute | solution.py:58
  209.9 10.4 %all-to-all-done.1 = f32[32,136,128]{2,1,0:T(8,128)S(1)} async-done(((f32[32,136,128]{2,1,0:T(8,128)}), f32[32,136,128]{2,1,0:T(8,128)S(1)}, u32[]{:S(2)}, u32[]{:S(2)}) %all-to-all-start.1) | async-done | bytes 2228256 | tf_op jit(solution)/shard_map/all_to_all | solution.py:501
  220.3 1.7 copy-done
  222.1 2.0 solve.1
  224.2 3.2 %collective-permute-start.31 = (f32[3,32,1024]{2,1,0:T(8,128)S(1)}, f32[3,32,1024]{2,1,0:T(8,128)S(1)}, u32[]{:S(2)}, u32[]{:S(2)}) collective-permute-start(f32[3,32,1024]{2,1,0:T(8,128)S(1)} %get-tuple-element.47.refs_0_.refs_8_), channel_id=1, source_target_pairs={{0,3},{1,0},{2,1},{3,2},{4,7},{5,4},{6,5},{7,6},{8,11},{9,8},{10,9... | collective-permute-start | bytes 1179656 | tf_op jit(solution)/shard_map/ppermute | solution.py:58
  227.4 1.5 collective-permute-start.27
  228.9 1.7 collective-permute-start.25
  230.7 6.7 %collective-permute-done.33.refs_14_ = f32[3,32,1024]{2,1,0:T(8,128)S(1)} collective-permute-done((f32[3,32,1024]{2,1,0:T(8,128)S(1)}, f32[3,32,1024]{2,1,0:T(8,128)S(1)}, u32[]{:S(2)}, u32[]{:S(2)}) %collective-permute-start.33) | collective-permute-done | bytes 393248 | tf_op jit(solution)/shard_map/ppermute | solution.py:58
  237.4 3.3 %collective-permute-start.26 = (f32[3,32,1024]{2,1,0:T(8,128)S(1)}, f32[3,32,1024]{2,1,0:T(8,128)S(1)}, u32[]{:S(2)}, u32[]{:S(2)}) collective-permute-start(f32[3,32,1024]{2,1,0:T(8,128)S(1)} %get-tuple-element.48.refs_1_.refs_9_), channel_id=1, source_target_pairs={{0,12},{4,0},{8,4},{12,8},{1,13},{5,1},{9,5},{13,9},{2,14},{6,2},{... | collective-permute-start | bytes 1179656 | tf_op jit(solution)/shard_map/ppermute | solution.py:58
  240.7 2.1 collective-permute-start.34
  242.8 3.0 %collective-permute-done.36.refs_15_ = f32[3,32,1024]{2,1,0:T(8,128)S(1)} collective-permute-done((f32[3,32,1024]{2,1,0:T(8,128)S(1)}, f32[3,32,1024]{2,1,0:T(8,128)S(1)}, u32[]{:S(2)}, u32[]{:S(2)}) %collective-permute-start.36) | collective-permute-done | bytes 393248 | tf_op jit(solution)/shard_map/ppermute | solution.py:58
  245.8 1.6 collective-permute-start.28
  247.4 3.3 %collective-permute-start.29 = (f32[3,32,1024]{2,1,0:T(8,128)S(1)}, f32[3,32,1024]{2,1,0:T(8,128)S(1)}, u32[]{:S(2)}, u32[]{:S(2)}) collective-permute-start(f32[3,32,1024]{2,1,0:T(8,128)S(1)} %collective-permute-done.26.refs_3_), channel_id=1, source_target_pairs={{0,12},{4,0},{8,4},{12,8},{1,13},{5,1},{9,5},{13,9},{2,14},{6,2},{... | collective-permute-start | bytes 1179656 | tf_op jit(solution)/shard_map/ppermute | solution.py:58
  250.6 1.9 collective-permute-done.30.refs_7_
  252.8 5.5 %collective-permute-done.28.refs_4_ = f32[3,32,1024]{2,1,0:T(8,128)S(1)} collective-permute-done((f32[3,32,1024]{2,1,0:T(8,128)S(1)}, f32[3,32,1024]{2,1,0:T(8,128)S(1)}, u32[]{:S(2)}, u32[]{:S(2)}) %collective-permute-start.28) | collective-permute-done | bytes 393248 | tf_op jit(solution)/shard_map/ppermute | solution.py:58
  258.4 4.4 %product.1 = (f32[16,8,32,128]{3,2,1,0:T(8,128)S(1)}, f32[2,128,1024]{2,1,0:T(8,128)S(1)}) custom-call(s32[3]{0:T(128)S(1)} %copy-done.3, f32[3,32,1024]{2,1,0:T(8,128)S(1)} %get-tuple-element.47.refs_0_.refs_8_, f32[3,32,1024]{2,1,0:T(8,128)S(1)} %get-tuple-element.48.refs_1_.refs_9_, f32[3,32,1024]{2,1,0:T(8,128)S(1)} %collective-permute-done.25.refs_2_, ...), custom_call_target="tpu_custom_call" | custom-call | flops 11000000512 | bytes 8388608 | tf_op jit(solution)/shard_map/product/pallas_call | solution.py:392
  262.7 1.3 copy-done.1
  264.1 5.1 %all-to-all-start.2 = ((f32[16,8,32,128]{3,2,1,0:T(8,128)}), f32[16,8,32,128]{3,2,1,0:T(8,128)}, u32[]{:S(2)}, u32[]{:S(2)}) async-start(f32[16,8,32,128]{3,2,1,0:T(8,128)} %copy-done.1), calls=%async_computation.2 | async-start | bytes 4194304 | tf_op jit(solution)/shard_map/all_to_all | solution.py:501
  269.2 2.8 base.1.before
  272.0 24.6 %all-to-all-done.2.change_in = f32[16,8,32,128]{3,2,1,0:T(8,128)} async-done(((f32[16,8,32,128]{3,2,1,0:T(8,128)}), f32[16,8,32,128]{3,2,1,0:T(8,128)}, u32[]{:S(2)}, u32[]{:S(2)}) %all-to-all-start.2) | async-done | bytes 2097184 | tf_op jit(solution)/shard_map/all_to_all | solution.py:501
  296.6 4.0 %finish.1 = f32[2,128,4096]{2,1,0:T(8,128)} custom-call(s32[3]{0:T(128)} %pad_add_fusion.position, f32[2,128,4096]{2,1,0:T(8,128)} %base.1.before, f32[2,128,4096]{2,1,0:T(8,128)} %bitcast.61, f32[16,8,32,128]{3,2,1,0:T(8,128)} %all-to-all-done.2.change_in), custom_call_target="tpu_custom_call", output_to_operand_aliasing={{}: (1, {})} | custom-call | tf_op jit(solution)/shard_map/finish/pallas_call | solution.py:471
  (92 shorter events, 13.6 us)
Async XLA Ops:
  1.0 10.6 %collective-permute-start = (f32[64,1024]{1,0:T(8,128)S(1)}, f32[64,1024]{1,0:T(8,128)S(1)}, u32[]{:S(2)}, u32[]{:S(2)}) collective-permute-start(f32[64,1024]{1,0:T(8,128)S(1)} %slice_bitcast_fusion), channel_id=1, source_target_pairs={{0,8},{4,12},{1,9},{5,13},{2,10},{6,14},{3,11},{7,15},{16,24},{20,... | collective-permute-start | bytes 786440 | tf_op jit(solution)/shard_map/ppermute | solution.py:510
  13.1 9.3 %collective-permute-start.5 = (f32[4,8,1024]{2,1,0:T(8,128)S(1)}, f32[4,8,1024]{2,1,0:T(8,128)S(1)}, u32[]{:S(2)}, u32[]{:S(2)}) collective-permute-start(f32[4,8,1024]{2,1,0:T(8,128)S(1)} %get-tuple-element.57), channel_id=1, source_target_pairs={{0,2},{1,3},{2,0},{3,1},{4,6},{5,7},{6,4},{7,5},{8,10},{9,11},{10,... | collective-permute-start | bytes 393224 | tf_op jit(solution)/shard_map/ppermute | solution.py:58
  16.4 8.0 %collective-permute-start.4 = (f32[4,8,1024]{2,1,0:T(8,128)S(1)}, f32[4,8,1024]{2,1,0:T(8,128)S(1)}, u32[]{:S(2)}, u32[]{:S(2)}) collective-permute-start(f32[4,8,1024]{2,1,0:T(8,128)S(1)} %get-tuple-element.57), channel_id=1, source_target_pairs={{0,3},{1,0},{2,1},{3,2},{4,7},{5,4},{6,5},{7,6},{8,11},{9,8},{10,9... | collective-permute-start | bytes 393224 | tf_op jit(solution)/shard_map/ppermute | solution.py:58
  17.5 7.0 %collective-permute-start.6 = (f32[4,8,1024]{2,1,0:T(8,128)S(1)}, f32[4,8,1024]{2,1,0:T(8,128)S(1)}, u32[]{:S(2)}, u32[]{:S(2)}) collective-permute-start(f32[4,8,1024]{2,1,0:T(8,128)S(1)} %get-tuple-element.57), channel_id=1, source_target_pairs={{0,1},{1,2},{2,3},{3,0},{4,5},{5,6},{6,7},{7,4},{8,9},{9,10},{10,1... | collective-permute-start | bytes 393224 | tf_op jit(solution)/shard_map/ppermute | solution.py:58
  18.4 8.0 %collective-permute-start.2 = (f32[4,8,1024]{2,1,0:T(8,128)S(1)}, f32[4,8,1024]{2,1,0:T(8,128)S(1)}, u32[]{:S(2)}, u32[]{:S(2)}) collective-permute-start(f32[4,8,1024]{2,1,0:T(8,128)S(1)} %get-tuple-element.58), channel_id=1, source_target_pairs={{0,8},{4,12},{8,0},{12,4},{1,9},{5,13},{9,1},{13,5},{2,10},{6,14},... | collective-permute-start | bytes 393224 | tf_op jit(solution)/shard_map/ppermute | solution.py:58
  22.4 5.0 %collective-permute-start.1 = (f32[4,8,1024]{2,1,0:T(8,128)S(1)}, f32[4,8,1024]{2,1,0:T(8,128)S(1)}, u32[]{:S(2)}, u32[]{:S(2)}) collective-permute-start(f32[4,8,1024]{2,1,0:T(8,128)S(1)} %get-tuple-element.58), channel_id=1, source_target_pairs={{0,12},{4,0},{8,4},{12,8},{1,13},{5,1},{9,5},{13,9},{2,14},{6,2},{... | collective-permute-start | bytes 393224 | tf_op jit(solution)/shard_map/ppermute | solution.py:58
  22.4 6.2 %collective-permute-start.3 = (f32[4,8,1024]{2,1,0:T(8,128)S(1)}, f32[4,8,1024]{2,1,0:T(8,128)S(1)}, u32[]{:S(2)}, u32[]{:S(2)}) collective-permute-start(f32[4,8,1024]{2,1,0:T(8,128)S(1)} %get-tuple-element.58), channel_id=1, source_target_pairs={{0,4},{4,8},{8,12},{12,0},{1,5},{5,9},{9,13},{13,1},{2,6},{6,10},{... | collective-permute-start | bytes 393224 | tf_op jit(solution)/shard_map/ppermute | solution.py:58
  24.5 20.3 %copy-start.4 = (f32[4,4,8,1024]{3,2,1,0:T(8,128)}, f32[4,4,8,1024]{3,2,1,0:T(8,128)S(1)}, u32[]{:S(2)}) copy-start(f32[4,4,8,1024]{3,2,1,0:T(8,128)S(1)} %pad_maximum_fusion.1.refs_5_) | copy-start | bytes 1572868
  28.6 16.1 %copy-start.5 = (f32[4,4,8,1024]{3,2,1,0:T(8,128)}, f32[4,4,8,1024]{3,2,1,0:T(8,128)S(1)}, u32[]{:S(2)}) copy-start(f32[4,4,8,1024]{3,2,1,0:T(8,128)S(1)} %pad_maximum_fusion.refs_0_) | copy-start | bytes 1572868
  28.7 16.1 %collective-permute-start.8 = (f32[4,4,8,1024]{3,2,1,0:T(8,128)S(1)}, f32[4,4,8,1024]{3,2,1,0:T(8,128)S(1)}, u32[]{:S(2)}, u32[]{:S(2)}) collective-permute-start(f32[4,4,8,1024]{3,2,1,0:T(8,128)S(1)} %pad_maximum_fusion.refs_0_), channel_id=1, source_target_pairs={{0,1},{1,2},{2,3},{3,0},{4,5},{5,6},{6,7},{7,4},{8,9},{9,10},{10,1... | collective-permute-start | bytes 1572872 | tf_op jit(solution)/shard_map/ppermute | solution.py:58
  29.4 15.4 %collective-permute-start.7 = (f32[4,4,8,1024]{3,2,1,0:T(8,128)S(1)}, f32[4,4,8,1024]{3,2,1,0:T(8,128)S(1)}, u32[]{:S(2)}, u32[]{:S(2)}) collective-permute-start(f32[4,4,8,1024]{3,2,1,0:T(8,128)S(1)} %pad_maximum_fusion.refs_0_), channel_id=1, source_target_pairs={{0,3},{1,0},{2,1},{3,2},{4,7},{5,4},{6,5},{7,6},{8,11},{9,8},{10,9... | collective-permute-start | bytes 1572872 | tf_op jit(solution)/shard_map/ppermute | solution.py:58
  32.0 12.9 %collective-permute-start.10 = (f32[4,4,8,1024]{3,2,1,0:T(8,128)S(1)}, f32[4,4,8,1024]{3,2,1,0:T(8,128)S(1)}, u32[]{:S(2)}, u32[]{:S(2)}) collective-permute-start(f32[4,4,8,1024]{3,2,1,0:T(8,128)S(1)} %pad_maximum_fusion.1.refs_5_), channel_id=1, source_target_pairs={{0,4},{4,8},{8,12},{12,0},{1,5},{5,9},{9,13},{13,1},{2,6},{6,10},{... | collective-permute-start | bytes 1572872 | tf_op jit(solution)/shard_map/ppermute | solution.py:58
  32.8 12.1 %collective-permute-start.9 = (f32[4,4,8,1024]{3,2,1,0:T(8,128)S(1)}, f32[4,4,8,1024]{3,2,1,0:T(8,128)S(1)}, u32[]{:S(2)}, u32[]{:S(2)}) collective-permute-start(f32[4,4,8,1024]{3,2,1,0:T(8,128)S(1)} %pad_maximum_fusion.1.refs_5_), channel_id=1, source_target_pairs={{0,12},{4,0},{8,4},{12,8},{1,13},{5,1},{9,5},{13,9},{2,14},{6,2},{... | collective-permute-start | bytes 1572872 | tf_op jit(solution)/shard_map/ppermute | solution.py:58
  44.8 7.3 %copy-start.6 = (f32[4,4,8,1024]{3,2,1,0:T(8,128)}, f32[4,4,8,1024]{3,2,1,0:T(8,128)S(1)}, u32[]{:S(2)}) copy-start(f32[4,4,8,1024]{3,2,1,0:T(8,128)S(1)} %collective-permute-done.8.refs_4_) | copy-start | bytes 1572868
  44.8 7.3 %copy-start.7 = (f32[4,4,8,1024]{3,2,1,0:T(8,128)}, f32[4,4,8,1024]{3,2,1,0:T(8,128)S(1)}, u32[]{:S(2)}) copy-start(f32[4,4,8,1024]{3,2,1,0:T(8,128)S(1)} %collective-permute-done.7.refs_1_) | copy-start | bytes 1572868
  44.8 7.3 %copy-start.8 = (f32[4,4,8,1024]{3,2,1,0:T(8,128)}, f32[4,4,8,1024]{3,2,1,0:T(8,128)S(1)}, u32[]{:S(2)}) copy-start(f32[4,4,8,1024]{3,2,1,0:T(8,128)S(1)} %collective-permute-done.10.refs_9_) | copy-start | bytes 1572868
  44.8 7.3 %copy-start.9 = (f32[4,4,8,1024]{3,2,1,0:T(8,128)}, f32[4,4,8,1024]{3,2,1,0:T(8,128)S(1)}, u32[]{:S(2)}) copy-start(f32[4,4,8,1024]{3,2,1,0:T(8,128)S(1)} %collective-permute-done.9.refs_6_) | copy-start | bytes 1572868
  45.0 14.5 %collective-permute-start.13 = (f32[2,4,8,1024]{3,2,1,0:T(8,128)S(1)}, f32[2,4,8,1024]{3,2,1,0:T(8,128)S(1)}, u32[]{:S(2)}, u32[]{:S(2)}) collective-permute-start(f32[2,4,8,1024]{3,2,1,0:T(8,128)S(1)} %slice.44), channel_id=1, source_target_pairs={{0,4},{4,8},{8,12},{12,0},{1,5},{5,9},{9,13},{13,1},{2,6},{6,10},{... | collective-permute-start | bytes 786440 | tf_op jit(solution)/shard_map/ppermute | solution.py:58
  45.0 14.4 %collective-permute-start.14 = (f32[2,4,8,1024]{3,2,1,0:T(8,128)S(1)}, f32[2,4,8,1024]{3,2,1,0:T(8,128)}, u32[]{:S(2)}, u32[]{:S(2)}) collective-permute-start(f32[2,4,8,1024]{3,2,1,0:T(8,128)S(1)} %slice.45), channel_id=1, source_target_pairs={{0,12},{4,0},{8,4},{12,8},{1,13},{5,1},{9,5},{13,9},{2,14},{6,2},{... | collective-permute-start | bytes 786440 | tf_op jit(solution)/shard_map/ppermute | solution.py:58
  48.3 11.2 %collective-permute-start.11 = (f32[2,4,8,1024]{3,2,1,0:T(8,128)S(1)}, f32[2,4,8,1024]{3,2,1,0:T(8,128)}, u32[]{:S(2)}, u32[]{:S(2)}) collective-permute-start(f32[2,4,8,1024]{3,2,1,0:T(8,128)S(1)} %slice.42), channel_id=1, source_target_pairs={{0,1},{1,2},{2,3},{3,0},{4,5},{5,6},{6,7},{7,4},{8,9},{9,10},{10,1... | collective-permute-start | bytes 786440 | tf_op jit(solution)/shard_map/ppermute | solution.py:58
  48.3 11.2 %collective-permute-start.12 = (f32[2,4,8,1024]{3,2,1,0:T(8,128)S(1)}, f32[2,4,8,1024]{3,2,1,0:T(8,128)}, u32[]{:S(2)}, u32[]{:S(2)}) collective-permute-start(f32[2,4,8,1024]{3,2,1,0:T(8,128)S(1)} %slice.43), channel_id=1, source_target_pairs={{0,3},{1,0},{2,1},{3,2},{4,7},{5,4},{6,5},{7,6},{8,11},{9,8},{10,9... | collective-permute-start | bytes 786440 | tf_op jit(solution)/shard_map/ppermute | solution.py:58
  52.1 110.7 %all-to-all-start = ((f32[128,128,128]{2,1,0:T(8,128)}), f32[128,128,128]{2,1,0:T(8,128)}, u32[]{:S(2)}, u32[]{:S(2)}) async-start(f32[128,128,128]{2,1,0:T(8,128)} %turn.1), calls=%async_computation | async-start | bytes 16777216 | tf_op jit(solution)/shard_map/all_to_all | solution.py:501
  146.0 16.8 %collective-permute-start.24 = (s32[16,128]{1,0:T(8,128)}, s32[16,128]{1,0:T(8,128)S(1)}, u32[]{:S(2)}, u32[]{:S(2)}) collective-permute-start(s32[16,128]{1,0:T(8,128)} %get-tuple-element.44), channel_id=1, source_target_pairs={{0,112},{16,96},{32,80},{48,64},{64,48},{80,32},{96,16},{112,0},{1... | collective-permute-start | bytes 24584 | tf_op jit(solution)/shard_map/ppermute | solution.py:63
  148.6 14.1 %collective-permute-start.23 = (s32[16,128]{1,0:T(8,128)}, s32[16,128]{1,0:T(8,128)S(1)}, u32[]{:S(2)}, u32[]{:S(2)}) collective-permute-start(s32[16,128]{1,0:T(8,128)} %get-tuple-element.44), channel_id=1, source_target_pairs={{0,96},{16,112},{32,64},{48,80},{64,32},{80,48},{96,0},{112,16},{1... | collective-permute-start | bytes 24584 | tf_op jit(solution)/shard_map/ppermute | solution.py:63
  149.2 13.6 %collective-permute-start.22 = (s32[16,128]{1,0:T(8,128)}, s32[16,128]{1,0:T(8,128)S(1)}, u32[]{:S(2)}, u32[]{:S(2)}) collective-permute-start(s32[16,128]{1,0:T(8,128)} %get-tuple-element.44), channel_id=1, source_target_pairs={{0,80},{16,64},{32,112},{48,96},{64,16},{80,0},{96,48},{112,32},{1... | collective-permute-start | bytes 24584 | tf_op jit(solution)/shard_map/ppermute | solution.py:63
  150.4 12.4 %collective-permute-start.21 = (s32[16,128]{1,0:T(8,128)}, s32[16,128]{1,0:T(8,128)S(1)}, u32[]{:S(2)}, u32[]{:S(2)}) collective-permute-start(s32[16,128]{1,0:T(8,128)} %get-tuple-element.44), channel_id=1, source_target_pairs={{0,64},{16,80},{32,96},{48,112},{64,0},{80,16},{96,32},{112,48},{1... | collective-permute-start | bytes 24584 | tf_op jit(solution)/shard_map/ppermute | solution.py:63
  152.3 1.4 collective-permute-start.18
  153.7 5.7 %collective-permute-start.19 = (s32[16,128]{1,0:T(8,128)}, s32[16,128]{1,0:T(8,128)S(1)}, u32[]{:S(2)}, u32[]{:S(2)}) collective-permute-start(s32[16,128]{1,0:T(8,128)} %get-tuple-element.44), channel_id=1, source_target_pairs={{0,32},{16,48},{32,0},{48,16},{64,96},{80,112},{96,64},{112,80},{1... | collective-permute-start | bytes 24584 | tf_op jit(solution)/shard_map/ppermute | solution.py:63
  159.5 3.3 %collective-permute-start.20 = (s32[16,128]{1,0:T(8,128)}, s32[16,128]{1,0:T(8,128)S(1)}, u32[]{:S(2)}, u32[]{:S(2)}) collective-permute-start(s32[16,128]{1,0:T(8,128)} %get-tuple-element.44), channel_id=1, source_target_pairs={{0,48},{16,32},{32,16},{48,0},{64,112},{80,96},{96,80},{112,64},{1... | collective-permute-start | bytes 24584 | tf_op jit(solution)/shard_map/ppermute | solution.py:63
  183.5 36.8 %copy-start.3 = (s32[3]{0:T(128)S(1)}, s32[3]{0:T(128)}, u32[]{:S(2)}) copy-start(s32[3]{0:T(128)} %pad_add_fusion.position) | copy-start | bytes 40
  183.5 36.8 %all-to-all-start.1 = ((f32[32,136,128]{2,1,0:T(8,128)}), f32[32,136,128]{2,1,0:T(8,128)S(1)}, u32[]{:S(2)}, u32[]{:S(2)}) async-start(f32[32,136,128]{2,1,0:T(8,128)} %bitcast.63), calls=%async_computation.1 | async-start | bytes 4456448 | tf_op jit(solution)/shard_map/all_to_all | solution.py:501
  191.4 15.0 %collective-permute-start.17 = (f32[2,32,1024]{2,1,0:T(8,128)S(1)}, f32[2,32,1024]{2,1,0:T(8,128)S(1)}, u32[]{:S(2)}, u32[]{:S(2)}) collective-permute-start(f32[2,32,1024]{2,1,0:T(8,128)S(1)} %get-tuple-element.51), channel_id=1, source_target_pairs={{0,12},{4,0},{8,4},{12,8},{1,13},{5,1},{9,5},{13,9},{2,14},{6,2},{... | collective-permute-start | bytes 786440 | tf_op jit(solution)/shard_map/ppermute | solution.py:58
  194.8 11.6 %collective-permute-start.16 = (f32[2,32,1024]{2,1,0:T(8,128)S(1)}, f32[2,32,1024]{2,1,0:T(8,128)S(1)}, u32[]{:S(2)}, u32[]{:S(2)}) collective-permute-start(f32[2,32,1024]{2,1,0:T(8,128)S(1)} %get-tuple-element.52), channel_id=1, source_target_pairs={{0,8},{4,12},{8,0},{12,4},{1,9},{5,13},{9,1},{13,5},{2,10},{6,14},... | collective-permute-start | bytes 786440 | tf_op jit(solution)/shard_map/ppermute | solution.py:58
  195.1 14.8 %collective-permute-start.15 = (f32[2,32,1024]{2,1,0:T(8,128)S(1)}, f32[2,32,1024]{2,1,0:T(8,128)S(1)}, u32[]{:S(2)}, u32[]{:S(2)}) collective-permute-start(f32[2,32,1024]{2,1,0:T(8,128)S(1)} %get-tuple-element.53), channel_id=1, source_target_pairs={{0,4},{4,8},{8,12},{12,0},{1,5},{5,9},{9,13},{13,1},{2,6},{6,10},{... | collective-permute-start | bytes 786440 | tf_op jit(solution)/shard_map/ppermute | solution.py:58
  224.1 13.3 %collective-permute-start.33 = (f32[3,32,1024]{2,1,0:T(8,128)S(1)}, f32[3,32,1024]{2,1,0:T(8,128)S(1)}, u32[]{:S(2)}, u32[]{:S(2)}) collective-permute-start(f32[3,32,1024]{2,1,0:T(8,128)S(1)} %get-tuple-element.47.refs_0_.refs_8_), channel_id=1, source_target_pairs={{0,1},{1,2},{2,3},{3,0},{4,5},{5,6},{6,7},{7,4},{8,9},{9,10},{10,1... | collective-permute-start | bytes 1179656 | tf_op jit(solution)/shard_map/ppermute | solution.py:58
  224.2 13.2 %collective-permute-start.31 = (f32[3,32,1024]{2,1,0:T(8,128)S(1)}, f32[3,32,1024]{2,1,0:T(8,128)S(1)}, u32[]{:S(2)}, u32[]{:S(2)}) collective-permute-start(f32[3,32,1024]{2,1,0:T(8,128)S(1)} %get-tuple-element.47.refs_0_.refs_8_), channel_id=1, source_target_pairs={{0,3},{1,0},{2,1},{3,2},{4,7},{5,4},{6,5},{7,6},{8,11},{9,8},{10,9... | collective-permute-start | bytes 1179656 | tf_op jit(solution)/shard_map/ppermute | solution.py:58
  227.4 13.3 %collective-permute-start.27 = (f32[3,32,1024]{2,1,0:T(8,128)S(1)}, f32[3,32,1024]{2,1,0:T(8,128)S(1)}, u32[]{:S(2)}, u32[]{:S(2)}) collective-permute-start(f32[3,32,1024]{2,1,0:T(8,128)S(1)} %get-tuple-element.47.refs_0_.refs_8_), channel_id=1, source_target_pairs={{0,4},{4,8},{8,12},{12,0},{1,5},{5,9},{9,13},{13,1},{2,6},{6,10},{... | collective-permute-start | bytes 1179656 | tf_op jit(solution)/shard_map/ppermute | solution.py:58
  228.9 11.8 %collective-permute-start.25 = (f32[3,32,1024]{2,1,0:T(8,128)S(1)}, f32[3,32,1024]{2,1,0:T(8,128)S(1)}, u32[]{:S(2)}, u32[]{:S(2)}) collective-permute-start(f32[3,32,1024]{2,1,0:T(8,128)S(1)} %get-tuple-element.47.refs_0_.refs_8_), channel_id=1, source_target_pairs={{0,12},{4,0},{8,4},{12,8},{1,13},{5,1},{9,5},{13,9},{2,14},{6,2},{... | collective-permute-start | bytes 1179656 | tf_op jit(solution)/shard_map/ppermute | solution.py:58
  230.7 15.2 %collective-permute-start.36 = (f32[3,32,1024]{2,1,0:T(8,128)S(1)}, f32[3,32,1024]{2,1,0:T(8,128)S(1)}, u32[]{:S(2)}, u32[]{:S(2)}) collective-permute-start(f32[3,32,1024]{2,1,0:T(8,128)S(1)} %get-tuple-element.48.refs_1_.refs_9_), channel_id=1, source_target_pairs={{0,1},{1,2},{2,3},{3,0},{4,5},{5,6},{6,7},{7,4},{8,9},{9,10},{10,1... | collective-permute-start | bytes 1179656 | tf_op jit(solution)/shard_map/ppermute | solution.py:58
  237.4 10.0 %collective-permute-start.32 = (f32[3,32,1024]{2,1,0:T(8,128)S(1)}, f32[3,32,1024]{2,1,0:T(8,128)S(1)}, u32[]{:S(2)}, u32[]{:S(2)}) collective-permute-start(f32[3,32,1024]{2,1,0:T(8,128)S(1)} %get-tuple-element.48.refs_1_.refs_9_), channel_id=1, source_target_pairs={{0,3},{1,0},{2,1},{3,2},{4,7},{5,4},{6,5},{7,6},{8,11},{9,8},{10,9... | collective-permute-start | bytes 1179656 | tf_op jit(solution)/shard_map/ppermute | solution.py:58
  237.4 10.0 %collective-permute-start.26 = (f32[3,32,1024]{2,1,0:T(8,128)S(1)}, f32[3,32,1024]{2,1,0:T(8,128)S(1)}, u32[]{:S(2)}, u32[]{:S(2)}) collective-permute-start(f32[3,32,1024]{2,1,0:T(8,128)S(1)} %get-tuple-element.48.refs_1_.refs_9_), channel_id=1, source_target_pairs={{0,12},{4,0},{8,4},{12,8},{1,13},{5,1},{9,5},{13,9},{2,14},{6,2},{... | collective-permute-start | bytes 1179656 | tf_op jit(solution)/shard_map/ppermute | solution.py:58
  240.7 11.9 %collective-permute-start.30 = (f32[3,32,1024]{2,1,0:T(8,128)S(1)}, f32[3,32,1024]{2,1,0:T(8,128)S(1)}, u32[]{:S(2)}, u32[]{:S(2)}) collective-permute-start(f32[3,32,1024]{2,1,0:T(8,128)S(1)} %get-tuple-element.48.refs_1_.refs_9_), channel_id=1, source_target_pairs={{0,4},{4,8},{8,12},{12,0},{1,5},{5,9},{9,13},{13,1},{2,6},{6,10},{... | collective-permute-start | bytes 1179656 | tf_op jit(solution)/shard_map/ppermute | solution.py:58
  240.7 12.2 %collective-permute-start.34 = (f32[3,32,1024]{2,1,0:T(8,128)S(1)}, f32[3,32,1024]{2,1,0:T(8,128)S(1)}, u32[]{:S(2)}, u32[]{:S(2)}) collective-permute-start(f32[3,32,1024]{2,1,0:T(8,128)S(1)} %collective-permute-done.33.refs_14_), channel_id=1, source_target_pairs={{0,1},{1,2},{2,3},{3,0},{4,5},{5,6},{6,7},{7,4},{8,9},{9,10},{10,1... | collective-permute-start | bytes 1179656 | tf_op jit(solution)/shard_map/ppermute | solution.py:58
  245.8 12.5 %collective-permute-start.28 = (f32[3,32,1024]{2,1,0:T(8,128)S(1)}, f32[3,32,1024]{2,1,0:T(8,128)S(1)}, u32[]{:S(2)}, u32[]{:S(2)}) collective-permute-start(f32[3,32,1024]{2,1,0:T(8,128)S(1)} %collective-permute-done.27.refs_6_), channel_id=1, source_target_pairs={{0,4},{4,8},{8,12},{12,0},{1,5},{5,9},{9,13},{13,1},{2,6},{6,10},{... | collective-permute-start | bytes 1179656 | tf_op jit(solution)/shard_map/ppermute | solution.py:58
  247.4 11.0 %collective-permute-start.35 = (f32[3,32,1024]{2,1,0:T(8,128)S(1)}, f32[3,32,1024]{2,1,0:T(8,128)S(1)}, u32[]{:S(2)}, u32[]{:S(2)}) collective-permute-start(f32[3,32,1024]{2,1,0:T(8,128)S(1)} %collective-permute-done.32.refs_11_), channel_id=1, source_target_pairs={{0,3},{1,0},{2,1},{3,2},{4,7},{5,4},{6,5},{7,6},{8,11},{9,8},{10,9... | collective-permute-start | bytes 1179656 | tf_op jit(solution)/shard_map/ppermute | solution.py:58
  247.4 11.0 %collective-permute-start.29 = (f32[3,32,1024]{2,1,0:T(8,128)S(1)}, f32[3,32,1024]{2,1,0:T(8,128)S(1)}, u32[]{:S(2)}, u32[]{:S(2)}) collective-permute-start(f32[3,32,1024]{2,1,0:T(8,128)S(1)} %collective-permute-done.26.refs_3_), channel_id=1, source_target_pairs={{0,12},{4,0},{8,4},{12,8},{1,13},{5,1},{9,5},{13,9},{2,14},{6,2},{... | collective-permute-start | bytes 1179656 | tf_op jit(solution)/shard_map/ppermute | solution.py:58
  264.1 5.1 %copy-start.2 = (f32[128,1024]{1,0:T(8,128)S(1)}, f32[128,1024]{1,0:T(8,128)}, u32[]{:S(2)}) copy-start(f32[128,1024]{1,0:T(8,128)} %get-tuple-element.42.lead_rows) | copy-start | bytes 1572868
  264.1 32.6 %all-to-all-start.2 = ((f32[16,8,32,128]{3,2,1,0:T(8,128)}), f32[16,8,32,128]{3,2,1,0:T(8,128)}, u32[]{:S(2)}, u32[]{:S(2)}) async-start(f32[16,8,32,128]{3,2,1,0:T(8,128)} %copy-done.1), calls=%async_computation.2 | async-start | bytes 4194304 | tf_op jit(solution)/shard_map/all_to_all | solution.py:501
  (4 other events, 4.4 us)
